TPU v7x, 32 devices: a whole 2x2x4 slice. The times are simulated.
32 devices in a mesh: item: 4 (over y, x), lat: 8 (over z, core).
Axes of the slice: x: 2, y: 2, z: 4, core: 2. Of those that a mesh axis runs over, the one named last changes fastest.
Arguments:
- noisy_state: float32 [4, 83, 8192], P('item', None, 'lat'), may hold values from -6 to 6
- target_state: float32 [4, 83, 8192], P('item', None, 'lat'), may hold values from -6 to 6
- sigmas: float32 [4], P('item'), may hold values from 0.5 to 8
- sh_basis: float32 [64, 8192], P(None, 'lat'), may hold values from -0.0625 to 0.0625
- lengths: int32 [4, 16], P('item'), may hold values from 1 to 4096, 8192 in all within a row
- grid_edges: int32 [8192, 4], P('lat'), may hold values from 0 to 1023
- mesh_edges: int32 [8192, 16], P('lat'), may hold values from 0 to 3071
- dec_edges: int32 [8192, 3], P('lat'), may hold values from 0 to 3071
- tables_copy: bfloat16 [2, 83, 512], replicated, may hold values from -0.625 to 0.625
- tables_master: float32 [2, 83, 512], P(None, None, 'lat'), may hold values from -0.625 to 0.625
- tables_first: float32 [2, 83, 512], P(None, None, 'lat'), may hold values from -1 to 1, as said below
- tables_second: float32 [2, 83, 512], P(None, None, 'lat'), may hold values from 0 to 1, as said below
- tables_ema: float32 [2, 83, 512], P(None, None, 'lat'), may hold values from -0.625 to 0.625
- attn_copy: bfloat16 [512, 2048], replicated, may hold values from -0.25 to 0.25
- attn_master: float32 [512, 2048], P('lat'), may hold values from -0.25 to 0.25
- attn_first: float32 [512, 2048], P('lat'), may hold values from -1 to 1, as said below
- attn_second: float32 [512, 2048], P('lat'), may hold values from 0 to 1, as said below
- attn_ema: float32 [512, 2048], P('lat'), may hold values from -0.25 to 0.25
- mlp_copy: bfloat16 [3, 512, 4096], replicated, may hold values from -0.25 to 0.25
- mlp_master: float32 [3, 512, 4096], P(None, 'lat'), may hold values from -0.25 to 0.25
- mlp_first: float32 [3, 512, 4096], P(None, 'lat'), may hold values from -1 to 1, as said below
- mlp_second: float32 [3, 512, 4096], P(None, 'lat'), may hold values from 0 to 1, as said below
- mlp_ema: float32 [3, 512, 4096], P(None, 'lat'), may hold values from -0.25 to 0.25
- gains_copy: bfloat16 [5, 512], replicated, may hold values from 0.5 to 6, as said below
- gains_master: float32 [5, 512], P(None, 'lat'), may hold values from 0.5 to 6, as said below
- gains_first: float32 [5, 512], P(None, 'lat'), may hold values from -1 to 1, as said below
- gains_second: float32 [5, 512], P(None, 'lat'), may hold values from 0 to 1, as said below
- gains_ema: float32 [5, 512], P(None, 'lat'), may hold values from 0.2 to 6, as said below
Outputs:
- loss_sum: float32 [], replicated
- grad_norm: float32 [], replicated
- tables_first_new: float32 [2, 83, 512], P(None, None, 'lat')
- tables_second_new: float32 [2, 83, 512], P(None, None, 'lat')
- tables_master_new: float32 [2, 83, 512], P(None, None, 'lat')
- tables_ema_new: float32 [2, 83, 512], P(None, None, 'lat')
- tables_copy_new: bfloat16 [2, 83, 512], P(None, None, 'lat')
- attn_first_new: float32 [512, 2048], P('lat')
- attn_second_new: float32 [512, 2048], P('lat')
- attn_master_new: float32 [512, 2048], P('lat')
- attn_ema_new: float32 [512, 2048], P('lat')
- attn_copy_new: bfloat16 [512, 2048], P('lat')
- mlp_first_new: float32 [3, 512, 4096], P(None, 'lat')
- mlp_second_new: float32 [3, 512, 4096], P(None, 'lat')
- mlp_master_new: float32 [3, 512, 4096], P(None, 'lat')
- mlp_ema_new: float32 [3, 512, 4096], P(None, 'lat')
- mlp_copy_new: bfloat16 [3, 512, 4096], P(None, 'lat')
- gains_first_new: float32 [5, 512], P(None, 'lat')
- gains_second_new: float32 [5, 512], P(None, 'lat')
- gains_master_new: float32 [5, 512], P(None, 'lat')
- gains_ema_new: float32 [5, 512], P(None, 'lat')
- gains_copy_new: bfloat16 [5, 512], P(None, 'lat')
Inputs may be any that keep to these rules, and one draw needn't show every extreme that they name: The lengths of an item sum to 8192. `tables_first`: first moments of both signs. `tables_second`: Positive. `attn_first`: first moments of both signs. `attn_second`: Positive. `mlp_first`: first moments of both signs. `mlp_second`: Positive. `gains_first`: first moments of both signs. `gains_second`: Positive. `gains_copy`: Positive. `gains_master`: Positive. `gains_ema`: Positive.
All inputs are finite; a program needn't handle non-finite values.
Results may differ from a plain program's by a relative error of at most 0.0076.
Values may be sent and summed in bfloat16 or wider, within the bound.
No kernel may reach another device: no remote copies, remote signals or barrier semaphores. Data moves between devices by JAX's collectives and lax.ppermute only.
A program may use at most 512 MiB of HBM per device.

v0:
```python
import jax
import jax.numpy as jnp
from jax import lax
from jax.sharding import PartitionSpec as P

HEADS = 4
STEP = 10


EPS_NORM = 1e-05
CLIP_LEVEL = 1.0
BETA_ONE = 0.9
BETA_TWO = 0.999
ADAM_EPS = 1e-08
EMA_DECAY = 0.9
RATE_MATRIX = 0.05
RATE_GAIN = 0.3
WEIGHT_DECAY = 0.1
HIGH_PRECISION = lax.Precision.HIGHEST


def padded(shard, sides, width):
    for axis, dim in sides:
        size, length = (lax.axis_size(axis), shard.shape[dim])
        up = [(i, (i + 1) % size) for i in range(size - 1)]
        down = [(j, i) for i, j in up]
        last = lax.slice_in_dim(shard, length - width, length, axis=dim)
        initial = lax.slice_in_dim(shard, 0, width, axis=dim)
        before = lax.ppermute(last, axis, up)
        after = lax.ppermute(initial, axis, down)
        shard = jnp.concatenate([before, shard, after], axis=dim)
    return shard


def contract(left, right, left_dim, right_dim):
    return lax.dot_general(
        left, right, (((left_dim,), (right_dim,)), ((), ())), preferred_element_type=jnp.float32
    )


def layer_norm(values, gain_row):
    center = values - jnp.mean(values, axis=-1, keepdims=True)
    spread = jnp.mean(center * center, axis=-1, keepdims=True)
    return center * lax.rsqrt(spread + EPS_NORM) * gain_row


def crop_of(crop_ends, nodes):
    return jnp.sum((crop_ends <= nodes[..., None]).astype(jnp.int32), axis=-1)


def mlp_forward(values, gain_row, weights):
    hidden = weights.shape[1] // 2
    normed = layer_norm(values, gain_row).astype(jnp.bfloat16)
    before = jnp.dot(normed, weights[:, :hidden], preferred_element_type=jnp.float32)
    active = jax.nn.gelu(before).astype(jnp.bfloat16)
    return (values + contract(active, weights[:, hidden:], 1, 1), (values, normed, before, active))


def mlp_backward(upstream, kept, gain_row, weights):
    values, normed, before, active = kept
    hidden = weights.shape[1] // 2
    rounded_values = upstream.astype(jnp.bfloat16)
    grad_down = contract(rounded_values, active, 0, 0)
    grad_active = jnp.dot(rounded_values, weights[:, hidden:], preferred_element_type=jnp.float32)
    grad_before = jax.vjp(jax.nn.gelu, before)[1](grad_active)[0].astype(jnp.bfloat16)
    grad_up = contract(normed, grad_before, 0, 0)
    grad_normed = contract(grad_before, weights[:, :hidden], 1, 1)
    grad_values, grad_gain = jax.vjp(layer_norm, values, gain_row)[1](grad_normed)
    return (upstream + grad_values, grad_gain, jnp.concatenate([grad_up, grad_down], axis=1))


def outer_rims(grad_window):
    input_rows = grad_window.shape[0] // 3
    return jnp.concatenate([grad_window[:input_rows], grad_window[2 * input_rows :]], axis=0)


def fold_rims(grad_window, arrived):
    input_rows = grad_window.shape[0] // 3
    return (
        grad_window[input_rows : 2 * input_rows] + arrived[:input_rows] + arrived[3 * input_rows :]
    )


def split_heads(queries, neighbours):
    input_rows, model_width = queries.shape
    head_width = model_width // HEADS
    split_query_heads = queries.reshape(input_rows, HEADS, head_width)
    key_head_rows = neighbours[..., :model_width].reshape(input_rows, -1, HEADS, head_width)
    value_head_rows = neighbours[..., model_width:].reshape(input_rows, -1, HEADS, head_width)
    return (split_query_heads, key_head_rows, value_head_rows, head_width ** (-0.5))


def attention_forward(queries, neighbours, allowed):
    split_query_heads, key_head_rows, value_head_rows, scale_factor = split_heads(
        queries, neighbours
    )
    score_matrix = (
        jnp.einsum(
            "yza,yvza->yzv", split_query_heads, key_head_rows, preferred_element_type=jnp.float32
        )
        * scale_factor
    )
    score_matrix = jnp.where(allowed[:, None, :], score_matrix, -1e30)
    softmax_probs = jax.nn.softmax(score_matrix, axis=-1)
    rounded_values = softmax_probs.astype(jnp.bfloat16)
    attended_values = jnp.einsum(
        "piv,pviu->piu", rounded_values, value_head_rows, preferred_element_type=jnp.float32
    )
    return (attended_values.reshape(queries.shape), softmax_probs, rounded_values)


def attention_backward(grad_attended, queries, neighbours, softmax_probs, rounded_values):
    split_query_heads, key_head_rows, value_head_rows, scale_factor = split_heads(
        queries, neighbours
    )
    input_rows, model_width = queries.shape
    grad_head_rows = grad_attended.reshape(split_query_heads.shape)
    grad_probs = jnp.einsum(
        "yza,yvza->yzv", grad_head_rows, value_head_rows, preferred_element_type=jnp.float32
    )
    grad_values = jnp.einsum(
        "tnr,tns->trns", rounded_values, grad_head_rows, preferred_element_type=jnp.float32
    )
    grad_score_matrix = softmax_probs * (
        grad_probs - jnp.sum(softmax_probs * grad_probs, axis=-1, keepdims=True)
    )
    grad_score_matrix = grad_score_matrix.astype(jnp.bfloat16)
    grad_q = (
        jnp.einsum(
            "piv,pviu->piu", grad_score_matrix, key_head_rows, preferred_element_type=jnp.float32
        )
        * scale_factor
    )
    grad_keys = (
        jnp.einsum(
            "tnr,tns->trns",
            grad_score_matrix,
            split_query_heads,
            preferred_element_type=jnp.float32,
        )
        * scale_factor
    )
    key_count = neighbours.shape[1]
    grad_near = jnp.concatenate(
        [
            grad_keys.reshape(input_rows, key_count, model_width),
            grad_values.reshape(input_rows, key_count, model_width),
        ],
        axis=-1,
    )
    return (grad_q.reshape(input_rows, model_width), grad_near)


def adam_update(gradient, master, moment_one, moment_two, average, step_rate, decay_rate):
    one_new = BETA_ONE * moment_one + (1.0 - BETA_ONE) * gradient
    two_new = BETA_TWO * moment_two + (1.0 - BETA_TWO) * gradient * gradient
    one_hat = one_new / (1.0 - BETA_ONE**STEP)
    two_hat = two_new / (1.0 - BETA_TWO**STEP)
    master_new = master - step_rate * (
        one_hat / (jnp.sqrt(two_hat) + ADAM_EPS) + decay_rate * master
    )
    average_new = EMA_DECAY * average + (1.0 - EMA_DECAY) * master_new
    return (one_new, two_new, master_new, average_new, master_new.astype(jnp.bfloat16))


def shards(
    noisy_state,
    target_state,
    sigmas,
    sh_basis,
    lengths,
    grid_edges,
    mesh_edges,
    dec_edges,
    tables_copy,
    tables_master,
    tables_first,
    tables_second,
    tables_ema,
    attn_copy,
    attn_master,
    attn_first,
    attn_second,
    attn_ema,
    mlp_copy,
    mlp_master,
    mlp_first,
    mlp_second,
    mlp_ema,
    gains_copy,
    gains_master,
    gains_first,
    gains_second,
    gains_ema,
):
    band_index = lax.axis_index("lat")
    node_rows = mesh_edges.shape[0]
    grid_rows = noisy_state.shape[2]
    model_width = attn_copy.shape[0]
    gains = gains_copy.astype(jnp.float32)
    noise_level = sigmas[0]
    square = noise_level * noise_level
    scale_in = lax.rsqrt(square + 1.0)
    scale_skip = 1.0 / (square + 1.0)
    scale_out = noise_level * scale_in
    weight_loss = (square + 1.0) / square
    noisy_field = noisy_state[0]
    target_field = target_state[0]
    inputs = (scale_in * noisy_field).astype(jnp.bfloat16)
    embedded = contract(inputs, tables_copy[0], 0, 0)
    pooled = jnp.mean(embedded[grid_edges], axis=1)
    encoded, kept_enc = mlp_forward(pooled, gains[0], mlp_copy[0])
    normed_attn = layer_norm(encoded, gains[1]).astype(jnp.bfloat16)
    project = jnp.dot(
        normed_attn, attn_copy[:, : 3 * model_width], preferred_element_type=jnp.float32
    ).astype(jnp.bfloat16)
    queries = project[:, :model_width]
    key_values = project[:, model_width:]
    window = padded(key_values, (("lat", 0),), node_rows)
    crop_ends = jnp.cumsum(lengths[0])
    own_nodes = band_index * node_rows + jnp.arange(node_rows)
    near_nodes = (band_index - 1) * node_rows + mesh_edges
    inside = (near_nodes >= 0) & (near_nodes < lax.axis_size("lat") * node_rows)
    allowed = inside & (crop_of(crop_ends, near_nodes) == crop_of(crop_ends, own_nodes)[:, None])
    allowed = jnp.concatenate([jnp.ones((node_rows, 1), jnp.bool_), allowed], axis=1)
    neighbours = jnp.concatenate([key_values[:, None], window[mesh_edges]], axis=1)
    attended_values, softmax_probs, rounded_probs = attention_forward(queries, neighbours, allowed)
    attended_values = attended_values.astype(jnp.bfloat16)
    residual = encoded + jnp.dot(
        attended_values, attn_copy[:, 3 * model_width :], preferred_element_type=jnp.float32
    )
    latent, kept_proc = mlp_forward(residual, gains[2], mlp_copy[1])
    latent_window = padded(latent.astype(jnp.bfloat16), (("lat", 0),), node_rows)
    gathered = jnp.mean(latent_window[dec_edges].astype(jnp.float32), axis=1)
    decoded, kept_dec = mlp_forward(embedded + gathered, gains[3], mlp_copy[2])
    final_normed = layer_norm(decoded, gains[4]).astype(jnp.bfloat16)
    output = contract(tables_copy[1], final_normed, 1, 1)
    error_field = scale_skip * noisy_field + scale_out * output - target_field
    partial_value = lax.dot_general(
        error_field,
        sh_basis,
        (((1,), (1,)), ((), ())),
        precision=HIGH_PRECISION,
        preferred_element_type=jnp.float32,
    )
    coeffs = lax.psum(partial_value, "lat")
    slice_width = coeffs.shape[1] // lax.axis_size("lat")
    own_coeffs = lax.dynamic_slice_in_dim(coeffs, band_index * slice_width, slice_width, 1)
    loss_item = weight_loss * jnp.sum(own_coeffs * own_coeffs)
    grad_coeffs = 2.0 * weight_loss * coeffs
    grad_error = jnp.dot(
        grad_coeffs, sh_basis, precision=HIGH_PRECISION, preferred_element_type=jnp.float32
    )
    grad_output = (scale_out * grad_error).astype(jnp.bfloat16)
    grad_table_out = contract(grad_output, final_normed, 1, 0)
    grad_final = contract(grad_output, tables_copy[1], 0, 0)
    grad_decoded, gain_final = jax.vjp(layer_norm, decoded, gains[4])[1](grad_final)
    grad_join, gain_dec, mlp_dec = mlp_backward(grad_decoded, kept_dec, gains[3], mlp_copy[2])
    dec_part = lax.psum_scatter(mlp_dec, "lat", scatter_dimension=0, tiled=True)
    dec_count = dec_edges.shape[1]
    spread_grad = (
        jnp.zeros((3 * node_rows, model_width), jnp.float32)
        .at[dec_edges]
        .add(
            jnp.broadcast_to(grad_join[:, None, :] / dec_count, (grid_rows, dec_count, model_width))
        )
    )
    arrived = padded(outer_rims(spread_grad), (("lat", 0),), node_rows)
    grad_latent = fold_rims(spread_grad, arrived)
    grad_residual, gain_proc, mlp_proc = mlp_backward(grad_latent, kept_proc, gains[2], mlp_copy[1])
    grad_branch = grad_residual.astype(jnp.bfloat16)
    grad_wout = contract(attended_values, grad_branch, 0, 0)
    grad_attended = contract(grad_branch, attn_copy[:, 3 * model_width :], 1, 1).astype(
        jnp.bfloat16
    )
    grad_queries, grad_near = attention_backward(
        grad_attended, queries, neighbours, softmax_probs, rounded_probs
    )
    near_grad = (
        jnp.zeros((3 * node_rows, 2 * model_width), jnp.float32)
        .at[mesh_edges]
        .add(grad_near[:, 1:])
    )
    arrived_pairs = padded(outer_rims(near_grad), (("lat", 0),), node_rows)
    grad_pairs = fold_rims(near_grad, arrived_pairs) + grad_near[:, 0]
    grad_project = jnp.concatenate([grad_queries, grad_pairs], axis=1).astype(jnp.bfloat16)
    grad_wqkv = contract(normed_attn, grad_project, 0, 0)
    grad_normed = contract(grad_project, attn_copy[:, : 3 * model_width], 1, 1)
    grad_enc_norm, gain_attn = jax.vjp(layer_norm, encoded, gains[1])[1](grad_normed)
    grad_attn = jnp.concatenate([grad_wqkv, grad_wout], axis=1)
    attn_part, proc_part = (
        lax.psum_scatter(grad_attn, "lat", scatter_dimension=0, tiled=True),
        lax.psum_scatter(mlp_proc, "lat", scatter_dimension=0, tiled=True),
    )
    grad_pooled, gain_enc, mlp_enc = mlp_backward(
        grad_residual + grad_enc_norm, kept_enc, gains[0], mlp_copy[0]
    )
    grid_count = grid_edges.shape[1]
    grad_embedded = grad_join + jnp.zeros((grid_rows, model_width), jnp.float32).at[grid_edges].add(
        jnp.broadcast_to(grad_pooled[:, None, :] / grid_count, (node_rows, grid_count, model_width))
    )
    grad_table_in = contract(inputs, grad_embedded.astype(jnp.bfloat16), 1, 0)
    grad_tables = jnp.stack([grad_table_in, grad_table_out])
    grad_gains = jnp.stack([gain_enc, gain_attn, gain_proc, gain_dec, gain_final])
    tab_part, enc_part, gain_part = (
        lax.psum_scatter(grad_tables, "lat", scatter_dimension=2, tiled=True),
        lax.psum_scatter(mlp_enc, "lat", scatter_dimension=0, tiled=True),
        lax.psum_scatter(grad_gains, "lat", scatter_dimension=1, tiled=True),
    )
    mlp_part = jnp.stack([enc_part, proc_part, dec_part])
    tab_sum, attn_sum, mlp_sum, gain_sum, loss_band = lax.psum(
        (tab_part, attn_part, mlp_part, gain_part, loss_item), "item"
    )
    squares = (
        jnp.sum(tab_sum * tab_sum)
        + jnp.sum(attn_sum * attn_sum)
        + jnp.sum(mlp_sum * mlp_sum)
        + jnp.sum(gain_sum * gain_sum)
    )
    squares_all, loss_sum = lax.psum((squares, loss_band), "lat")
    grad_norm = jnp.sqrt(squares_all)
    scale_factor = CLIP_LEVEL / jnp.maximum(grad_norm, CLIP_LEVEL)
    tab = adam_update(
        scale_factor * tab_sum,
        tables_master,
        tables_first,
        tables_second,
        tables_ema,
        RATE_MATRIX,
        WEIGHT_DECAY,
    )
    att = adam_update(
        scale_factor * attn_sum,
        attn_master,
        attn_first,
        attn_second,
        attn_ema,
        RATE_MATRIX,
        WEIGHT_DECAY,
    )
    mlps = adam_update(
        scale_factor * mlp_sum,
        mlp_master,
        mlp_first,
        mlp_second,
        mlp_ema,
        RATE_MATRIX,
        WEIGHT_DECAY,
    )
    gns = adam_update(
        scale_factor * gain_sum, gains_master, gains_first, gains_second, gains_ema, RATE_GAIN, 0.0
    )
    return (
        loss_sum,
        grad_norm,
        tab[0],
        tab[1],
        tab[2],
        tab[3],
        tab[4],
        att[0],
        att[1],
        att[2],
        att[3],
        att[4],
        mlps[0],
        mlps[1],
        mlps[2],
        mlps[3],
        mlps[4],
        gns[0],
        gns[1],
        gns[2],
        gns[3],
        gns[4],
    )


def solution(mesh):
    placed = (
        P("item", None, "lat"),
        P("item", None, "lat"),
        P("item"),
        P(None, "lat"),
        P("item", None),
        P("lat", None),
        P("lat", None),
        P("lat", None),
        P(),
        P(None, None, "lat"),
        P(None, None, "lat"),
        P(None, None, "lat"),
        P(None, None, "lat"),
        P(),
        P("lat", None),
        P("lat", None),
        P("lat", None),
        P("lat", None),
        P(),
        P(None, "lat", None),
        P(None, "lat", None),
        P(None, "lat", None),
        P(None, "lat", None),
        P(),
        P(None, "lat"),
        P(None, "lat"),
        P(None, "lat"),
        P(None, "lat"),
    )
    return jax.shard_map(
        shards,
        mesh=mesh,
        in_specs=placed,
        out_specs=(
            P(),
            P(),
            P(None, None, "lat"),
            P(None, None, "lat"),
            P(None, None, "lat"),
            P(None, None, "lat"),
            P(None, None, "lat"),
            P("lat", None),
            P("lat", None),
            P("lat", None),
            P("lat", None),
            P("lat", None),
            P(None, "lat", None),
            P(None, "lat", None),
            P(None, "lat", None),
            P(None, "lat", None),
            P(None, "lat", None),
            P(None, "lat"),
            P(None, "lat"),
            P(None, "lat"),
            P(None, "lat"),
            P(None, "lat"),
        ),
        check_vma=False,
    )
```

profile of v0, /device:TPU:0, one launch (start us, length us, event | category | flops | bytes accessed | tf_op | source)
XLA Modules:
  0.0 1387.9 jit_solution(2376228455781315618)
XLA Ops:
  18.4 16.8 %gather_fusion = f32[4096,512]{1,0:T(8,128)} fusion(f32[1024,512]{1,0:T(8,128)S(1)} %copy.247, s32[4096]{0:T(1024)S(1)} %broadcast_clamp_fusion.1), kind=kCustom, calls=%fused_computation | custom fusion | bytes 16793600 | tf_op jit(solution)/shard_map/gather | solution.py:211
  35.1 9.8 reshape.281
  44.9 9.7 reduce_sum.315
  94.2 83.8 %gather_fusion.1 = bf16[16384,1024]{1,0:T(8,128)(2,1)} fusion(bf16[3072,1024]{1,0:T(8,128)(2,1)} %pad_maximum_fusion.4, s32[16384]{0:T(1024)S(1)} %broadcast_clamp_fusion), kind=kCustom, calls=%fused_computation.1 | custom fusion | bytes 67174400 | tf_op jit(solution)/shard_map/gather | solution.py:226
  178.0 45.2 %copy.252 = bf16[1024,16,1024]{0,2,1:T(8,128)(2,1)} copy(bf16[1024,16,1024]{2,1,0:T(8,128)(2,1)} %bitcast.112) | data formatting | bytes 67108864 | tf_op jit(solution)/shard_map/gather | solution.py:226
  223.1 17.4 %pad_maximum_fusion = bf16[1024,17,512]{0,2,1:T(8,128)(2,1)} fusion(bf16[1024,16,1024]{0,2,1:T(8,128)(2,1)} %copy.252, bf16[1024,1,1024]{0,2,1:T(8,128)(2,1)S(1)} %copy.251), kind=kLoop, calls=%fused_computation.17 | loop fusion | flops 35651584 | bytes 53477376 | tf_op jit(solution)/shard_map/concatenate | solution.py:226
  278.7 21.4 %collective-permute-start.2 = (bf16[1024,512]{0,1:T(8,128)(2,1)S(1)}, bf16[1024,512]{0,1:T(8,128)(2,1)}, u32[]{:S(2)}, u32[]{:S(2)}) collective-permute-start(bf16[1024,512]{0,1:T(8,128)(2,1)S(1)} %add_convert_fusion), channel_id=1, source_target_pairs={{0,1},{1,2},{2,3},{3,4},{4,5},{5,6},{6,7},{8,9},{9,10},{10,11},{11... | collective-permute-start | bytes 3145736 | tf_op jit(solution)/shard_map/ppermute | solution.py:29
  307.7 13.3 gather_fusion.2
  321.0 9.7 reshape.336
  330.7 9.7 reduce_sum.331
  353.9 39.1 %psum.56 = f32[83,64]{0,1:T(8,128)S(1)} all-reduce(f32[83,64]{0,1:T(8,128)S(1)} %fusion.132), channel_id=1, replica_groups=mesh['item'=4,'lat'=8] {'lat'}, use_global_device_ids=true, to_apply=%region_17.18 | all-reduce | flops 5312 | bytes 42496 | tf_op jit(solution)/shard_map/psum | solution.py:246
  433.8 10.8 reshape.304
  444.6 22.3 %scatter_custom_fusion = f32[3072,512]{1,0:T(8,128)} fusion(s32[3072]{0:T(1024)S(1)} %reshape.294, f32[3072,512]{1,0:T(8,128)} %reshape.304, f32[]{:T(128)} %constant.42.clone.1), kind=kCustom, calls=%fused_computation.78 | custom fusion | flops 1572864 | bytes 6291968 | tf_op jit(solution)/shard_map/scatter-add | solution.py:264
  491.1 10.3 fusion.15
  522.0 21.3 %multiply_reduce_fusion.1 = (f32[1024,4,17]{0,1,2:T(4,128)S(1)}, f32[1024,4,128,17]{0,2,1,3:T(8,128)}) fusion(f32[1024,4,128]{0,2,1:T(8,128)} %bitcast_convert_fusion, f32[1024,4,17]{0,1,2:T(4,128)S(1)} %copy-done.43, bf16[1024,16,1024]{0,2,1:T(8,128)(2,1)} %copy.252, bf16[1024,1,1024]{0,2,1:T(8,128)(2,1)S(1)} %copy-done.8), kind=kLoop, calls=%fused_computation.12 | loop fusion | flops 71233536 | bytes 73957376 | tf_op jit(solution)/shard_map/yza,yvza->yzv/dot_general | solution.py:118
  543.4 35.9 %copy.264 = f32[1024,17,512]{2,0,1:T(8,128)} copy(f32[1024,17,512]{0,2,1:T(8,128)} %bitcast.110) | data formatting | bytes 71303168 | tf_op jit(solution)/shard_map/reshape | solution.py:147
  579.4 12.2 multiply_multiply_fusion
  591.6 35.7 %copy.263 = f32[1024,17,512]{2,0,1:T(8,128)} copy(f32[1024,17,512]{0,2,1:T(8,128)} %bitcast.111) | data formatting | bytes 71303168 | tf_op jit(solution)/shard_map/reshape | solution.py:146
  627.4 43.7 %fusion = f32[1024,16,1024]{2,0,1:T(8,128)} fusion(f32[1024,17,512]{2,0,1:T(8,128)} %copy.263, f32[1024,17,512]{2,0,1:T(8,128)} %copy.264), kind=kLoop, calls=%fused_computation.8 | loop fusion | flops 16777216 | bytes 138412032 | tf_op jit(solution)/shard_map/concatenate | solution.py:144
  671.0 56.5 %copy.265 = f32[1024,16,1024]{2,1,0:T(8,128)} copy(f32[1024,16,1024]{2,0,1:T(8,128)} %fusion) | data formatting | bytes 134217728 | tf_op jit(solution)/shard_map/slice | solution.py:282
  727.5 145.5 %scatter_custom_fusion.1 = f32[3072,1024]{1,0:T(8,128)} fusion(s32[16384]{0:T(1024)} %copy-done.61, f32[16384,1024]{1,0:T(8,128)} %bitcast.31, f32[]{:T(128)} %constant.42.clone.1), kind=kCustom, calls=%fused_computation.53 | custom fusion | flops 16777216 | bytes 12583424 | tf_op jit(solution)/shard_map/scatter-add | solution.py:282
  881.4 41.5 %collective-permute-start.6 = (f32[1024,1024]{1,0:T(8,128)}, f32[1024,1024]{1,0:T(8,128)}, u32[]{:S(2)}, u32[]{:S(2)}) collective-permute-start(f32[1024,1024]{1,0:T(8,128)} %get-tuple-element.199), channel_id=1, source_target_pairs={{0,1},{1,2},{2,3},{3,4},{4,5},{5,6},{6,7},{8,9},{9,10},{10,11},{11... | collective-permute-start | bytes 12582920 | tf_op jit(solution)/shard_map/ppermute | solution.py:29
  947.9 10.3 fusion.8
  1003.9 10.0 reshape.320
  1013.9 26.4 %scatter_fusion = f32[1024,512]{1,0:T(8,128)S(1)} fusion(f32[1024,512]{1,0:T(8,128)S(1)} %copy.267, s32[4096]{0:T(1024)S(1)} %copy-done.15, f32[4096,512]{1,0:T(8,128)} %reshape.320), kind=kCustom, calls=%fused_computation.5 | custom fusion | flops 2097152 | bytes 25182208 | tf_op jit(solution)/shard_map/scatter-add | solution.py:299
  1041.9 57.4 %reduce-scatter.10.cloned.1.call-done = f32[64,4096]{1,0:T(8,128)} async-done(((f32[512,4096]{1,0:T(8,128)}), f32[64,4096]{1,0:T(8,128)}) %reduce-scatter.10.cloned.1.call-update) | async-done | bytes 1048592 | tf_op jit(solution)/shard_map/reduce_scatter | solution.py:307
  1103.1 46.7 %reduce-scatter.8.cloned.1.call-done = f32[64,2048]{1,0:T(8,128)} async-done(((f32[512,2048]{1,0:T(8,128)}), f32[64,2048]{1,0:T(8,128)}) %reduce-scatter.8.cloned.1.call-update) | async-done | bytes 524304 | tf_op jit(solution)/shard_map/reduce_scatter | solution.py:292
  1153.1 27.9 %reduce-scatter.16.cloned.1.call-done = f32[64,5]{1,0:T(8,128)} async-done(((f32[512,5]{1,0:T(8,128)}), f32[64,5]{1,0:T(8,128)}) %reduce-scatter.16.cloned.1.call-update) | async-done | bytes 1296
  1181.9 56.4 %all-reduce.8.cloned.1.call-done = f32[2,83,512]{1,0,2:T(2,128)} async-done(((f32[2,83,512]{1,0,2:T(2,128)}), f32[2,83,512]{1,0,2:T(2,128)}) %all-reduce.8.cloned.1.call-update) | async-done | bytes 339984
  1239.1 19.0 %all-reduce.3 = (f32[]{:T(128)}, f32[2,83,64]{1,2,0:T(8,128)S(1)}, f32[5,64]{1,0:T(8,128)S(1)}) all-reduce(f32[]{:T(128)S(6)} %mul.755, f32[2,83,64]{1,2,0:T(8,128)S(1)} %copy.269, f32[5,64]{1,0:T(8,128)S(1)} %copy.298), channel_id=1, replica_groups=mesh['item'=4,'lat'=8] {'item'}, use_global_device_ids=true, to_apply=%region_19.20 | all-reduce | flops 10945 | bytes 87560 | tf_op jit(solution)/shard_map/psum | solution.py:311
  1259.3 78.6 %all-reduce.10.cloned.1.call-done = (f32[64,2048]{1,0:T(8,128)}, f32[3,64,4096]{2,1,0:T(8,128)}) async-done(((f32[64,2048]{1,0:T(8,128)}, f32[3,64,4096]{2,1,0:T(8,128)}), (f32[64,2048]{1,0:T(8,128)}, f32[3,64,4096]{2,1,0:T(8,128)})) %all-reduce.10.cloned.1.call-update) | async-done | bytes 3670032 | tf_op jit(solution)/shard_map/psum | solution.py:311
  1344.9 17.0 %all-reduce.2 = (f32[]{:T(128)}, f32[]{:T(128)}) all-reduce(f32[]{:T(128)} %get-tuple-element.166, f32[]{:T(128)S(6)} %add.318), channel_id=1, replica_groups=mesh['item'=4,'lat'=8] {'lat'}, use_global_device_ids=true, to_apply=%region_20.21 | all-reduce | flops 2 | bytes 16 | tf_op jit(solution)/shard_map/psum | solution.py:320
  (411 shorter events, 303.4 us)
Async XLA Ops:
  7.2 346.2 %copy-start = (f32[64,1024]{1,0:T(8,128)S(1)}, f32[64,1024]{1,0:T(8,128)}, u32[]{:S(2)}) copy-start(f32[64,1024]{1,0:T(8,128)} %param.31) | copy-start | bytes 786436
  7.2 1034.7 %reduce-scatter.14.cloned.1.call-start = ((), (), s32[]{:S(2)}) async-start(), calls=%async_computation.8 | async-start | bytes 9437184 | tf_op jit(solution)/shard_map/reduce_scatter | solution.py:259
  9.5 55.4 %copy-start.90 = (f32[1,512]{1,0:T(1,128)}, f32[1,512]{1,0:T(1,128)S(1)}, u32[]{:S(2)}) copy-start(f32[1,512]{1,0:T(1,128)S(1)} %get-tuple-element.219) | copy-start | bytes 6148
  9.5 61.9 %copy-start.92 = (f32[1,512]{1,0:T(1,128)}, f32[1,512]{1,0:T(1,128)S(1)}, u32[]{:S(2)}) copy-start(f32[1,512]{1,0:T(1,128)S(1)} %get-tuple-element.218) | copy-start | bytes 6148
  75.9 12.0 collective-permute-start.1
  77.2 10.7 collective-permute-start
  87.6 153.0 %copy-start.7 = (bf16[1024,1,1024]{0,2,1:T(8,128)(2,1)}, bf16[1024,1,1024]{0,2,1:T(8,128)(2,1)S(1)}, u32[]{:S(2)}) copy-start(bf16[1024,1,1024]{0,2,1:T(8,128)(2,1)S(1)} %copy.251) | copy-start | bytes 6291460
  277.4 23.4 %collective-permute-start.3 = (bf16[1024,512]{0,1:T(8,128)(2,1)S(1)}, bf16[1024,512]{0,1:T(8,128)(2,1)S(1)}, u32[]{:S(2)}, u32[]{:S(2)}) collective-permute-start(bf16[1024,512]{0,1:T(8,128)(2,1)S(1)} %add_convert_fusion), channel_id=1, source_target_pairs={{1,0},{2,1},{3,2},{4,3},{5,4},{6,5},{7,6},{9,8},{10,9},{11,10},{12... | collective-permute-start | bytes 3145736 | tf_op jit(solution)/shard_map/ppermute | solution.py:30
  278.7 22.8 %collective-permute-start.2 = (bf16[1024,512]{0,1:T(8,128)(2,1)S(1)}, bf16[1024,512]{0,1:T(8,128)(2,1)}, u32[]{:S(2)}, u32[]{:S(2)}) collective-permute-start(bf16[1024,512]{0,1:T(8,128)(2,1)S(1)} %add_convert_fusion), channel_id=1, source_target_pairs={{0,1},{1,2},{2,3},{3,4},{4,5},{5,6},{6,7},{8,9},{9,10},{10,11},{11... | collective-permute-start | bytes 3145736 | tf_op jit(solution)/shard_map/ppermute | solution.py:29
  352.5 42.4 %copy-start.6 = (f32[1024,512]{0,1:T(8,128)}, f32[1024,512]{0,1:T(8,128)S(1)}, u32[]{:S(2)}) copy-start(f32[1024,512]{0,1:T(8,128)S(1)} %get-tuple-element.225) | copy-start | bytes 6291460
  352.5 42.3 %copy-start.63 = (f32[1024]{0:T(1024)}, f32[1024]{0:T(1024)S(1)}, u32[]{:S(2)}) copy-start(f32[1024]{0:T(1024)S(1)} %broadcast_multiply_fusion.2) | copy-start | bytes 12292
  352.9 42.0 %copy-start.65 = (f32[1024]{0:T(1024)}, f32[1024]{0:T(1024)S(1)}, u32[]{:S(2)}) copy-start(f32[1024]{0:T(1024)S(1)} %fusion.103) | copy-start | bytes 12292
  416.9 625.0 %reduce-scatter.12.cloned.1.call-start = ((), (), s32[]{:S(2)}) async-start(), calls=%async_computation.7 | async-start | bytes 9437184 | tf_op jit(solution)/shard_map/reduce_scatter | solution.py:293
  478.7 7.7 collective-permute-start.5
  479.9 7.2 collective-permute-start.4
  520.5 578.8 %reduce-scatter.10.cloned.1.call-start = ((), (), s32[]{:S(2)}) async-start(), calls=%async_computation.6 | async-start | bytes 9437184 | tf_op jit(solution)/shard_map/reduce_scatter | solution.py:307
  543.3 35.9 %copy-start.41 = (f32[1024,4,17]{0,1,2:T(4,128)S(1)}, f32[1024,4,17]{0,1,2:T(4,128)}, u32[]{:S(2)}) copy-start(f32[1024,4,17]{0,1,2:T(4,128)} %get-tuple-element.196) | copy-start | bytes 835588
  543.3 36.1 %copy-start.17 = (f32[1024,4,128]{0,2,1:T(8,128)S(1)}, f32[1024,4,128]{0,2,1:T(8,128)}, u32[]{:S(2)}) copy-start(f32[1024,4,128]{0,2,1:T(8,128)} %copy.306) | copy-start | bytes 6291460
  881.4 52.1 %collective-permute-start.6 = (f32[1024,1024]{1,0:T(8,128)}, f32[1024,1024]{1,0:T(8,128)}, u32[]{:S(2)}, u32[]{:S(2)}) collective-permute-start(f32[1024,1024]{1,0:T(8,128)} %get-tuple-element.199), channel_id=1, source_target_pairs={{0,1},{1,2},{2,3},{3,4},{4,5},{5,6},{6,7},{8,9},{9,10},{10,11},{11... | collective-permute-start | bytes 12582920 | tf_op jit(solution)/shard_map/ppermute | solution.py:29
  922.9 10.6 collective-permute-start.7
  972.4 177.4 %reduce-scatter.8.cloned.1.call-start = ((), (), s32[]{:S(2)}) async-start(), calls=%async_computation.5 | async-start | bytes 4718592 | tf_op jit(solution)/shard_map/reduce_scatter | solution.py:292
  980.0 201.0 %reduce-scatter.16.cloned.1.call-start = ((), (), s32[]{:S(2)}) async-start(), calls=%async_computation.9 | async-start | bytes 294912
  1040.7 197.6 %all-reduce.8.cloned.1.call-start = ((), (), s32[]{:S(2)}) async-start(), calls=%async_computation.10 | async-start | bytes 1048576
  1041.8 296.1 %all-reduce.10.cloned.1.call-start = ((), (), s32[]{:S(2)}) async-start(), calls=%async_computation.11 | async-start | bytes 7340032 | tf_op jit(solution)/shard_map/psum | solution.py:311
  1103.1 46.8 %copy-start.105 = (u32[32]{0:T(128)S(1)}, u32[32]{0:T(128)}, u32[]{:S(2)}) copy-start(u32[32]{0:T(128)} %constant.158) | copy-start | bytes 388
  1149.8 212.8 %copy-start.100 = (f32[5,64]{1,0:T(8,128)S(1)}, f32[5,64]{1,0:T(8,128)}, u32[]{:S(2)}) copy-start(f32[5,64]{1,0:T(8,128)} %param.52) | copy-start | bytes 3844
  1149.8 212.8 %copy-start.101 = (f32[5,64]{1,0:T(8,128)S(1)}, f32[5,64]{1,0:T(8,128)}, u32[]{:S(2)}) copy-start(f32[5,64]{1,0:T(8,128)} %param.54) | copy-start | bytes 3844
  1149.8 212.8 %copy-start.102 = (f32[5,64]{1,0:T(8,128)S(1)}, f32[5,64]{1,0:T(8,128)}, u32[]{:S(2)}) copy-start(f32[5,64]{1,0:T(8,128)} %param.53) | copy-start | bytes 3844
  1149.8 214.7 %copy-start.72 = (f32[2,83,64]{1,2,0:T(8,128)S(1)}, f32[2,83,64]{1,2,0:T(8,128)}, u32[]{:S(2)}) copy-start(f32[2,83,64]{1,2,0:T(8,128)} %param.37) | copy-start | bytes 127492
  1149.8 214.7 %copy-start.73 = (f32[2,83,64]{1,2,0:T(8,128)S(1)}, f32[2,83,64]{1,2,0:T(8,128)}, u32[]{:S(2)}) copy-start(f32[2,83,64]{1,2,0:T(8,128)} %param.39) | copy-start | bytes 127492
  1149.9 214.7 %copy-start.74 = (f32[2,83,64]{1,2,0:T(8,128)S(1)}, f32[2,83,64]{1,2,0:T(8,128)}, u32[]{:S(2)}) copy-start(f32[2,83,64]{1,2,0:T(8,128)} %param.38) | copy-start | bytes 127492
  1149.9 215.4 %copy-start.75 = (f32[2,83,64]{1,2,0:T(8,128)S(1)}, f32[2,83,64]{1,2,0:T(8,128)}, u32[]{:S(2)}) copy-start(f32[2,83,64]{1,2,0:T(8,128)} %param.40) | copy-start | bytes 127492
  (98 other events, 590.4 us)
Sparse Core Ops, SparseCore 0:
  417.0 99.2 reduce-scatter.13
  520.6 126.4 reduce-scatter.11
  972.6 126.7 reduce-scatter.9
  1101.5 48.3 reduce-scatter.7
  1152.5 28.4 reduce-scatter.15
  1183.9 54.3 all-reduce.7
  1242.0 95.8 all-reduce.9
where the time goes:
time: 1400 us; the launch traced here: 1390 us
  local copies, waits for them, and re-layouts  425 us (30%)
  other arithmetic  415 us (30%)
  waiting for transfers between devices  269 us (19%)
  matrix products  104 us (7%)
  starting transfers between devices  77.9 us (6%)
  blocking collectives  75 us (5%)
  between operations  23.3 us (2%)
    scatter-add x1, other arithmetic, shards(): near_grad = jnp.zeros((3 * node_rows, 2 * model_width), jnp.float32).at[m...  146 us
    gather x2, local copies, waits for them, and re-layouts, shards(): window[mesh_edges]  129 us
    unnamed x9, waiting for transfers between devices  84.5 us
    psum x1, waiting for transfers between devices, shards(): lax.psum((tab_part, attn_part, mlp_part, gain_part, loss_item), 'item')  78.6 us
    ppermute x4, starting transfers between devices, padded(): before = lax.ppermute(last, axis, up)  71.8 us
    dot_general x21, matrix products, contract(): lax.dot_general(left, right, (((left_dim,), (right_dim,)), ((), ())), pre...  60.8 us
    reduce_scatter x1, waiting for transfers between devices, shards(): lax.psum_scatter(mlp_enc, 'lat', scatter_dimension=0, tiled=True)  57.4 us
    slice x1, local copies, waits for them, and re-layouts, shards(): grad_near[:, 1:]  56.5 us
  transfers between devices with their start and end apart: 15, of which 7 were waited for; matrix products, arithmetic and copies ran while one was open for 42% of the time, Pallas kernels for 0%

commit v1 on v0

v1 whole, which is shorter than its diff:
```python
import functools

import jax
import jax.numpy as jnp
from jax import lax
from jax.experimental import pallas as pl
from jax.experimental.pallas import tpu as pltpu
from jax.sharding import PartitionSpec as P

HEADS = 4
STEP = 10

EPS_NORM = 1e-05
CLIP_LEVEL = 1.0
BETA_ONE = 0.9
BETA_TWO = 0.999
ADAM_EPS = 1e-08
EMA_DECAY = 0.9
RATE_MATRIX = 0.05
RATE_GAIN = 0.3
WEIGHT_DECAY = 0.1
HIGH_PRECISION = lax.Precision.HIGHEST

F32 = jnp.float32
BF16 = jnp.bfloat16
LOG2E = 1.4426950408889634
CHANNEL_PAD = 128
ROWS = 256
VMEM_BYTES = 60 * 1024 * 1024


def dot(left, right, left_dim, right_dim):
    return lax.dot_general(
        left, right, (((left_dim,), (right_dim,)), ((), ())), preferred_element_type=F32
    )


def call(kernel, grid, outs, in_specs, out_specs, operands, scratch=(), flops=0, moved=0):
    return pl.pallas_call(
        kernel,
        grid=grid,
        out_shape=outs,
        in_specs=in_specs,
        out_specs=out_specs,
        scratch_shapes=list(scratch),
        cost_estimate=pl.CostEstimate(flops=flops, bytes_accessed=moved, transcendentals=0),
        compiler_params=pltpu.CompilerParams(vmem_limit_bytes=VMEM_BYTES),
    )(*operands)


def whole(shape):
    return pl.BlockSpec(shape, lambda *_: (0,) * len(shape))


def rows_of(width, rows=ROWS):
    return pl.BlockSpec((rows, width), lambda i: (i, 0))


def lanes_of(height, lanes=ROWS):
    return pl.BlockSpec((height, lanes), lambda i: (0, i))


def shape(dims, kind):
    return jax.ShapeDtypeStruct(dims, kind)


def norm_parts(values):
    center = values - jnp.mean(values, axis=-1, keepdims=True)
    spread = jnp.mean(center * center, axis=-1, keepdims=True)
    inverse = lax.rsqrt(spread + EPS_NORM)
    return center * inverse, inverse


def norm_back(upstream, values, gain_row):
    unit, inverse = norm_parts(values)
    scaled = upstream * gain_row
    along = jnp.mean(scaled * unit, axis=-1, keepdims=True)
    grad = inverse * (scaled - jnp.mean(scaled, axis=-1, keepdims=True) - unit * along)
    gain_grad = jnp.sum(upstream * unit, axis=0, keepdims=True)
    return grad, gain_grad


def gelu_parts(u):
    root = 0.7978845608028654
    cubic = 0.044715
    square = u * u
    t = jnp.tanh(root * u * (1.0 + cubic * square))
    half = 0.5 * (1.0 + t)
    slope = half + 0.5 * u * (1.0 - t * t) * (root + (3.0 * root * cubic) * square)
    return u * half, slope


def mlp_forward(values, gain_row, w_ref, normed_ref, slope_ref, active_ref, step=512):
    hidden = w_ref.shape[-1] // 2
    normed = (norm_parts(values)[0] * gain_row).astype(BF16)
    normed_ref[...] = normed
    result = jnp.zeros(values.shape, F32)
    for start in range(0, hidden, step):
        part = slice(start, start + step)
        before = dot(normed, w_ref[0, :, part], 1, 0)
        active, slope = gelu_parts(before)
        active = active.astype(BF16)
        slope_ref[:, part] = slope
        active_ref[:, part] = active
        result = result + dot(active, w_ref[0, :, hidden + start : hidden + start + step], 1, 1)
    return values + result


def mlp_backward(upstream, values, gain_row, w_ref, slope_ref, rounded_ref, before_ref, step=512):
    hidden = w_ref.shape[-1] // 2
    rounded = upstream.astype(BF16)
    rounded_ref[...] = rounded
    grad_normed = jnp.zeros(values.shape, F32)
    for start in range(0, hidden, step):
        part = slice(start, start + step)
        grad_active = dot(rounded, w_ref[0, :, hidden + start : hidden + start + step], 1, 0)
        grad_before = (grad_active * slope_ref[:, part]).astype(BF16)
        before_ref[:, part] = grad_before
        grad_normed = grad_normed + dot(grad_before, w_ref[0, :, part], 1, 1)
    grad, gain_grad = norm_back(grad_normed, values, gain_row)
    return upstream + grad, gain_grad


def two_parts(values):
    high = values.astype(BF16)
    return high, (values - high.astype(F32)).astype(BF16)


def add_up(ref, value):
    step = pl.program_id(0)

    @pl.when(step == 0)
    def _():
        ref[...] = value

    @pl.when(step > 0)
    def _():
        ref[...] += value


def encoder_kernel(
    edges, x, table, gains, mlp, attn,
    pin_ref, pooled_ref, encoded_ref, normed_ref, slope_ref, active_ref, normed_attn_ref, q_ref, kv_ref,
):
    rows, count = edges.shape
    width = attn.shape[0]
    lanes = lax.broadcasted_iota(jnp.int32, (rows, x.shape[1]), 1)
    tally = jnp.zeros(lanes.shape, F32)
    for j in range(count):
        tally = tally + jnp.where(edges[:, j : j + 1] == lanes, 1.0, 0.0)
    pin = dot(tally.astype(BF16), x[...], 1, 1) / count
    high, low = two_parts(pin)
    pin_ref[...] = jnp.concatenate([high, low], axis=1)
    pooled = dot(high, table[0], 1, 0) + dot(low, table[0], 1, 0)
    pooled_ref[...] = pooled
    encoded = mlp_forward(pooled, gains[0:1], mlp, normed_ref, slope_ref, active_ref)
    encoded_ref[...] = encoded
    normed_attn = (norm_parts(encoded)[0] * gains[1:2]).astype(BF16)
    normed_attn_ref[...] = normed_attn
    q_ref[...] = dot(attn[:, :width], normed_attn, 0, 1).astype(BF16)
    kv_ref[...] = dot(normed_attn, attn[:, width : 3 * width], 1, 0).astype(BF16)


def bias_kernel(places, ends, edges, bias_ref, *, crops):
    count, lanes = edges.shape
    rows = bias_ref.shape[1]
    window = bias_ref.shape[0] * rows
    col = pl.program_id(0)
    nodes = col * lanes + lax.broadcasted_iota(jnp.int32, (1, lanes), 1)
    first = places[0] * rows
    low = jnp.zeros((1, lanes), jnp.int32)
    high = jnp.full((1, lanes), places[1] * rows, jnp.int32)
    for c in range(crops - 1, -1, -1):
        high = jnp.where(ends[c] > first + nodes, ends[c], high)
    for c in range(crops):
        low = jnp.where(ends[c] <= first + nodes, ends[c], low)
    near = edges[...] + (first - rows)
    place = jnp.where((near >= low) & (near < high), edges[...], -1)
    place = jnp.concatenate([place, rows + nodes], axis=0)
    tile = 128
    tiles = window // tile
    each = 6
    fine = jnp.where(place < 0, -1, place % tile)
    coarse = place // tile
    sub = lax.broadcasted_iota(jnp.int32, (tile, lanes), 0)
    for start in range(0, tiles, each):
        here = (coarse >= start) & (coarse < start + each)
        amount = jnp.where(here, jnp.left_shift(1, 5 * jnp.where(here, coarse - start, 0)), 0)
        total = jnp.zeros((tile, lanes), jnp.int32)
        for j in range(count + 1):
            total = total + jnp.where(sub == fine[j : j + 1], amount[j : j + 1], 0)
        for t in range(start, min(tiles, start + each)):
            tally = jnp.bitwise_and(jnp.right_shift(total, 5 * (t - start)), 31)
            value = jnp.where(tally == 0, -1e30, jnp.log2(jnp.maximum(tally, 1).astype(F32)))
            at = t * tile
            bias_ref[at // rows, at % rows : at % rows + tile, :] = value


def attend_kernel(q_ref, k0, k1, k2, v0, v1, v2, bias, o_ref, l_ref, scores, *, chunk):
    depth, lanes = q_ref.shape
    rows = k0.shape[0]
    factor = depth**-0.5 * LOG2E
    q = q_ref[...]
    top = jnp.full((8, lanes), -3e38, F32)
    for w, keys in enumerate((k0, k1, k2)):
        for start in range(0, rows, chunk):
            part = slice(start, start + chunk)
            score = dot(keys[part, :], q, 1, 0) * factor + bias[w, part, :]
            scores[w, part, :] = score
            top = jnp.maximum(top, jnp.max(score.reshape(chunk // 8, 8, lanes), axis=0))
    top = jnp.max(top, axis=0, keepdims=True)
    total = jnp.zeros((8, lanes), F32)
    result = jnp.zeros((depth, lanes), F32)
    for w, values in enumerate((v0, v1, v2)):
        for start in range(0, rows, chunk):
            part = slice(start, start + chunk)
            e = jnp.exp2(scores[w, part, :] - top)
            total = total + jnp.sum(e.reshape(chunk // 8, 8, lanes), axis=0)
            result = result + dot(values[part, :], e.astype(BF16), 0, 0)
    total = jnp.sum(total, axis=0, keepdims=True)
    o_ref[...] = result * (1.0 / total)
    l_ref[...] = jnp.broadcast_to((top + jnp.log2(total))[None], l_ref.shape)


def processor_kernel(
    o_ref, encoded, gains, mlp, attn,
    attended_ref, residual_ref, normed_ref, slope_ref, active_ref, sent_ref,
):
    width = encoded.shape[1]
    attended = o_ref[...].astype(BF16)
    attended_ref[...] = attended
    residual = encoded[...] + dot(attended, attn[:, 3 * width :], 0, 0)
    residual_ref[...] = residual
    latent = mlp_forward(residual, gains[2:3], mlp, normed_ref, slope_ref, active_ref)
    sent_ref[...] = latent.astype(BF16)


def decoder_kernel(
    edges, s0, s1, s2, x, tables, gains, mlp,
    joined_ref, normed_ref, slope_ref, active_ref, decoded_ref, final_ref, output_ref,
):
    lanes_total = s0.shape[0]
    rows, count = edges.shape
    gathered = jnp.zeros(joined_ref.shape, F32)
    lanes = lax.broadcasted_iota(jnp.int32, (rows, lanes_total), 1)
    for w, sent in enumerate((s0, s1, s2)):
        tally = jnp.zeros((rows, lanes_total), F32)
        for j in range(count):
            tally = tally + jnp.where(edges[:, j : j + 1] - w * lanes_total == lanes, 1.0, 0.0)
        gathered = gathered + dot(tally.astype(BF16), sent[...], 1, 0)
    joined = dot(x[...], tables[0], 0, 0) + gathered / count
    joined_ref[...] = joined
    decoded = mlp_forward(joined, gains[3:4], mlp, normed_ref, slope_ref, active_ref)
    decoded_ref[...] = decoded
    final = (norm_parts(decoded)[0] * gains[4:5]).astype(BF16)
    final_ref[...] = final
    output_ref[...] = dot(tables[1], final, 1, 1)


def decoder_back_kernel(
    grad_output, tables, decoded, final, joined, slope, gains, mlp,
    grad_join_ref, rounded_ref, before_ref, table_ref, gain_ref,
):
    grad_final = dot(grad_output[...], tables[1], 0, 0)
    add_up(table_ref, dot(final[...], grad_output[...], 0, 1))
    grad_decoded, gain_final = norm_back(grad_final, decoded[...], gains[4:5])
    grad_join, gain_dec = mlp_backward(
        grad_decoded, joined[...], gains[3:4], mlp, slope, rounded_ref, before_ref
    )
    grad_join_ref[...] = grad_join
    add_up(gain_ref, jnp.concatenate([gain_dec, gain_final], axis=0))


def scatter_kernel(edges, grad, out0, out1, out2, high_ref, low_ref):
    rows = out0.shape[0]
    count = edges.shape[0]
    step = pl.program_id(0)

    @pl.when(step == 0)
    def _():
        high, low = two_parts(grad[...])
        high_ref[...] = high
        low_ref[...] = low

    total = grad.shape[0]
    for w, out in enumerate((out0, out1, out2)):
        sub = lax.broadcasted_iota(jnp.int32, (rows, total), 0) + (step * rows + w * total)
        tally = jnp.zeros((rows, total), F32)
        for j in range(count):
            tally = tally + jnp.where(edges[j : j + 1, :] == sub, 1.0, 0.0)
        tally = tally.astype(BF16)
        value = dot(tally, high_ref[...], 1, 0) + dot(tally, low_ref[...], 1, 0)
        out[...] = (value / count).astype(out.dtype)


def processor_back_kernel(
    g0, g1, g2, residual, slope, gains, mlp, attn, o_ref,
    grad_residual_ref, rounded_ref, before_ref, gain_ref, branch_ref, grad_o_ref, delta_ref,
):
    width = residual.shape[1]
    upstream = g1[...] + g0[...].astype(F32) + g2[...].astype(F32)
    grad, gain = mlp_backward(
        upstream, residual[...], gains[2:3], mlp, slope, rounded_ref, before_ref
    )
    add_up(gain_ref, gain)
    grad_residual_ref[...] = grad
    branch = grad.astype(BF16)
    branch_ref[...] = branch
    grad_o = dot(attn[:, 3 * width :], branch, 1, 1).astype(BF16)
    grad_o_ref[...] = grad_o
    depth = width // HEADS
    together = grad_o.astype(F32) * o_ref[...]
    for h in range(HEADS):
        row = jnp.sum(together[h * depth : (h + 1) * depth], axis=0, keepdims=True)
        delta_ref[h] = jnp.broadcast_to(row, delta_ref.shape[1:])


def attend_back_kernel(
    q_ref, do_ref, lse_ref, delta_ref, k0, k1, k2, v0, v1, v2, bias,
    dq_ref, out0, out1, out2, p_ref, ds_ref, *, chunk,
):
    block, depth = k0.shape
    scale = depth**-0.5
    factor = scale * LOG2E
    step, h = pl.program_id(0), pl.program_id(1)
    here = pl.ds(pl.multiple_of(h * depth, depth), depth)
    q = q_ref[here, :]
    do = do_ref[here, :]
    lse = lse_ref[h, 0:1, :]
    delta = delta_ref[h, 0:1, :]
    total = jnp.zeros(q.shape, F32)
    for w, (keys, values, out) in enumerate(((k0, v0, out0), (k1, v1, out1), (k2, v2, out2))):
        for start in range(0, block, chunk):
            part = slice(start, start + chunk)
            p = jnp.exp2(dot(keys[part, :], q, 1, 0) * factor + bias[w, part, :] - lse)
            ds = p * (dot(values[part, :], do, 1, 0) - delta)
            p_ref[part, :] = p.astype(BF16)
            ds_ref[part, :] = ds.astype(BF16)
            out[0, :, part] = (dot(q, ds_ref[part, :], 1, 1) * scale).astype(out.dtype)
            out[1, :, part] = dot(do, p_ref[part, :], 1, 1).astype(out.dtype)
            total = total + dot(keys[part, :], ds_ref[part, :], 0, 0)

    @pl.when(step == 0)
    def _():
        dq_ref[here, :] = total * scale

    @pl.when(step > 0)
    def _():
        dq_ref[here, :] += total * scale


def hand_out(core, value, keep_ref, send_ref, columns):
    bands, rows = keep_ref.shape[1:3]
    for parity in range(2):

        @pl.when(core == parity)
        def _(parity=parity):
            for band in range(bands):
                for side, ref in ((parity, keep_ref), (1 - parity, send_ref)):
                    at = (2 * band + side) * rows
                    ref[0, band, :, columns] = value[at : at + rows].astype(ref.dtype)


def weights_kernel(places, normed, rounded, before, active, keep_ref, send_ref):
    quarter = pl.program_id(0)
    columns = slice(0, before.shape[1])

    @pl.when(quarter < 2)
    def _():
        hand_out(places[2], dot(normed[...], before[...], 0, 0), keep_ref, send_ref, columns)

    @pl.when(quarter >= 2)
    def _():
        hand_out(places[2], dot(rounded[...], active[...], 0, 0), keep_ref, send_ref, columns)


def last_weights_kernel(
    places, normed, rounded, before, active, normed_attn, project, attended, branch, table_in, table_out, gain,
    keep_ref, send_ref,
):
    quarter = pl.program_id(0)
    weights_kernel(places, normed, rounded, before, active, keep_ref, send_ref)
    start = before.shape[1]
    width = normed_attn.shape[1]
    columns = slice(start, start + width)

    @pl.when(quarter < 3)
    def _():
        hand_out(places[2], dot(normed_attn[...], project[...], 0, 1), keep_ref, send_ref, columns)

    @pl.when(quarter == 3)
    def _():
        hand_out(places[2], dot(attended[...], branch[...], 1, 0), keep_ref, send_ref, columns)

    columns = slice(start + width, start + width + table_in.shape[1])
    for index, ref in enumerate((table_in, table_out, gain)):

        @pl.when(quarter == index)
        def _(ref=ref):
            hand_out(places[2], ref[...], keep_ref, send_ref, columns)

    @pl.when(quarter == 3)
    def _():
        hand_out(places[2], jnp.zeros(table_in.shape, F32), keep_ref, send_ref, columns)


def item_kernel(places, *refs, pairs, exact):
    ins, outs = refs[: 2 * pairs], refs[2 * pairs :]
    step = pl.program_id(0)
    for index, out in enumerate(outs):

        @pl.when(step == index)
        def _(index=index, out=out):
            start = 0
            for pair in range(pairs):
                keep, came = ins[2 * pair : 2 * pair + 2]
                value = keep[0] + came[0]
                size = value.shape[-1]
                out[:, :, start : start + size] = value.astype(out.dtype)
                if index > 0 and exact and pair == pairs - 1:
                    part = value[:, :, size - exact :]
                    rest = part - part.astype(out.dtype).astype(F32)
                    out[:, :, start + size : start + size + exact] = rest.astype(out.dtype)
                start += size


def band_kernel(places, own, *refs, count, exact):
    came, outs = refs[:count], refs[count:]
    step = pl.program_id(0)
    size = own.shape[-1]
    total = own[0]
    for ref in came:
        total = total + ref[0, :, :size].astype(F32)
    if exact:
        rest = sum(ref[0, :, size:].astype(F32) for ref in came)
    for index, out in enumerate(outs):

        @pl.when(step == index)
        def _(index=index, out=out):
            out[:, :size] = total.astype(out.dtype)
            if exact:
                part = total[:, size - exact :] + rest
                if index == 0:
                    out[:, size - exact :] = part
                else:
                    high = part.astype(out.dtype)
                    out[:, size - exact : size] = high
                    out[:, size:] = (part - high.astype(F32)).astype(out.dtype)


def exchange(value, axis, distance):
    size = lax.axis_size(axis)
    return lax.ppermute(value, axis, [(i, i ^ distance) for i in range(size)])


def prefetched(kernel, grid, outs, in_specs, out_specs, places, operands, moved):
    return pl.pallas_call(
        kernel,
        grid_spec=pltpu.PrefetchScalarGridSpec(
            num_scalar_prefetch=1, grid=grid, in_specs=in_specs, out_specs=out_specs
        ),
        out_shape=outs,
        cost_estimate=pl.CostEstimate(flops=moved, bytes_accessed=moved, transcendentals=0),
        compiler_params=pltpu.CompilerParams(vmem_limit_bytes=VMEM_BYTES),
    )(places, *operands)


def sort_shares(keeps, sends, places, exact=0):
    items = lax.axis_size("item")
    came = [exchange(send, "lat", 1) for send in sends]
    quarters, bands, rows, _ = keeps[0].shape
    size = sum(keep.shape[-1] for keep in keeps)
    wide = size + exact
    operands = [x for pair in zip(keeps, came) for x in pair]
    return prefetched(
        functools.partial(item_kernel, pairs=len(keeps), exact=exact),
        (items,),
        [shape((bands, rows, size), F32)] + [shape((bands, rows, wide), BF16)] * (items - 1),
        [pl.BlockSpec((1,) + x.shape[1:], lambda j, s: (s[3] ^ j, 0, 0, 0)) for x in operands],
        [pl.BlockSpec((bands, rows, size), lambda j, s: (0, 0, 0))]
        + [pl.BlockSpec((bands, rows, wide), lambda j, s: (0, 0, 0))] * (items - 1),
        places,
        operands,
        moved=14 * bands * rows * size * items,
    )


def sum_shares(sorted_shares, places, exact=0):
    items = lax.axis_size("item")
    own, *others = sorted_shares
    bands, rows, size = own.shape
    wide = size + exact
    came = [exchange(x, "item", k + 1) for k, x in enumerate(others)]
    own, *others = prefetched(
        functools.partial(band_kernel, count=items - 1, exact=exact),
        (bands,),
        [shape((rows, size), F32)] + [shape((rows, wide), BF16)] * (bands - 1),
        [pl.BlockSpec((1, rows, size), lambda j, s: (s[4] ^ j, 0, 0))]
        + [pl.BlockSpec((1, rows, wide), lambda j, s: (s[4] ^ j, 0, 0))] * (items - 1),
        [pl.BlockSpec((rows, size), lambda j, s: (0, 0))]
        + [pl.BlockSpec((rows, wide), lambda j, s: (0, 0))] * (bands - 1),
        places,
        (own, *came),
        moved=14 * bands * rows * size,
    )
    came = [exchange(x, "lat", 2 * (k + 1)) for k, x in enumerate(others)]
    total = own
    for x in came:
        total = total + x[:, :size].astype(F32)
    if exact:
        rest = sum(x[:, size:].astype(F32) for x in came)
        total = jnp.concatenate([total[:, : size - exact], total[:, size - exact :] + rest], axis=1)
    return total


def after(value, *others):
    return lax.optimization_barrier((value, *others))[0]


def all_items(value):
    return [value] + [exchange(value, "item", k) for k in range(1, lax.axis_size("item"))]


def sum_over(value, axis):
    distance = 1
    while distance < lax.axis_size(axis):
        value = value + exchange(value, axis, distance)
        distance *= 2
    return value


def adam_kernel(places, factor, *refs):
    first, second = refs[:4], refs[4:8]
    mlp, attn = refs[8:12], refs[12:16]
    mlp_out, attn_out = refs[16:21], refs[21:26]
    block = mlp[0].shape[-1]
    width = attn[0].shape[-1]
    step = pl.program_id(0)
    for index in range(4):

        @pl.when(step == index)
        def _(index=index):
            scale = factor[0]
            shares = (
                second[index][:, :block], first[index][:, block : 2 * block], first[index][:, :block]
            )
            for layer, share in enumerate(shares):
                new = adam_update(scale * share, *(ref[layer] for ref in mlp), RATE_MATRIX, WEIGHT_DECAY)
                for ref, value in zip(mlp_out, new):
                    ref[layer] = value
            share = second[index][:, block : block + width]
            new = adam_update(scale * share, *(ref[...] for ref in attn), RATE_MATRIX, WEIGHT_DECAY)
            for ref, value in zip(attn_out, new):
                ref[...] = value


def encoder_back_kernel(
    dq, g0, g1, g2, grad_residual, encoded, pooled, slope, gains, mlp, attn, x, pin, grad_join,
    rounded_ref, before_ref, project_ref, table_ref, gain_ref,
):
    width = encoded.shape[1]
    pairs = g1[...] + g0[...].astype(F32) + g2[...].astype(F32)
    project = jnp.concatenate([dq[...], pairs], axis=0).astype(BF16)
    project_ref[...] = project
    grad_normed = dot(project, attn[:, : 3 * width], 0, 1)
    grad_encoded, gain_attn = norm_back(grad_normed, encoded[...], gains[1:2])
    grad_pooled, gain_enc = mlp_backward(
        grad_residual[...] + grad_encoded, pooled[...], gains[0:1], mlp, slope, rounded_ref, before_ref
    )
    add_up(gain_ref, jnp.concatenate([gain_enc, gain_attn], axis=0))
    high, low = two_parts(grad_pooled)
    both = dot(high, pin[...], 0, 0) + dot(low, pin[...], 0, 0)
    channels = x.shape[0]
    high, low = two_parts(grad_join[...])
    direct = dot(high, x[...], 0, 1) + dot(low, x[...], 0, 1)
    add_up(table_ref, direct + both[:, :channels] + both[:, channels:])


def weights(normed, rounded, before, active, places, last=()):
    rows, width = normed.shape
    hidden = before.shape[1]
    bands = lax.axis_size("lat") // 2
    block = hidden // 2
    columns = block + (width + CHANNEL_PAD if last else 0)
    out = shape((4, bands, width // (2 * bands), columns), F32)
    out_spec = pl.BlockSpec((1,) + out.shape[1:], lambda i: (i, 0, 0, 0))
    specs = [
        pl.BlockSpec(memory_space=pltpu.SMEM),
        whole((rows, width)),
        whole((rows, width)),
        pl.BlockSpec((rows, block), lambda i: (0, jnp.minimum(i, 1))),
        pl.BlockSpec((rows, block), lambda i: (0, jnp.maximum(i - 2, 0))),
    ]
    if last:
        specs += [whole((rows, width)), pl.BlockSpec((width, rows), lambda i: (jnp.minimum(i, 2), 0))]
        specs += [whole(x.shape) for x in last[2:]]
    return call(
        last_weights_kernel if last else weights_kernel,
        (4,),
        [out, out],
        specs,
        [out_spec, out_spec],
        (places, normed, rounded, before, active, *last),
        flops=4 * rows * width * hidden,
        moved=4 * rows * hidden + 8 * width * hidden,
    )


def adam_update(gradient, master, moment_one, moment_two, average, step_rate, decay_rate):
    one_new = BETA_ONE * moment_one + (1.0 - BETA_ONE) * gradient
    two_new = BETA_TWO * moment_two + (1.0 - BETA_TWO) * gradient * gradient
    one_hat = one_new / (1.0 - BETA_ONE**STEP)
    two_hat = two_new / (1.0 - BETA_TWO**STEP)
    master_new = master - step_rate * (
        one_hat / (jnp.sqrt(two_hat) + ADAM_EPS) + decay_rate * master
    )
    average_new = EMA_DECAY * average + (1.0 - EMA_DECAY) * master_new
    return (one_new, two_new, master_new, average_new, master_new.astype(jnp.bfloat16))


def from_sides(to_left, to_right):
    size = lax.axis_size("lat")
    up = [(i, (i + 1) % size) for i in range(size - 1)]
    down = [(j, i) for i, j in up]
    return lax.ppermute(to_right, "lat", up), lax.ppermute(to_left, "lat", down)


def shards(
    noisy_state,
    target_state,
    sigmas,
    sh_basis,
    lengths,
    grid_edges,
    mesh_edges,
    dec_edges,
    tables_copy,
    tables_master,
    tables_first,
    tables_second,
    tables_ema,
    attn_copy,
    attn_master,
    attn_first,
    attn_second,
    attn_ema,
    mlp_copy,
    mlp_master,
    mlp_first,
    mlp_second,
    mlp_ema,
    gains_copy,
    gains_master,
    gains_first,
    gains_second,
    gains_ema,
):
    band_index = lax.axis_index("lat")
    bands = lax.axis_size("lat")
    item_index = lax.axis_index("item")
    places = jnp.stack([band_index, bands, band_index % 2, item_index, band_index // 2]).astype(jnp.int32)
    rows = mesh_edges.shape[0]
    grid_rows = noisy_state.shape[2]
    width = attn_copy.shape[0]
    channels = noisy_state.shape[1]
    padded = CHANNEL_PAD
    hidden = mlp_copy.shape[2] // 2
    depth = width // HEADS
    gains = gains_copy.astype(F32)
    gain_rows = gains.shape[0]
    noise_level = sigmas[0]
    square = noise_level * noise_level
    scale_in = lax.rsqrt(square + 1.0)
    scale_skip = 1.0 / (square + 1.0)
    scale_out = noise_level * scale_in
    weight_loss = (square + 1.0) / square
    noisy_field = noisy_state[0]
    target_field = target_state[0]
    extra = padded - channels
    inputs = jnp.pad((scale_in * noisy_field).astype(BF16), ((0, extra), (0, 0)))
    tables = jnp.pad(tables_copy, ((0, 0), (0, extra), (0, 0)))

    def weights_spec(index):
        return pl.BlockSpec((1, width, 2 * hidden), lambda *_: (index, 0, 0))

    attn_spec = whole(attn_copy.shape)
    gains_spec = whole(gains.shape)
    tables_spec = whole(tables.shape)
    steps = rows // ROWS
    kept_shapes = [shape((rows, width), BF16), shape((rows, hidden), F32), shape((rows, hidden), BF16)]
    kept_specs = [rows_of(width), rows_of(hidden), rows_of(hidden)]
    mlp_flops = 4 * rows * width * hidden

    pin, pooled, encoded, normed_enc, slope_enc, active_enc, normed_attn, queries, pairs = call(
        encoder_kernel,
        (steps,),
        [shape((rows, 2 * padded), BF16), shape((rows, width), F32), shape((rows, width), F32)]
        + kept_shapes
        + [shape((rows, width), BF16), shape((width, rows), BF16), shape((rows, 2 * width), BF16)],
        [
            rows_of(grid_edges.shape[1]), whole((padded, grid_rows)), tables_spec, gains_spec,
            weights_spec(0), attn_spec,
        ],
        [rows_of(2 * padded), rows_of(width), rows_of(width)]
        + kept_specs
        + [rows_of(width), lanes_of(width), rows_of(2 * width)],
        (grid_edges, inputs, tables, gains, mlp_copy, attn_copy),
        flops=mlp_flops + 6 * rows * width * width,
        moved=30 * rows * width,
    )

    before_pairs, after_pairs = from_sides(pairs, pairs)

    crops = lengths.shape[1]
    smem = pl.BlockSpec(memory_space=pltpu.SMEM)
    bias_lanes = 128
    bias = call(
        functools.partial(bias_kernel, crops=crops),
        (rows // bias_lanes,),
        shape((3, rows, rows), F32),
        [smem, smem, lanes_of(mesh_edges.shape[1], bias_lanes)],
        pl.BlockSpec((3, rows, bias_lanes), lambda i: (0, 0, i)),
        (places, jnp.cumsum(lengths[0]), mesh_edges.T),
        flops=2 * 10**9,
        moved=12 * rows * rows,
    )

    lanes = 512
    window = [before_pairs, pairs, after_pairs]
    attended, lse = call(
        functools.partial(attend_kernel, chunk=256),
        (rows // lanes, HEADS),
        [shape((width, rows), F32), shape((HEADS, 8, rows), F32)],
        [pl.BlockSpec((depth, lanes), lambda i, h: (h, i))]
        + [pl.BlockSpec((rows, depth), lambda i, h: (0, h))] * 3
        + [pl.BlockSpec((rows, depth), lambda i, h: (0, HEADS + h))] * 3
        + [pl.BlockSpec((3, rows, lanes), lambda i, h: (0, 0, i))],
        [
            pl.BlockSpec((depth, lanes), lambda i, h: (h, i)),
            pl.BlockSpec((1, 8, lanes), lambda i, h: (h, 0, i)),
        ],
        (queries, *window, *window, bias),
        scratch=[pltpu.VMEM((3, rows, lanes), F32)],
        flops=24 * rows * rows * width,
        moved=12 * rows * rows,
    )

    rounded_o, residual, normed_proc, slope_proc, active_proc, sent = call(
        processor_kernel,
        (steps,),
        [shape((width, rows), BF16), shape((rows, width), F32)] + kept_shapes + [shape((rows, width), BF16)],
        [lanes_of(width), rows_of(width), gains_spec, weights_spec(1), attn_spec],
        [lanes_of(width), rows_of(width)] + kept_specs + [rows_of(width)],
        (attended, encoded, gains, mlp_copy, attn_copy),
        flops=mlp_flops + 2 * rows * width * width,
        moved=24 * rows * width,
    )

    before_sent, after_sent = from_sides(sent, sent)

    joined, normed_dec, slope_dec, active_dec, decoded, final, output = call(
        decoder_kernel,
        (grid_rows // ROWS,),
        [shape((grid_rows, width), F32)]
        + kept_shapes
        + [shape((grid_rows, width), F32), shape((grid_rows, width), BF16), shape((padded, grid_rows), F32)],
        [
            rows_of(dec_edges.shape[1]), whole((rows, width)), whole((rows, width)), whole((rows, width)),
            lanes_of(padded), tables_spec, gains_spec, weights_spec(2),
        ],
        [rows_of(width)] + kept_specs + [rows_of(width), rows_of(width), lanes_of(padded)],
        (dec_edges, before_sent, sent, after_sent, inputs, tables, gains, mlp_copy),
        flops=mlp_flops + 6 * rows * rows * width,
        moved=24 * rows * width,
    )

    error_field = scale_skip * noisy_field + scale_out * output[:channels] - target_field
    partial_value = lax.dot_general(
        error_field,
        sh_basis,
        (((1,), (1,)), ((), ())),
        precision=HIGH_PRECISION,
        preferred_element_type=F32,
    )
    coeffs = sum_over(partial_value, "lat")
    slice_width = coeffs.shape[1] // bands
    own_coeffs = lax.dynamic_slice_in_dim(coeffs, band_index * slice_width, slice_width, 1)
    loss_item = weight_loss * jnp.sum(own_coeffs * own_coeffs)
    grad_error = jnp.dot(
        2.0 * weight_loss * coeffs, sh_basis, precision=HIGH_PRECISION, preferred_element_type=F32
    )
    grad_output = jnp.pad((scale_out * grad_error).astype(BF16), ((0, extra), (0, 0)))

    grad_join, rounded_dec, before_dec, table_out, gain_dec = call(
        decoder_back_kernel,
        (grid_rows // ROWS,),
        [
            shape((grid_rows, width), F32), shape((grid_rows, width), BF16), shape((grid_rows, hidden), BF16),
            shape((width, padded), F32), shape((2, width), F32),
        ],
        [
            lanes_of(padded), tables_spec, rows_of(width), rows_of(width), rows_of(width), rows_of(hidden),
            gains_spec, weights_spec(2),
        ],
        [rows_of(width), rows_of(width), rows_of(hidden), whole((width, padded)), whole((2, width))],
        (grad_output, tables, decoded, final, joined, slope_dec, gains, mlp_copy),
        flops=mlp_flops,
        moved=24 * rows * width,
    )

    to_left, grad_own, to_right = call(
        scatter_kernel,
        (steps,),
        [shape((rows, width), BF16), shape((rows, width), F32), shape((rows, width), BF16)],
        [whole((dec_edges.shape[1], grid_rows)), whole((grid_rows, width))],
        [rows_of(width)] * 3,
        (dec_edges.T, grad_join),
        scratch=[pltpu.VMEM((grid_rows, width), BF16), pltpu.VMEM((grid_rows, width), BF16)],
        flops=12 * rows * grid_rows * width,
        moved=12 * rows * width,
    )
    from_left, from_right = from_sides(to_left, to_right)
    keep_dec, send_dec = weights(normed_dec, rounded_dec, before_dec, active_dec, places)

    grad_residual, rounded_proc, before_proc, gain_proc, branch, grad_o, delta = call(
        processor_back_kernel,
        (steps,),
        [
            shape((rows, width), F32), shape((rows, width), BF16), shape((rows, hidden), BF16),
            shape((1, width), F32), shape((rows, width), BF16), shape((width, rows), BF16),
            shape((HEADS, 8, rows), F32),
        ],
        [rows_of(width)] * 4 + [rows_of(hidden), gains_spec, weights_spec(1), attn_spec, lanes_of(width)],
        [
            rows_of(width), rows_of(width), rows_of(hidden), whole((1, width)), rows_of(width), lanes_of(width),
            pl.BlockSpec((HEADS, 8, ROWS), lambda i: (0, 0, i)),
        ],
        (from_left, after(grad_own, keep_dec, send_dec), from_right, residual, slope_proc, gains, mlp_copy, attn_copy, attended),
        flops=mlp_flops + 2 * rows * width * width,
        moved=24 * rows * width,
    )

    block = 512
    side = pl.BlockSpec((2, depth, block), lambda i, h: (0, h, i))
    grad_queries, pairs_left, pairs_own, pairs_right = call(
        functools.partial(attend_back_kernel, chunk=256),
        (rows // block, HEADS),
        [
            shape((width, rows), F32), shape((2, width, rows), BF16), shape((2, width, rows), F32),
            shape((2, width, rows), BF16),
        ],
        [whole((width, rows)), whole((width, rows)), whole((HEADS, 8, rows)), whole((HEADS, 8, rows))]
        + [pl.BlockSpec((block, depth), lambda i, h: (i, h))] * 3
        + [pl.BlockSpec((block, depth), lambda i, h: (i, HEADS + h))] * 3
        + [pl.BlockSpec((3, block, rows), lambda i, h: (0, i, 0))],
        [whole((width, rows)), side, side, side],
        (queries, grad_o, lse, delta, *window, *window, bias),
        scratch=[pltpu.VMEM((block, rows), BF16), pltpu.VMEM((block, rows), BF16)],
        flops=60 * rows * rows * width,
        moved=12 * rows * rows,
    )
    before_grad, after_grad = from_sides(
        pairs_left.reshape(2 * width, rows), pairs_right.reshape(2 * width, rows)
    )
    keep_proc, send_proc = weights(normed_proc, rounded_proc, before_proc, active_proc, places)
    first_sorted = sort_shares([keep_dec, keep_proc], [send_dec, send_proc], places)
    first_total = sum_shares(first_sorted, places)
    first_all = all_items(first_total)

    rounded_enc, before_enc, project, table_in, gain_enc = call(
        encoder_back_kernel,
        (steps,),
        [
            shape((rows, width), BF16), shape((rows, hidden), BF16), shape((3 * width, rows), BF16),
            shape((width, padded), F32), shape((2, width), F32),
        ],
        [lanes_of(width)] + [lanes_of(2 * width)] * 3 + [rows_of(width)] * 3
        + [rows_of(hidden), gains_spec, weights_spec(0), attn_spec, lanes_of(padded), rows_of(2 * padded), rows_of(width)],
        [rows_of(width), rows_of(hidden), lanes_of(3 * width), whole((width, padded)), whole((2, width))],
        (
            grad_queries, before_grad, pairs_own.reshape(2 * width, rows), after_grad,
            after(grad_residual, *first_sorted), encoded,
            pooled, slope_enc, gains, mlp_copy, attn_copy, inputs, pin, grad_join,
        ),
        flops=mlp_flops + 6 * rows * width * width,
        moved=24 * rows * width,
    )
    grad_gains = jnp.concatenate([gain_enc, gain_proc, gain_dec], axis=0)
    gain_columns = jnp.pad(grad_gains.T, ((0, 0), (0, padded - gain_rows)))
    keep_last, send_last = weights(
        normed_enc, rounded_enc, before_enc, active_enc, places,
        (normed_attn, project, rounded_o, branch, table_in, table_out, gain_columns),
    )
    last_total = sum_shares(
        sort_shares([keep_last], [send_last], places, exact=padded), places, exact=padded
    )
    squares = jnp.sum(first_total * first_total) + jnp.sum(last_total * last_total)
    scalars = sum_over(sum_over(jnp.stack([squares, loss_item])[None], "lat"), "item")
    last_all = all_items(last_total)
    loss_sum = scalars[0, 1]
    grad_norm = jnp.sqrt(scalars[0, 0])
    scale_factor = CLIP_LEVEL / jnp.maximum(grad_norm, CLIP_LEVEL)

    shard_rows = attn_master.shape[0]
    quarter = hidden // 2
    mlp_spec = pl.BlockSpec((mlp_master.shape[0], shard_rows, quarter), lambda j, s: (0, 0, s[3] ^ j))
    attn_part = pl.BlockSpec((shard_rows, width), lambda j, s: (0, s[3] ^ j))
    kinds = [F32, F32, F32, F32, BF16]
    updated = prefetched(
        adam_kernel,
        (4,),
        [shape(mlp_master.shape, kind) for kind in kinds] + [shape(attn_master.shape, kind) for kind in kinds],
        [smem]
        + [pl.BlockSpec(x.shape, lambda j, s: (0, 0)) for x in (*first_all, *last_all)]
        + [mlp_spec] * 4
        + [attn_part] * 4,
        [mlp_spec] * 5 + [attn_part] * 5,
        places,
        (
            scale_factor[None], *first_all, *last_all, mlp_master, mlp_first, mlp_second, mlp_ema,
            attn_master, attn_first, attn_second, attn_ema,
        ),
        moved=34 * (mlp_master.size + attn_master.size),
    )
    mlps, att = updated[:5], updated[5:]
    small = jnp.stack([x[:, quarter + width :] for x in last_all])
    tab_sum = jnp.stack(
        [lax.dynamic_index_in_dim(small, item_index ^ q, 0, False)[:, :channels].T for q in range(2)]
    )
    gain_sum = lax.dynamic_index_in_dim(small, item_index ^ 2, 0, False)[:, :gain_rows].T
    tab = adam_update(
        scale_factor * tab_sum, tables_master, tables_first, tables_second, tables_ema, RATE_MATRIX, WEIGHT_DECAY
    )
    gns = adam_update(
        scale_factor * gain_sum, gains_master, gains_first, gains_second, gains_ema, RATE_GAIN, 0.0
    )
    return (loss_sum, grad_norm, *tab, *att, *mlps, *gns)


def solution(mesh):
    table = P(None, None, "lat")
    attn = P("lat", None)
    mlp = P(None, "lat", None)
    gain = P(None, "lat")
    placed = (
        P("item", None, "lat"),
        P("item", None, "lat"),
        P("item"),
        P(None, "lat"),
        P("item", None),
        P("lat", None),
        P("lat", None),
        P("lat", None),
        P(), table, table, table, table,
        P(), attn, attn, attn, attn,
        P(), mlp, mlp, mlp, mlp,
        P(), gain, gain, gain, gain,
    )
    return jax.shard_map(
        shards,
        mesh=mesh,
        in_specs=placed,
        out_specs=(P(), P(), *([table] * 5), *([attn] * 5), *([mlp] * 5), *([gain] * 5)),
        check_vma=False,
    )
```

time: 1400 us -> 527 us (0.38)
  local copies, waits for them, and re-layouts: 425 us -> 17.8 us
  other arithmetic: 415 us -> 9.71 us
  Pallas kernels: 0 us -> 276 us
  waiting for transfers between devices: 269 us -> 115 us
  matrix products: 104 us -> 1.99 us
  blocking collectives: 75 us -> 0 us
  between operations: 23.3 us -> 6.08 us
    pallas_call x0 -> x18, Pallas kernels: none -> 276 us  [the longest x13 233 us: call(): pl.pallas_call(kernel, grid=grid, out_shape=outs, in_specs=in_specs, out_...]
    scatter-add x3 -> x0, other arithmetic: 194 us -> none  [the longest x1 146 us: shards(): near_grad = jnp.zeros((3 * node_rows, 2 * model_width), jnp.float32).at[m...]
    gather x5 -> x0, local copies, waits for them, and re-layouts: 169 us -> none  [the longest x2 129 us: shards(): window[mesh_edges]]
    ppermute x8 -> x37, waiting for transfers between devices: 1.52 us -> 115 us  [the longest x29 113 us: exchange(): return lax.ppermute(value, axis, [(i, i ^ distance) for i in range(size)])]
    reduce_scatter x4 -> x0, waiting for transfers between devices: 104 us -> none  [the longest x1 57.4 us: shards(): lax.psum_scatter(mlp_enc, 'lat', scatter_dimension=0, tiled=True)]
    dot_general x30 -> x1, matrix products: 103 us -> 0.49 us  [shards(): jnp.dot(2.0 * weight_loss * coeffs, sh_basis, precision=HIGH_PRECISION, p...]
    unnamed x9 -> x0, waiting for transfers between devices: 84.5 us -> none
    concatenate x8 -> x2, other arithmetic: 83.9 us -> 1.41 us  [the longest x1 0.71 us: sum_shares(): jnp.concatenate([total[:, :size - exact], total[:, size - exact:] + rest]...]
  transfers between devices with their start and end apart: 15 -> 37, of which waited for: 7 -> 17; matrix products, arithmetic and copies ran while one was open for 42% -> 2% of each run, Pallas kernels for 0% -> 22%
where the time goes in v1:
time: 527 us; the launch traced here: 519 us
  Pallas kernels  276 us (52%)
  waiting for transfers between devices  115 us (22%)
  starting transfers between devices  91.6 us (17%)
  local copies, waits for them, and re-layouts  17.8 us (3%)
  other arithmetic  9.71 us (2%)
  between operations  6.08 us (1%)
    pallas_call x13, Pallas kernels, call(): pl.pallas_call(kernel, grid=grid, out_shape=outs, in_specs=in_specs, out_...  233 us
    ppermute x29, waiting for transfers between devices, exchange(): return lax.ppermute(value, axis, [(i, i ^ distance) for i in range(size)])  113 us
    ppermute x29, starting transfers between devices, exchange(): return lax.ppermute(value, axis, [(i, i ^ distance) for i in range(size)])  62 us
    pallas_call x5, Pallas kernels, prefetched(): pl.pallas_call(kernel, grid_spec=pltpu.PrefetchScalarGridSpec(num_scalar_...  42.9 us
    ppermute x4, starting transfers between devices, from_sides(): lax.ppermute(to_right, 'lat', up)  23.4 us
    unnamed x76, local copies, waits for them, and re-layouts  12.6 us
  transfers between devices with their start and end apart: 37, of which 17 were waited for; matrix products, arithmetic and copies ran while one was open for 2% of the time, Pallas kernels for 22%

profile of v1, /device:TPU:0, one launch (start us, length us, event | category | flops | bytes accessed | tf_op | source)
XLA Modules:
  0.0 518.9 jit_solution(1826178110336219416)
XLA Ops:
  7.9 21.2 %shard_map.435 = (bf16[1024,256]{1,0:T(8,128)(2,1)}, f32[1024,512]{1,0:T(8,128)}, f32[1024,512]{1,0:T(8,128)}, bf16[1024,512]{1,0:T(8,128)(2,1)}, f32[1024,2048]...) custom-call(s32[1024,4]{1,0:T(8,128)} %copy.105.edges, ...), custom_call_target="tpu_custom_call" | custom-call | flops 5905580032 | bytes 15728640 | tf_op jit(solution)/shard_map/pallas_call | solution.py:39
  34.4 10.6 %shard_map.436.bias = f32[3,1024,1024]{2,1,0:T(8,128)} custom-call(s32[5]{0:T(128)} %stack.52.places, s32[16]{0:T(128)} %reduce.ends, s32[16,1024]{1,0:T(8,128)} %bitcast.71), custom_call_target="tpu_custom_call" | custom-call | flops 2000000000 | bytes 12582912 | tf_op jit(solution)/shard_map/pallas_call | solution.py:39
  46.3 25.4 %shard_map.437 = (f32[512,1024]{1,0:T(8,128)}, f32[4,8,1024]{2,1,0:T(8,128)}) custom-call(bf16[512,1024]{1,0:T(8,128)(2,1)} %get-tuple-element.104.q_ref, bf16[1024,1024]{1,0:T(8,128)(2,1)} %copy-done.33, bf16[1024,1024]{1,0:T(8,128)(2,1)} %get-tuple-element.105.k1.v1, bf16[1024,1024]{1,0:T(8,128)(2,1)} %collective-permute-done.1.k2.v2, ...), custom_call_target="tpu_custom_call" | custom-call | flops 12884901888 | bytes 12582912 | tf_op jit(solution)/shard_map/pallas_call | solution.py:39
  71.8 16.0 %shard_map.438 = (bf16[512,1024]{1,0:T(8,128)(2,1)}, f32[1024,512]{1,0:T(8,128)}, bf16[1024,512]{1,0:T(8,128)(2,1)}, f32[1024,2048]{1,0:T(8,128)}, bf16[1024,204...) custom-call(f32[512,1024]{1,0:T(8,128)} %get-tuple-element.106.o_ref, f32[1024,512]{1,0:T(8,128)} %get-tuple-element.107.encoded, ...), custom_call_target="tpu_custom_call" | custom-call | flops 4831838208 | bytes 12582912 | tf_op jit(solution)/shard_map/pallas_call | solution.py:39
  87.7 17.5 %collective-permute-start.2 = (bf16[1024,512]{1,0:T(8,128)(2,1)}, bf16[1024,512]{1,0:T(8,128)(2,1)S(1)}, u32[]{:S(2)}, u32[]{:S(2)}) collective-permute-start(bf16[1024,512]{1,0:T(8,128)(2,1)} %get-tuple-element.108.s1), channel_id=1, source_target_pairs={{0,1},{1,2},{2,3},{3,4},{4,5},{5,6},{6,7},{8,9},{9,10},{10,11},{11... | collective-permute-start | bytes 3145736 | tf_op jit(solution)/shard_map/ppermute | solution.py:625
  111.0 22.5 %shard_map.439 = (f32[1024,512]{1,0:T(8,128)}, bf16[1024,512]{1,0:T(8,128)(2,1)}, f32[1024,2048]{1,0:T(8,128)}, bf16[1024,2048]{1,0:T(8,128)(2,1)}, f32[1024,512...) custom-call(s32[1024,3]{1,0:T(8,128)} %copy.107.edges, bf16[1024,512]{1,0:T(8,128)(2,1)} %copy-done.34, ...), custom_call_target="tpu_custom_call" | custom-call | flops 7516192768 | bytes 12582912 | tf_op jit(solution)/shard_map/pallas_call | solution.py:39
  135.1 11.6 %collective-permute-start.4 = (f32[83,64]{0,1:T(8,128)S(1)}, f32[83,64]{0,1:T(8,128)S(1)}, u32[]{:S(2)}, u32[]{:S(2)}) collective-permute-start(f32[83,64]{0,1:T(8,128)S(1)} %fusion.1), channel_id=1, source_target_pairs={{0,1},{1,0},{2,3},{3,2},{4,5},{5,4},{6,7},{7,6},{8,9},{9,8},{10,11... | collective-permute-start | bytes 63752 | tf_op jit(solution)/shard_map/ppermute | solution.py:453
  157.5 14.8 %shard_map.440 = (f32[1024,512]{1,0:T(8,128)}, bf16[1024,512]{1,0:T(8,128)(2,1)}, bf16[1024,2048]{1,0:T(8,128)(2,1)}, f32[512,128]{1,0:T(8,128)}, f32[2,512]{1,0:T(2,128)}) custom-call(bf16[128,1024]{1,0:T(8,128)(2,1)} %pad.17.grad_output, bf16[2,128,512]{2,1,0:T(8,128)(2,1)} %pad.16.table.tables, f32[1024,512]{1,0:T(8,128)} %get-tuple-element.111.decoded, ...), custom_call_target="tpu_custom_call" | custom-call | flops 4294967296 | bytes 12582912 | tf_op jit(solution)/shard_map/pallas_call | solution.py:39
  172.2 10.0 %shard_map.442 = (bf16[1024,512]{1,0:T(8,128)(2,1)}, f32[1024,512]{1,0:T(8,128)}, bf16[1024,512]{1,0:T(8,128)(2,1)}) custom-call(s32[3,1024]{1,0:T(4,128)} %bitcast.72, f32[1024,512]{1,0:T(8,128)} %get-tuple-element.121.grad.grad_join), custom_call_target="tpu_custom_call" | custom-call | flops 6442450944 | bytes 6291456 | tf_op jit(solution)/shard_map/pallas_call | solution.py:39
  185.5 10.8 %shard_map.441 = (f32[4,4,64,1024]{3,2,1,0:T(8,128)}, f32[4,4,64,1024]{3,2,1,0:T(8,128)}) custom-call(s32[5]{0:T(128)} %stack.52.places, bf16[1024,512]{1,0:T(8,128)(2,1)} %get-tuple-element.109.normed, bf16[1024,512]{1,0:T(8,128)(2,1)} %get-tuple-element.115.rounded, bf16[1024,2048]{1,0:T(8,128)(2,1)} %get-tuple-element.116.before, ...), custom_call_target="tpu_custom_call" | custom-call | flops 4294967296 | bytes 16777216 | tf_op jit(solution)/shard_map/pallas_call | solution.py:39
  200.5 14.6 %shard_map.443 = (f32[1024,512]{1,0:T(8,128)}, bf16[1024,512]{1,0:T(8,128)(2,1)}, bf16[1024,2048]{1,0:T(8,128)(2,1)}, f32[1,512]{1,0:T(1,128)}, bf16[1024,512]{1...) custom-call(bf16[1024,512]{1,0:T(8,128)(2,1)} %copy-done.6, f32[1024,512]{1,0:T(8,128)} %get-tuple-element.124.g1, ...), custom_call_target="tpu_custom_call" | custom-call | flops 4831838208 | bytes 12582912 | tf_op jit(solution)/shard_map/pallas_call | solution.py:39
  215.0 10.9 %shard_map.444 = (f32[4,4,64,1024]{3,2,1,0:T(8,128)}, f32[4,4,64,1024]{3,2,1,0:T(8,128)}) custom-call(s32[5]{0:T(128)} %stack.52.places, bf16[1024,512]{1,0:T(8,128)(2,1)} %get-tuple-element.120.normed, bf16[1024,512]{1,0:T(8,128)(2,1)} %get-tuple-element.128.rounded, bf16[1024,2048]{1,0:T(8,128)(2,1)} %get-tuple-element.129.before, ...), custom_call_target="tpu_custom_call" | custom-call | flops 4294967296 | bytes 16777216 | tf_op jit(solution)/shard_map/pallas_call | solution.py:39
  228.7 40.6 %shard_map.447 = (f32[512,1024]{1,0:T(8,128)}, bf16[2,512,1024]{2,1,0:T(8,128)(2,1)}, f32[2,512,1024]{2,1,0:T(8,128)}, bf16[2,512,1024]{2,1,0:T(8,128)(2,1)}) custom-call(bf16[512,1024]{1,0:T(8,128)(2,1)} %get-tuple-element.104.q_ref, bf16[512,1024]{1,0:T(8,128)(2,1)} %get-tuple-element.142.do_ref, f32[4,8,1024]{2,1,0:T(8,128)} %get-tuple-element.143.lse_ref, ...), custom_call_target="tpu_custom_call" | custom-call | flops 32212254720 | bytes 12582912 | tf_op jit(solution)/shard_map/pallas_call | solution.py:39
  272.9 9.3 %shard_map.445 = (f32[4,64,2048]{2,1,0:T(8,128)}, bf16[4,64,2048]{2,1,0:T(8,128)(2,1)}, bf16[4,64,2048]{2,1,0:T(8,128)(2,1)}, bf16[4,64,2048]{2,1,0:T(8,128)(2,1)}) custom-call(s32[5]{0:T(128)} %stack.52.places, f32[4,4,64,1024]{3,2,1,0:T(8,128)} %get-tuple-element.118.refs_0_, f32[4,4,64,1024]{3,2,1,0:T(8,128)} %collective-permute-done.7.refs_1_, ...), custom_call_target="tpu_custom_call" | custom-call | flops 29360128 | bytes 29360128 | tf_op jit(solution)/shard_map/pallas_call | solution.py:457
  283.4 20.3 %shard_map.448 = (bf16[1024,512]{1,0:T(8,128)(2,1)}, bf16[1024,2048]{1,0:T(8,128)(2,1)}, bf16[1536,1024]{1,0:T(8,128)(2,1)}, f32[512,128]{1,0:T(8,128)}, f32[2,512]{1,0:T(2,128)}) custom-call(f32[512,1024]{1,0:T(8,128)} %get-tuple-element.145.dq, bf16[1024,1024]{1,0:T(8,128)(2,1)} %copy-done.2, f32[1024,1024]{1,0:T(8,128)} %bitcast.67, ...), custom_call_target="tpu_custom_call" | custom-call | flops 5905580032 | bytes 12582912 | tf_op jit(solution)/shard_map/pallas_call | solution.py:39
  305.3 15.6 %shard_map.449 = (f32[4,4,64,1664]{3,2,1,0:T(8,128)}, f32[4,4,64,1664]{3,2,1,0:T(8,128)}) custom-call(s32[5]{0:T(128)} %stack.52.places, bf16[1024,512]{1,0:T(8,128)(2,1)} %get-tuple-element.141.normed, bf16[1024,512]{1,0:T(8,128)(2,1)} %get-tuple-element.154.rounded, bf16[1024,2048]{1,0:T(8,128)(2,1)} %get-tuple-element.155.before, ...), custom_call_target="tpu_custom_call" | custom-call | flops 4294967296 | bytes 16777216 | tf_op jit(solution)/shard_map/pallas_call | solution.py:39
  321.0 17.3 %collective-permute-start.19 = (f32[4,4,64,1664]{3,2,1,0:T(8,128)}, f32[4,4,64,1664]{3,2,1,0:T(8,128)}, u32[]{:S(2)}, u32[]{:S(2)}) collective-permute-start(f32[4,4,64,1664]{3,2,1,0:T(8,128)} %get-tuple-element.167), channel_id=1, source_target_pairs={{0,1},{1,0},{2,3},{3,2},{4,5},{5,4},{6,7},{7,6},{8,9},{9,8},{10,11... | collective-permute-start | bytes 20447240 | tf_op jit(solution)/shard_map/ppermute | solution.py:453
  341.7 7.4 %collective-permute-done.19.refs_1_ = f32[4,4,64,1664]{3,2,1,0:T(8,128)} collective-permute-done((f32[4,4,64,1664]{3,2,1,0:T(8,128)}, f32[4,4,64,1664]{3,2,1,0:T(8,128)}, u32[]{:S(2)}, u32[]{:S(2)}) %collective-permute-start.19) | collective-permute-done | bytes 6815776 | tf_op jit(solution)/shard_map/ppermute | solution.py:453
  349.1 8.3 %shard_map.450 = (f32[4,64,1664]{2,1,0:T(8,128)}, bf16[4,64,1792]{2,1,0:T(8,128)(2,1)}, bf16[4,64,1792]{2,1,0:T(8,128)(2,1)}, bf16[4,64,1792]{2,1,0:T(8,128)(2,1)}) custom-call(s32[5]{0:T(128)} %stack.52.places, f32[4,4,64,1664]{3,2,1,0:T(8,128)} %get-tuple-element.166.refs_0_, f32[4,4,64,1664]{3,2,1,0:T(8,128)} %collective-permute-done.19.refs_1_), custom_call_target="tpu_custom_call" | custom-call | flops 23855104 | bytes 23855104 | tf_op jit(solution)/shard_map/pallas_call | solution.py:457
  360.4 4.0 collective-permute-done.11.refs_0_
  366.9 21.5 %collective-permute-done.12.refs_1_ = bf16[4,64,2048]{2,1,0:T(8,128)(2,1)S(1)} collective-permute-done((bf16[4,64,2048]{2,1,0:T(8,128)(2,1)}, bf16[4,64,2048]{2,1,0:T(8,128)(2,1)S(1)}, u32[]{:S(2)}, u32[]{:S(2)}) %collective-permute-start.12) | collective-permute-done | bytes 1048608 | tf_op jit(solution)/shard_map/ppermute | solution.py:453
  390.4 5.2 shard_map.446
  397.2 9.4 %collective-permute-done.20.refs_0_ = bf16[4,64,1792]{2,1,0:T(8,128)(2,1)S(1)} collective-permute-done((bf16[4,64,1792]{2,1,0:T(8,128)(2,1)}, bf16[4,64,1792]{2,1,0:T(8,128)(2,1)S(1)}, u32[]{:S(2)}, u32[]{:S(2)}) %collective-permute-start.20) | collective-permute-done | bytes 917536 | tf_op jit(solution)/shard_map/ppermute | solution.py:453
  408.1 18.6 %collective-permute-done.21.refs_1_ = bf16[4,64,1792]{2,1,0:T(8,128)(2,1)} collective-permute-done((bf16[4,64,1792]{2,1,0:T(8,128)(2,1)}, bf16[4,64,1792]{2,1,0:T(8,128)(2,1)}, u32[]{:S(2)}, u32[]{:S(2)}) %collective-permute-start.21) | collective-permute-done | bytes 917536 | tf_op jit(solution)/shard_map/ppermute | solution.py:453
  426.7 4.9 shard_map.451
  439.0 3.4 collective-permute-done.25
  442.4 10.5 %collective-permute-done.24 = bf16[64,1792]{1,0:T(8,128)(2,1)S(1)} collective-permute-done((bf16[64,1792]{1,0:T(8,128)(2,1)}, bf16[64,1792]{1,0:T(8,128)(2,1)S(1)}, u32[]{:S(2)}, u32[]{:S(2)}) %collective-permute-start.24) | collective-permute-done | bytes 229408 | tf_op jit(solution)/shard_map/ppermute | solution.py:453
  460.3 3.5 collective-permute-done.27
  463.9 4.4 collective-permute-done.28
  472.4 3.0 collective-permute-done.30
  479.6 18.0 %collective-permute-done.31.refs_5_ = f32[64,1664]{1,0:T(8,128)S(1)} collective-permute-done((f32[64,1664]{1,0:T(8,128)S(1)}, f32[64,1664]{1,0:T(8,128)S(1)}, u32[]{:S(2)}, u32[]{:S(2)}) %collective-permute-start.31) | collective-permute-done | bytes 426016 | tf_op jit(solution)/shard_map/ppermute | solution.py:453
  502.2 15.2 %shard_map.452 = (f32[3,64,4096]{2,1,0:T(8,128)}, f32[3,64,4096]{2,1,0:T(8,128)}, f32[3,64,4096]{2,1,0:T(8,128)}, f32[3,64,4096]{2,1,0:T(8,128)}, bf16[3,64,4096...) custom-call(s32[5]{0:T(128)} %stack.52.places, ...), custom_call_target="tpu_custom_call" | custom-call | flops 31195136 | bytes 31195136 | tf_op jit(solution)/shard_map/pallas_call | solution.py:457
  (176 shorter events, 86.3 us)
Async XLA Ops:
  29.1 15.9 %collective-permute-start = (bf16[1024,1024]{1,0:T(8,128)(2,1)}, bf16[1024,1024]{1,0:T(8,128)(2,1)S(1)}, u32[]{:S(2)}, u32[]{:S(2)}) collective-permute-start(bf16[1024,1024]{1,0:T(8,128)(2,1)} %get-tuple-element.105.k1.v1), channel_id=1, source_target_pairs={{0,1},{1,2},{2,3},{3,4},{4,5},{5,6},{6,7},{8,9},{9,10},{10,11},{11... | collective-permute-start | bytes 6291464 | tf_op jit(solution)/shard_map/ppermute | solution.py:625
  31.6 13.4 %collective-permute-start.1 = (bf16[1024,1024]{1,0:T(8,128)(2,1)}, bf16[1024,1024]{1,0:T(8,128)(2,1)}, u32[]{:S(2)}, u32[]{:S(2)}) collective-permute-start(bf16[1024,1024]{1,0:T(8,128)(2,1)} %get-tuple-element.105.k1.v1), channel_id=1, source_target_pairs={{1,0},{2,1},{3,2},{4,3},{5,4},{6,5},{7,6},{9,8},{10,9},{11,10},{12... | collective-permute-start | bytes 6291464 | tf_op jit(solution)/shard_map/ppermute | solution.py:625
  87.7 20.2 %collective-permute-start.2 = (bf16[1024,512]{1,0:T(8,128)(2,1)}, bf16[1024,512]{1,0:T(8,128)(2,1)S(1)}, u32[]{:S(2)}, u32[]{:S(2)}) collective-permute-start(bf16[1024,512]{1,0:T(8,128)(2,1)} %get-tuple-element.108.s1), channel_id=1, source_target_pairs={{0,1},{1,2},{2,3},{3,4},{4,5},{5,6},{6,7},{8,9},{9,10},{10,11},{11... | collective-permute-start | bytes 3145736 | tf_op jit(solution)/shard_map/ppermute | solution.py:625
  105.3 4.8 collective-permute-start.3
  135.1 12.4 %collective-permute-start.4 = (f32[83,64]{0,1:T(8,128)S(1)}, f32[83,64]{0,1:T(8,128)S(1)}, u32[]{:S(2)}, u32[]{:S(2)}) collective-permute-start(f32[83,64]{0,1:T(8,128)S(1)} %fusion.1), channel_id=1, source_target_pairs={{0,1},{1,0},{2,3},{3,2},{4,5},{5,4},{6,7},{7,6},{8,9},{9,8},{10,11... | collective-permute-start | bytes 63752 | tf_op jit(solution)/shard_map/ppermute | solution.py:453
  151.4 4.8 collective-permute-start.6
  182.3 16.9 %collective-permute-start.8 = (bf16[1024,512]{1,0:T(8,128)(2,1)}, bf16[1024,512]{1,0:T(8,128)(2,1)S(1)}, u32[]{:S(2)}, u32[]{:S(2)}) collective-permute-start(bf16[1024,512]{1,0:T(8,128)(2,1)} %get-tuple-element.122), channel_id=1, source_target_pairs={{0,1},{1,2},{2,3},{3,4},{4,5},{5,6},{6,7},{8,9},{9,10},{10,11},{11... | collective-permute-start | bytes 3145736 | tf_op jit(solution)/shard_map/ppermute | solution.py:625
  183.6 15.5 %collective-permute-start.9 = (bf16[1024,512]{1,0:T(8,128)(2,1)}, bf16[1024,512]{1,0:T(8,128)(2,1)S(1)}, u32[]{:S(2)}, u32[]{:S(2)}) collective-permute-start(bf16[1024,512]{1,0:T(8,128)(2,1)} %get-tuple-element.125), channel_id=1, source_target_pairs={{1,0},{2,1},{3,2},{4,3},{5,4},{6,5},{7,6},{9,8},{10,9},{11,10},{12... | collective-permute-start | bytes 3145736 | tf_op jit(solution)/shard_map/ppermute | solution.py:625
  196.3 76.6 %collective-permute-start.7 = (f32[4,4,64,1024]{3,2,1,0:T(8,128)}, f32[4,4,64,1024]{3,2,1,0:T(8,128)}, u32[]{:S(2)}, u32[]{:S(2)}) collective-permute-start(f32[4,4,64,1024]{3,2,1,0:T(8,128)} %get-tuple-element.119), channel_id=1, source_target_pairs={{0,1},{1,0},{2,3},{3,2},{4,5},{5,4},{6,7},{7,6},{8,9},{9,8},{10,11... | collective-permute-start | bytes 12582920 | tf_op jit(solution)/shard_map/ppermute | solution.py:453
  225.9 46.9 %collective-permute-start.10 = (f32[4,4,64,1024]{3,2,1,0:T(8,128)}, f32[4,4,64,1024]{3,2,1,0:T(8,128)}, u32[]{:S(2)}, u32[]{:S(2)}) collective-permute-start(f32[4,4,64,1024]{3,2,1,0:T(8,128)} %get-tuple-element.132), channel_id=1, source_target_pairs={{0,1},{1,0},{2,3},{3,2},{4,5},{5,4},{6,7},{7,6},{8,9},{9,8},{10,11... | collective-permute-start | bytes 12582920 | tf_op jit(solution)/shard_map/ppermute | solution.py:453
  269.3 12.8 %collective-permute-start.17 = (bf16[1024,1024]{1,0:T(8,128)(2,1)}, bf16[1024,1024]{1,0:T(8,128)(2,1)S(1)}, u32[]{:S(2)}, u32[]{:S(2)}) collective-permute-start(bf16[1024,1024]{1,0:T(8,128)(2,1)} %bitcast.75), channel_id=1, source_target_pairs={{0,1},{1,2},{2,3},{3,4},{4,5},{5,6},{6,7},{8,9},{9,10},{10,11},{11... | collective-permute-start | bytes 6291464 | tf_op jit(solution)/shard_map/ppermute | solution.py:625
  271.4 10.8 %collective-permute-start.18 = (bf16[1024,1024]{1,0:T(8,128)(2,1)}, bf16[1024,1024]{1,0:T(8,128)(2,1)}, u32[]{:S(2)}, u32[]{:S(2)}) collective-permute-start(bf16[1024,1024]{1,0:T(8,128)(2,1)} %bitcast.74), channel_id=1, source_target_pairs={{1,0},{2,1},{3,2},{4,3},{5,4},{6,5},{7,6},{9,8},{10,9},{11,10},{12... | collective-permute-start | bytes 6291464 | tf_op jit(solution)/shard_map/ppermute | solution.py:625
  321.0 28.2 %collective-permute-start.19 = (f32[4,4,64,1664]{3,2,1,0:T(8,128)}, f32[4,4,64,1664]{3,2,1,0:T(8,128)}, u32[]{:S(2)}, u32[]{:S(2)}) collective-permute-start(f32[4,4,64,1664]{3,2,1,0:T(8,128)} %get-tuple-element.167), channel_id=1, source_target_pairs={{0,1},{1,0},{2,3},{3,2},{4,5},{5,4},{6,7},{7,6},{8,9},{9,8},{10,11... | collective-permute-start | bytes 20447240 | tf_op jit(solution)/shard_map/ppermute | solution.py:453
  338.3 26.2 %collective-permute-start.11 = (bf16[4,64,2048]{2,1,0:T(8,128)(2,1)}, bf16[4,64,2048]{2,1,0:T(8,128)(2,1)S(1)}, u32[]{:S(2)}, u32[]{:S(2)}) collective-permute-start(bf16[4,64,2048]{2,1,0:T(8,128)(2,1)} %get-tuple-element.134), channel_id=1, source_target_pairs={{0,8},{8,0},{16,24},{24,16},{1,9},{9,1},{17,25},{25,17},{2,10},{10... | collective-permute-start | bytes 3145736 | tf_op jit(solution)/shard_map/ppermute | solution.py:453
  339.7 48.7 %collective-permute-start.12 = (bf16[4,64,2048]{2,1,0:T(8,128)(2,1)}, bf16[4,64,2048]{2,1,0:T(8,128)(2,1)S(1)}, u32[]{:S(2)}, u32[]{:S(2)}) collective-permute-start(bf16[4,64,2048]{2,1,0:T(8,128)(2,1)} %get-tuple-element.135), channel_id=1, source_target_pairs={{0,16},{8,24},{16,0},{24,8},{1,17},{9,25},{17,1},{25,9},{2,18},{10... | collective-permute-start | bytes 3145736 | tf_op jit(solution)/shard_map/ppermute | solution.py:453
  341.3 47.2 %collective-permute-start.13 = (bf16[4,64,2048]{2,1,0:T(8,128)(2,1)}, bf16[4,64,2048]{2,1,0:T(8,128)(2,1)S(1)}, u32[]{:S(2)}, u32[]{:S(2)}) collective-permute-start(bf16[4,64,2048]{2,1,0:T(8,128)(2,1)} %get-tuple-element.136), channel_id=1, source_target_pairs={{0,24},{8,16},{16,8},{24,0},{1,25},{9,17},{17,9},{25,1},{2,26},{10... | collective-permute-start | bytes 3145736 | tf_op jit(solution)/shard_map/ppermute | solution.py:453
  357.4 49.3 %collective-permute-start.20 = (bf16[4,64,1792]{2,1,0:T(8,128)(2,1)}, bf16[4,64,1792]{2,1,0:T(8,128)(2,1)S(1)}, u32[]{:S(2)}, u32[]{:S(2)}) collective-permute-start(bf16[4,64,1792]{2,1,0:T(8,128)(2,1)} %get-tuple-element.169), channel_id=1, source_target_pairs={{0,8},{8,0},{16,24},{24,16},{1,9},{9,1},{17,25},{25,17},{2,10},{10... | collective-permute-start | bytes 2752520 | tf_op jit(solution)/shard_map/ppermute | solution.py:453
  358.9 67.8 %collective-permute-start.21 = (bf16[4,64,1792]{2,1,0:T(8,128)(2,1)}, bf16[4,64,1792]{2,1,0:T(8,128)(2,1)}, u32[]{:S(2)}, u32[]{:S(2)}) collective-permute-start(bf16[4,64,1792]{2,1,0:T(8,128)(2,1)} %get-tuple-element.170), channel_id=1, source_target_pairs={{0,16},{8,24},{16,0},{24,8},{1,17},{9,25},{17,1},{25,9},{2,18},{10... | collective-permute-start | bytes 2752520 | tf_op jit(solution)/shard_map/ppermute | solution.py:453
  364.5 62.2 %collective-permute-start.22 = (bf16[4,64,1792]{2,1,0:T(8,128)(2,1)}, bf16[4,64,1792]{2,1,0:T(8,128)(2,1)}, u32[]{:S(2)}, u32[]{:S(2)}) collective-permute-start(bf16[4,64,1792]{2,1,0:T(8,128)(2,1)} %get-tuple-element.171), channel_id=1, source_target_pairs={{0,24},{8,16},{16,8},{24,0},{1,25},{9,17},{17,9},{25,1},{2,26},{10... | collective-permute-start | bytes 2752520 | tf_op jit(solution)/shard_map/ppermute | solution.py:453
  395.6 37.8 %collective-permute-start.16 = (bf16[64,2048]{1,0:T(8,128)(2,1)}, bf16[64,2048]{1,0:T(8,128)(2,1)S(1)}, u32[]{:S(2)}, u32[]{:S(2)}) collective-permute-start(bf16[64,2048]{1,0:T(8,128)(2,1)} %get-tuple-element.140), channel_id=1, source_target_pairs={{0,6},{1,7},{2,4},{3,5},{4,2},{5,3},{6,0},{7,1},{8,14},{9,15},{10,... | collective-permute-start | bytes 786440 | tf_op jit(solution)/shard_map/ppermute | solution.py:453
  395.6 40.6 %collective-permute-start.15 = (bf16[64,2048]{1,0:T(8,128)(2,1)}, bf16[64,2048]{1,0:T(8,128)(2,1)S(1)}, u32[]{:S(2)}, u32[]{:S(2)}) collective-permute-start(bf16[64,2048]{1,0:T(8,128)(2,1)} %get-tuple-element.139), channel_id=1, source_target_pairs={{0,4},{1,5},{2,6},{3,7},{4,0},{5,1},{6,2},{7,3},{8,12},{9,13},{10,... | collective-permute-start | bytes 786440 | tf_op jit(solution)/shard_map/ppermute | solution.py:453
  406.7 29.5 %collective-permute-start.14 = (bf16[64,2048]{1,0:T(8,128)(2,1)}, bf16[64,2048]{1,0:T(8,128)(2,1)S(1)}, u32[]{:S(2)}, u32[]{:S(2)}) collective-permute-start(bf16[64,2048]{1,0:T(8,128)(2,1)} %get-tuple-element.138), channel_id=1, source_target_pairs={{0,2},{1,3},{2,0},{3,1},{4,6},{5,7},{6,4},{7,5},{8,10},{9,11},{10,... | collective-permute-start | bytes 786440 | tf_op jit(solution)/shard_map/ppermute | solution.py:453
  431.7 10.7 %collective-permute-start.25 = (bf16[64,1792]{1,0:T(8,128)(2,1)}, bf16[64,1792]{1,0:T(8,128)(2,1)S(1)}, u32[]{:S(2)}, u32[]{:S(2)}) collective-permute-start(bf16[64,1792]{1,0:T(8,128)(2,1)} %get-tuple-element.175), channel_id=1, source_target_pairs={{0,6},{1,7},{2,4},{3,5},{4,2},{5,3},{6,0},{7,1},{8,14},{9,15},{10,... | collective-permute-start | bytes 688136 | tf_op jit(solution)/shard_map/ppermute | solution.py:453
  431.8 21.1 %collective-permute-start.24 = (bf16[64,1792]{1,0:T(8,128)(2,1)}, bf16[64,1792]{1,0:T(8,128)(2,1)S(1)}, u32[]{:S(2)}, u32[]{:S(2)}) collective-permute-start(bf16[64,1792]{1,0:T(8,128)(2,1)} %get-tuple-element.174), channel_id=1, source_target_pairs={{0,4},{1,5},{2,6},{3,7},{4,0},{5,1},{6,2},{7,3},{8,12},{9,13},{10,... | collective-permute-start | bytes 688136 | tf_op jit(solution)/shard_map/ppermute | solution.py:453
  433.4 19.5 %collective-permute-start.23 = (bf16[64,1792]{1,0:T(8,128)(2,1)}, bf16[64,1792]{1,0:T(8,128)(2,1)S(1)}, u32[]{:S(2)}, u32[]{:S(2)}) collective-permute-start(bf16[64,1792]{1,0:T(8,128)(2,1)} %get-tuple-element.173), channel_id=1, source_target_pairs={{0,2},{1,3},{2,0},{3,1},{4,6},{5,7},{6,4},{7,5},{8,10},{9,11},{10,... | collective-permute-start | bytes 688136 | tf_op jit(solution)/shard_map/ppermute | solution.py:453
  436.9 64.2 %collective-permute-start.34 = (f32[64,2048]{1,0:T(8,128)S(1)}, f32[64,2048]{1,0:T(8,128)S(1)}, u32[]{:S(2)}, u32[]{:S(2)}) collective-permute-start(f32[64,2048]{1,0:T(8,128)S(1)} %get-tuple-element.239.refs_0_), channel_id=1, source_target_pairs={{0,8},{8,0},{16,24},{24,16},{1,9},{9,1},{17,25},{25,17},{2,10},{10... | collective-permute-start | bytes 1572872 | tf_op jit(solution)/shard_map/ppermute | solution.py:453
  438.2 62.9 %collective-permute-start.35 = (f32[64,2048]{1,0:T(8,128)S(1)}, f32[64,2048]{1,0:T(8,128)S(1)}, u32[]{:S(2)}, u32[]{:S(2)}) collective-permute-start(f32[64,2048]{1,0:T(8,128)S(1)} %get-tuple-element.239.refs_0_), channel_id=1, source_target_pairs={{0,16},{8,24},{16,0},{24,8},{1,17},{9,25},{17,1},{25,9},{2,18},{10... | collective-permute-start | bytes 1572872 | tf_op jit(solution)/shard_map/ppermute | solution.py:453
  454.8 22.7 %collective-permute-start.33 = (f32[64,1664]{1,0:T(8,128)S(1)}, f32[64,1664]{1,0:T(8,128)S(1)}, u32[]{:S(2)}, u32[]{:S(2)}) collective-permute-start(f32[64,1664]{1,0:T(8,128)S(1)} %get-tuple-element.240.refs_4_), channel_id=1, source_target_pairs={{0,24},{8,16},{16,8},{24,0},{1,25},{9,17},{17,9},{25,1},{2,26},{10... | collective-permute-start | bytes 1277960 | tf_op jit(solution)/shard_map/ppermute | solution.py:453
  456.2 22.6 %collective-permute-start.32 = (f32[64,1664]{1,0:T(8,128)S(1)}, f32[64,1664]{1,0:T(8,128)}, u32[]{:S(2)}, u32[]{:S(2)}) collective-permute-start(f32[64,1664]{1,0:T(8,128)S(1)} %get-tuple-element.240.refs_4_), channel_id=1, source_target_pairs={{0,16},{8,24},{16,0},{24,8},{1,17},{9,25},{17,1},{25,9},{2,18},{10... | collective-permute-start | bytes 1277960 | tf_op jit(solution)/shard_map/ppermute | solution.py:453
  463.9 4.4 collective-permute-start.28
  475.4 25.7 %collective-permute-start.36 = (f32[64,2048]{1,0:T(8,128)S(1)}, f32[64,2048]{1,0:T(8,128)S(1)}, u32[]{:S(2)}, u32[]{:S(2)}) collective-permute-start(f32[64,2048]{1,0:T(8,128)S(1)} %get-tuple-element.239.refs_0_), channel_id=1, source_target_pairs={{0,24},{8,16},{16,8},{24,0},{1,25},{9,17},{17,9},{25,1},{2,26},{10... | collective-permute-start | bytes 1572872 | tf_op jit(solution)/shard_map/ppermute | solution.py:453
  477.5 20.1 %collective-permute-start.31 = (f32[64,1664]{1,0:T(8,128)S(1)}, f32[64,1664]{1,0:T(8,128)S(1)}, u32[]{:S(2)}, u32[]{:S(2)}) collective-permute-start(f32[64,1664]{1,0:T(8,128)S(1)} %get-tuple-element.240.refs_4_), channel_id=1, source_target_pairs={{0,8},{8,0},{16,24},{24,16},{1,9},{9,1},{17,25},{25,17},{2,10},{10... | collective-permute-start | bytes 1277960 | tf_op jit(solution)/shard_map/ppermute | solution.py:453
  (41 other events, 1120.4 us)

commit v2 on v1

--- a/solution.py
+++ b/solution.py
@@ -8,6 +8,9 @@
 from jax.sharding import PartitionSpec as P
 
 HEADS = 4
+GROUPS = 2
+WEIGH = 30
+LARGE = 1 << 20
 STEP = 10
 
 EPS_NORM = 1e-05
@@ -26,7 +29,7 @@
 LOG2E = 1.4426950408889634
 CHANNEL_PAD = 128
 ROWS = 256
-VMEM_BYTES = 60 * 1024 * 1024
+VMEM_BYTES = 36 * 1024 * 1024
 
 
 def dot(left, right, left_dim, right_dim):
@@ -35,17 +38,34 @@
     )
 
 
-def call(kernel, grid, outs, in_specs, out_specs, operands, scratch=(), flops=0, moved=0):
-    return pl.pallas_call(
+FAR = []
+
+
+def is_far(value):
+    return any(value is x for x in FAR)
+
+
+def far(value):
+    return pltpu.with_memory_space_constraint(value, pltpu.HBM) if is_far(value) else value
+
+
+def call(kernel, grid, outs, in_specs, out_specs, operands, scratch=(), flops=0, moved=0, near=False):
+    single = not isinstance(outs, list)
+    kinds = [outs] if single else outs
+    large = [not near and x.size * x.dtype.itemsize >= LARGE for x in kinds]
+    kinds = [pltpu.HBM(x.shape, x.dtype) if flag else x for x, flag in zip(kinds, large)]
+    results = pl.pallas_call(
         kernel,
         grid=grid,
-        out_shape=outs,
+        out_shape=kinds[0] if single else kinds,
         in_specs=in_specs,
         out_specs=out_specs,
         scratch_shapes=list(scratch),
-        cost_estimate=pl.CostEstimate(flops=flops, bytes_accessed=moved, transcendentals=0),
+        cost_estimate=pl.CostEstimate(flops=flops * WEIGH, bytes_accessed=moved * WEIGH, transcendentals=0),
         compiler_params=pltpu.CompilerParams(vmem_limit_bytes=VMEM_BYTES),
-    )(*operands)
+    )(*[far(x) for x in operands])
+    FAR.extend(x for x, flag in zip([results] if single else results, large) if flag)
+    return results
 
 
 def whole(shape):
@@ -84,9 +104,9 @@
     root = 0.7978845608028654
     cubic = 0.044715
     square = u * u
-    t = jnp.tanh(root * u * (1.0 + cubic * square))
-    half = 0.5 * (1.0 + t)
-    slope = half + 0.5 * u * (1.0 - t * t) * (root + (3.0 * root * cubic) * square)
+    inner = u * (root + (root * cubic) * square)
+    half = 0.5 + 0.5 * jnp.tanh(inner)
+    slope = half * (1.0 + (1.0 - half) * (6.0 * inner - (4.0 * root) * u))
     return u * half, slope
 
 
@@ -95,10 +115,13 @@
     normed = (norm_parts(values)[0] * gain_row).astype(BF16)
     normed_ref[...] = normed
     result = jnp.zeros(values.shape, F32)
-    for start in range(0, hidden, step):
+    starts = range(0, hidden, step)
+    befores = [dot(normed, w_ref[0, :, :step], 1, 0)]
+    for start in starts:
         part = slice(start, start + step)
-        before = dot(normed, w_ref[0, :, part], 1, 0)
-        active, slope = gelu_parts(before)
+        if start + step < hidden:
+            befores.append(dot(normed, w_ref[0, :, start + step : start + 2 * step], 1, 0))
+        active, slope = gelu_parts(befores.pop(0))
         active = active.astype(BF16)
         slope_ref[:, part] = slope
         active_ref[:, part] = active
@@ -126,6 +149,13 @@
     return high, (values - high.astype(F32)).astype(BF16)
 
 
+def named(edges, places):
+    tally = jnp.zeros(places.shape, F32)
+    for j in range(edges.shape[0]):
+        tally = tally + jnp.where(edges[j : j + 1, :] == places, 1.0, 0.0)
+    return tally.astype(BF16)
+
+
 def add_up(ref, value):
     step = pl.program_id(0)
 
@@ -140,15 +170,12 @@
 
 def encoder_kernel(
     edges, x, table, gains, mlp, attn,
-    pin_ref, pooled_ref, encoded_ref, normed_ref, slope_ref, active_ref, normed_attn_ref, q_ref, kv_ref,
+    pin_ref, pooled_ref, encoded_ref, normed_ref, slope_ref, active_ref, normed_attn_ref, q_ref, *pair_refs,
 ):
-    rows, count = edges.shape
+    count, rows = edges.shape
     width = attn.shape[0]
-    lanes = lax.broadcasted_iota(jnp.int32, (rows, x.shape[1]), 1)
-    tally = jnp.zeros(lanes.shape, F32)
-    for j in range(count):
-        tally = tally + jnp.where(edges[:, j : j + 1] == lanes, 1.0, 0.0)
-    pin = dot(tally.astype(BF16), x[...], 1, 1) / count
+    places = lax.broadcasted_iota(jnp.int32, (x.shape[1], rows), 0)
+    pin = dot(named(edges, places), x[...], 0, 1) / count
     high, low = two_parts(pin)
     pin_ref[...] = jnp.concatenate([high, low], axis=1)
     pooled = dot(high, table[0], 1, 0) + dot(low, table[0], 1, 0)
@@ -158,7 +185,13 @@
     normed_attn = (norm_parts(encoded)[0] * gains[1:2]).astype(BF16)
     normed_attn_ref[...] = normed_attn
     q_ref[...] = dot(attn[:, :width], normed_attn, 0, 1).astype(BF16)
-    kv_ref[...] = dot(normed_attn, attn[:, width : 3 * width], 1, 0).astype(BF16)
+    part = width // len(pair_refs)
+    for g, ref in enumerate(pair_refs):
+        for side in range(2):
+            start = (1 + side) * width + g * part
+            ref[:, side * part : (side + 1) * part] = dot(
+                normed_attn, attn[:, start : start + part], 1, 0
+            ).astype(BF16)
 
 
 def bias_kernel(places, ends, edges, bias_ref, *, crops):
@@ -223,13 +256,12 @@
 
 
 def processor_kernel(
-    o_ref, encoded, gains, mlp, attn,
+    o0, o1, encoded, gains, mlp, attn,
     attended_ref, residual_ref, normed_ref, slope_ref, active_ref, sent_ref,
 ):
-    width = encoded.shape[1]
-    attended = o_ref[...].astype(BF16)
+    attended = jnp.concatenate([o0[...], o1[...]], axis=0).astype(BF16)
     attended_ref[...] = attended
-    residual = encoded[...] + dot(attended, attn[:, 3 * width :], 0, 0)
+    residual = encoded[...] + dot(attended, attn[...], 0, 0)
     residual_ref[...] = residual
     latent = mlp_forward(residual, gains[2:3], mlp, normed_ref, slope_ref, active_ref)
     sent_ref[...] = latent.astype(BF16)
@@ -239,15 +271,12 @@
     edges, s0, s1, s2, x, tables, gains, mlp,
     joined_ref, normed_ref, slope_ref, active_ref, decoded_ref, final_ref, output_ref,
 ):
-    lanes_total = s0.shape[0]
-    rows, count = edges.shape
+    count, rows = edges.shape
+    band = s0.shape[0]
     gathered = jnp.zeros(joined_ref.shape, F32)
-    lanes = lax.broadcasted_iota(jnp.int32, (rows, lanes_total), 1)
+    places = lax.broadcasted_iota(jnp.int32, (band, rows), 0)
     for w, sent in enumerate((s0, s1, s2)):
-        tally = jnp.zeros((rows, lanes_total), F32)
-        for j in range(count):
-            tally = tally + jnp.where(edges[:, j : j + 1] - w * lanes_total == lanes, 1.0, 0.0)
-        gathered = gathered + dot(tally.astype(BF16), sent[...], 1, 0)
+        gathered = gathered + dot(named(edges, places + w * band), sent[...], 0, 0)
     joined = dot(x[...], tables[0], 0, 0) + gathered / count
     joined_ref[...] = joined
     decoded = mlp_forward(joined, gains[3:4], mlp, normed_ref, slope_ref, active_ref)
@@ -285,16 +314,13 @@
     total = grad.shape[0]
     for w, out in enumerate((out0, out1, out2)):
         sub = lax.broadcasted_iota(jnp.int32, (rows, total), 0) + (step * rows + w * total)
-        tally = jnp.zeros((rows, total), F32)
-        for j in range(count):
-            tally = tally + jnp.where(edges[j : j + 1, :] == sub, 1.0, 0.0)
-        tally = tally.astype(BF16)
+        tally = named(edges, sub)
         value = dot(tally, high_ref[...], 1, 0) + dot(tally, low_ref[...], 1, 0)
         out[...] = (value / count).astype(out.dtype)
 
 
 def processor_back_kernel(
-    g0, g1, g2, residual, slope, gains, mlp, attn, o_ref,
+    g0, g1, g2, residual, slope, gains, mlp, attn, o0, o1,
     grad_residual_ref, rounded_ref, before_ref, gain_ref, branch_ref, grad_o_ref, delta_ref,
 ):
     width = residual.shape[1]
@@ -306,10 +332,11 @@
     grad_residual_ref[...] = grad
     branch = grad.astype(BF16)
     branch_ref[...] = branch
-    grad_o = dot(attn[:, 3 * width :], branch, 1, 1).astype(BF16)
+    grad_o = dot(attn[...], branch, 1, 1).astype(BF16)
     grad_o_ref[...] = grad_o
     depth = width // HEADS
-    together = grad_o.astype(F32) * o_ref[...]
+    attended = jnp.concatenate([o0[...], o1[...]], axis=0)
+    together = grad_o.astype(F32) * attended
     for h in range(HEADS):
         row = jnp.sum(together[h * depth : (h + 1) * depth], axis=0, keepdims=True)
         delta_ref[h] = jnp.broadcast_to(row, delta_ref.shape[1:])
@@ -361,38 +388,44 @@
                     ref[0, band, :, columns] = value[at : at + rows].astype(ref.dtype)
 
 
-def weights_kernel(places, normed, rounded, before, active, keep_ref, send_ref):
-    quarter = pl.program_id(0)
-    columns = slice(0, before.shape[1])
-
-    @pl.when(quarter < 2)
+def turn(pairs):
+    @pl.when(pl.program_id(0) == 0)
     def _():
-        hand_out(places[2], dot(normed[...], before[...], 0, 0), keep_ref, send_ref, columns)
-
-    @pl.when(quarter >= 2)
-    def _():
-        hand_out(places[2], dot(rounded[...], active[...], 0, 0), keep_ref, send_ref, columns)
-
-
-def last_weights_kernel(
-    places, normed, rounded, before, active, normed_attn, project, attended, branch, table_in, table_out, gain,
-    keep_ref, send_ref,
+        for ref, kept in pairs:
+            kept[...] = ref[...].T
+
+
+def weights_kernel(places, normed, rounded, before, active, keep_ref, send_ref, normed_turned, rounded_turned):
+    size = before.shape[1]
+    turn(((normed, normed_turned), (rounded, rounded_turned)))
+    hand_out(places[2], dot(normed_turned[...], before[...], 1, 0), keep_ref, send_ref, slice(0, size))
+    hand_out(places[2], dot(rounded_turned[...], active[...], 1, 0), keep_ref, send_ref, slice(size, 2 * size))
+
+
+def down_weights_kernel(
+    places, rounded, active, normed_attn, project, attended, branch, keep_ref, send_ref, rounded_turned, normed_turned
 ):
     quarter = pl.program_id(0)
-    weights_kernel(places, normed, rounded, before, active, keep_ref, send_ref)
-    start = before.shape[1]
-    width = normed_attn.shape[1]
-    columns = slice(start, start + width)
+    size = active.shape[1]
+    turn(((rounded, rounded_turned), (normed_attn, normed_turned)))
+    hand_out(places[2], dot(rounded_turned[...], active[...], 1, 0), keep_ref, send_ref, slice(0, size))
+    columns = slice(size, size + normed_attn.shape[1])
 
     @pl.when(quarter < 3)
     def _():
-        hand_out(places[2], dot(normed_attn[...], project[...], 0, 1), keep_ref, send_ref, columns)
+        hand_out(places[2], dot(normed_turned[...], project[...], 1, 1), keep_ref, send_ref, columns)
 
     @pl.when(quarter == 3)
     def _():
         hand_out(places[2], dot(attended[...], branch[...], 1, 0), keep_ref, send_ref, columns)
 
-    columns = slice(start + width, start + width + table_in.shape[1])
+
+def up_weights_kernel(places, normed, before, table_in, table_out, gain, keep_ref, send_ref, normed_turned):
+    quarter = pl.program_id(0)
+    size = before.shape[1]
+    turn(((normed, normed_turned),))
+    hand_out(places[2], dot(normed_turned[...], before[...], 1, 0), keep_ref, send_ref, slice(0, size))
+    columns = slice(size, size + table_in.shape[1])
     for index, ref in enumerate((table_in, table_out, gain)):
 
         @pl.when(quarter == index)
@@ -424,28 +457,33 @@
                 start += size
 
 
-def band_kernel(places, own, *refs, count, exact):
-    came, outs = refs[:count], refs[count:]
+def band_kernel(places, *refs, groups, count, exact):
+    ins, outs = refs[: groups * (1 + count)], refs[groups * (1 + count) :]
     step = pl.program_id(0)
-    size = own.shape[-1]
-    total = own[0]
-    for ref in came:
-        total = total + ref[0, :, :size].astype(F32)
-    if exact:
-        rest = sum(ref[0, :, size:].astype(F32) for ref in came)
-    for index, out in enumerate(outs):
-
-        @pl.when(step == index)
-        def _(index=index, out=out):
-            out[:, :size] = total.astype(out.dtype)
-            if exact:
-                part = total[:, size - exact :] + rest
-                if index == 0:
-                    out[:, size - exact :] = part
-                else:
-                    high = part.astype(out.dtype)
-                    out[:, size - exact : size] = high
-                    out[:, size:] = (part - high.astype(F32)).astype(out.dtype)
+    start = 0
+    for group in range(groups):
+        own, *came = ins[group * (1 + count) : (group + 1) * (1 + count)]
+        size = own.shape[-1]
+        total = own[0]
+        for ref in came:
+            total = total + ref[0, :, :size].astype(F32)
+        last = exact and group == groups - 1
+        if last:
+            part = total[:, size - exact :] + sum(ref[0, :, size:].astype(F32) for ref in came)
+            high = part.astype(BF16)
+            rest = (part - high.astype(F32)).astype(BF16)
+        for index, out in enumerate(outs):
+
+            @pl.when(step == index)
+            def _(index=index, out=out):
+                out[:, start : start + size] = total.astype(out.dtype)
+                if last and index == 0:
+                    out[:, start + size - exact : start + size] = part
+                elif last:
+                    out[:, start + size - exact : start + size] = high
+                    out[:, start + size : start + size + exact] = rest
+
+        start += size
 
 
 def exchange(value, axis, distance):
@@ -453,25 +491,25 @@
     return lax.ppermute(value, axis, [(i, i ^ distance) for i in range(size)])
 
 
-def prefetched(kernel, grid, outs, in_specs, out_specs, places, operands, moved):
+def prefetched(kernel, grid, outs, in_specs, out_specs, places, operands, moved, weight=1):
     return pl.pallas_call(
         kernel,
         grid_spec=pltpu.PrefetchScalarGridSpec(
             num_scalar_prefetch=1, grid=grid, in_specs=in_specs, out_specs=out_specs
         ),
         out_shape=outs,
-        cost_estimate=pl.CostEstimate(flops=moved, bytes_accessed=moved, transcendentals=0),
+        cost_estimate=pl.CostEstimate(flops=moved * WEIGH * weight, bytes_accessed=moved * WEIGH, transcendentals=0),
         compiler_params=pltpu.CompilerParams(vmem_limit_bytes=VMEM_BYTES),
-    )(places, *operands)
-
-
-def sort_shares(keeps, sends, places, exact=0):
+    )(places, *[far(x) for x in operands])
+
+
+def sort_shares(keeps, sends, places, exact=0, late=()):
     items = lax.axis_size("item")
     came = [exchange(send, "lat", 1) for send in sends]
     quarters, bands, rows, _ = keeps[0].shape
     size = sum(keep.shape[-1] for keep in keeps)
     wide = size + exact
-    operands = [x for pair in zip(keeps, came) for x in pair]
+    operands = [after(x, *late) for pair in zip(keeps, came) for x in pair]
     return prefetched(
         functools.partial(item_kernel, pairs=len(keeps), exact=exact),
         (items,),
@@ -485,26 +523,36 @@
     )
 
 
-def sum_shares(sorted_shares, places, exact=0):
-    items = lax.axis_size("item")
+def swap_items(sorted_shares):
     own, *others = sorted_shares
-    bands, rows, size = own.shape
+    return [own] + [exchange(x, "item", k + 1) for k, x in enumerate(others)]
+
+
+def sum_items(groups, places, exact=0):
+    items = len(groups[0])
+    bands, rows, _ = groups[0][0].shape
+    operands = [x for group in groups for x in group]
+    size = sum(group[0].shape[-1] for group in groups)
     wide = size + exact
-    came = [exchange(x, "item", k + 1) for k, x in enumerate(others)]
-    own, *others = prefetched(
-        functools.partial(band_kernel, count=items - 1, exact=exact),
+    return prefetched(
+        functools.partial(band_kernel, groups=len(groups), count=items - 1, exact=exact),
         (bands,),
         [shape((rows, size), F32)] + [shape((rows, wide), BF16)] * (bands - 1),
-        [pl.BlockSpec((1, rows, size), lambda j, s: (s[4] ^ j, 0, 0))]
-        + [pl.BlockSpec((1, rows, wide), lambda j, s: (s[4] ^ j, 0, 0))] * (items - 1),
+        [pl.BlockSpec((1,) + x.shape[1:], lambda j, s: (s[4] ^ j, 0, 0)) for x in operands],
         [pl.BlockSpec((rows, size), lambda j, s: (0, 0))]
         + [pl.BlockSpec((rows, wide), lambda j, s: (0, 0))] * (bands - 1),
         places,
-        (own, *came),
+        operands,
         moved=14 * bands * rows * size,
-    )
+        weight=10000,
+    )
+
+
+def sum_bands(parts, exact=0, late=()):
+    own, *others = parts
+    size = own.shape[-1]
     came = [exchange(x, "lat", 2 * (k + 1)) for k, x in enumerate(others)]
-    total = own
+    total = after(own, *late) if late else own
     for x in came:
         total = total + x[:, :size].astype(F32)
     if exact:
@@ -514,7 +562,34 @@
 
 
 def after(value, *others):
-    return lax.optimization_barrier((value, *others))[0]
+    result = lax.optimization_barrier((value, *others))[0]
+    if is_far(value):
+        FAR.append(result)
+    return result
+
+
+def total_kernel(own, *refs):
+    *came, out = refs
+    total = own[...]
+    for ref in came:
+        total = total + ref[...].astype(F32)
+    out[...] = total.astype(out.dtype)
+
+
+def add_bands(parts, late):
+    own, *others = parts
+    came = [exchange(x, "lat", 2 * (k + 1)) for k, x in enumerate(others)]
+    return call(
+        total_kernel,
+        (1,),
+        shape(own.shape, BF16),
+        [whole(own.shape)] * len(parts),
+        whole(own.shape),
+        (after(own, *late), *came),
+        flops=10**11,
+        moved=16 * own.size,
+        near=True,
+    )
 
 
 def all_items(value):
@@ -530,44 +605,60 @@
 
 
 def adam_kernel(places, factor, *refs):
-    first, second = refs[:4], refs[4:8]
-    mlp, attn = refs[8:12], refs[12:16]
-    mlp_out, attn_out = refs[16:21], refs[21:26]
-    block = mlp[0].shape[-1]
-    width = attn[0].shape[-1]
-    step = pl.program_id(0)
+    first, down, up = refs[:4], refs[4:8], refs[8:12]
+    mlp, attn = refs[12:16], refs[16:20]
+    mlp_out, attn_out = refs[20:25], refs[25:30]
+    size = mlp[0].shape[-1]
+    part = attn[0].shape[-1]
+    half = pl.program_id(1)
     for index in range(4):
-
-        @pl.when(step == index)
-        def _(index=index):
-            scale = factor[0]
-            shares = (
-                second[index][:, :block], first[index][:, block : 2 * block], first[index][:, :block]
-            )
-            for layer, share in enumerate(shares):
-                new = adam_update(scale * share, *(ref[layer] for ref in mlp), RATE_MATRIX, WEIGHT_DECAY)
-                for ref, value in zip(mlp_out, new):
-                    ref[layer] = value
-            share = second[index][:, block : block + width]
-            new = adam_update(scale * share, *(ref[...] for ref in attn), RATE_MATRIX, WEIGHT_DECAY)
-            for ref, value in zip(attn_out, new):
-                ref[...] = value
+        for side in range(2):
+
+            @pl.when((pl.program_id(0) == index) & (half == side))
+            def _(index=index, side=side):
+                scale = factor[0]
+                here = slice(side * size, (side + 1) * size)
+                there = slice((2 + side) * size, (3 + side) * size)
+                shares = ((down if side else up)[index][:, :size], first[index][:, there], first[index][:, here])
+                for layer, share in enumerate(shares):
+                    new = adam_update(
+                        scale * share.astype(F32), *(ref[layer] for ref in mlp), RATE_MATRIX, WEIGHT_DECAY
+                    )
+                    for ref, value in zip(mlp_out, new):
+                        ref[layer] = value
+                share = down[index][:, size + side * part : size + (side + 1) * part]
+                new = adam_update(scale * share, *(ref[...] for ref in attn), RATE_MATRIX, WEIGHT_DECAY)
+                for ref, value in zip(attn_out, new):
+                    ref[...] = value
+
+
+def projection_back_kernel(
+    dq0, dq1, left0, left1, own0, own1, right0, right1, grad_residual, encoded, gains, attn,
+    upstream_ref, rounded_ref, project_ref, gain_ref,
+):
+    pairs = [
+        own[...] + left[...].astype(F32) + right[...].astype(F32)
+        for left, own, right in ((left0, own0, right0), (left1, own1, right1))
+    ]
+    project = jnp.concatenate(
+        [dq0[...], dq1[...], pairs[0][0], pairs[1][0], pairs[0][1], pairs[1][1]], axis=0
+    ).astype(BF16)
+    project_ref[...] = project
+    grad_normed = dot(project, attn[...], 0, 1)
+    grad_encoded, gain_attn = norm_back(grad_normed, encoded[...], gains[1:2])
+    upstream = grad_residual[...] + grad_encoded
+    upstream_ref[...] = upstream
+    rounded_ref[...] = upstream.astype(BF16)
+    add_up(gain_ref, gain_attn)
 
 
 def encoder_back_kernel(
-    dq, g0, g1, g2, grad_residual, encoded, pooled, slope, gains, mlp, attn, x, pin, grad_join,
-    rounded_ref, before_ref, project_ref, table_ref, gain_ref,
+    upstream, pooled, slope, gains, mlp, x, pin, grad_join, before_ref, table_ref, gain_ref, rounded_ref
 ):
-    width = encoded.shape[1]
-    pairs = g1[...] + g0[...].astype(F32) + g2[...].astype(F32)
-    project = jnp.concatenate([dq[...], pairs], axis=0).astype(BF16)
-    project_ref[...] = project
-    grad_normed = dot(project, attn[:, : 3 * width], 0, 1)
-    grad_encoded, gain_attn = norm_back(grad_normed, encoded[...], gains[1:2])
     grad_pooled, gain_enc = mlp_backward(
-        grad_residual[...] + grad_encoded, pooled[...], gains[0:1], mlp, slope, rounded_ref, before_ref
-    )
-    add_up(gain_ref, jnp.concatenate([gain_enc, gain_attn], axis=0))
+        upstream[...], pooled[...], gains[0:1], mlp, slope, rounded_ref, before_ref
+    )
+    add_up(gain_ref, gain_enc)
     high, low = two_parts(grad_pooled)
     both = dot(high, pin[...], 0, 0) + dot(low, pin[...], 0, 0)
     channels = x.shape[0]
@@ -576,33 +667,22 @@
     add_up(table_ref, direct + both[:, :channels] + both[:, channels:])
 
 
-def weights(normed, rounded, before, active, places, last=()):
-    rows, width = normed.shape
-    hidden = before.shape[1]
+def weights(kernel, places, operands, specs, columns, flops, turned):
+    rows, width = operands[0].shape
     bands = lax.axis_size("lat") // 2
-    block = hidden // 2
-    columns = block + (width + CHANNEL_PAD if last else 0)
     out = shape((4, bands, width // (2 * bands), columns), F32)
     out_spec = pl.BlockSpec((1,) + out.shape[1:], lambda i: (i, 0, 0, 0))
-    specs = [
-        pl.BlockSpec(memory_space=pltpu.SMEM),
-        whole((rows, width)),
-        whole((rows, width)),
-        pl.BlockSpec((rows, block), lambda i: (0, jnp.minimum(i, 1))),
-        pl.BlockSpec((rows, block), lambda i: (0, jnp.maximum(i - 2, 0))),
-    ]
-    if last:
-        specs += [whole((rows, width)), pl.BlockSpec((width, rows), lambda i: (jnp.minimum(i, 2), 0))]
-        specs += [whole(x.shape) for x in last[2:]]
     return call(
-        last_weights_kernel if last else weights_kernel,
+        kernel,
         (4,),
         [out, out],
-        specs,
+        [pl.BlockSpec(memory_space=pltpu.SMEM)] + specs,
         [out_spec, out_spec],
-        (places, normed, rounded, before, active, *last),
-        flops=4 * rows * width * hidden,
-        moved=4 * rows * hidden + 8 * width * hidden,
+        (places, *operands),
+        flops=flops,
+        moved=8 * width * columns * 4,
+        scratch=[pltpu.VMEM((width, rows), BF16)] * turned,
+        near=True,
     )
 
 
@@ -655,6 +735,7 @@
     gains_second,
     gains_ema,
 ):
+    FAR.clear()
     band_index = lax.axis_index("lat")
     bands = lax.axis_size("lat")
     item_index = lax.axis_index("item")
@@ -666,6 +747,8 @@
     padded = CHANNEL_PAD
     hidden = mlp_copy.shape[2] // 2
     depth = width // HEADS
+    FAR.extend([mlp_copy, attn_copy, mlp_master, mlp_first, mlp_second, mlp_ema])
+    FAR.extend([attn_master, attn_first, attn_second, attn_ema])
     gains = gains_copy.astype(F32)
     gain_rows = gains.shape[0]
     noise_level = sigmas[0]
@@ -683,7 +766,9 @@
     def weights_spec(index):
         return pl.BlockSpec((1, width, 2 * hidden), lambda *_: (index, 0, 0))
 
-    attn_spec = whole(attn_copy.shape)
+    wout_spec = pl.BlockSpec((width, width), lambda *_: (0, 3))
+    few = HEADS // GROUPS
+    part = few * depth
     gains_spec = whole(gains.shape)
     tables_spec = whole(tables.shape)
     steps = rows // ROWS
@@ -691,25 +776,25 @@
     kept_specs = [rows_of(width), rows_of(hidden), rows_of(hidden)]
     mlp_flops = 4 * rows * width * hidden
 
-    pin, pooled, encoded, normed_enc, slope_enc, active_enc, normed_attn, queries, pairs = call(
+    pin, pooled, encoded, normed_enc, slope_enc, active_enc, normed_attn, queries, *pairs = call(
         encoder_kernel,
         (steps,),
         [shape((rows, 2 * padded), BF16), shape((rows, width), F32), shape((rows, width), F32)]
         + kept_shapes
-        + [shape((rows, width), BF16), shape((width, rows), BF16), shape((rows, 2 * width), BF16)],
+        + [shape((rows, width), BF16), shape((width, rows), BF16)]
+        + [shape((rows, width), BF16)] * GROUPS,
         [
-            rows_of(grid_edges.shape[1]), whole((padded, grid_rows)), tables_spec, gains_spec,
-            weights_spec(0), attn_spec,
+            lanes_of(grid_edges.shape[1]), whole((padded, grid_rows)), tables_spec, gains_spec,
+            weights_spec(0), pl.BlockSpec((width, 3 * width), lambda i: (0, 0)),
         ],
         [rows_of(2 * padded), rows_of(width), rows_of(width)]
         + kept_specs
-        + [rows_of(width), lanes_of(width), rows_of(2 * width)],
-        (grid_edges, inputs, tables, gains, mlp_copy, attn_copy),
+        + [rows_of(width), lanes_of(width)]
+        + [rows_of(width)] * GROUPS,
+        (grid_edges.T, inputs, tables, gains, mlp_copy, attn_copy),
         flops=mlp_flops + 6 * rows * width * width,
         moved=30 * rows * width,
     )
-
-    before_pairs, after_pairs = from_sides(pairs, pairs)
 
     crops = lengths.shape[1]
     smem = pl.BlockSpec(memory_space=pltpu.SMEM)
@@ -725,33 +810,43 @@
         moved=12 * rows * rows,
     )
 
+    windows = []
+    for own in pairs:
+        if windows:
+            own = after(own, *windows[-1], bias)
+        came = from_sides(own, own)
+        windows.append([came[0], own, came[1]])
+
     lanes = 512
-    window = [before_pairs, pairs, after_pairs]
-    attended, lse = call(
-        functools.partial(attend_kernel, chunk=256),
-        (rows // lanes, HEADS),
-        [shape((width, rows), F32), shape((HEADS, 8, rows), F32)],
-        [pl.BlockSpec((depth, lanes), lambda i, h: (h, i))]
-        + [pl.BlockSpec((rows, depth), lambda i, h: (0, h))] * 3
-        + [pl.BlockSpec((rows, depth), lambda i, h: (0, HEADS + h))] * 3
-        + [pl.BlockSpec((3, rows, lanes), lambda i, h: (0, 0, i))],
-        [
-            pl.BlockSpec((depth, lanes), lambda i, h: (h, i)),
-            pl.BlockSpec((1, 8, lanes), lambda i, h: (h, 0, i)),
-        ],
-        (queries, *window, *window, bias),
-        scratch=[pltpu.VMEM((3, rows, lanes), F32)],
-        flops=24 * rows * rows * width,
-        moved=12 * rows * rows,
-    )
+    attended, lse = [], []
+    for g, window in enumerate(windows):
+        result, logs = call(
+            functools.partial(attend_kernel, chunk=256),
+            (rows // lanes, few),
+            [shape((part, rows), F32), shape((few, 8, rows), F32)],
+            [pl.BlockSpec((depth, lanes), lambda i, h, g=g: (g * few + h, i))]
+            + [pl.BlockSpec((rows, depth), lambda i, h: (0, h))] * 3
+            + [pl.BlockSpec((rows, depth), lambda i, h: (0, few + h))] * 3
+            + [pl.BlockSpec((3, rows, lanes), lambda i, h: (0, 0, i))],
+            [
+                pl.BlockSpec((depth, lanes), lambda i, h: (h, i)),
+                pl.BlockSpec((1, 8, lanes), lambda i, h: (h, 0, i)),
+            ],
+            (queries, *window, *window, bias),
+            scratch=[pltpu.VMEM((3, rows, lanes), F32)],
+            flops=24 * rows * rows * part,
+            moved=12 * rows * rows,
+        )
+        attended.append(result)
+        lse.append(logs)
 
     rounded_o, residual, normed_proc, slope_proc, active_proc, sent = call(
         processor_kernel,
         (steps,),
         [shape((width, rows), BF16), shape((rows, width), F32)] + kept_shapes + [shape((rows, width), BF16)],
-        [lanes_of(width), rows_of(width), gains_spec, weights_spec(1), attn_spec],
+        [lanes_of(part)] * GROUPS + [rows_of(width), gains_spec, weights_spec(1), wout_spec],
         [lanes_of(width), rows_of(width)] + kept_specs + [rows_of(width)],
-        (attended, encoded, gains, mlp_copy, attn_copy),
+        (*attended, encoded, gains, mlp_copy, attn_copy),
         flops=mlp_flops + 2 * rows * width * width,
         moved=24 * rows * width,
     )
@@ -765,11 +860,11 @@
         + kept_shapes
         + [shape((grid_rows, width), F32), shape((grid_rows, width), BF16), shape((padded, grid_rows), F32)],
         [
-            rows_of(dec_edges.shape[1]), whole((rows, width)), whole((rows, width)), whole((rows, width)),
+            lanes_of(dec_edges.shape[1]), whole((rows, width)), whole((rows, width)), whole((rows, width)),
             lanes_of(padded), tables_spec, gains_spec, weights_spec(2),
         ],
         [rows_of(width)] + kept_specs + [rows_of(width), rows_of(width), lanes_of(padded)],
-        (dec_edges, before_sent, sent, after_sent, inputs, tables, gains, mlp_copy),
+        (dec_edges.T, before_sent, sent, after_sent, inputs, tables, gains, mlp_copy),
         flops=mlp_flops + 6 * rows * rows * width,
         moved=24 * rows * width,
     )
@@ -820,7 +915,20 @@
         moved=12 * rows * width,
     )
     from_left, from_right = from_sides(to_left, to_right)
-    keep_dec, send_dec = weights(normed_dec, rounded_dec, before_dec, active_dec, places)
+    quarter = hidden // 4
+    columns_of = pl.BlockSpec((rows, quarter), lambda i: (0, i))
+    table_spec = whole((width, padded))
+    full = whole((rows, width))
+    product = 2 * rows * width * width
+
+    def layer_weights(*operands):
+        return weights(
+            weights_kernel, places, operands, [full, full, columns_of, columns_of], 2 * quarter, 8 * product, 2
+        )
+
+    keep_dec, send_dec = layer_weights(normed_dec, after(rounded_dec, to_left, to_right), before_dec, active_dec)
+    sorted_dec = sort_shares([keep_dec], [send_dec], places)
+    swapped_dec = swap_items(sorted_dec)
 
     grad_residual, rounded_proc, before_proc, gain_proc, branch, grad_o, delta = call(
         processor_back_kernel,
@@ -830,100 +938,147 @@
             shape((1, width), F32), shape((rows, width), BF16), shape((width, rows), BF16),
             shape((HEADS, 8, rows), F32),
         ],
-        [rows_of(width)] * 4 + [rows_of(hidden), gains_spec, weights_spec(1), attn_spec, lanes_of(width)],
+        [rows_of(width)] * 4 + [rows_of(hidden), gains_spec, weights_spec(1), wout_spec] + [lanes_of(part)] * GROUPS,
         [
             rows_of(width), rows_of(width), rows_of(hidden), whole((1, width)), rows_of(width), lanes_of(width),
             pl.BlockSpec((HEADS, 8, ROWS), lambda i: (0, 0, i)),
         ],
-        (from_left, after(grad_own, keep_dec, send_dec), from_right, residual, slope_proc, gains, mlp_copy, attn_copy, attended),
+        (from_left, after(grad_own, keep_dec, send_dec), from_right, residual, slope_proc, gains, mlp_copy, attn_copy,
+            *attended,
+        ),
         flops=mlp_flops + 2 * rows * width * width,
         moved=24 * rows * width,
     )
 
+    keep_proc, send_proc = layer_weights(normed_proc, rounded_proc, before_proc, active_proc)
     block = 512
     side = pl.BlockSpec((2, depth, block), lambda i, h: (0, h, i))
-    grad_queries, pairs_left, pairs_own, pairs_right = call(
-        functools.partial(attend_back_kernel, chunk=256),
-        (rows // block, HEADS),
+    group_spec = whole((few, 8, rows))
+    grad_queries, sides = [], []
+    ahead = (keep_proc, send_proc)
+    for g, window in enumerate(windows):
+        row_spec = pl.BlockSpec((part, rows), lambda i, h, g=g: (g, 0))
+        dq, left, own, right = call(
+            functools.partial(attend_back_kernel, chunk=256),
+            (rows // block, few),
+            [
+                shape((part, rows), F32), shape((2, part, rows), BF16), shape((2, part, rows), F32),
+                shape((2, part, rows), BF16),
+            ],
+            [row_spec, row_spec, group_spec, pl.BlockSpec((few, 8, rows), lambda i, h, g=g: (g, 0, 0))]
+            + [pl.BlockSpec((block, depth), lambda i, h: (i, h))] * 3
+            + [pl.BlockSpec((block, depth), lambda i, h: (i, few + h))] * 3
+            + [pl.BlockSpec((3, block, rows), lambda i, h: (0, i, 0))],
+            [whole((part, rows)), side, side, side],
+            (queries, after(grad_o, *ahead), lse[g], delta, *window, *window, bias),
+            scratch=[pltpu.VMEM((block, rows), BF16), pltpu.VMEM((block, rows), BF16)],
+            flops=60 * rows * rows * part,
+            moved=12 * rows * rows,
+        )
+        if sides:
+            left = after(left, *sides[-1], *swapped_proc)
+            right = after(right, *sides[-1], *swapped_proc)
+        came = from_sides(left, right)
+        sides.append([came[0], own, came[1]])
+        grad_queries.append(dq)
+        if g == 0:
+            sorted_proc = sort_shares([after(keep_proc, dq)], [send_proc], places)
+            swapped_proc = swap_items(sorted_proc)
+            ahead = (*sorted_proc, *swapped_dec)
+
+    first_parts = sum_items([swapped_dec, swapped_proc], places)
+    first_parts = [first_parts[0]] + [after(x, *sides[-1]) for x in first_parts[1:]]
+    side_spec = pl.BlockSpec((2, part, ROWS), lambda i: (0, 0, i))
+    upstream, rounded_enc, project, gain_attn = call(
+        projection_back_kernel,
+        (steps,),
         [
-            shape((width, rows), F32), shape((2, width, rows), BF16), shape((2, width, rows), F32),
-            shape((2, width, rows), BF16),
+            shape((rows, width), F32), shape((rows, width), BF16), shape((3 * width, rows), BF16),
+            shape((1, width), F32),
         ],
-        [whole((width, rows)), whole((width, rows)), whole((HEADS, 8, rows)), whole((HEADS, 8, rows))]
-        + [pl.BlockSpec((block, depth), lambda i, h: (i, h))] * 3
-        + [pl.BlockSpec((block, depth), lambda i, h: (i, HEADS + h))] * 3
-        + [pl.BlockSpec((3, block, rows), lambda i, h: (0, i, 0))],
-        [whole((width, rows)), side, side, side],
-        (queries, grad_o, lse, delta, *window, *window, bias),
-        scratch=[pltpu.VMEM((block, rows), BF16), pltpu.VMEM((block, rows), BF16)],
-        flops=60 * rows * rows * width,
-        moved=12 * rows * rows,
-    )
-    before_grad, after_grad = from_sides(
-        pairs_left.reshape(2 * width, rows), pairs_right.reshape(2 * width, rows)
-    )
-    keep_proc, send_proc = weights(normed_proc, rounded_proc, before_proc, active_proc, places)
-    first_sorted = sort_shares([keep_dec, keep_proc], [send_dec, send_proc], places)
-    first_total = sum_shares(first_sorted, places)
-    first_all = all_items(first_total)
-
-    rounded_enc, before_enc, project, table_in, gain_enc = call(
+        [lanes_of(part)] * 2 + [side_spec] * 6
+        + [rows_of(width)] * 2 + [gains_spec, pl.BlockSpec((width, 3 * width), lambda i: (0, 0))],
+        [rows_of(width), rows_of(width), lanes_of(3 * width), whole((1, width))],
+        (
+            *grad_queries, sides[0][0], sides[1][0], sides[0][1], sides[1][1], sides[0][2], sides[1][2],
+            after(grad_residual, first_parts[0]), encoded, gains, attn_copy,
+        ),
+        flops=3 * product,
+        moved=24 * rows * width,
+    )
+    keep_down, send_down = weights(
+        down_weights_kernel,
+        places,
+        (rounded_enc, active_enc, normed_attn, project, rounded_o, branch),
+        [full, columns_of, full, pl.BlockSpec((width, rows), lambda i: (jnp.minimum(i, 2), 0)), whole((width, rows)), full],
+        quarter + width,
+        8 * product,
+        2,
+    )
+    first_total = add_bands(first_parts, (keep_down,))
+    sorted_down = sort_shares([keep_down], [send_down], places, late=(first_total,))
+    swapped_down = swap_items(sorted_down)
+    before_enc, table_in, gain_enc, _ = call(
         encoder_back_kernel,
         (steps,),
         [
-            shape((rows, width), BF16), shape((rows, hidden), BF16), shape((3 * width, rows), BF16),
-            shape((width, padded), F32), shape((2, width), F32),
+            shape((rows, hidden), BF16), shape((width, padded), F32), shape((1, width), F32),
+            shape((rows, width), BF16),
         ],
-        [lanes_of(width)] + [lanes_of(2 * width)] * 3 + [rows_of(width)] * 3
-        + [rows_of(hidden), gains_spec, weights_spec(0), attn_spec, lanes_of(padded), rows_of(2 * padded), rows_of(width)],
-        [rows_of(width), rows_of(hidden), lanes_of(3 * width), whole((width, padded)), whole((2, width))],
-        (
-            grad_queries, before_grad, pairs_own.reshape(2 * width, rows), after_grad,
-            after(grad_residual, *first_sorted), encoded,
-            pooled, slope_enc, gains, mlp_copy, attn_copy, inputs, pin, grad_join,
-        ),
-        flops=mlp_flops + 6 * rows * width * width,
+        [rows_of(width)] * 2
+        + [rows_of(hidden), gains_spec, weights_spec(0), lanes_of(padded), rows_of(2 * padded), rows_of(width)],
+        [rows_of(hidden), table_spec, whole((1, width)), rows_of(width)],
+        (after(upstream, *sorted_down), pooled, slope_enc, gains, mlp_copy, inputs, pin, grad_join),
+        flops=mlp_flops,
         moved=24 * rows * width,
     )
-    grad_gains = jnp.concatenate([gain_enc, gain_proc, gain_dec], axis=0)
+    grad_gains = jnp.concatenate([gain_enc, gain_attn, gain_proc, gain_dec], axis=0)
     gain_columns = jnp.pad(grad_gains.T, ((0, 0), (0, padded - gain_rows)))
-    keep_last, send_last = weights(
-        normed_enc, rounded_enc, before_enc, active_enc, places,
-        (normed_attn, project, rounded_o, branch, table_in, table_out, gain_columns),
-    )
-    last_total = sum_shares(
-        sort_shares([keep_last], [send_last], places, exact=padded), places, exact=padded
-    )
-    squares = jnp.sum(first_total * first_total) + jnp.sum(last_total * last_total)
-    scalars = sum_over(sum_over(jnp.stack([squares, loss_item])[None], "lat"), "item")
-    last_all = all_items(last_total)
+    keep_up, send_up = weights(
+        up_weights_kernel,
+        places,
+        (normed_enc, before_enc, table_in, table_out, gain_columns),
+        [full, columns_of, table_spec, table_spec, table_spec],
+        quarter + padded,
+        4 * product,
+        1,
+    )
+    down_parts = sum_items([swapped_down], places)
+    down_total = sum_bands(down_parts)
+    sorted_up = sort_shares([keep_up], [send_up], places, exact=padded, late=(down_parts[0],))
+    swapped_up = swap_items([sorted_up[0]] + [after(x, *swapped_down) for x in sorted_up[1:]])
+    first_all = all_items(after(first_total, *swapped_up))
+    up_total = sum_bands(sum_items([swapped_up], places, exact=padded), exact=padded)
+    squares = sum(jnp.sum(jnp.square(x.astype(F32))) for x in (first_total, down_total, up_total))
+    down_all = all_items(down_total)
+    up_all = all_items(up_total)
+    scalars = after(jnp.stack([squares, loss_item])[None], *down_all)
+    scalars = all_items(after(sum_over(scalars, "lat"), *up_all))
+    scalars = (scalars[0] + scalars[1]) + (scalars[2] + scalars[3])
     loss_sum = scalars[0, 1]
     grad_norm = jnp.sqrt(scalars[0, 0])
     scale_factor = CLIP_LEVEL / jnp.maximum(grad_norm, CLIP_LEVEL)
 
     shard_rows = attn_master.shape[0]
-    quarter = hidden // 2
-    mlp_spec = pl.BlockSpec((mlp_master.shape[0], shard_rows, quarter), lambda j, s: (0, 0, s[3] ^ j))
-    attn_part = pl.BlockSpec((shard_rows, width), lambda j, s: (0, s[3] ^ j))
+    mlp_spec = pl.BlockSpec((mlp_master.shape[0], shard_rows, quarter), lambda j, k, s: (0, 0, k * 4 + (s[3] ^ j)))
+    attn_part = pl.BlockSpec((shard_rows, width // 2), lambda j, k, s: (0, (s[3] ^ j) * 2 + k))
     kinds = [F32, F32, F32, F32, BF16]
+    shares = (*first_all, *down_all, *up_all)
     updated = prefetched(
         adam_kernel,
-        (4,),
+        (4, 2),
         [shape(mlp_master.shape, kind) for kind in kinds] + [shape(attn_master.shape, kind) for kind in kinds],
-        [smem]
-        + [pl.BlockSpec(x.shape, lambda j, s: (0, 0)) for x in (*first_all, *last_all)]
-        + [mlp_spec] * 4
-        + [attn_part] * 4,
+        [smem] + [pl.BlockSpec(x.shape, lambda *_: (0, 0)) for x in shares] + [mlp_spec] * 4 + [attn_part] * 4,
         [mlp_spec] * 5 + [attn_part] * 5,
         places,
         (
-            scale_factor[None], *first_all, *last_all, mlp_master, mlp_first, mlp_second, mlp_ema,
+            scale_factor[None], *shares, mlp_master, mlp_first, mlp_second, mlp_ema,
             attn_master, attn_first, attn_second, attn_ema,
         ),
         moved=34 * (mlp_master.size + attn_master.size),
     )
     mlps, att = updated[:5], updated[5:]
-    small = jnp.stack([x[:, quarter + width :] for x in last_all])
+    small = jnp.stack([x[:, quarter:] for x in up_all])
     tab_sum = jnp.stack(
         [lax.dynamic_index_in_dim(small, item_index ^ q, 0, False)[:, :channels].T for q in range(2)]
     )

time: 527 us -> 468 us (0.89)
  waiting for transfers between devices: 115 us -> 55.3 us
  local copies, waits for them, and re-layouts: 17.8 us -> 3.76 us
  starting transfers between devices: 91.6 us -> 103 us
  Pallas kernels: 276 us -> 283 us
    ppermute x29 -> x43, waiting for transfers between devices: 113 us -> 52.2 us  [exchange(): return lax.ppermute(value, axis, [(i, i ^ distance) for i in range(size)])]
    unnamed x76 -> x72, local copies, waits for them, and re-layouts: 12.6 us -> 2.74 us
    ppermute x29 -> x43, starting transfers between devices: 62 us -> 71.3 us  [exchange(): return lax.ppermute(value, axis, [(i, i ^ distance) for i in range(size)])]
    pallas_call x13 -> x18, Pallas kernels: 233 us -> 241 us  [call(): pl.pallas_call(kernel, grid=grid, out_shape=kinds[0] if single else kinds...]
    ppermute x4 -> x6, starting transfers between devices: 23.4 us -> 23 us  [from_sides(): lax.ppermute(to_right, 'lat', up)]
    pallas_call x5 -> x8, Pallas kernels: 42.9 us -> 42.5 us  [prefetched(): pl.pallas_call(kernel, grid_spec=pltpu.PrefetchScalarGridSpec(num_scalar_...]
  transfers between devices with their start and end apart: 37 -> 55, of which waited for: 17 -> 19; matrix products, arithmetic and copies ran while one was open for 2% -> 2% of each run, Pallas kernels for 22% -> 36%
where the time goes in v2:
time: 468 us; the launch traced here: 462 us
  Pallas kernels  283 us (60%)
  starting transfers between devices  103 us (22%)
  waiting for transfers between devices  55.3 us (12%)
  other arithmetic  9.05 us (2%)
  between operations  6.86 us (1%)
    pallas_call x18, Pallas kernels, call(): pl.pallas_call(kernel, grid=grid, out_shape=kinds[0] if single else kinds...  241 us
    ppermute x43, starting transfers between devices, exchange(): return lax.ppermute(value, axis, [(i, i ^ distance) for i in range(size)])  71.3 us
    ppermute x43, waiting for transfers between devices, exchange(): return lax.ppermute(value, axis, [(i, i ^ distance) for i in range(size)])  52.2 us
    pallas_call x8, Pallas kernels, prefetched(): pl.pallas_call(kernel, grid_spec=pltpu.PrefetchScalarGridSpec(num_scalar_...  42.5 us
    ppermute x6, starting transfers between devices, from_sides(): lax.ppermute(to_right, 'lat', up)  23 us
  transfers between devices with their start and end apart: 55, of which 19 were waited for; matrix products, arithmetic and copies ran while one was open for 2% of the time, Pallas kernels for 36%

profile of v2, /device:TPU:0, one launch (start us, length us, event | category | flops | bytes accessed | tf_op | source)
XLA Modules:
  0.0 462.3 jit_solution(8603702370711842125)
XLA Ops:
  4.9 18.8 %shard_map.435 = (bf16[1024,256]{1,0:T(8,128)(2,1)S(1)}, f32[1024,512]{1,0:T(8,128)}, f32[1024,512]{1,0:T(8,128)}, bf16[1024,512]{1,0:T(8,128)(2,1)}, f32[1024,2...) custom-call(s32[4,1024]{1,0:T(4,128)S(1)} %bitcast.62, ...), custom_call_target="tpu_custom_call" | custom-call | flops 177167400960 | bytes 471859200 | tf_op jit(solution)/shard_map/pallas_call | solution.py:57
  28.7 10.4 %shard_map.436.bias = f32[3,1024,1024]{2,1,0:T(8,128)} custom-call(s32[5]{0:T(128)S(1)} %stack.52.places, s32[16]{0:T(128)S(1)} %reduce.ends, s32[16,1024]{1,0:T(8,128)S(1)} %bitcast.61), custom_call_target="tpu_custom_call" | custom-call | flops 60000002048 | bytes 377487360 | tf_op jit(solution)/shard_map/pallas_call | solution.py:57
  39.1 9.8 %collective-permute-start.2 = (bf16[1024,512]{1,0:T(8,128)(2,1)}, bf16[1024,512]{1,0:T(8,128)(2,1)}, u32[]{:S(2)}, u32[]{:S(2)}) collective-permute-start(bf16[1024,512]{1,0:T(8,128)(2,1)} %get-tuple-element.153.k1.v1), channel_id=1, source_target_pairs={{0,1},{1,2},{2,3},{3,4},{4,5},{5,6},{6,7},{8,9},{9,10},{10,11},{11... | collective-permute-start | bytes 3145736 | tf_op jit(solution)/shard_map/ppermute | solution.py:705
  50.4 14.7 %shard_map.437 = (f32[256,1024]{1,0:T(8,128)}, f32[2,8,1024]{2,1,0:T(8,128)S(1)}) custom-call(bf16[512,1024]{1,0:T(8,128)(2,1)} %get-tuple-element.149.q_ref, bf16[1024,512]{1,0:T(8,128)(2,1)S(1)} %collective-permute-done.k0.v0, bf16[1024,512]{1,0:T(8,128)(2,1)} %get-tuple-element.150.k1.v1, bf16[1024,512]{1,0:T(8,128)(2,1)S(1)} %collective-permute-done.1.k2.v2, ...), custom_call_target="tpu_custom_call" | custom-call | flops 193273528320 | bytes 377487360 | tf_op jit(solution)/shard_map/pallas_call | solution.py:57
  65.1 15.3 %shard_map.438 = (f32[256,1024]{1,0:T(8,128)}, f32[2,8,1024]{2,1,0:T(8,128)S(1)}) custom-call(bf16[512,1024]{1,0:T(8,128)(2,1)} %get-tuple-element.149.q_ref, bf16[1024,512]{1,0:T(8,128)(2,1)} %collective-permute-done.2.k0.v0, bf16[1024,512]{1,0:T(8,128)(2,1)} %get-tuple-element.153.k1.v1, bf16[1024,512]{1,0:T(8,128)(2,1)} %collective-permute-done.3.k2.v2, ...), custom_call_target="tpu_custom_call" | custom-call | flops 193273528320 | bytes 377487360 | tf_op jit(solution)/shard_map/pallas_call | solution.py:57
  80.4 14.7 %shard_map.439 = (bf16[512,1024]{1,0:T(8,128)(2,1)}, f32[1024,512]{1,0:T(8,128)}, bf16[1024,512]{1,0:T(8,128)(2,1)}, f32[1024,2048]{1,0:T(8,128)}, bf16[1024,204...) custom-call(f32[256,1024]{1,0:T(8,128)} %get-tuple-element.151.o0, f32[256,1024]{1,0:T(8,128)} %get-tuple-element.154.o1, ...), custom_call_target="tpu_custom_call" | custom-call | flops 144955146240 | bytes 377487360 | tf_op jit(solution)/shard_map/pallas_call | solution.py:57
  103.2 20.2 %shard_map.440 = (f32[1024,512]{1,0:T(8,128)}, bf16[1024,512]{1,0:T(8,128)(2,1)}, f32[1024,2048]{1,0:T(8,128)}, bf16[1024,2048]{1,0:T(8,128)(2,1)}, f32[1024,512...) custom-call(s32[3,1024]{1,0:T(4,128)S(1)} %bitcast.63, ...), custom_call_target="tpu_custom_call" | custom-call | flops 225485783040 | bytes 377487360 | tf_op jit(solution)/shard_map/pallas_call | solution.py:57
  123.9 11.8 %collective-permute-start.6 = (f32[83,64]{0,1:T(8,128)S(1)}, f32[83,64]{0,1:T(8,128)S(1)}, u32[]{:S(2)}, u32[]{:S(2)}) collective-permute-start(f32[83,64]{0,1:T(8,128)S(1)} %fusion.1), channel_id=1, source_target_pairs={{0,1},{1,0},{2,3},{3,2},{4,5},{5,4},{6,7},{7,6},{8,9},{9,8},{10,11... | collective-permute-start | bytes 63752 | tf_op jit(solution)/shard_map/ppermute | solution.py:491
  145.8 14.2 %shard_map.441 = (f32[1024,512]{1,0:T(8,128)}, bf16[1024,512]{1,0:T(8,128)(2,1)}, bf16[1024,2048]{1,0:T(8,128)(2,1)}, f32[512,128]{1,0:T(8,128)S(1)}, f32[2,512]{1,0:T(2,128)S(1)}) custom-call(bf16[128,1024]{1,0:T(8,128)(2,1)S(1)} %pad.17.grad_output, bf16[2,128,512]{2,1,0:T(8,128)(2,1)S(1)} %copy-done.5, f32[1024,512]{1,0:T(8,128)} %get-tuple-element.159.decoded, ...), custom_call_target="tpu_custom_call" | custom-call | flops 128849018880 | bytes 377487360 | tf_op jit(solution)/shard_map/pallas_call | solution.py:57
  160.1 10.0 %shard_map.442 = (bf16[1024,512]{1,0:T(8,128)(2,1)}, f32[1024,512]{1,0:T(8,128)}, bf16[1024,512]{1,0:T(8,128)(2,1)}) custom-call(s32[3,1024]{1,0:T(4,128)S(1)} %bitcast.64, f32[1024,512]{1,0:T(8,128)} %get-tuple-element.164.grad.grad_join), custom_call_target="tpu_custom_call" | custom-call | flops 193273528320 | bytes 188743680 | tf_op jit(solution)/shard_map/pallas_call | solution.py:57
  173.0 10.4 %shard_map.443 = (f32[4,4,64,1024]{3,2,1,0:T(8,128)S(1)}, f32[4,4,64,1024]{3,2,1,0:T(8,128)}) custom-call(s32[5]{0:T(128)S(1)} %copy-done.7, bf16[1024,512]{1,0:T(8,128)(2,1)} %get-tuple-element.157.normed, bf16[1024,512]{1,0:T(8,128)(2,1)} %get-tuple-element.167.rounded, bf16[1024,2048]{1,0:T(8,128)(2,1)} %get-tuple-element.168.before, ...), custom_call_target="tpu_custom_call" | custom-call | flops 128849018880 | bytes 503316480 | tf_op jit(solution)/shard_map/pallas_call | solution.py:57
  186.4 14.2 %shard_map.445 = (f32[1024,512]{1,0:T(8,128)}, bf16[1024,512]{1,0:T(8,128)(2,1)}, bf16[1024,2048]{1,0:T(8,128)(2,1)}, f32[1,512]{1,0:T(1,128)S(1)}, bf16[1024,51...) custom-call(bf16[1024,512]{1,0:T(8,128)(2,1)S(1)} %collective-permute-done.13.g0, ...), custom_call_target="tpu_custom_call" | custom-call | flops 144955146240 | bytes 377487360 | tf_op jit(solution)/shard_map/pallas_call | solution.py:57
  200.6 10.4 %shard_map.446 = (f32[4,4,64,1024]{3,2,1,0:T(8,128)S(1)}, f32[4,4,64,1024]{3,2,1,0:T(8,128)}) custom-call(s32[5]{0:T(128)S(1)} %copy-done.8, bf16[1024,512]{1,0:T(8,128)(2,1)} %get-tuple-element.176.normed, bf16[1024,512]{1,0:T(8,128)(2,1)} %get-tuple-element.181.rounded, bf16[1024,2048]{1,0:T(8,128)(2,1)} %get-tuple-element.182.before, ...), custom_call_target="tpu_custom_call" | custom-call | flops 128849018880 | bytes 503316480 | tf_op jit(solution)/shard_map/pallas_call | solution.py:57
  214.8 4.7 %shard_map.444 = (f32[4,64,1024]{2,1,0:T(8,128)S(1)}, bf16[4,64,1024]{2,1,0:T(8,128)(2,1)}, bf16[4,64,1024]{2,1,0:T(8,128)(2,1)}, bf16[4,64,1024]{2,1,0:T(8,128)(2,1)}) custom-call(s32[5]{0:T(128)S(1)} %copy-done.8, f32[4,4,64,1024]{3,2,1,0:T(8,128)S(1)} %get-tuple-element.170.refs_0_, f32[4,4,64,1024]{3,2,1,0:T(8,128)} %collective-permute-done.9.refs_1_), custom_call_target="tpu_custom_call" | custom-call | flops 440401920 | bytes 440401920 | tf_op jit(solution)/shard_map/pallas_call | solution.py:495
  223.0 22.3 %shard_map.447 = (f32[256,1024]{1,0:T(8,128)}, bf16[2,256,1024]{2,1,0:T(8,128)(2,1)}, f32[2,256,1024]{2,1,0:T(8,128)}, bf16[2,256,1024]{2,1,0:T(8,128)(2,1)}) custom-call(bf16[512,1024]{1,0:T(8,128)(2,1)} %get-tuple-element.149.q_ref, bf16[512,1024]{1,0:T(8,128)(2,1)} %get-tuple-element.197.do_ref, f32[2,8,1024]{2,1,0:T(8,128)S(1)} %get-tuple-element.188.lse_ref, ...), custom_call_target="tpu_custom_call" | custom-call | flops 483183820800 | bytes 377487360 | tf_op jit(solution)/shard_map/pallas_call | solution.py:57
  248.9 4.8 %shard_map.448 = (f32[4,64,1024]{2,1,0:T(8,128)S(1)}, bf16[4,64,1024]{2,1,0:T(8,128)(2,1)}, bf16[4,64,1024]{2,1,0:T(8,128)(2,1)}, bf16[4,64,1024]{2,1,0:T(8,128)(2,1)}) custom-call(s32[5]{0:T(128)S(1)} %copy-done.9, f32[4,4,64,1024]{3,2,1,0:T(8,128)S(1)} %get-tuple-element.191.refs_0_, f32[4,4,64,1024]{3,2,1,0:T(8,128)} %collective-permute-done.15.refs_1_), custom_call_target="tpu_custom_call" | custom-call | flops 440401920 | bytes 440401920 | tf_op jit(solution)/shard_map/pallas_call | solution.py:495
  257.1 22.3 %shard_map.450 = (f32[256,1024]{1,0:T(8,128)}, bf16[2,256,1024]{2,1,0:T(8,128)(2,1)}, f32[2,256,1024]{2,1,0:T(8,128)}, bf16[2,256,1024]{2,1,0:T(8,128)(2,1)}) custom-call(bf16[512,1024]{1,0:T(8,128)(2,1)} %get-tuple-element.149.q_ref, bf16[512,1024]{1,0:T(8,128)(2,1)} %get-tuple-element.197.do_ref, f32[2,8,1024]{2,1,0:T(8,128)S(1)} %get-tuple-element.198.lse_ref, ...), custom_call_target="tpu_custom_call" | custom-call | flops 483183820800 | bytes 377487360 | tf_op jit(solution)/shard_map/pallas_call | solution.py:57
  280.0 4.1 collective-permute-start.21
  285.7 4.5 shard_map.449
  290.1 11.1 %collective-permute-start.23 = (bf16[64,2048]{1,0:T(8,128)(2,1)}, bf16[64,2048]{1,0:T(8,128)(2,1)}, u32[]{:S(2)}, u32[]{:S(2)}) collective-permute-start(bf16[64,2048]{1,0:T(8,128)(2,1)} %get-tuple-element.219), channel_id=1, source_target_pairs={{0,2},{1,3},{2,0},{3,1},{4,6},{5,7},{6,4},{7,5},{8,10},{9,11},{10,... | collective-permute-start | bytes 786440 | tf_op jit(solution)/shard_map/ppermute | solution.py:491
  303.6 10.2 %shard_map.451 = (f32[1024,512]{1,0:T(8,128)}, bf16[1024,512]{1,0:T(8,128)(2,1)}, bf16[1536,1024]{1,0:T(8,128)(2,1)}, f32[1,512]{1,0:T(1,128)S(1)}) custom-call(f32[256,1024]{1,0:T(8,128)} %get-tuple-element.190.dq0, f32[256,1024]{1,0:T(8,128)} %get-tuple-element.199.dq1, bf16[2,256,1024]{2,1,0:T(8,128)(2,1)} %collective-permute-done.19.left0, ...), custom_call_target="tpu_custom_call" | custom-call | flops 48318382080 | bytes 377487360 | tf_op jit(solution)/shard_map/pallas_call | solution.py:57
  313.8 11.1 %shard_map.452 = (f32[4,4,64,1024]{3,2,1,0:T(8,128)S(1)}, f32[4,4,64,1024]{3,2,1,0:T(8,128)}) custom-call(s32[5]{0:T(128)S(1)} %copy-done.10, bf16[1024,512]{1,0:T(8,128)(2,1)} %get-tuple-element.210.rounded, bf16[1024,2048]{1,0:T(8,128)(2,1)} %get-tuple-element.211.active, bf16[1024,512]{1,0:T(8,128)(2,1)} %get-tuple-element.212.normed_attn, ...), custom_call_target="tpu_custom_call" | custom-call | flops 128849018880 | bytes 503316480 | tf_op jit(solution)/shard_map/pallas_call | solution.py:57
  327.8 5.8 %collective-permute-done.26.refs_1_ = f32[4,4,64,1024]{3,2,1,0:T(8,128)} collective-permute-done((f32[4,4,64,1024]{3,2,1,0:T(8,128)}, f32[4,4,64,1024]{3,2,1,0:T(8,128)}, u32[]{:S(2)}, u32[]{:S(2)}) %collective-permute-start.26) | collective-permute-done | bytes 4194336 | tf_op jit(solution)/shard_map/ppermute | solution.py:491
  333.6 4.7 %shard_map.454 = (f32[4,64,1024]{2,1,0:T(8,128)S(1)}, bf16[4,64,1024]{2,1,0:T(8,128)(2,1)}, bf16[4,64,1024]{2,1,0:T(8,128)(2,1)}, bf16[4,64,1024]{2,1,0:T(8,128)(2,1)}) custom-call(s32[5]{0:T(128)S(1)} %copy-done.11, f32[4,4,64,1024]{3,2,1,0:T(8,128)S(1)} %get-tuple-element.224.refs_0_, f32[4,4,64,1024]{3,2,1,0:T(8,128)} %collective-permute-done.26.refs_1_), custom_call_target="tpu_custom_call" | custom-call | flops 440401920 | bytes 440401920 | tf_op jit(solution)/shard_map/pallas_call | solution.py:495
  341.9 13.5 %shard_map.456 = (bf16[1024,2048]{1,0:T(8,128)(2,1)}, f32[512,128]{1,0:T(8,128)S(1)}, f32[1,512]{1,0:T(1,128)S(1)}, bf16[1024,512]{1,0:T(8,128)(2,1)}) custom-call(f32[1024,512]{1,0:T(8,128)} %get-tuple-element.237.upstream, f32[1024,512]{1,0:T(8,128)} %get-tuple-element.238.pooled, f32[1024,2048]{1,0:T(8,128)} %get-tuple-element.239.slope, ...), custom_call_target="tpu_custom_call" | custom-call | flops 128849018880 | bytes 377487360 | tf_op jit(solution)/shard_map/pallas_call | solution.py:57
  355.5 6.8 %shard_map.457 = (f32[4,4,64,640]{3,2,1,0:T(8,128)S(1)}, f32[4,4,64,640]{3,2,1,0:T(8,128)}) custom-call(s32[5]{0:T(128)S(1)} %copy-done.11, bf16[1024,512]{1,0:T(8,128)(2,1)} %get-tuple-element.235.normed, bf16[1024,2048]{1,0:T(8,128)(2,1)} %get-tuple-element.241.before, f32[512,128]{1,0:T(8,128)S(1)} %get-tuple-element.242.table_in, ...), custom_call_target="tpu_custom_call" | custom-call | flops 64424509440 | bytes 314572800 | tf_op jit(solution)/shard_map/pallas_call | solution.py:57
  369.1 3.9 shard_map.458
  379.5 5.7 %collective-permute-done.34.refs_1_ = bf16[4,64,768]{2,1,0:T(8,128)(2,1)S(1)} collective-permute-done((bf16[4,64,768]{2,1,0:T(8,128)(2,1)}, bf16[4,64,768]{2,1,0:T(8,128)(2,1)S(1)}, u32[]{:S(2)}, u32[]{:S(2)}) %collective-permute-start.34) | collective-permute-done | bytes 393248 | tf_op jit(solution)/shard_map/ppermute | solution.py:491
  385.2 6.1 %collective-permute-done.35.refs_2_ = bf16[4,64,768]{2,1,0:T(8,128)(2,1)S(1)} collective-permute-done((bf16[4,64,768]{2,1,0:T(8,128)(2,1)S(1)}, bf16[4,64,768]{2,1,0:T(8,128)(2,1)S(1)}, u32[]{:S(2)}, u32[]{:S(2)}) %collective-permute-start.35) | collective-permute-done | bytes 393248 | tf_op jit(solution)/shard_map/ppermute | solution.py:491
  421.5 4.4 collective-permute-done.45
  431.0 7.0 %collective-permute-done.50 = f32[1,2]{1,0:T(1,128)S(1)} collective-permute-done((f32[1,2]{1,0:T(1,128)S(1)}, f32[1,2]{1,0:T(1,128)S(1)}, u32[]{:S(2)}, u32[]{:S(2)}) %collective-permute-start.50) | collective-permute-done | bytes 40 | tf_op jit(solution)/shard_map/ppermute | solution.py:491
  445.6 15.3 %shard_map.460 = (f32[3,64,4096]{2,1,0:T(8,128)}, f32[3,64,4096]{2,1,0:T(8,128)}, f32[3,64,4096]{2,1,0:T(8,128)}, f32[3,64,4096]{2,1,0:T(8,128)}, bf16[3,64,4096...) custom-call(s32[5]{0:T(128)S(1)} %copy-done.11, ...), custom_call_target="tpu_custom_call" | custom-call | flops 935854080 | bytes 935854080 | tf_op jit(solution)/shard_map/pallas_call | solution.py:495
  (216 shorter events, 112.4 us)
Async XLA Ops:
  39.1 26.0 %collective-permute-start.2 = (bf16[1024,512]{1,0:T(8,128)(2,1)}, bf16[1024,512]{1,0:T(8,128)(2,1)}, u32[]{:S(2)}, u32[]{:S(2)}) collective-permute-start(bf16[1024,512]{1,0:T(8,128)(2,1)} %get-tuple-element.153.k1.v1), channel_id=1, source_target_pairs={{0,1},{1,2},{2,3},{3,4},{4,5},{5,6},{6,7},{8,9},{9,10},{10,11},{11... | collective-permute-start | bytes 3145736 | tf_op jit(solution)/shard_map/ppermute | solution.py:705
  48.8 16.2 %collective-permute-start.3 = (bf16[1024,512]{1,0:T(8,128)(2,1)}, bf16[1024,512]{1,0:T(8,128)(2,1)}, u32[]{:S(2)}, u32[]{:S(2)}) collective-permute-start(bf16[1024,512]{1,0:T(8,128)(2,1)} %get-tuple-element.153.k1.v1), channel_id=1, source_target_pairs={{1,0},{2,1},{3,2},{4,3},{5,4},{6,5},{7,6},{9,8},{10,9},{11,10},{12... | collective-permute-start | bytes 3145736 | tf_op jit(solution)/shard_map/ppermute | solution.py:705
  170.1 16.3 %collective-permute-start.13 = (bf16[1024,512]{1,0:T(8,128)(2,1)}, bf16[1024,512]{1,0:T(8,128)(2,1)S(1)}, u32[]{:S(2)}, u32[]{:S(2)}) collective-permute-start(bf16[1024,512]{1,0:T(8,128)(2,1)} %get-tuple-element.166), channel_id=1, source_target_pairs={{0,1},{1,2},{2,3},{3,4},{4,5},{5,6},{6,7},{8,9},{9,10},{10,11},{11... | collective-permute-start | bytes 3145736 | tf_op jit(solution)/shard_map/ppermute | solution.py:705
  171.5 14.9 %collective-permute-start.14 = (bf16[1024,512]{1,0:T(8,128)(2,1)}, bf16[1024,512]{1,0:T(8,128)(2,1)S(1)}, u32[]{:S(2)}, u32[]{:S(2)}) collective-permute-start(bf16[1024,512]{1,0:T(8,128)(2,1)} %get-tuple-element.165), channel_id=1, source_target_pairs={{1,0},{2,1},{3,2},{4,3},{5,4},{6,5},{7,6},{9,8},{10,9},{11,10},{12... | collective-permute-start | bytes 3145736 | tf_op jit(solution)/shard_map/ppermute | solution.py:705
  183.4 31.4 %collective-permute-start.9 = (f32[4,4,64,1024]{3,2,1,0:T(8,128)}, f32[4,4,64,1024]{3,2,1,0:T(8,128)}, u32[]{:S(2)}, u32[]{:S(2)}) collective-permute-start(f32[4,4,64,1024]{3,2,1,0:T(8,128)} %get-tuple-element.171), channel_id=1, source_target_pairs={{0,1},{1,0},{2,3},{3,2},{4,5},{5,4},{6,7},{7,6},{8,9},{9,8},{10,11... | collective-permute-start | bytes 12582920 | tf_op jit(solution)/shard_map/ppermute | solution.py:491
  211.0 36.5 %collective-permute-start.15 = (f32[4,4,64,1024]{3,2,1,0:T(8,128)}, f32[4,4,64,1024]{3,2,1,0:T(8,128)}, u32[]{:S(2)}, u32[]{:S(2)}) collective-permute-start(f32[4,4,64,1024]{3,2,1,0:T(8,128)} %get-tuple-element.186), channel_id=1, source_target_pairs={{0,1},{1,0},{2,3},{3,2},{4,5},{5,4},{6,7},{7,6},{8,9},{9,8},{10,11... | collective-permute-start | bytes 12582920 | tf_op jit(solution)/shard_map/ppermute | solution.py:491
  219.6 34.1 %collective-permute-start.10 = (bf16[4,64,1024]{2,1,0:T(8,128)(2,1)}, bf16[4,64,1024]{2,1,0:T(8,128)(2,1)}, u32[]{:S(2)}, u32[]{:S(2)}) collective-permute-start(bf16[4,64,1024]{2,1,0:T(8,128)(2,1)} %get-tuple-element.173), channel_id=1, source_target_pairs={{0,8},{8,0},{16,24},{24,16},{1,9},{9,1},{17,25},{25,17},{2,10},{10... | collective-permute-start | bytes 1572872 | tf_op jit(solution)/shard_map/ppermute | solution.py:491
  221.0 34.1 %collective-permute-start.11 = (bf16[4,64,1024]{2,1,0:T(8,128)(2,1)}, bf16[4,64,1024]{2,1,0:T(8,128)(2,1)}, u32[]{:S(2)}, u32[]{:S(2)}) collective-permute-start(bf16[4,64,1024]{2,1,0:T(8,128)(2,1)} %get-tuple-element.174), channel_id=1, source_target_pairs={{0,16},{8,24},{16,0},{24,8},{1,17},{9,25},{17,1},{25,9},{2,18},{10... | collective-permute-start | bytes 1572872 | tf_op jit(solution)/shard_map/ppermute | solution.py:491
  222.6 34.1 %collective-permute-start.12 = (bf16[4,64,1024]{2,1,0:T(8,128)(2,1)}, bf16[4,64,1024]{2,1,0:T(8,128)(2,1)}, u32[]{:S(2)}, u32[]{:S(2)}) collective-permute-start(bf16[4,64,1024]{2,1,0:T(8,128)(2,1)} %get-tuple-element.175), channel_id=1, source_target_pairs={{0,24},{8,16},{16,8},{24,0},{1,25},{9,17},{17,9},{25,1},{2,26},{10... | collective-permute-start | bytes 1572872 | tf_op jit(solution)/shard_map/ppermute | solution.py:491
  245.3 34.1 %collective-permute-start.19 = (bf16[2,256,1024]{2,1,0:T(8,128)(2,1)}, bf16[2,256,1024]{2,1,0:T(8,128)(2,1)}, u32[]{:S(2)}, u32[]{:S(2)}) collective-permute-start(bf16[2,256,1024]{2,1,0:T(8,128)(2,1)} %get-tuple-element.200), channel_id=1, source_target_pairs={{0,1},{1,2},{2,3},{3,4},{4,5},{5,6},{6,7},{8,9},{9,10},{10,11},{11... | collective-permute-start | bytes 3145736 | tf_op jit(solution)/shard_map/ppermute | solution.py:705
  247.6 31.8 %collective-permute-start.20 = (bf16[2,256,1024]{2,1,0:T(8,128)(2,1)}, bf16[2,256,1024]{2,1,0:T(8,128)(2,1)}, u32[]{:S(2)}, u32[]{:S(2)}) collective-permute-start(bf16[2,256,1024]{2,1,0:T(8,128)(2,1)} %get-tuple-element.203), channel_id=1, source_target_pairs={{1,0},{2,1},{3,2},{4,3},{5,4},{6,5},{7,6},{9,8},{10,9},{11,10},{12... | collective-permute-start | bytes 3145736 | tf_op jit(solution)/shard_map/ppermute | solution.py:705
  253.6 25.8 %collective-permute-start.16 = (bf16[4,64,1024]{2,1,0:T(8,128)(2,1)}, bf16[4,64,1024]{2,1,0:T(8,128)(2,1)}, u32[]{:S(2)}, u32[]{:S(2)}) collective-permute-start(bf16[4,64,1024]{2,1,0:T(8,128)(2,1)} %get-tuple-element.193), channel_id=1, source_target_pairs={{0,8},{8,0},{16,24},{24,16},{1,9},{9,1},{17,25},{25,17},{2,10},{10... | collective-permute-start | bytes 1572872 | tf_op jit(solution)/shard_map/ppermute | solution.py:491
  255.1 24.5 %collective-permute-start.17 = (bf16[4,64,1024]{2,1,0:T(8,128)(2,1)}, bf16[4,64,1024]{2,1,0:T(8,128)(2,1)}, u32[]{:S(2)}, u32[]{:S(2)}) collective-permute-start(bf16[4,64,1024]{2,1,0:T(8,128)(2,1)} %get-tuple-element.194), channel_id=1, source_target_pairs={{0,16},{8,24},{16,0},{24,8},{1,17},{9,25},{17,1},{25,9},{2,18},{10... | collective-permute-start | bytes 1572872 | tf_op jit(solution)/shard_map/ppermute | solution.py:491
  256.6 23.4 %collective-permute-start.18 = (bf16[4,64,1024]{2,1,0:T(8,128)(2,1)}, bf16[4,64,1024]{2,1,0:T(8,128)(2,1)}, u32[]{:S(2)}, u32[]{:S(2)}) collective-permute-start(bf16[4,64,1024]{2,1,0:T(8,128)(2,1)} %get-tuple-element.195), channel_id=1, source_target_pairs={{0,24},{8,16},{16,8},{24,0},{1,25},{9,17},{17,9},{25,1},{2,26},{10... | collective-permute-start | bytes 1572872 | tf_op jit(solution)/shard_map/ppermute | solution.py:491
  290.1 36.3 %collective-permute-start.23 = (bf16[64,2048]{1,0:T(8,128)(2,1)}, bf16[64,2048]{1,0:T(8,128)(2,1)}, u32[]{:S(2)}, u32[]{:S(2)}) collective-permute-start(bf16[64,2048]{1,0:T(8,128)(2,1)} %get-tuple-element.219), channel_id=1, source_target_pairs={{0,2},{1,3},{2,0},{3,1},{4,6},{5,7},{6,4},{7,5},{8,10},{9,11},{10,... | collective-permute-start | bytes 786440 | tf_op jit(solution)/shard_map/ppermute | solution.py:491
  301.2 25.3 %collective-permute-start.24 = (bf16[64,2048]{1,0:T(8,128)(2,1)}, bf16[64,2048]{1,0:T(8,128)(2,1)}, u32[]{:S(2)}, u32[]{:S(2)}) collective-permute-start(bf16[64,2048]{1,0:T(8,128)(2,1)} %get-tuple-element.221), channel_id=1, source_target_pairs={{0,4},{1,5},{2,6},{3,7},{4,0},{5,1},{6,2},{7,3},{8,12},{9,13},{10,... | collective-permute-start | bytes 786440 | tf_op jit(solution)/shard_map/ppermute | solution.py:491
  301.2 25.3 %collective-permute-start.25 = (bf16[64,2048]{1,0:T(8,128)(2,1)}, bf16[64,2048]{1,0:T(8,128)(2,1)}, u32[]{:S(2)}, u32[]{:S(2)}) collective-permute-start(bf16[64,2048]{1,0:T(8,128)(2,1)} %get-tuple-element.223), channel_id=1, source_target_pairs={{0,6},{1,7},{2,4},{3,5},{4,2},{5,3},{6,0},{7,1},{8,14},{9,15},{10,... | collective-permute-start | bytes 786440 | tf_op jit(solution)/shard_map/ppermute | solution.py:491
  338.4 24.0 %collective-permute-start.27 = (bf16[4,64,1024]{2,1,0:T(8,128)(2,1)}, bf16[4,64,1024]{2,1,0:T(8,128)(2,1)}, u32[]{:S(2)}, u32[]{:S(2)}) collective-permute-start(bf16[4,64,1024]{2,1,0:T(8,128)(2,1)} %get-tuple-element.228), channel_id=1, source_target_pairs={{0,8},{8,0},{16,24},{24,16},{1,9},{9,1},{17,25},{25,17},{2,10},{10... | collective-permute-start | bytes 1572872 | tf_op jit(solution)/shard_map/ppermute | solution.py:491
  339.9 25.5 %collective-permute-start.28 = (bf16[4,64,1024]{2,1,0:T(8,128)(2,1)}, bf16[4,64,1024]{2,1,0:T(8,128)(2,1)}, u32[]{:S(2)}, u32[]{:S(2)}) collective-permute-start(bf16[4,64,1024]{2,1,0:T(8,128)(2,1)} %get-tuple-element.229), channel_id=1, source_target_pairs={{0,16},{8,24},{16,0},{24,8},{1,17},{9,25},{17,1},{25,9},{2,18},{10... | collective-permute-start | bytes 1572872 | tf_op jit(solution)/shard_map/ppermute | solution.py:491
  341.4 23.9 %collective-permute-start.29 = (bf16[4,64,1024]{2,1,0:T(8,128)(2,1)}, bf16[4,64,1024]{2,1,0:T(8,128)(2,1)}, u32[]{:S(2)}, u32[]{:S(2)}) collective-permute-start(bf16[4,64,1024]{2,1,0:T(8,128)(2,1)} %get-tuple-element.230), channel_id=1, source_target_pairs={{0,24},{8,16},{16,8},{24,0},{1,25},{9,17},{17,9},{25,1},{2,26},{10... | collective-permute-start | bytes 1572872 | tf_op jit(solution)/shard_map/ppermute | solution.py:491
  374.2 17.1 %collective-permute-start.35 = (bf16[4,64,768]{2,1,0:T(8,128)(2,1)S(1)}, bf16[4,64,768]{2,1,0:T(8,128)(2,1)S(1)}, u32[]{:S(2)}, u32[]{:S(2)}) collective-permute-start(bf16[4,64,768]{2,1,0:T(8,128)(2,1)S(1)} %get-tuple-element.256), channel_id=1, source_target_pairs={{0,16},{8,24},{16,0},{24,8},{1,17},{9,25},{17,1},{25,9},{2,18},{10... | collective-permute-start | bytes 1179656 | tf_op jit(solution)/shard_map/ppermute | solution.py:491
  375.0 17.9 %collective-permute-start.36 = (bf16[4,64,768]{2,1,0:T(8,128)(2,1)S(1)}, bf16[4,64,768]{2,1,0:T(8,128)(2,1)S(1)}, u32[]{:S(2)}, u32[]{:S(2)}) collective-permute-start(bf16[4,64,768]{2,1,0:T(8,128)(2,1)S(1)} %get-tuple-element.258), channel_id=1, source_target_pairs={{0,24},{8,16},{16,8},{24,0},{1,25},{9,17},{17,9},{25,1},{2,26},{10... | collective-permute-start | bytes 1179656 | tf_op jit(solution)/shard_map/ppermute | solution.py:491
  378.4 16.4 %collective-permute-start.32 = (bf16[64,1024]{1,0:T(8,128)(2,1)}, bf16[64,1024]{1,0:T(8,128)(2,1)}, u32[]{:S(2)}, u32[]{:S(2)}) collective-permute-start(bf16[64,1024]{1,0:T(8,128)(2,1)} %get-tuple-element.234), channel_id=1, source_target_pairs={{0,6},{1,7},{2,4},{3,5},{4,2},{5,3},{6,0},{7,1},{8,14},{9,15},{10,... | collective-permute-start | bytes 393224 | tf_op jit(solution)/shard_map/ppermute | solution.py:491
  378.7 19.6 %collective-permute-start.31 = (bf16[64,1024]{1,0:T(8,128)(2,1)}, bf16[64,1024]{1,0:T(8,128)(2,1)}, u32[]{:S(2)}, u32[]{:S(2)}) collective-permute-start(bf16[64,1024]{1,0:T(8,128)(2,1)} %get-tuple-element.233), channel_id=1, source_target_pairs={{0,4},{1,5},{2,6},{3,7},{4,0},{5,1},{6,2},{7,3},{8,12},{9,13},{10,... | collective-permute-start | bytes 393224 | tf_op jit(solution)/shard_map/ppermute | solution.py:491
  400.8 14.9 %collective-permute-start.41 = (f32[64,1024]{1,0:T(8,128)S(1)}, f32[64,1024]{1,0:T(8,128)S(1)}, u32[]{:S(2)}, u32[]{:S(2)}) collective-permute-start(f32[64,1024]{1,0:T(8,128)S(1)} %get-tuple-element.329.refs_4_), channel_id=1, source_target_pairs={{0,16},{8,24},{16,0},{24,8},{1,17},{9,25},{17,1},{25,9},{2,18},{10... | collective-permute-start | bytes 786440 | tf_op jit(solution)/shard_map/ppermute | solution.py:491
  402.0 14.8 %collective-permute-start.42 = (f32[64,1024]{1,0:T(8,128)S(1)}, f32[64,1024]{1,0:T(8,128)S(1)}, u32[]{:S(2)}, u32[]{:S(2)}) collective-permute-start(f32[64,1024]{1,0:T(8,128)S(1)} %get-tuple-element.329.refs_4_), channel_id=1, source_target_pairs={{0,24},{8,16},{16,8},{24,0},{1,25},{9,17},{17,9},{25,1},{2,26},{10... | collective-permute-start | bytes 786440 | tf_op jit(solution)/shard_map/ppermute | solution.py:491
  404.3 22.5 %collective-permute-start.46 = (f32[64,640]{1,0:T(8,128)S(1)}, f32[64,640]{1,0:T(8,128)S(1)}, u32[]{:S(2)}, u32[]{:S(2)}) collective-permute-start(f32[64,640]{1,0:T(8,128)S(1)} %get-tuple-element.330.refs_8_), channel_id=1, source_target_pairs={{0,8},{8,0},{16,24},{24,16},{1,9},{9,1},{17,25},{25,17},{2,10},{10... | collective-permute-start | bytes 491528 | tf_op jit(solution)/shard_map/ppermute | solution.py:491
  405.1 23.2 %collective-permute-start.47 = (f32[64,640]{1,0:T(8,128)S(1)}, f32[64,640]{1,0:T(8,128)S(1)}, u32[]{:S(2)}, u32[]{:S(2)}) collective-permute-start(f32[64,640]{1,0:T(8,128)S(1)} %get-tuple-element.330.refs_8_), channel_id=1, source_target_pairs={{0,16},{8,24},{16,0},{24,8},{1,17},{9,25},{17,1},{25,9},{2,18},{10... | collective-permute-start | bytes 491528 | tf_op jit(solution)/shard_map/ppermute | solution.py:491
  409.3 19.1 %collective-permute-start.48 = (f32[64,640]{1,0:T(8,128)S(1)}, f32[64,640]{1,0:T(8,128)S(1)}, u32[]{:S(2)}, u32[]{:S(2)}) collective-permute-start(f32[64,640]{1,0:T(8,128)S(1)} %get-tuple-element.330.refs_8_), channel_id=1, source_target_pairs={{0,24},{8,16},{16,8},{24,0},{1,25},{9,17},{17,9},{25,1},{2,26},{10... | collective-permute-start | bytes 491528 | tf_op jit(solution)/shard_map/ppermute | solution.py:491
  415.7 29.8 %collective-permute-start.52 = (bf16[64,2048]{1,0:T(8,128)(2,1)S(1)}, bf16[64,2048]{1,0:T(8,128)(2,1)S(1)}, u32[]{:S(2)}, u32[]{:S(2)}) collective-permute-start(bf16[64,2048]{1,0:T(8,128)(2,1)S(1)} %shard_map.453.refs_0_), channel_id=1, source_target_pairs={{0,8},{8,0},{16,24},{24,16},{1,9},{9,1},{17,25},{25,17},{2,10},{10... | collective-permute-start | bytes 786440 | tf_op jit(solution)/shard_map/ppermute | solution.py:491
  425.9 19.6 %collective-permute-start.53 = (bf16[64,2048]{1,0:T(8,128)(2,1)S(1)}, bf16[64,2048]{1,0:T(8,128)(2,1)S(1)}, u32[]{:S(2)}, u32[]{:S(2)}) collective-permute-start(bf16[64,2048]{1,0:T(8,128)(2,1)S(1)} %shard_map.453.refs_0_), channel_id=1, source_target_pairs={{0,16},{8,24},{16,0},{24,8},{1,17},{9,25},{17,1},{25,9},{2,18},{10... | collective-permute-start | bytes 786440 | tf_op jit(solution)/shard_map/ppermute | solution.py:491
  426.8 18.7 %collective-permute-start.54 = (bf16[64,2048]{1,0:T(8,128)(2,1)S(1)}, bf16[64,2048]{1,0:T(8,128)(2,1)S(1)}, u32[]{:S(2)}, u32[]{:S(2)}) collective-permute-start(bf16[64,2048]{1,0:T(8,128)(2,1)S(1)} %shard_map.453.refs_0_), channel_id=1, source_target_pairs={{0,24},{8,16},{16,8},{24,0},{1,25},{9,17},{17,9},{25,1},{2,26},{10... | collective-permute-start | bytes 786440 | tf_op jit(solution)/shard_map/ppermute | solution.py:491
  (58 other events, 1147.5 us)

commit v3 on v2

--- a/solution.py
+++ b/solution.py
@@ -49,10 +49,10 @@
     return pltpu.with_memory_space_constraint(value, pltpu.HBM) if is_far(value) else value
 
 
-def call(kernel, grid, outs, in_specs, out_specs, operands, scratch=(), flops=0, moved=0, near=False):
+def call(kernel, grid, outs, in_specs, out_specs, operands, scratch=(), flops=0, moved=0, near=()):
     single = not isinstance(outs, list)
     kinds = [outs] if single else outs
-    large = [not near and x.size * x.dtype.itemsize >= LARGE for x in kinds]
+    large = [i not in near and x.size * x.dtype.itemsize >= LARGE for i, x in enumerate(kinds)]
     kinds = [pltpu.HBM(x.shape, x.dtype) if flag else x for x, flag in zip(kinds, large)]
     results = pl.pallas_call(
         kernel,
@@ -134,10 +134,12 @@
     rounded = upstream.astype(BF16)
     rounded_ref[...] = rounded
     grad_normed = jnp.zeros(values.shape, F32)
+    ahead = [dot(rounded, w_ref[0, :, hidden : hidden + step], 1, 0)]
     for start in range(0, hidden, step):
         part = slice(start, start + step)
-        grad_active = dot(rounded, w_ref[0, :, hidden + start : hidden + start + step], 1, 0)
-        grad_before = (grad_active * slope_ref[:, part]).astype(BF16)
+        if start + step < hidden:
+            ahead.append(dot(rounded, w_ref[0, :, hidden + start + step : hidden + start + 2 * step], 1, 0))
+        grad_before = (ahead.pop(0) * slope_ref[:, part]).astype(BF16)
         before_ref[:, part] = grad_before
         grad_normed = grad_normed + dot(grad_before, w_ref[0, :, part], 1, 1)
     grad, gain_grad = norm_back(grad_normed, values, gain_row)
@@ -287,8 +289,8 @@
 
 
 def decoder_back_kernel(
-    grad_output, tables, decoded, final, joined, slope, gains, mlp,
-    grad_join_ref, rounded_ref, before_ref, table_ref, gain_ref,
+    grad_output, tables, decoded, final, joined, slope, gains, mlp, x,
+    high_ref, low_ref, rounded_ref, before_ref, table_ref, gain_ref, direct_ref,
 ):
     grad_final = dot(grad_output[...], tables[1], 0, 0)
     add_up(table_ref, dot(final[...], grad_output[...], 0, 1))
@@ -296,26 +298,20 @@
     grad_join, gain_dec = mlp_backward(
         grad_decoded, joined[...], gains[3:4], mlp, slope, rounded_ref, before_ref
     )
-    grad_join_ref[...] = grad_join
+    high, low = two_parts(grad_join)
+    high_ref[...] = high
+    low_ref[...] = low
+    add_up(direct_ref, dot(high, x[...], 0, 1) + dot(low, x[...], 0, 1))
     add_up(gain_ref, jnp.concatenate([gain_dec, gain_final], axis=0))
 
 
-def scatter_kernel(edges, grad, out0, out1, out2, high_ref, low_ref):
+def scatter_kernel(edges, high, low, out0, out1, out2):
     rows = out0.shape[0]
-    count = edges.shape[0]
-    step = pl.program_id(0)
-
-    @pl.when(step == 0)
-    def _():
-        high, low = two_parts(grad[...])
-        high_ref[...] = high
-        low_ref[...] = low
-
-    total = grad.shape[0]
+    count, total = edges.shape
     for w, out in enumerate((out0, out1, out2)):
-        sub = lax.broadcasted_iota(jnp.int32, (rows, total), 0) + (step * rows + w * total)
+        sub = lax.broadcasted_iota(jnp.int32, (rows, total), 0) + (pl.program_id(0) * rows + w * total)
         tally = named(edges, sub)
-        value = dot(tally, high_ref[...], 1, 0) + dot(tally, low_ref[...], 1, 0)
+        value = dot(tally, high[...], 1, 0) + dot(tally, low[...], 1, 0)
         out[...] = (value / count).astype(out.dtype)
 
 
@@ -420,13 +416,18 @@
         hand_out(places[2], dot(attended[...], branch[...], 1, 0), keep_ref, send_ref, columns)
 
 
-def up_weights_kernel(places, normed, before, table_in, table_out, gain, keep_ref, send_ref, normed_turned):
+def up_weights_kernel(places, normed, before, table_in, table_direct, table_out, gain, keep_ref, send_ref, normed_turned):
     quarter = pl.program_id(0)
     size = before.shape[1]
     turn(((normed, normed_turned),))
     hand_out(places[2], dot(normed_turned[...], before[...], 1, 0), keep_ref, send_ref, slice(0, size))
     columns = slice(size, size + table_in.shape[1])
-    for index, ref in enumerate((table_in, table_out, gain)):
+
+    @pl.when(quarter == 0)
+    def _():
+        hand_out(places[2], table_in[...] + table_direct[...], keep_ref, send_ref, columns)
+
+    for index, ref in ((1, table_out), (2, gain)):
 
         @pl.when(quarter == index)
         def _(ref=ref):
@@ -499,7 +500,7 @@
         ),
         out_shape=outs,
         cost_estimate=pl.CostEstimate(flops=moved * WEIGH * weight, bytes_accessed=moved * WEIGH, transcendentals=0),
-        compiler_params=pltpu.CompilerParams(vmem_limit_bytes=VMEM_BYTES),
+        compiler_params=pltpu.CompilerParams(vmem_limit_bytes=VMEM_BYTES * 2 // 3),
     )(places, *[far(x) for x in operands])
 
 
@@ -569,11 +570,13 @@
 
 
 def total_kernel(own, *refs):
-    *came, out = refs
+    *came, out0, out1 = refs
     total = own[...]
     for ref in came:
         total = total + ref[...].astype(F32)
-    out[...] = total.astype(out.dtype)
+    half = out0.shape[-1]
+    out0[...] = total[:, :half]
+    out1[...] = total[:, half:]
 
 
 def add_bands(parts, late):
@@ -582,18 +585,23 @@
     return call(
         total_kernel,
         (1,),
-        shape(own.shape, BF16),
+        [shape((own.shape[0], own.shape[1] // 2), F32)] * 2,
         [whole(own.shape)] * len(parts),
-        whole(own.shape),
+        [whole((own.shape[0], own.shape[1] // 2))] * 2,
         (after(own, *late), *came),
         flops=10**11,
         moved=16 * own.size,
-        near=True,
-    )
-
-
-def all_items(value):
-    return [value] + [exchange(value, "item", k) for k in range(1, lax.axis_size("item"))]
+        near=(0, 1),
+    )
+
+
+def all_items(one, two):
+    one_near, two_far = exchange(one, "item", 1), exchange(two, "item", 2)
+    one_far, two_near = exchange(one, "item", 2), exchange(two, "item", 1)
+    return [
+        (one, two), (one_near, two_near), (one_far, two_far),
+        (exchange(one_near, "item", 2), exchange(two_far, "item", 1)),
+    ]
 
 
 def sum_over(value, axis):
@@ -605,12 +613,13 @@
 
 
 def adam_kernel(places, factor, *refs):
-    first, down, up = refs[:4], refs[4:8], refs[8:12]
-    mlp, attn = refs[12:16], refs[16:20]
-    mlp_out, attn_out = refs[20:25], refs[25:30]
+    dec, proc, down, up = refs[:4], refs[4:8], refs[8:12], refs[12:16]
+    mlp, attn, tables, gains = refs[16:20], refs[20:24], refs[24:28], refs[28:32]
+    mlp_out, attn_out, tables_out, gains_out = refs[32:37], refs[37:42], refs[42:47], refs[47:52]
     size = mlp[0].shape[-1]
     part = attn[0].shape[-1]
     half = pl.program_id(1)
+    quarter = places[3] ^ pl.program_id(0)
     for index in range(4):
         for side in range(2):
 
@@ -618,11 +627,10 @@
             def _(index=index, side=side):
                 scale = factor[0]
                 here = slice(side * size, (side + 1) * size)
-                there = slice((2 + side) * size, (3 + side) * size)
-                shares = ((down if side else up)[index][:, :size], first[index][:, there], first[index][:, here])
+                shares = ((down if side else up)[index][:, :size], proc[index][:, here], dec[index][:, here])
                 for layer, share in enumerate(shares):
                     new = adam_update(
-                        scale * share.astype(F32), *(ref[layer] for ref in mlp), RATE_MATRIX, WEIGHT_DECAY
+                        scale * share, *(ref[layer] for ref in mlp), RATE_MATRIX, WEIGHT_DECAY
                     )
                     for ref, value in zip(mlp_out, new):
                         ref[layer] = value
@@ -630,6 +638,26 @@
                 new = adam_update(scale * share, *(ref[...] for ref in attn), RATE_MATRIX, WEIGHT_DECAY)
                 for ref, value in zip(attn_out, new):
                     ref[...] = value
+
+                if side:
+                    return
+                share = scale * up[index][:, size:]
+                for table in range(2):
+
+                    @pl.when(quarter == table)
+                    def _(table=table):
+                        new = adam_update(
+                            share[:, : tables[0].shape[-1]], *(ref[table] for ref in tables), RATE_MATRIX, WEIGHT_DECAY
+                        )
+                        for ref, value in zip(tables_out, new):
+                            ref[table] = value
+
+                @pl.when(quarter == 2)
+                def _():
+                    turned = share.T[: gains[0].shape[0]]
+                    new = adam_update(turned, *(ref[...] for ref in gains), RATE_GAIN, 0.0)
+                    for ref, value in zip(gains_out, new):
+                        ref[...] = value
 
 
 def projection_back_kernel(
@@ -653,7 +681,7 @@
 
 
 def encoder_back_kernel(
-    upstream, pooled, slope, gains, mlp, x, pin, grad_join, before_ref, table_ref, gain_ref, rounded_ref
+    upstream, pooled, slope, gains, mlp, pin, before_ref, table_ref, gain_ref, rounded_ref
 ):
     grad_pooled, gain_enc = mlp_backward(
         upstream[...], pooled[...], gains[0:1], mlp, slope, rounded_ref, before_ref
@@ -661,10 +689,8 @@
     add_up(gain_ref, gain_enc)
     high, low = two_parts(grad_pooled)
     both = dot(high, pin[...], 0, 0) + dot(low, pin[...], 0, 0)
-    channels = x.shape[0]
-    high, low = two_parts(grad_join[...])
-    direct = dot(high, x[...], 0, 1) + dot(low, x[...], 0, 1)
-    add_up(table_ref, direct + both[:, :channels] + both[:, channels:])
+    channels = both.shape[1] // 2
+    add_up(table_ref, both[:, :channels] + both[:, channels:])
 
 
 def weights(kernel, places, operands, specs, columns, flops, turned):
@@ -682,15 +708,15 @@
         flops=flops,
         moved=8 * width * columns * 4,
         scratch=[pltpu.VMEM((width, rows), BF16)] * turned,
-        near=True,
+        near=(0, 1),
     )
 
 
 def adam_update(gradient, master, moment_one, moment_two, average, step_rate, decay_rate):
     one_new = BETA_ONE * moment_one + (1.0 - BETA_ONE) * gradient
     two_new = BETA_TWO * moment_two + (1.0 - BETA_TWO) * gradient * gradient
-    one_hat = one_new / (1.0 - BETA_ONE**STEP)
-    two_hat = two_new / (1.0 - BETA_TWO**STEP)
+    one_hat = one_new * (1.0 / (1.0 - BETA_ONE**STEP))
+    two_hat = two_new * (1.0 / (1.0 - BETA_TWO**STEP))
     master_new = master - step_rate * (
         one_hat / (jnp.sqrt(two_hat) + ADAM_EPS) + decay_rate * master
     )
@@ -849,6 +875,7 @@
         (*attended, encoded, gains, mlp_copy, attn_copy),
         flops=mlp_flops + 2 * rows * width * width,
         moved=24 * rows * width,
+        near=(5,),
     )
 
     before_sent, after_sent = from_sides(sent, sent)
@@ -886,31 +913,36 @@
     )
     grad_output = jnp.pad((scale_out * grad_error).astype(BF16), ((0, extra), (0, 0)))
 
-    grad_join, rounded_dec, before_dec, table_out, gain_dec = call(
+    join_high, join_low, rounded_dec, before_dec, table_out, gain_dec, table_direct = call(
         decoder_back_kernel,
         (grid_rows // ROWS,),
         [
-            shape((grid_rows, width), F32), shape((grid_rows, width), BF16), shape((grid_rows, hidden), BF16),
-            shape((width, padded), F32), shape((2, width), F32),
+            shape((grid_rows, width), BF16), shape((grid_rows, width), BF16), shape((grid_rows, width), BF16),
+            shape((grid_rows, hidden), BF16), shape((width, padded), F32), shape((2, width), F32),
+            shape((width, padded), F32),
         ],
         [
             lanes_of(padded), tables_spec, rows_of(width), rows_of(width), rows_of(width), rows_of(hidden),
-            gains_spec, weights_spec(2),
+            gains_spec, weights_spec(2), lanes_of(padded),
         ],
-        [rows_of(width), rows_of(width), rows_of(hidden), whole((width, padded)), whole((2, width))],
-        (grad_output, tables, decoded, final, joined, slope_dec, gains, mlp_copy),
+        [
+            rows_of(width), rows_of(width), rows_of(width), rows_of(hidden), whole((width, padded)),
+            whole((2, width)), whole((width, padded)),
+        ],
+        (grad_output, tables, decoded, final, joined, slope_dec, gains, mlp_copy, inputs),
         flops=mlp_flops,
         moved=24 * rows * width,
+        near=(0, 1, 2),
     )
 
     to_left, grad_own, to_right = call(
         scatter_kernel,
         (steps,),
         [shape((rows, width), BF16), shape((rows, width), F32), shape((rows, width), BF16)],
-        [whole((dec_edges.shape[1], grid_rows)), whole((grid_rows, width))],
+        [whole((dec_edges.shape[1], grid_rows)), whole((grid_rows, width)), whole((grid_rows, width))],
         [rows_of(width)] * 3,
-        (dec_edges.T, grad_join),
-        scratch=[pltpu.VMEM((grid_rows, width), BF16), pltpu.VMEM((grid_rows, width), BF16)],
+        (dec_edges.T, join_high, join_low),
+        near=(0, 1, 2),
         flops=12 * rows * grid_rows * width,
         moved=12 * rows * width,
     )
@@ -948,6 +980,7 @@
         ),
         flops=mlp_flops + 2 * rows * width * width,
         moved=24 * rows * width,
+        near=(1, 5),
     )
 
     keep_proc, send_proc = layer_weights(normed_proc, rounded_proc, before_proc, active_proc)
@@ -974,6 +1007,7 @@
             scratch=[pltpu.VMEM((block, rows), BF16), pltpu.VMEM((block, rows), BF16)],
             flops=60 * rows * rows * part,
             moved=12 * rows * rows,
+            near=(0, 1, 2, 3),
         )
         if sides:
             left = after(left, *sides[-1], *swapped_proc)
@@ -1005,6 +1039,7 @@
         ),
         flops=3 * product,
         moved=24 * rows * width,
+        near=(0, 1, 2),
     )
     keep_down, send_down = weights(
         down_weights_kernel,
@@ -1016,7 +1051,7 @@
         2,
     )
     first_total = add_bands(first_parts, (keep_down,))
-    sorted_down = sort_shares([keep_down], [send_down], places, late=(first_total,))
+    sorted_down = sort_shares([keep_down], [send_down], places, late=tuple(first_total))
     swapped_down = swap_items(sorted_down)
     before_enc, table_in, gain_enc, _ = call(
         encoder_back_kernel,
@@ -1026,9 +1061,9 @@
             shape((rows, width), BF16),
         ],
         [rows_of(width)] * 2
-        + [rows_of(hidden), gains_spec, weights_spec(0), lanes_of(padded), rows_of(2 * padded), rows_of(width)],
+        + [rows_of(hidden), gains_spec, weights_spec(0), rows_of(2 * padded)],
         [rows_of(hidden), table_spec, whole((1, width)), rows_of(width)],
-        (after(upstream, *sorted_down), pooled, slope_enc, gains, mlp_copy, inputs, pin, grad_join),
+        (after(upstream, *sorted_down), pooled, slope_enc, gains, mlp_copy, pin),
         flops=mlp_flops,
         moved=24 * rows * width,
     )
@@ -1037,8 +1072,8 @@
     keep_up, send_up = weights(
         up_weights_kernel,
         places,
-        (normed_enc, before_enc, table_in, table_out, gain_columns),
-        [full, columns_of, table_spec, table_spec, table_spec],
+        (normed_enc, before_enc, table_in, table_direct, table_out, gain_columns),
+        [full, columns_of, table_spec, table_spec, table_spec, table_spec],
         quarter + padded,
         4 * product,
         1,
@@ -1047,48 +1082,49 @@
     down_total = sum_bands(down_parts)
     sorted_up = sort_shares([keep_up], [send_up], places, exact=padded, late=(down_parts[0],))
     swapped_up = swap_items([sorted_up[0]] + [after(x, *swapped_down) for x in sorted_up[1:]])
-    first_all = all_items(after(first_total, *swapped_up))
+    first_all = all_items(*[after(x, *swapped_up) for x in first_total])
+    ready = [x for pair in first_all for x in pair]
     up_total = sum_bands(sum_items([swapped_up], places, exact=padded), exact=padded)
-    squares = sum(jnp.sum(jnp.square(x.astype(F32))) for x in (first_total, down_total, up_total))
-    down_all = all_items(down_total)
-    up_all = all_items(up_total)
-    scalars = after(jnp.stack([squares, loss_item])[None], *down_all)
-    scalars = all_items(after(sum_over(scalars, "lat"), *up_all))
+    squares = sum(jnp.sum(jnp.square(x.astype(F32))) for x in (*first_total, down_total, up_total))
+    scalars = sum_over(jnp.stack([squares, loss_item])[None], "lat")
+    place = [lax.broadcasted_iota(jnp.int32, up_total.shape, dim) for dim in range(2)]
+    carried = jnp.where(place[0] == 0, scalars[0, 0], scalars[0, 1])
+    up_total = jnp.where((place[1] == up_total.shape[1] - 1) & (place[0] < 2), carried, up_total)
+    last_all = all_items(after(down_total, *ready), after(up_total, *ready))
+    scalars = [x[:2, -1] for _, x in last_all]
     scalars = (scalars[0] + scalars[1]) + (scalars[2] + scalars[3])
-    loss_sum = scalars[0, 1]
-    grad_norm = jnp.sqrt(scalars[0, 0])
+    loss_sum = scalars[1]
+    grad_norm = jnp.sqrt(scalars[0])
     scale_factor = CLIP_LEVEL / jnp.maximum(grad_norm, CLIP_LEVEL)
 
     shard_rows = attn_master.shape[0]
     mlp_spec = pl.BlockSpec((mlp_master.shape[0], shard_rows, quarter), lambda j, k, s: (0, 0, k * 4 + (s[3] ^ j)))
     attn_part = pl.BlockSpec((shard_rows, width // 2), lambda j, k, s: (0, (s[3] ^ j) * 2 + k))
     kinds = [F32, F32, F32, F32, BF16]
-    shares = (*first_all, *down_all, *up_all)
+    shares = [x for pair in zip(*first_all) for x in pair] + [x for pair in zip(*last_all) for x in pair]
+    state = (mlp_master, mlp_first, mlp_second, mlp_ema, attn_master, attn_first, attn_second, attn_ema)
+    table_state = [jnp.swapaxes(x, 1, 2) for x in (tables_master, tables_first, tables_second, tables_ema)]
+    FAR.extend(table_state)
     updated = prefetched(
         adam_kernel,
         (4, 2),
-        [shape(mlp_master.shape, kind) for kind in kinds] + [shape(attn_master.shape, kind) for kind in kinds],
-        [smem] + [pl.BlockSpec(x.shape, lambda *_: (0, 0)) for x in shares] + [mlp_spec] * 4 + [attn_part] * 4,
-        [mlp_spec] * 5 + [attn_part] * 5,
+        [shape(x.shape, kind) for x in (mlp_master, attn_master, table_state[0], gains_master) for kind in kinds],
+        [smem]
+        + [pl.BlockSpec(x.shape, lambda *_: (0, 0)) for x in shares]
+        + [mlp_spec] * 4
+        + [attn_part] * 4
+        + [whole(table_state[0].shape)] * 4
+        + [whole(gains_master.shape)] * 4,
+        [mlp_spec] * 5 + [attn_part] * 5 + [whole(table_state[0].shape)] * 5 + [whole(gains_master.shape)] * 5,
         places,
         (
-            scale_factor[None], *shares, mlp_master, mlp_first, mlp_second, mlp_ema,
-            attn_master, attn_first, attn_second, attn_ema,
+            scale_factor[None], *shares, *state, *table_state,
+            gains_master, gains_first, gains_second, gains_ema,
         ),
         moved=34 * (mlp_master.size + attn_master.size),
     )
-    mlps, att = updated[:5], updated[5:]
-    small = jnp.stack([x[:, quarter:] for x in up_all])
-    tab_sum = jnp.stack(
-        [lax.dynamic_index_in_dim(small, item_index ^ q, 0, False)[:, :channels].T for q in range(2)]
-    )
-    gain_sum = lax.dynamic_index_in_dim(small, item_index ^ 2, 0, False)[:, :gain_rows].T
-    tab = adam_update(
-        scale_factor * tab_sum, tables_master, tables_first, tables_second, tables_ema, RATE_MATRIX, WEIGHT_DECAY
-    )
-    gns = adam_update(
-        scale_factor * gain_sum, gains_master, gains_first, gains_second, gains_ema, RATE_GAIN, 0.0
-    )
+    mlps, att, gns = updated[:5], updated[5:10], updated[15:]
+    tab = [jnp.swapaxes(x, 1, 2) for x in updated[10:15]]
     return (loss_sum, grad_norm, *tab, *att, *mlps, *gns)
 
 

time: 468 us -> 458 us (0.979)
  waiting for transfers between devices: 55.3 us -> 39.7 us
  Pallas kernels: 283 us -> 275 us
  starting transfers between devices: 103 us -> 111 us
  local copies, waits for them, and re-layouts: 3.76 us -> 8.97 us
    ppermute x43, waiting for transfers between devices: 52.2 us -> 38.8 us  [exchange(): return lax.ppermute(value, axis, [(i, i ^ distance) for i in range(size)])]
    pallas_call x18, Pallas kernels: 241 us -> 230 us  [call(): pl.pallas_call(kernel, grid=grid, out_shape=kinds[0] if single else kinds...]
    ppermute x43, starting transfers between devices: 71.3 us -> 76.1 us  [exchange(): return lax.ppermute(value, axis, [(i, i ^ distance) for i in range(size)])]
    unnamed x72 -> x79, local copies, waits for them, and re-layouts: 2.74 us -> 7.45 us
  transfers between devices with their start and end apart: 55 -> 55, of which waited for: 19 -> 22; matrix products, arithmetic and copies ran while one was open for 2% -> 2% of each run, Pallas kernels for 36% -> 35%
where the time goes in v3:
time: 458 us; the launch traced here: 452 us
  Pallas kernels  275 us (60%)
  starting transfers between devices  111 us (24%)
  waiting for transfers between devices  39.7 us (9%)
  other arithmetic  9.06 us (2%)
  local copies, waits for them, and re-layouts  8.97 us (2%)
  between operations  7.59 us (2%)
    pallas_call x18, Pallas kernels, call(): pl.pallas_call(kernel, grid=grid, out_shape=kinds[0] if single else kinds...  230 us
    ppermute x43, starting transfers between devices, exchange(): return lax.ppermute(value, axis, [(i, i ^ distance) for i in range(size)])  76.1 us
    pallas_call x8, Pallas kernels, prefetched(): pl.pallas_call(kernel, grid_spec=pltpu.PrefetchScalarGridSpec(num_scalar_...  45.2 us
    ppermute x43, waiting for transfers between devices, exchange(): return lax.ppermute(value, axis, [(i, i ^ distance) for i in range(size)])  38.8 us
    ppermute x6, starting transfers between devices, from_sides(): lax.ppermute(to_right, 'lat', up)  27.4 us
  transfers between devices with their start and end apart: 55, of which 22 were waited for; matrix products, arithmetic and copies ran while one was open for 2% of the time, Pallas kernels for 35%

profile of v3, /device:TPU:0, one launch (start us, length us, event | category | flops | bytes accessed | tf_op | source)
XLA Modules:
  0.0 452.4 jit_solution(9649449757551522820)
XLA Ops:
  4.9 18.8 %shard_map.435 = (bf16[1024,256]{1,0:T(8,128)(2,1)S(1)}, f32[1024,512]{1,0:T(8,128)}, f32[1024,512]{1,0:T(8,128)}, bf16[1024,512]{1,0:T(8,128)(2,1)}, f32[1024,2...) custom-call(s32[4,1024]{1,0:T(4,128)S(1)} %bitcast.48, ...), custom_call_target="tpu_custom_call" | custom-call | flops 177167400960 | bytes 471859200 | tf_op jit(solution)/shard_map/pallas_call | solution.py:57
  29.3 10.4 %shard_map.436.bias = f32[3,1024,1024]{2,1,0:T(8,128)} custom-call(s32[5]{0:T(128)S(1)} %stack.28.places, s32[16]{0:T(128)S(1)} %reduce.ends, s32[16,1024]{1,0:T(8,128)S(1)} %bitcast.47), custom_call_target="tpu_custom_call" | custom-call | flops 60000002048 | bytes 377487360 | tf_op jit(solution)/shard_map/pallas_call | solution.py:57
  41.0 7.7 %collective-permute-start.2 = (bf16[1024,512]{1,0:T(8,128)(2,1)}, bf16[1024,512]{1,0:T(8,128)(2,1)}, u32[]{:S(2)}, u32[]{:S(2)}) collective-permute-start(bf16[1024,512]{1,0:T(8,128)(2,1)} %get-tuple-element.168.k1.v1), channel_id=1, source_target_pairs={{0,1},{1,2},{2,3},{3,4},{4,5},{5,6},{6,7},{8,9},{9,10},{10,11},{11... | collective-permute-start | bytes 3145736 | tf_op jit(solution)/shard_map/ppermute | solution.py:731
  48.7 14.6 %shard_map.437 = (f32[256,1024]{1,0:T(8,128)}, f32[2,8,1024]{2,1,0:T(8,128)S(1)}) custom-call(bf16[512,1024]{1,0:T(8,128)(2,1)} %get-tuple-element.164.q_ref, bf16[1024,512]{1,0:T(8,128)(2,1)S(1)} %collective-permute-done.k0.v0, bf16[1024,512]{1,0:T(8,128)(2,1)} %get-tuple-element.165.k1.v1, bf16[1024,512]{1,0:T(8,128)(2,1)S(1)} %collective-permute-done.1.k2.v2, ...), custom_call_target="tpu_custom_call" | custom-call | flops 193273528320 | bytes 377487360 | tf_op jit(solution)/shard_map/pallas_call | solution.py:57
  63.3 15.3 %shard_map.438 = (f32[256,1024]{1,0:T(8,128)}, f32[2,8,1024]{2,1,0:T(8,128)S(1)}) custom-call(bf16[512,1024]{1,0:T(8,128)(2,1)} %get-tuple-element.164.q_ref, bf16[1024,512]{1,0:T(8,128)(2,1)} %collective-permute-done.2.k0.v0, bf16[1024,512]{1,0:T(8,128)(2,1)} %get-tuple-element.168.k1.v1, bf16[1024,512]{1,0:T(8,128)(2,1)} %collective-permute-done.3.k2.v2, ...), custom_call_target="tpu_custom_call" | custom-call | flops 193273528320 | bytes 377487360 | tf_op jit(solution)/shard_map/pallas_call | solution.py:57
  78.7 14.4 %shard_map.439 = (bf16[512,1024]{1,0:T(8,128)(2,1)}, f32[1024,512]{1,0:T(8,128)}, bf16[1024,512]{1,0:T(8,128)(2,1)}, f32[1024,2048]{1,0:T(8,128)}, bf16[1024,204...) custom-call(f32[256,1024]{1,0:T(8,128)} %get-tuple-element.166.o0, f32[256,1024]{1,0:T(8,128)} %get-tuple-element.169.o1, ...), custom_call_target="tpu_custom_call" | custom-call | flops 144955146240 | bytes 377487360 | tf_op jit(solution)/shard_map/pallas_call | solution.py:57
  94.4 5.4 %collective-permute-start.4 = (bf16[1024,512]{1,0:T(8,128)(2,1)S(1)}, bf16[1024,512]{1,0:T(8,128)(2,1)}, u32[]{:S(2)}, u32[]{:S(2)}) collective-permute-start(bf16[1024,512]{1,0:T(8,128)(2,1)S(1)} %get-tuple-element.171.s1), channel_id=1, source_target_pairs={{0,1},{1,2},{2,3},{3,4},{4,5},{5,6},{6,7},{8,9},{9,10},{10,11},{11... | collective-permute-start | bytes 3145736 | tf_op jit(solution)/shard_map/ppermute | solution.py:731
  100.8 20.2 %shard_map.440 = (f32[1024,512]{1,0:T(8,128)}, bf16[1024,512]{1,0:T(8,128)(2,1)}, f32[1024,2048]{1,0:T(8,128)}, bf16[1024,2048]{1,0:T(8,128)(2,1)}, f32[1024,512...) custom-call(s32[3,1024]{1,0:T(4,128)S(1)} %bitcast.49, bf16[1024,512]{1,0:T(8,128)(2,1)} %collective-permute-done.4.s0, ...), custom_call_target="tpu_custom_call" | custom-call | flops 225485783040 | bytes 377487360 | tf_op jit(solution)/shard_map/pallas_call | solution.py:57
  121.4 11.1 %collective-permute-start.6 = (f32[83,64]{0,1:T(8,128)S(1)}, f32[83,64]{0,1:T(8,128)S(1)}, u32[]{:S(2)}, u32[]{:S(2)}) collective-permute-start(f32[83,64]{0,1:T(8,128)S(1)} %fusion.1), channel_id=1, source_target_pairs={{0,1},{1,0},{2,3},{3,2},{4,5},{5,4},{6,7},{7,6},{8,9},{9,8},{10,11... | collective-permute-start | bytes 63752 | tf_op jit(solution)/shard_map/ppermute | solution.py:492
  143.6 15.3 %shard_map.441 = (bf16[1024,512]{1,0:T(8,128)(2,1)S(1)}, bf16[1024,512]{1,0:T(8,128)(2,1)S(1)}, bf16[1024,512]{1,0:T(8,128)(2,1)S(1)}, bf16[1024,2048]{1,0:T(8,1...) custom-call(bf16[128,1024]{1,0:T(8,128)(2,1)S(1)} %pad.17.grad_output, ...), custom_call_target="tpu_custom_call" | custom-call | flops 128849018880 | bytes 377487360 | tf_op jit(solution)/shard_map/pallas_call | solution.py:57
  158.9 7.3 %shard_map.442 = (bf16[1024,512]{1,0:T(8,128)(2,1)S(1)}, f32[1024,512]{1,0:T(8,128)S(1)}, bf16[1024,512]{1,0:T(8,128)(2,1)S(1)}) custom-call(s32[3,1024]{1,0:T(4,128)S(1)} %bitcast.50, bf16[1024,512]{1,0:T(8,128)(2,1)S(1)} %get-tuple-element.179.high, bf16[1024,512]{1,0:T(8,128)(2,1)S(1)} %get-tuple-element.180.low), custom_call_target="tpu_custom_call" | custom-call | flops 193273528320 | bytes 188743680 | tf_op jit(solution)/shard_map/pallas_call | solution.py:57
  170.8 10.1 %shard_map.443 = (f32[4,4,64,1024]{3,2,1,0:T(8,128)S(1)}, f32[4,4,64,1024]{3,2,1,0:T(8,128)}) custom-call(s32[5]{0:T(128)S(1)} %copy-done.17, bf16[1024,512]{1,0:T(8,128)(2,1)} %get-tuple-element.172.normed, bf16[1024,512]{1,0:T(8,128)(2,1)S(1)} %get-tuple-element.183.rounded, bf16[1024,2048]{1,0:T(8,128)(2,1)} %get-tuple-element.184.before, ...), custom_call_target="tpu_custom_call" | custom-call | flops 128849018880 | bytes 503316480 | tf_op jit(solution)/shard_map/pallas_call | solution.py:57
  182.6 13.1 %shard_map.445 = (f32[1024,512]{1,0:T(8,128)}, bf16[1024,512]{1,0:T(8,128)(2,1)S(1)}, bf16[1024,2048]{1,0:T(8,128)(2,1)}, f32[1,512]{1,0:T(1,128)S(1)}, bf16[102...) custom-call(bf16[1024,512]{1,0:T(8,128)(2,1)S(1)} %collective-permute-done.13.g0, ...), custom_call_target="tpu_custom_call" | custom-call | flops 144955146240 | bytes 377487360 | tf_op jit(solution)/shard_map/pallas_call | solution.py:57
  195.7 10.1 %shard_map.446 = (f32[4,4,64,1024]{3,2,1,0:T(8,128)S(1)}, f32[4,4,64,1024]{3,2,1,0:T(8,128)}) custom-call(s32[5]{0:T(128)S(1)} %copy-done.18, bf16[1024,512]{1,0:T(8,128)(2,1)} %get-tuple-element.192.normed, bf16[1024,512]{1,0:T(8,128)(2,1)S(1)} %get-tuple-element.197.rounded, bf16[1024,2048]{1,0:T(8,128)(2,1)} %get-tuple-element.198.before, ...), custom_call_target="tpu_custom_call" | custom-call | flops 128849018880 | bytes 503316480 | tf_op jit(solution)/shard_map/pallas_call | solution.py:57
  207.2 4.7 %shard_map.444 = (f32[4,64,1024]{2,1,0:T(8,128)S(1)}, bf16[4,64,1024]{2,1,0:T(8,128)(2,1)}, bf16[4,64,1024]{2,1,0:T(8,128)(2,1)}, bf16[4,64,1024]{2,1,0:T(8,128)(2,1)}) custom-call(s32[5]{0:T(128)S(1)} %copy-done.18, f32[4,4,64,1024]{3,2,1,0:T(8,128)S(1)} %get-tuple-element.186.refs_0_, f32[4,4,64,1024]{3,2,1,0:T(8,128)} %collective-permute-done.9.refs_1_), custom_call_target="tpu_custom_call" | custom-call | flops 440401920 | bytes 440401920 | tf_op jit(solution)/shard_map/pallas_call | solution.py:496
  215.5 21.6 %shard_map.447 = (f32[256,1024]{1,0:T(8,128)S(1)}, bf16[2,256,1024]{2,1,0:T(8,128)(2,1)}, f32[2,256,1024]{2,1,0:T(8,128)S(1)}, bf16[2,256,1024]{2,1,0:T(8,128)(2,1)}) custom-call(bf16[512,1024]{1,0:T(8,128)(2,1)} %get-tuple-element.164.q_ref, bf16[512,1024]{1,0:T(8,128)(2,1)S(1)} %get-tuple-element.213.do_ref, f32[2,8,1024]{2,1,0:T(8,128)S(1)} %get-tuple-element.204.lse_ref, ...), custom_call_target="tpu_custom_call" | custom-call | flops 483183820800 | bytes 377487360 | tf_op jit(solution)/shard_map/pallas_call | solution.py:57
  240.6 4.7 %shard_map.448 = (f32[4,64,1024]{2,1,0:T(8,128)S(1)}, bf16[4,64,1024]{2,1,0:T(8,128)(2,1)}, bf16[4,64,1024]{2,1,0:T(8,128)(2,1)}, bf16[4,64,1024]{2,1,0:T(8,128)(2,1)}) custom-call(s32[5]{0:T(128)S(1)} %copy-done.18, f32[4,4,64,1024]{3,2,1,0:T(8,128)S(1)} %get-tuple-element.207.refs_0_, f32[4,4,64,1024]{3,2,1,0:T(8,128)} %collective-permute-done.15.refs_1_), custom_call_target="tpu_custom_call" | custom-call | flops 440401920 | bytes 440401920 | tf_op jit(solution)/shard_map/pallas_call | solution.py:496
  248.8 21.7 %shard_map.450 = (f32[256,1024]{1,0:T(8,128)S(1)}, bf16[2,256,1024]{2,1,0:T(8,128)(2,1)}, f32[2,256,1024]{2,1,0:T(8,128)S(1)}, bf16[2,256,1024]{2,1,0:T(8,128)(2,1)}) custom-call(bf16[512,1024]{1,0:T(8,128)(2,1)} %get-tuple-element.164.q_ref, bf16[512,1024]{1,0:T(8,128)(2,1)S(1)} %get-tuple-element.213.do_ref, f32[2,8,1024]{2,1,0:T(8,128)S(1)} %get-tuple-element.214.lse_ref, ...), custom_call_target="tpu_custom_call" | custom-call | flops 483183820800 | bytes 377487360 | tf_op jit(solution)/shard_map/pallas_call | solution.py:57
  272.3 5.7 %collective-permute-start.21 = (bf16[2,256,1024]{2,1,0:T(8,128)(2,1)}, bf16[2,256,1024]{2,1,0:T(8,128)(2,1)}, u32[]{:S(2)}, u32[]{:S(2)}) collective-permute-start(bf16[2,256,1024]{2,1,0:T(8,128)(2,1)} %get-tuple-element.220), channel_id=1, source_target_pairs={{0,1},{1,2},{2,3},{3,4},{4,5},{5,6},{6,7},{8,9},{9,10},{10,11},{11... | collective-permute-start | bytes 3145736 | tf_op jit(solution)/shard_map/ppermute | solution.py:731
  278.0 4.5 shard_map.449
  282.5 14.1 %collective-permute-start.25 = (bf16[64,2048]{1,0:T(8,128)(2,1)}, bf16[64,2048]{1,0:T(8,128)(2,1)}, u32[]{:S(2)}, u32[]{:S(2)}) collective-permute-start(bf16[64,2048]{1,0:T(8,128)(2,1)} %get-tuple-element.239), channel_id=1, source_target_pairs={{0,6},{1,7},{2,4},{3,5},{4,2},{5,3},{6,0},{7,1},{8,14},{9,15},{10,... | collective-permute-start | bytes 786440 | tf_op jit(solution)/shard_map/ppermute | solution.py:492
  297.2 6.8 %shard_map.451 = (f32[1024,512]{1,0:T(8,128)S(1)}, bf16[1024,512]{1,0:T(8,128)(2,1)S(1)}, bf16[1536,1024]{1,0:T(8,128)(2,1)S(1)}, f32[1,512]{1,0:T(1,128)S(1)}) custom-call(f32[256,1024]{1,0:T(8,128)S(1)} %get-tuple-element.206.dq0, f32[256,1024]{1,0:T(8,128)S(1)} %get-tuple-element.215.dq1, bf16[2,256,1024]{2,1,0:T(8,128)(2,1)} %collective-permute-done.19.left0, ...), custom_call_target="tpu_custom_call" | custom-call | flops 48318382080 | bytes 377487360 | tf_op jit(solution)/shard_map/pallas_call | solution.py:57
  303.9 10.1 %shard_map.452 = (f32[4,4,64,1024]{3,2,1,0:T(8,128)S(1)}, f32[4,4,64,1024]{3,2,1,0:T(8,128)}) custom-call(s32[5]{0:T(128)S(1)} %copy-done.18, bf16[1024,512]{1,0:T(8,128)(2,1)S(1)} %get-tuple-element.226.rounded, bf16[1024,2048]{1,0:T(8,128)(2,1)} %get-tuple-element.227.active, bf16[1024,512]{1,0:T(8,128)(2,1)} %get-tuple-element.228.normed_attn, ...), custom_call_target="tpu_custom_call" | custom-call | flops 128849018880 | bytes 503316480 | tf_op jit(solution)/shard_map/pallas_call | solution.py:57
  314.1 4.7 %collective-permute-done.24.refs_1_ = bf16[64,2048]{1,0:T(8,128)(2,1)} collective-permute-done((bf16[64,2048]{1,0:T(8,128)(2,1)}, bf16[64,2048]{1,0:T(8,128)(2,1)}, u32[]{:S(2)}, u32[]{:S(2)}) %collective-permute-start.24) | collective-permute-done | bytes 262176 | tf_op jit(solution)/shard_map/ppermute | solution.py:492
  321.6 4.7 %shard_map.454 = (f32[4,64,1024]{2,1,0:T(8,128)S(1)}, bf16[4,64,1024]{2,1,0:T(8,128)(2,1)}, bf16[4,64,1024]{2,1,0:T(8,128)(2,1)}, bf16[4,64,1024]{2,1,0:T(8,128)(2,1)}) custom-call(s32[5]{0:T(128)S(1)} %copy-done.18, f32[4,4,64,1024]{3,2,1,0:T(8,128)S(1)} %get-tuple-element.242.refs_0_, f32[4,4,64,1024]{3,2,1,0:T(8,128)} %collective-permute-done.26.refs_1_), custom_call_target="tpu_custom_call" | custom-call | flops 440401920 | bytes 440401920 | tf_op jit(solution)/shard_map/pallas_call | solution.py:496
  329.8 11.9 %shard_map.456 = (bf16[1024,2048]{1,0:T(8,128)(2,1)}, f32[512,128]{1,0:T(8,128)S(1)}, f32[1,512]{1,0:T(1,128)S(1)}, bf16[1024,512]{1,0:T(8,128)(2,1)}) custom-call(f32[1024,512]{1,0:T(8,128)S(1)} %get-tuple-element.255.upstream, f32[1024,512]{1,0:T(8,128)} %get-tuple-element.256.pooled, f32[1024,2048]{1,0:T(8,128)} %get-tuple-element.257.slope, ...), custom_call_target="tpu_custom_call" | custom-call | flops 128849018880 | bytes 377487360 | tf_op jit(solution)/shard_map/pallas_call | solution.py:57
  341.9 6.8 %shard_map.457 = (f32[4,4,64,640]{3,2,1,0:T(8,128)S(1)}, f32[4,4,64,640]{3,2,1,0:T(8,128)}) custom-call(s32[5]{0:T(128)S(1)} %copy-done.19, bf16[1024,512]{1,0:T(8,128)(2,1)} %get-tuple-element.253.normed, bf16[1024,2048]{1,0:T(8,128)(2,1)} %get-tuple-element.259.before, f32[512,128]{1,0:T(8,128)S(1)} %get-tuple-element.260.table_in, ...), custom_call_target="tpu_custom_call" | custom-call | flops 64424509440 | bytes 314572800 | tf_op jit(solution)/shard_map/pallas_call | solution.py:57
  352.8 3.7 shard_map.455
  356.5 3.9 shard_map.458
  373.5 3.8 collective-permute-start.32
  417.5 3.4 collective-permute-done.50.refs_14_
  434.7 16.3 %shard_map.460 = (f32[3,64,4096]{2,1,0:T(8,128)}, f32[3,64,4096]{2,1,0:T(8,128)}, f32[3,64,4096]{2,1,0:T(8,128)}, f32[3,64,4096]{2,1,0:T(8,128)}, bf16[3,64,4096...) custom-call(s32[5]{0:T(128)S(1)} %copy-done.19, ...), custom_call_target="tpu_custom_call" | custom-call | flops 935854080 | bytes 935854080 | tf_op jit(solution)/shard_map/pallas_call | solution.py:496
  (218 shorter events, 117.9 us)
Async XLA Ops:
  24.6 15.1 %collective-permute-start.1 = (bf16[1024,512]{1,0:T(8,128)(2,1)}, bf16[1024,512]{1,0:T(8,128)(2,1)S(1)}, u32[]{:S(2)}, u32[]{:S(2)}) collective-permute-start(bf16[1024,512]{1,0:T(8,128)(2,1)} %get-tuple-element.165.k1.v1), channel_id=1, source_target_pairs={{1,0},{2,1},{3,2},{4,3},{5,4},{6,5},{7,6},{9,8},{10,9},{11,10},{12... | collective-permute-start | bytes 3145736 | tf_op jit(solution)/shard_map/ppermute | solution.py:731
  25.8 13.8 %collective-permute-start = (bf16[1024,512]{1,0:T(8,128)(2,1)}, bf16[1024,512]{1,0:T(8,128)(2,1)S(1)}, u32[]{:S(2)}, u32[]{:S(2)}) collective-permute-start(bf16[1024,512]{1,0:T(8,128)(2,1)} %get-tuple-element.165.k1.v1), channel_id=1, source_target_pairs={{0,1},{1,2},{2,3},{3,4},{4,5},{5,6},{6,7},{8,9},{9,10},{10,11},{11... | collective-permute-start | bytes 3145736 | tf_op jit(solution)/shard_map/ppermute | solution.py:731
  39.7 23.6 %collective-permute-start.3 = (bf16[1024,512]{1,0:T(8,128)(2,1)}, bf16[1024,512]{1,0:T(8,128)(2,1)}, u32[]{:S(2)}, u32[]{:S(2)}) collective-permute-start(bf16[1024,512]{1,0:T(8,128)(2,1)} %get-tuple-element.168.k1.v1), channel_id=1, source_target_pairs={{1,0},{2,1},{3,2},{4,3},{5,4},{6,5},{7,6},{9,8},{10,9},{11,10},{12... | collective-permute-start | bytes 3145736 | tf_op jit(solution)/shard_map/ppermute | solution.py:731
  41.0 22.3 %collective-permute-start.2 = (bf16[1024,512]{1,0:T(8,128)(2,1)}, bf16[1024,512]{1,0:T(8,128)(2,1)}, u32[]{:S(2)}, u32[]{:S(2)}) collective-permute-start(bf16[1024,512]{1,0:T(8,128)(2,1)} %get-tuple-element.168.k1.v1), channel_id=1, source_target_pairs={{0,1},{1,2},{2,3},{3,4},{4,5},{5,6},{6,7},{8,9},{9,10},{10,11},{11... | collective-permute-start | bytes 3145736 | tf_op jit(solution)/shard_map/ppermute | solution.py:731
  166.2 16.3 %collective-permute-start.14 = (bf16[1024,512]{1,0:T(8,128)(2,1)S(1)}, bf16[1024,512]{1,0:T(8,128)(2,1)S(1)}, u32[]{:S(2)}, u32[]{:S(2)}) collective-permute-start(bf16[1024,512]{1,0:T(8,128)(2,1)S(1)} %get-tuple-element.181), channel_id=1, source_target_pairs={{1,0},{2,1},{3,2},{4,3},{5,4},{6,5},{7,6},{9,8},{10,9},{11,10},{12... | collective-permute-start | bytes 3145736 | tf_op jit(solution)/shard_map/ppermute | solution.py:731
  167.5 15.0 %collective-permute-start.13 = (bf16[1024,512]{1,0:T(8,128)(2,1)S(1)}, bf16[1024,512]{1,0:T(8,128)(2,1)S(1)}, u32[]{:S(2)}, u32[]{:S(2)}) collective-permute-start(bf16[1024,512]{1,0:T(8,128)(2,1)S(1)} %get-tuple-element.182), channel_id=1, source_target_pairs={{0,1},{1,2},{2,3},{3,4},{4,5},{5,6},{6,7},{8,9},{9,10},{10,11},{11... | collective-permute-start | bytes 3145736 | tf_op jit(solution)/shard_map/ppermute | solution.py:731
  180.9 26.3 %collective-permute-start.9 = (f32[4,4,64,1024]{3,2,1,0:T(8,128)}, f32[4,4,64,1024]{3,2,1,0:T(8,128)}, u32[]{:S(2)}, u32[]{:S(2)}) collective-permute-start(f32[4,4,64,1024]{3,2,1,0:T(8,128)} %get-tuple-element.187), channel_id=1, source_target_pairs={{0,1},{1,0},{2,3},{3,2},{4,5},{5,4},{6,7},{7,6},{8,9},{9,8},{10,11... | collective-permute-start | bytes 12582920 | tf_op jit(solution)/shard_map/ppermute | solution.py:492
  205.8 33.5 %collective-permute-start.15 = (f32[4,4,64,1024]{3,2,1,0:T(8,128)}, f32[4,4,64,1024]{3,2,1,0:T(8,128)}, u32[]{:S(2)}, u32[]{:S(2)}) collective-permute-start(f32[4,4,64,1024]{3,2,1,0:T(8,128)} %get-tuple-element.202), channel_id=1, source_target_pairs={{0,1},{1,0},{2,3},{3,2},{4,5},{5,4},{6,7},{7,6},{8,9},{9,8},{10,11... | collective-permute-start | bytes 12582920 | tf_op jit(solution)/shard_map/ppermute | solution.py:492
  212.0 33.4 %collective-permute-start.10 = (bf16[4,64,1024]{2,1,0:T(8,128)(2,1)}, bf16[4,64,1024]{2,1,0:T(8,128)(2,1)}, u32[]{:S(2)}, u32[]{:S(2)}) collective-permute-start(bf16[4,64,1024]{2,1,0:T(8,128)(2,1)} %get-tuple-element.189), channel_id=1, source_target_pairs={{0,8},{8,0},{16,24},{24,16},{1,9},{9,1},{17,25},{25,17},{2,10},{10... | collective-permute-start | bytes 1572872 | tf_op jit(solution)/shard_map/ppermute | solution.py:492
  213.5 33.4 %collective-permute-start.11 = (bf16[4,64,1024]{2,1,0:T(8,128)(2,1)}, bf16[4,64,1024]{2,1,0:T(8,128)(2,1)}, u32[]{:S(2)}, u32[]{:S(2)}) collective-permute-start(bf16[4,64,1024]{2,1,0:T(8,128)(2,1)} %get-tuple-element.190), channel_id=1, source_target_pairs={{0,16},{8,24},{16,0},{24,8},{1,17},{9,25},{17,1},{25,9},{2,18},{10... | collective-permute-start | bytes 1572872 | tf_op jit(solution)/shard_map/ppermute | solution.py:492
  215.0 33.4 %collective-permute-start.12 = (bf16[4,64,1024]{2,1,0:T(8,128)(2,1)}, bf16[4,64,1024]{2,1,0:T(8,128)(2,1)}, u32[]{:S(2)}, u32[]{:S(2)}) collective-permute-start(bf16[4,64,1024]{2,1,0:T(8,128)(2,1)} %get-tuple-element.191), channel_id=1, source_target_pairs={{0,24},{8,16},{16,8},{24,0},{1,25},{9,17},{17,9},{25,1},{2,26},{10... | collective-permute-start | bytes 1572872 | tf_op jit(solution)/shard_map/ppermute | solution.py:492
  237.1 33.4 %collective-permute-start.19 = (bf16[2,256,1024]{2,1,0:T(8,128)(2,1)}, bf16[2,256,1024]{2,1,0:T(8,128)(2,1)}, u32[]{:S(2)}, u32[]{:S(2)}) collective-permute-start(bf16[2,256,1024]{2,1,0:T(8,128)(2,1)} %get-tuple-element.216), channel_id=1, source_target_pairs={{0,1},{1,2},{2,3},{3,4},{4,5},{5,6},{6,7},{8,9},{9,10},{10,11},{11... | collective-permute-start | bytes 3145736 | tf_op jit(solution)/shard_map/ppermute | solution.py:731
  239.3 31.2 %collective-permute-start.20 = (bf16[2,256,1024]{2,1,0:T(8,128)(2,1)}, bf16[2,256,1024]{2,1,0:T(8,128)(2,1)}, u32[]{:S(2)}, u32[]{:S(2)}) collective-permute-start(bf16[2,256,1024]{2,1,0:T(8,128)(2,1)} %get-tuple-element.219), channel_id=1, source_target_pairs={{1,0},{2,1},{3,2},{4,3},{5,4},{6,5},{7,6},{9,8},{10,9},{11,10},{12... | collective-permute-start | bytes 3145736 | tf_op jit(solution)/shard_map/ppermute | solution.py:731
  245.3 25.2 %collective-permute-start.16 = (bf16[4,64,1024]{2,1,0:T(8,128)(2,1)}, bf16[4,64,1024]{2,1,0:T(8,128)(2,1)}, u32[]{:S(2)}, u32[]{:S(2)}) collective-permute-start(bf16[4,64,1024]{2,1,0:T(8,128)(2,1)} %get-tuple-element.209), channel_id=1, source_target_pairs={{0,8},{8,0},{16,24},{24,16},{1,9},{9,1},{17,25},{25,17},{2,10},{10... | collective-permute-start | bytes 1572872 | tf_op jit(solution)/shard_map/ppermute | solution.py:492
  246.8 23.7 %collective-permute-start.17 = (bf16[4,64,1024]{2,1,0:T(8,128)(2,1)}, bf16[4,64,1024]{2,1,0:T(8,128)(2,1)}, u32[]{:S(2)}, u32[]{:S(2)}) collective-permute-start(bf16[4,64,1024]{2,1,0:T(8,128)(2,1)} %get-tuple-element.210), channel_id=1, source_target_pairs={{0,16},{8,24},{16,0},{24,8},{1,17},{9,25},{17,1},{25,9},{2,18},{10... | collective-permute-start | bytes 1572872 | tf_op jit(solution)/shard_map/ppermute | solution.py:492
  248.4 22.6 %collective-permute-start.18 = (bf16[4,64,1024]{2,1,0:T(8,128)(2,1)}, bf16[4,64,1024]{2,1,0:T(8,128)(2,1)}, u32[]{:S(2)}, u32[]{:S(2)}) collective-permute-start(bf16[4,64,1024]{2,1,0:T(8,128)(2,1)} %get-tuple-element.211), channel_id=1, source_target_pairs={{0,24},{8,16},{16,8},{24,0},{1,25},{9,17},{17,9},{25,1},{2,26},{10... | collective-permute-start | bytes 1572872 | tf_op jit(solution)/shard_map/ppermute | solution.py:492
  282.5 31.6 %collective-permute-start.25 = (bf16[64,2048]{1,0:T(8,128)(2,1)}, bf16[64,2048]{1,0:T(8,128)(2,1)}, u32[]{:S(2)}, u32[]{:S(2)}) collective-permute-start(bf16[64,2048]{1,0:T(8,128)(2,1)} %get-tuple-element.239), channel_id=1, source_target_pairs={{0,6},{1,7},{2,4},{3,5},{4,2},{5,3},{6,0},{7,1},{8,14},{9,15},{10,... | collective-permute-start | bytes 786440 | tf_op jit(solution)/shard_map/ppermute | solution.py:492
  296.6 22.2 %collective-permute-start.24 = (bf16[64,2048]{1,0:T(8,128)(2,1)}, bf16[64,2048]{1,0:T(8,128)(2,1)}, u32[]{:S(2)}, u32[]{:S(2)}) collective-permute-start(bf16[64,2048]{1,0:T(8,128)(2,1)} %get-tuple-element.237), channel_id=1, source_target_pairs={{0,4},{1,5},{2,6},{3,7},{4,0},{5,1},{6,2},{7,3},{8,12},{9,13},{10,... | collective-permute-start | bytes 786440 | tf_op jit(solution)/shard_map/ppermute | solution.py:492
  296.6 22.2 %collective-permute-start.23 = (bf16[64,2048]{1,0:T(8,128)(2,1)}, bf16[64,2048]{1,0:T(8,128)(2,1)}, u32[]{:S(2)}, u32[]{:S(2)}) collective-permute-start(bf16[64,2048]{1,0:T(8,128)(2,1)} %get-tuple-element.235), channel_id=1, source_target_pairs={{0,2},{1,3},{2,0},{3,1},{4,6},{5,7},{6,4},{7,5},{8,10},{9,11},{10,... | collective-permute-start | bytes 786440 | tf_op jit(solution)/shard_map/ppermute | solution.py:492
  326.3 22.4 %collective-permute-start.27 = (bf16[4,64,1024]{2,1,0:T(8,128)(2,1)}, bf16[4,64,1024]{2,1,0:T(8,128)(2,1)}, u32[]{:S(2)}, u32[]{:S(2)}) collective-permute-start(bf16[4,64,1024]{2,1,0:T(8,128)(2,1)} %get-tuple-element.246), channel_id=1, source_target_pairs={{0,8},{8,0},{16,24},{24,16},{1,9},{9,1},{17,25},{25,17},{2,10},{10... | collective-permute-start | bytes 1572872 | tf_op jit(solution)/shard_map/ppermute | solution.py:492
  327.5 23.6 %collective-permute-start.28 = (bf16[4,64,1024]{2,1,0:T(8,128)(2,1)}, bf16[4,64,1024]{2,1,0:T(8,128)(2,1)}, u32[]{:S(2)}, u32[]{:S(2)}) collective-permute-start(bf16[4,64,1024]{2,1,0:T(8,128)(2,1)} %get-tuple-element.247), channel_id=1, source_target_pairs={{0,16},{8,24},{16,0},{24,8},{1,17},{9,25},{17,1},{25,9},{2,18},{10... | collective-permute-start | bytes 1572872 | tf_op jit(solution)/shard_map/ppermute | solution.py:492
  328.4 24.4 %collective-permute-start.29 = (bf16[4,64,1024]{2,1,0:T(8,128)(2,1)}, bf16[4,64,1024]{2,1,0:T(8,128)(2,1)}, u32[]{:S(2)}, u32[]{:S(2)}) collective-permute-start(bf16[4,64,1024]{2,1,0:T(8,128)(2,1)} %get-tuple-element.248), channel_id=1, source_target_pairs={{0,24},{8,16},{16,8},{24,0},{1,25},{9,17},{17,9},{25,1},{2,26},{10... | collective-permute-start | bytes 1572872 | tf_op jit(solution)/shard_map/ppermute | solution.py:492
  360.4 13.2 %collective-permute-start.36 = (bf16[4,64,768]{2,1,0:T(8,128)(2,1)}, bf16[4,64,768]{2,1,0:T(8,128)(2,1)S(1)}, u32[]{:S(2)}, u32[]{:S(2)}) collective-permute-start(bf16[4,64,768]{2,1,0:T(8,128)(2,1)} %get-tuple-element.277), channel_id=1, source_target_pairs={{0,24},{8,16},{16,8},{24,0},{1,25},{9,17},{17,9},{25,1},{2,26},{10... | collective-permute-start | bytes 1179656 | tf_op jit(solution)/shard_map/ppermute | solution.py:492
  362.1 17.9 %collective-permute-start.35 = (bf16[4,64,768]{2,1,0:T(8,128)(2,1)S(1)}, bf16[4,64,768]{2,1,0:T(8,128)(2,1)S(1)}, u32[]{:S(2)}, u32[]{:S(2)}) collective-permute-start(bf16[4,64,768]{2,1,0:T(8,128)(2,1)S(1)} %get-tuple-element.275), channel_id=1, source_target_pairs={{0,16},{8,24},{16,0},{24,8},{1,17},{9,25},{17,1},{25,9},{2,18},{10... | collective-permute-start | bytes 1179656 | tf_op jit(solution)/shard_map/ppermute | solution.py:492
  362.6 17.4 %collective-permute-start.34 = (bf16[4,64,768]{2,1,0:T(8,128)(2,1)S(1)}, bf16[4,64,768]{2,1,0:T(8,128)(2,1)}, u32[]{:S(2)}, u32[]{:S(2)}) collective-permute-start(bf16[4,64,768]{2,1,0:T(8,128)(2,1)S(1)} %get-tuple-element.273), channel_id=1, source_target_pairs={{0,8},{8,0},{16,24},{24,16},{1,9},{9,1},{17,25},{25,17},{2,10},{10... | collective-permute-start | bytes 1179656 | tf_op jit(solution)/shard_map/ppermute | solution.py:492
  368.9 18.3 %collective-permute-start.30 = (bf16[64,1024]{1,0:T(8,128)(2,1)}, bf16[64,1024]{1,0:T(8,128)(2,1)}, u32[]{:S(2)}, u32[]{:S(2)}) collective-permute-start(bf16[64,1024]{1,0:T(8,128)(2,1)} %get-tuple-element.250), channel_id=1, source_target_pairs={{0,2},{1,3},{2,0},{3,1},{4,6},{5,7},{6,4},{7,5},{8,10},{9,11},{10,... | collective-permute-start | bytes 393224 | tf_op jit(solution)/shard_map/ppermute | solution.py:492
  370.4 16.8 %collective-permute-start.31 = (bf16[64,1024]{1,0:T(8,128)(2,1)}, bf16[64,1024]{1,0:T(8,128)(2,1)}, u32[]{:S(2)}, u32[]{:S(2)}) collective-permute-start(bf16[64,1024]{1,0:T(8,128)(2,1)} %get-tuple-element.251), channel_id=1, source_target_pairs={{0,4},{1,5},{2,6},{3,7},{4,0},{5,1},{6,2},{7,3},{8,12},{9,13},{10,... | collective-permute-start | bytes 393224 | tf_op jit(solution)/shard_map/ppermute | solution.py:492
  373.5 13.7 %collective-permute-start.32 = (bf16[64,1024]{1,0:T(8,128)(2,1)}, bf16[64,1024]{1,0:T(8,128)(2,1)}, u32[]{:S(2)}, u32[]{:S(2)}) collective-permute-start(bf16[64,1024]{1,0:T(8,128)(2,1)} %get-tuple-element.252), channel_id=1, source_target_pairs={{0,6},{1,7},{2,4},{3,5},{4,2},{5,3},{6,0},{7,1},{8,14},{9,15},{10,... | collective-permute-start | bytes 393224 | tf_op jit(solution)/shard_map/ppermute | solution.py:492
  389.6 21.0 %collective-permute-start.45 = (f32[64,1024]{1,0:T(8,128)S(1)}, f32[64,1024]{1,0:T(8,128)S(1)}, u32[]{:S(2)}, u32[]{:S(2)}) collective-permute-start(f32[64,1024]{1,0:T(8,128)S(1)} %copy-done.3), channel_id=1, source_target_pairs={{0,16},{8,24},{16,0},{24,8},{1,17},{9,25},{17,1},{25,9},{2,18},{10... | collective-permute-start | bytes 786440 | tf_op jit(solution)/shard_map/ppermute | solution.py:492
  390.5 16.6 %collective-permute-start.43 = (f32[64,1024]{1,0:T(8,128)S(1)}, f32[64,1024]{1,0:T(8,128)S(1)}, u32[]{:S(2)}, u32[]{:S(2)}) collective-permute-start(f32[64,1024]{1,0:T(8,128)S(1)} %copy-done.3), channel_id=1, source_target_pairs={{0,8},{8,0},{16,24},{24,16},{1,9},{9,1},{17,25},{25,17},{2,10},{10... | collective-permute-start | bytes 786440 | tf_op jit(solution)/shard_map/ppermute | solution.py:492
  391.6 16.7 %collective-permute-start.46 = (f32[64,1024]{1,0:T(8,128)S(1)}, f32[64,1024]{1,0:T(8,128)S(1)}, u32[]{:S(2)}, u32[]{:S(2)}) collective-permute-start(f32[64,1024]{1,0:T(8,128)S(1)} %copy-done.5), channel_id=1, source_target_pairs={{0,16},{8,24},{16,0},{24,8},{1,17},{9,25},{17,1},{25,9},{2,18},{10... | collective-permute-start | bytes 786440 | tf_op jit(solution)/shard_map/ppermute | solution.py:492
  395.0 15.7 %collective-permute-start.44 = (f32[64,1024]{1,0:T(8,128)S(1)}, f32[64,1024]{1,0:T(8,128)S(1)}, u32[]{:S(2)}, u32[]{:S(2)}) collective-permute-start(f32[64,1024]{1,0:T(8,128)S(1)} %copy-done.5), channel_id=1, source_target_pairs={{0,8},{8,0},{16,24},{24,16},{1,9},{9,1},{17,25},{25,17},{2,10},{10... | collective-permute-start | bytes 786440 | tf_op jit(solution)/shard_map/ppermute | solution.py:492
  (62 other events, 1030.2 us)

commit v4 on v3

--- a/solution.py
+++ b/solution.py
@@ -49,7 +49,7 @@
     return pltpu.with_memory_space_constraint(value, pltpu.HBM) if is_far(value) else value
 
 
-def call(kernel, grid, outs, in_specs, out_specs, operands, scratch=(), flops=0, moved=0, near=()):
+def call(kernel, grid, outs, in_specs, out_specs, operands, scratch=(), flops=0, moved=0, near=(), vmem=VMEM_BYTES):
     single = not isinstance(outs, list)
     kinds = [outs] if single else outs
     large = [i not in near and x.size * x.dtype.itemsize >= LARGE for i, x in enumerate(kinds)]
@@ -62,7 +62,7 @@
         out_specs=out_specs,
         scratch_shapes=list(scratch),
         cost_estimate=pl.CostEstimate(flops=flops * WEIGH, bytes_accessed=moved * WEIGH, transcendentals=0),
-        compiler_params=pltpu.CompilerParams(vmem_limit_bytes=VMEM_BYTES),
+        compiler_params=pltpu.CompilerParams(vmem_limit_bytes=vmem),
     )(*[far(x) for x in operands])
     FAR.extend(x for x, flag in zip([results] if single else results, large) if flag)
     return results
@@ -269,17 +269,22 @@
     sent_ref[...] = latent.astype(BF16)
 
 
+def window_kernel(edges, sent, x, tables, tally_ref, partial_ref):
+    count = edges.shape[0]
+    bands, band, rows = tally_ref.shape
+    places = lax.broadcasted_iota(jnp.int32, (band, rows), 0)
+    for w in range(bands):
+        tally_ref[w] = named(edges, places + w * band)
+    gathered = dot(tally_ref[1], sent[...], 0, 0)
+    partial_ref[...] = dot(x[...], tables[0], 0, 0) + gathered / count
+
+
 def decoder_kernel(
-    edges, s0, s1, s2, x, tables, gains, mlp,
-    joined_ref, normed_ref, slope_ref, active_ref, decoded_ref, final_ref, output_ref,
+    tally, s0, s2, partial, tables, gains, mlp,
+    joined_ref, normed_ref, slope_ref, active_ref, decoded_ref, final_ref, output_ref, *, count,
 ):
-    count, rows = edges.shape
-    band = s0.shape[0]
-    gathered = jnp.zeros(joined_ref.shape, F32)
-    places = lax.broadcasted_iota(jnp.int32, (band, rows), 0)
-    for w, sent in enumerate((s0, s1, s2)):
-        gathered = gathered + dot(named(edges, places + w * band), sent[...], 0, 0)
-    joined = dot(x[...], tables[0], 0, 0) + gathered / count
+    gathered = dot(tally[0], s0[...], 0, 0) + dot(tally[2], s2[...], 0, 0)
+    joined = partial[...] + gathered / count
     joined_ref[...] = joined
     decoded = mlp_forward(joined, gains[3:4], mlp, normed_ref, slope_ref, active_ref)
     decoded_ref[...] = decoded
@@ -305,12 +310,12 @@
     add_up(gain_ref, jnp.concatenate([gain_dec, gain_final], axis=0))
 
 
-def scatter_kernel(edges, high, low, out0, out1, out2):
-    rows = out0.shape[0]
+def scatter_kernel(edges, high, low, *outs):
+    rows = outs[0].shape[0]
     count, total = edges.shape
-    for w, out in enumerate((out0, out1, out2)):
-        sub = lax.broadcasted_iota(jnp.int32, (rows, total), 0) + (pl.program_id(0) * rows + w * total)
-        tally = named(edges, sub)
+    sub = lax.broadcasted_iota(jnp.int32, (rows, total), 0) + pl.program_id(0) * rows
+    for w, out in enumerate(outs):
+        tally = named(edges, sub + w * total)
         value = dot(tally, high[...], 1, 0) + dot(tally, low[...], 1, 0)
         out[...] = (value / count).astype(out.dtype)
 
@@ -613,51 +618,48 @@
 
 
 def adam_kernel(places, factor, *refs):
-    dec, proc, down, up = refs[:4], refs[4:8], refs[8:12], refs[12:16]
-    mlp, attn, tables, gains = refs[16:20], refs[20:24], refs[24:28], refs[28:32]
-    mlp_out, attn_out, tables_out, gains_out = refs[32:37], refs[37:42], refs[42:47], refs[47:52]
-    size = mlp[0].shape[-1]
-    part = attn[0].shape[-1]
-    half = pl.program_id(1)
-    quarter = places[3] ^ pl.program_id(0)
-    for index in range(4):
-        for side in range(2):
-
-            @pl.when((pl.program_id(0) == index) & (half == side))
-            def _(index=index, side=side):
-                scale = factor[0]
-                here = slice(side * size, (side + 1) * size)
-                shares = ((down if side else up)[index][:, :size], proc[index][:, here], dec[index][:, here])
-                for layer, share in enumerate(shares):
-                    new = adam_update(
-                        scale * share, *(ref[layer] for ref in mlp), RATE_MATRIX, WEIGHT_DECAY
-                    )
-                    for ref, value in zip(mlp_out, new):
-                        ref[layer] = value
-                share = down[index][:, size + side * part : size + (side + 1) * part]
-                new = adam_update(scale * share, *(ref[...] for ref in attn), RATE_MATRIX, WEIGHT_DECAY)
-                for ref, value in zip(attn_out, new):
-                    ref[...] = value
-
-                if side:
-                    return
-                share = scale * up[index][:, size:]
-                for table in range(2):
-
-                    @pl.when(quarter == table)
-                    def _(table=table):
-                        new = adam_update(
-                            share[:, : tables[0].shape[-1]], *(ref[table] for ref in tables), RATE_MATRIX, WEIGHT_DECAY
-                        )
-                        for ref, value in zip(tables_out, new):
-                            ref[table] = value
-
-                @pl.when(quarter == 2)
-                def _():
-                    turned = share.T[: gains[0].shape[0]]
-                    new = adam_update(turned, *(ref[...] for ref in gains), RATE_GAIN, 0.0)
-                    for ref, value in zip(gains_out, new):
-                        ref[...] = value
+    dec, proc, down, up, whole_up = (refs[4 * i : 4 * i + 4] for i in range(5))
+    mlp, attn, tables, gains = (refs[20 + 4 * i : 24 + 4 * i] for i in range(4))
+    mlp_out, attn_out, tables_out, gains_out = (refs[36 + 5 * i : 41 + 5 * i] for i in range(4))
+    size = down[0].shape[-1] - attn[0].shape[-1] // 4
+    part = attn[0].shape[-1] // 4
+    scale = factor[0]
+    block, layer = pl.program_id(0), pl.program_id(1)
+
+    def update(share, state, new_state, at, rate, decay):
+        new = adam_update(scale * share, *(ref[at] for ref in state), rate, decay)
+        for ref, value in zip(new_state, new):
+            ref[at] = value
+
+    for k in range(4):
+        quarter = places[3] ^ k
+        for index, sides in enumerate(((up, down), (proc, proc), (dec, dec))):
+
+            @pl.when(layer == index)
+            def _(k=k, index=index, sides=sides, quarter=quarter):
+                for side, shares in enumerate(sides):
+                    start = 0 if index == 0 else side * size
+                    columns = pl.ds(pl.multiple_of((4 * side + quarter) * size, size), size)
+                    share = shares[k][:, start : start + size]
+                    update(share, mlp, mlp_out, (0, slice(None), columns), RATE_MATRIX, WEIGHT_DECAY)
+
+        @pl.when(layer == 0)
+        def _(k=k, quarter=quarter):
+            columns = pl.ds(pl.multiple_of(quarter * part, part), part)
+            update(down[k][:, size:], attn, attn_out, (slice(None), columns), RATE_MATRIX, WEIGHT_DECAY)
+
+        small = (layer == 0) & (block == 0)
+        for table in range(2):
+
+            @pl.when(small & (quarter == table))
+            def _(k=k, table=table):
+                share = whole_up[k][:, size : size + tables[0].shape[-1]]
+                update(share, tables, tables_out, (table,), RATE_MATRIX, WEIGHT_DECAY)
+
+        @pl.when(small & (quarter == 2))
+        def _(k=k):
+            turned = whole_up[k][:, size:].T[: gains[0].shape[0]]
+            update(turned, gains, gains_out, (slice(None),), RATE_GAIN, 0.0)
 
 
 def projection_back_kernel(
@@ -708,6 +710,7 @@
         flops=flops,
         moved=8 * width * columns * 4,
         scratch=[pltpu.VMEM((width, rows), BF16)] * turned,
+        vmem=VMEM_BYTES * 2 // 3,
         near=(0, 1),
     )
 
@@ -880,18 +883,29 @@
 
     before_sent, after_sent = from_sides(sent, sent)
 
+    dec_count = dec_edges.shape[1]
+    tally, partial = call(
+        window_kernel,
+        (grid_rows // ROWS,),
+        [shape((3, rows, grid_rows), BF16), shape((grid_rows, width), F32)],
+        [lanes_of(dec_count), whole((rows, width)), lanes_of(padded), tables_spec],
+        [pl.BlockSpec((3, rows, ROWS), lambda i: (0, 0, i)), rows_of(width)],
+        (dec_edges.T, sent, inputs, tables),
+        flops=2 * rows * rows * width,
+        moved=24 * rows * width,
+    )
     joined, normed_dec, slope_dec, active_dec, decoded, final, output = call(
-        decoder_kernel,
+        functools.partial(decoder_kernel, count=dec_count),
         (grid_rows // ROWS,),
         [shape((grid_rows, width), F32)]
         + kept_shapes
         + [shape((grid_rows, width), F32), shape((grid_rows, width), BF16), shape((padded, grid_rows), F32)],
         [
-            lanes_of(dec_edges.shape[1]), whole((rows, width)), whole((rows, width)), whole((rows, width)),
-            lanes_of(padded), tables_spec, gains_spec, weights_spec(2),
+            pl.BlockSpec((3, rows, ROWS), lambda i: (0, 0, i)), whole((rows, width)), whole((rows, width)),
+            rows_of(width), tables_spec, gains_spec, weights_spec(2),
         ],
         [rows_of(width)] + kept_specs + [rows_of(width), rows_of(width), lanes_of(padded)],
-        (dec_edges.T, before_sent, sent, after_sent, inputs, tables, gains, mlp_copy),
+        (tally, before_sent, after_sent, partial, tables, gains, mlp_copy),
         flops=mlp_flops + 6 * rows * rows * width,
         moved=24 * rows * width,
     )
@@ -939,7 +953,7 @@
         scatter_kernel,
         (steps,),
         [shape((rows, width), BF16), shape((rows, width), F32), shape((rows, width), BF16)],
-        [whole((dec_edges.shape[1], grid_rows)), whole((grid_rows, width)), whole((grid_rows, width))],
+        [whole((dec_count, grid_rows)), whole((grid_rows, width)), whole((grid_rows, width))],
         [rows_of(width)] * 3,
         (dec_edges.T, join_high, join_low),
         near=(0, 1, 2),
@@ -983,12 +997,11 @@
         near=(1, 5),
     )
 
-    keep_proc, send_proc = layer_weights(normed_proc, rounded_proc, before_proc, active_proc)
     block = 512
     side = pl.BlockSpec((2, depth, block), lambda i, h: (0, h, i))
     group_spec = whole((few, 8, rows))
     grad_queries, sides = [], []
-    ahead = (keep_proc, send_proc)
+    ahead = tuple(sorted_dec)
     for g, window in enumerate(windows):
         row_spec = pl.BlockSpec((part, rows), lambda i, h, g=g: (g, 0))
         dq, left, own, right = call(
@@ -1007,21 +1020,15 @@
             scratch=[pltpu.VMEM((block, rows), BF16), pltpu.VMEM((block, rows), BF16)],
             flops=60 * rows * rows * part,
             moved=12 * rows * rows,
-            near=(0, 1, 2, 3),
         )
         if sides:
-            left = after(left, *sides[-1], *swapped_proc)
-            right = after(right, *sides[-1], *swapped_proc)
+            left, right = after(left, *sides[-1]), after(right, *sides[-1])
         came = from_sides(left, right)
         sides.append([came[0], own, came[1]])
         grad_queries.append(dq)
-        if g == 0:
-            sorted_proc = sort_shares([after(keep_proc, dq)], [send_proc], places)
-            swapped_proc = swap_items(sorted_proc)
-            ahead = (*sorted_proc, *swapped_dec)
-
-    first_parts = sum_items([swapped_dec, swapped_proc], places)
-    first_parts = [first_parts[0]] + [after(x, *sides[-1]) for x in first_parts[1:]]
+        ahead = tuple(swapped_dec)
+
+    keep_proc, send_proc = layer_weights(normed_proc, after(rounded_proc, left, right), before_proc, active_proc)
     side_spec = pl.BlockSpec((2, part, ROWS), lambda i: (0, 0, i))
     upstream, rounded_enc, project, gain_attn = call(
         projection_back_kernel,
@@ -1035,24 +1042,24 @@
         [rows_of(width), rows_of(width), lanes_of(3 * width), whole((1, width))],
         (
             *grad_queries, sides[0][0], sides[1][0], sides[0][1], sides[1][1], sides[0][2], sides[1][2],
-            after(grad_residual, first_parts[0]), encoded, gains, attn_copy,
+            after(grad_residual, keep_proc, send_proc), encoded, gains, attn_copy,
         ),
         flops=3 * product,
         moved=24 * rows * width,
         near=(0, 1, 2),
     )
+    sorted_proc = sort_shares([keep_proc], [send_proc], places, late=(upstream,))
+    swapped_proc = swap_items(sorted_proc)
     keep_down, send_down = weights(
         down_weights_kernel,
         places,
-        (rounded_enc, active_enc, normed_attn, project, rounded_o, branch),
+        (after(rounded_enc, *sorted_proc), active_enc, normed_attn, project, rounded_o, branch),
         [full, columns_of, full, pl.BlockSpec((width, rows), lambda i: (jnp.minimum(i, 2), 0)), whole((width, rows)), full],
         quarter + width,
         8 * product,
         2,
     )
-    first_total = add_bands(first_parts, (keep_down,))
-    sorted_down = sort_shares([keep_down], [send_down], places, late=tuple(first_total))
-    swapped_down = swap_items(sorted_down)
+    sorted_down = sort_shares([keep_down], [send_down], places)
     before_enc, table_in, gain_enc, _ = call(
         encoder_back_kernel,
         (steps,),
@@ -1069,10 +1076,14 @@
     )
     grad_gains = jnp.concatenate([gain_enc, gain_attn, gain_proc, gain_dec], axis=0)
     gain_columns = jnp.pad(grad_gains.T, ((0, 0), (0, padded - gain_rows)))
+    swapped_down = swap_items([sorted_down[0]] + [after(x, *swapped_proc, before_enc) for x in sorted_down[1:]])
+    own_proc = [after(swapped_proc[0], before_enc)] + swapped_proc[1:]
+    first_parts = sum_items([swapped_dec, own_proc], places)
+    first_total = add_bands(first_parts, (first_parts[0],))
     keep_up, send_up = weights(
         up_weights_kernel,
         places,
-        (normed_enc, before_enc, table_in, table_direct, table_out, gain_columns),
+        (normed_enc, after(before_enc, first_parts[0]), table_in, table_direct, table_out, gain_columns),
         [full, columns_of, table_spec, table_spec, table_spec, table_spec],
         quarter + padded,
         4 * product,
@@ -1080,7 +1091,7 @@
     )
     down_parts = sum_items([swapped_down], places)
     down_total = sum_bands(down_parts)
-    sorted_up = sort_shares([keep_up], [send_up], places, exact=padded, late=(down_parts[0],))
+    sorted_up = sort_shares([keep_up], [send_up], places, exact=padded, late=(down_parts[0], *first_total))
     swapped_up = swap_items([sorted_up[0]] + [after(x, *swapped_down) for x in sorted_up[1:]])
     first_all = all_items(*[after(x, *swapped_up) for x in first_total])
     ready = [x for pair in first_all for x in pair]
@@ -1098,19 +1109,21 @@
     scale_factor = CLIP_LEVEL / jnp.maximum(grad_norm, CLIP_LEVEL)
 
     shard_rows = attn_master.shape[0]
-    mlp_spec = pl.BlockSpec((mlp_master.shape[0], shard_rows, quarter), lambda j, k, s: (0, 0, k * 4 + (s[3] ^ j)))
-    attn_part = pl.BlockSpec((shard_rows, width // 2), lambda j, k, s: (0, (s[3] ^ j) * 2 + k))
+    block_rows = min(shard_rows, 32)
+    mlp_spec = pl.BlockSpec((1, block_rows, 2 * hidden), lambda r, l, s: (l, r, 0))
+    attn_part = pl.BlockSpec((block_rows, attn_master.shape[1]), lambda r, l, s: (r, 0))
     kinds = [F32, F32, F32, F32, BF16]
     shares = [x for pair in zip(*first_all) for x in pair] + [x for pair in zip(*last_all) for x in pair]
     state = (mlp_master, mlp_first, mlp_second, mlp_ema, attn_master, attn_first, attn_second, attn_ema)
     table_state = [jnp.swapaxes(x, 1, 2) for x in (tables_master, tables_first, tables_second, tables_ema)]
-    FAR.extend(table_state)
+    FAR.extend([*table_state, *shares])
     updated = prefetched(
         adam_kernel,
-        (4, 2),
+        (shard_rows // block_rows, mlp_master.shape[0]),
         [shape(x.shape, kind) for x in (mlp_master, attn_master, table_state[0], gains_master) for kind in kinds],
         [smem]
-        + [pl.BlockSpec(x.shape, lambda *_: (0, 0)) for x in shares]
+        + [pl.BlockSpec((block_rows, x.shape[1]), lambda r, l, s: (r, 0)) for x in shares]
+        + [pl.BlockSpec(x.shape, lambda *_: (0, 0)) for x in shares[-4:]]
         + [mlp_spec] * 4
         + [attn_part] * 4
         + [whole(table_state[0].shape)] * 4
@@ -1118,7 +1131,7 @@
         [mlp_spec] * 5 + [attn_part] * 5 + [whole(table_state[0].shape)] * 5 + [whole(gains_master.shape)] * 5,
         places,
         (
-            scale_factor[None], *shares, *state, *table_state,
+            scale_factor[None], *shares, *shares[-4:], *state, *table_state,
             gains_master, gains_first, gains_second, gains_ema,
         ),
         moved=34 * (mlp_master.size + attn_master.size),

time: 458 us -> 454 us (level)
  waiting for transfers between devices: 39.7 us -> 55.4 us
  starting transfers between devices: 111 us -> 96.9 us
  Pallas kernels: 275 us -> 270 us
    ppermute x43, waiting for transfers between devices: 38.8 us -> 55.4 us  [exchange(): return lax.ppermute(value, axis, [(i, i ^ distance) for i in range(size)])]
    ppermute x43, starting transfers between devices: 76.1 us -> 62.4 us  [exchange(): return lax.ppermute(value, axis, [(i, i ^ distance) for i in range(size)])]
    pallas_call x8, Pallas kernels: 45.2 us -> 38.1 us  [prefetched(): pl.pallas_call(kernel, grid_spec=pltpu.PrefetchScalarGridSpec(num_scalar_...]
    pallas_call x18 -> x19, Pallas kernels: 230 us -> 232 us  [call(): pl.pallas_call(kernel, grid=grid, out_shape=kinds[0] if single else kinds...]
  transfers between devices with their start and end apart: 55 -> 55, of which waited for: 22 -> 19; matrix products, arithmetic and copies ran while one was open for 2% -> 2% of each run, Pallas kernels for 35% -> 32%
where the time goes in v4:
time: 454 us; the launch traced here: 448 us
  Pallas kernels  270 us (59%)
  starting transfers between devices  96.9 us (21%)
  waiting for transfers between devices  55.4 us (12%)
  other arithmetic  9.11 us (2%)
  between operations  7.79 us (2%)
  local copies, waits for them, and re-layouts  7.43 us (2%)
    pallas_call x19, Pallas kernels, call(): pl.pallas_call(kernel, grid=grid, out_shape=kinds[0] if single else kinds...  232 us
    ppermute x43, starting transfers between devices, exchange(): return lax.ppermute(value, axis, [(i, i ^ distance) for i in range(size)])  62.4 us
    ppermute x43, waiting for transfers between devices, exchange(): return lax.ppermute(value, axis, [(i, i ^ distance) for i in range(size)])  55.4 us
    pallas_call x8, Pallas kernels, prefetched(): pl.pallas_call(kernel, grid_spec=pltpu.PrefetchScalarGridSpec(num_scalar_...  38.1 us
    ppermute x6, starting transfers between devices, from_sides(): lax.ppermute(to_right, 'lat', up)  25.7 us
  transfers between devices with their start and end apart: 55, of which 19 were waited for; matrix products, arithmetic and copies ran while one was open for 2% of the time, Pallas kernels for 32%

profile of v4, /device:TPU:0, one launch (start us, length us, event | category | flops | bytes accessed | tf_op | source)
XLA Modules:
  0.0 448.0 jit_solution(3164127771170417755)
XLA Ops:
  4.9 18.8 %shard_map.435 = (bf16[1024,256]{1,0:T(8,128)(2,1)S(1)}, f32[1024,512]{1,0:T(8,128)}, f32[1024,512]{1,0:T(8,128)}, bf16[1024,512]{1,0:T(8,128)(2,1)}, f32[1024,2...) custom-call(s32[4,1024]{1,0:T(4,128)S(1)} %bitcast.48, ...), custom_call_target="tpu_custom_call" | custom-call | flops 177167400960 | bytes 471859200 | tf_op jit(solution)/shard_map/pallas_call | solution.py:57
  27.9 10.3 %shard_map.436.bias = f32[3,1024,1024]{2,1,0:T(8,128)} custom-call(s32[5]{0:T(128)S(1)} %stack.28.places, s32[16]{0:T(128)S(1)} %reduce.ends, s32[16,1024]{1,0:T(8,128)S(1)} %bitcast.47), custom_call_target="tpu_custom_call" | custom-call | flops 60000002048 | bytes 377487360 | tf_op jit(solution)/shard_map/pallas_call | solution.py:57
  38.3 9.8 %collective-permute-start.2 = (bf16[1024,512]{1,0:T(8,128)(2,1)}, bf16[1024,512]{1,0:T(8,128)(2,1)}, u32[]{:S(2)}, u32[]{:S(2)}) collective-permute-start(bf16[1024,512]{1,0:T(8,128)(2,1)} %get-tuple-element.173.k1.v1), channel_id=1, source_target_pairs={{0,1},{1,2},{2,3},{3,4},{4,5},{5,6},{6,7},{8,9},{9,10},{10,11},{11... | collective-permute-start | bytes 3145736 | tf_op jit(solution)/shard_map/ppermute | solution.py:734
  49.6 14.6 %shard_map.437 = (f32[256,1024]{1,0:T(8,128)}, f32[2,8,1024]{2,1,0:T(8,128)S(1)}) custom-call(bf16[512,1024]{1,0:T(8,128)(2,1)} %get-tuple-element.169.q_ref, bf16[1024,512]{1,0:T(8,128)(2,1)S(1)} %collective-permute-done.k0.v0, bf16[1024,512]{1,0:T(8,128)(2,1)} %get-tuple-element.170.k1.v1, bf16[1024,512]{1,0:T(8,128)(2,1)S(1)} %collective-permute-done.1.k2.v2, ...), custom_call_target="tpu_custom_call" | custom-call | flops 193273528320 | bytes 377487360 | tf_op jit(solution)/shard_map/pallas_call | solution.py:57
  64.3 15.3 %shard_map.438 = (f32[256,1024]{1,0:T(8,128)}, f32[2,8,1024]{2,1,0:T(8,128)S(1)}) custom-call(bf16[512,1024]{1,0:T(8,128)(2,1)} %get-tuple-element.169.q_ref, bf16[1024,512]{1,0:T(8,128)(2,1)} %collective-permute-done.2.k0.v0, bf16[1024,512]{1,0:T(8,128)(2,1)} %get-tuple-element.173.k1.v1, bf16[1024,512]{1,0:T(8,128)(2,1)} %collective-permute-done.3.k2.v2, ...), custom_call_target="tpu_custom_call" | custom-call | flops 193273528320 | bytes 377487360 | tf_op jit(solution)/shard_map/pallas_call | solution.py:57
  79.6 14.4 %shard_map.439 = (bf16[512,1024]{1,0:T(8,128)(2,1)}, f32[1024,512]{1,0:T(8,128)}, bf16[1024,512]{1,0:T(8,128)(2,1)}, f32[1024,2048]{1,0:T(8,128)}, bf16[1024,204...) custom-call(f32[256,1024]{1,0:T(8,128)} %get-tuple-element.171.o0, f32[256,1024]{1,0:T(8,128)} %get-tuple-element.174.o1, ...), custom_call_target="tpu_custom_call" | custom-call | flops 144955146240 | bytes 377487360 | tf_op jit(solution)/shard_map/pallas_call | solution.py:57
  99.0 6.7 %shard_map.440 = (bf16[3,1024,1024]{2,1,0:T(8,128)(2,1)}, f32[1024,512]{1,0:T(8,128)}) custom-call(s32[3,1024]{1,0:T(4,128)S(1)} %bitcast.49, bf16[1024,512]{1,0:T(8,128)(2,1)S(1)} %get-tuple-element.176.sent, bf16[128,1024]{1,0:T(8,128)(2,1)S(1)} %copy-done.7, bf16[2,128,512]{2,1,0:T(8,128)(2,1)S(1)} %copy-done.10), custom_call_target="tpu_custom_call" | custom-call | flops 32212254720 | bytes 377487360 | tf_op jit(solution)/shard_map/pallas_call | solution.py:57
  105.7 17.5 %shard_map.441 = (f32[1024,512]{1,0:T(8,128)}, bf16[1024,512]{1,0:T(8,128)(2,1)}, f32[1024,2048]{1,0:T(8,128)}, bf16[1024,2048]{1,0:T(8,128)(2,1)}, f32[1024,512...) custom-call(bf16[3,1024,1024]{2,1,0:T(8,128)(2,1)} %get-tuple-element.177.tally, ...), custom_call_target="tpu_custom_call" | custom-call | flops 225485783040 | bytes 377487360 | tf_op jit(solution)/shard_map/pallas_call | solution.py:57
  123.8 7.8 %collective-permute-start.6 = (f32[83,64]{0,1:T(8,128)S(1)}, f32[83,64]{0,1:T(8,128)S(1)}, u32[]{:S(2)}, u32[]{:S(2)}) collective-permute-start(f32[83,64]{0,1:T(8,128)S(1)} %fusion.1), channel_id=1, source_target_pairs={{0,1},{1,0},{2,3},{3,2},{4,5},{5,4},{6,7},{7,6},{8,9},{9,8},{10,11... | collective-permute-start | bytes 63752 | tf_op jit(solution)/shard_map/ppermute | solution.py:497
  141.8 15.2 %shard_map.442 = (bf16[1024,512]{1,0:T(8,128)(2,1)S(1)}, bf16[1024,512]{1,0:T(8,128)(2,1)S(1)}, bf16[1024,512]{1,0:T(8,128)(2,1)S(1)}, bf16[1024,2048]{1,0:T(8,1...) custom-call(bf16[128,1024]{1,0:T(8,128)(2,1)S(1)} %pad.17.grad_output, ...), custom_call_target="tpu_custom_call" | custom-call | flops 128849018880 | bytes 377487360 | tf_op jit(solution)/shard_map/pallas_call | solution.py:57
  157.1 8.1 %shard_map.443 = (bf16[1024,512]{1,0:T(8,128)(2,1)S(1)}, f32[1024,512]{1,0:T(8,128)S(1)}, bf16[1024,512]{1,0:T(8,128)(2,1)S(1)}) custom-call(s32[3,1024]{1,0:T(4,128)S(1)} %bitcast.50, bf16[1024,512]{1,0:T(8,128)(2,1)S(1)} %get-tuple-element.186.high, bf16[1024,512]{1,0:T(8,128)(2,1)S(1)} %get-tuple-element.187.low), custom_call_target="tpu_custom_call" | custom-call | flops 193273528320 | bytes 188743680 | tf_op jit(solution)/shard_map/pallas_call | solution.py:57
  168.0 10.1 %shard_map.444 = (f32[4,4,64,1024]{3,2,1,0:T(8,128)S(1)}, f32[4,4,64,1024]{3,2,1,0:T(8,128)}) custom-call(s32[5]{0:T(128)S(1)} %copy-done.12, bf16[1024,512]{1,0:T(8,128)(2,1)} %get-tuple-element.179.normed, bf16[1024,512]{1,0:T(8,128)(2,1)S(1)} %get-tuple-element.190.rounded, bf16[1024,2048]{1,0:T(8,128)(2,1)} %get-tuple-element.191.before, ...), custom_call_target="tpu_custom_call" | custom-call | flops 128849018880 | bytes 503316480 | tf_op jit(solution)/shard_map/pallas_call | solution.py:57
  181.1 13.1 %shard_map.446 = (f32[1024,512]{1,0:T(8,128)}, bf16[1024,512]{1,0:T(8,128)(2,1)S(1)}, bf16[1024,2048]{1,0:T(8,128)(2,1)}, f32[1,512]{1,0:T(1,128)S(1)}, bf16[102...) custom-call(bf16[1024,512]{1,0:T(8,128)(2,1)S(1)} %collective-permute-done.13.g0, ...), custom_call_target="tpu_custom_call" | custom-call | flops 144955146240 | bytes 377487360 | tf_op jit(solution)/shard_map/pallas_call | solution.py:57
  194.3 4.9 %shard_map.445 = (f32[4,64,1024]{2,1,0:T(8,128)S(1)}, bf16[4,64,1024]{2,1,0:T(8,128)(2,1)}, bf16[4,64,1024]{2,1,0:T(8,128)(2,1)}, bf16[4,64,1024]{2,1,0:T(8,128)(2,1)}) custom-call(s32[5]{0:T(128)S(1)} %copy-done.13, f32[4,4,64,1024]{3,2,1,0:T(8,128)S(1)} %get-tuple-element.193.refs_0_, f32[4,4,64,1024]{3,2,1,0:T(8,128)} %collective-permute-done.9.refs_1_), custom_call_target="tpu_custom_call" | custom-call | flops 440401920 | bytes 440401920 | tf_op jit(solution)/shard_map/pallas_call | solution.py:501
  202.7 22.1 %shard_map.448 = (f32[256,1024]{1,0:T(8,128)}, bf16[2,256,1024]{2,1,0:T(8,128)(2,1)}, f32[2,256,1024]{2,1,0:T(8,128)}, bf16[2,256,1024]{2,1,0:T(8,128)(2,1)}) custom-call(bf16[512,1024]{1,0:T(8,128)(2,1)} %get-tuple-element.169.q_ref, bf16[512,1024]{1,0:T(8,128)(2,1)S(1)} %get-tuple-element.206.do_ref, f32[2,8,1024]{2,1,0:T(8,128)S(1)} %get-tuple-element.211.lse_ref, ...), custom_call_target="tpu_custom_call" | custom-call | flops 483183820800 | bytes 377487360 | tf_op jit(solution)/shard_map/pallas_call | solution.py:57
  224.8 5.8 %collective-permute-start.15 = (bf16[2,256,1024]{2,1,0:T(8,128)(2,1)}, bf16[2,256,1024]{2,1,0:T(8,128)(2,1)}, u32[]{:S(2)}, u32[]{:S(2)}) collective-permute-start(bf16[2,256,1024]{2,1,0:T(8,128)(2,1)} %get-tuple-element.212), channel_id=1, source_target_pairs={{0,1},{1,2},{2,3},{3,4},{4,5},{5,6},{6,7},{8,9},{9,10},{10,11},{11... | collective-permute-start | bytes 3145736 | tf_op jit(solution)/shard_map/ppermute | solution.py:734
  231.9 22.1 %shard_map.447 = (f32[256,1024]{1,0:T(8,128)}, bf16[2,256,1024]{2,1,0:T(8,128)(2,1)}, f32[2,256,1024]{2,1,0:T(8,128)}, bf16[2,256,1024]{2,1,0:T(8,128)(2,1)}) custom-call(bf16[512,1024]{1,0:T(8,128)(2,1)} %get-tuple-element.169.q_ref, bf16[512,1024]{1,0:T(8,128)(2,1)S(1)} %get-tuple-element.206.do_ref, f32[2,8,1024]{2,1,0:T(8,128)S(1)} %get-tuple-element.207.lse_ref, ...), custom_call_target="tpu_custom_call" | custom-call | flops 483183820800 | bytes 377487360 | tf_op jit(solution)/shard_map/pallas_call | solution.py:57
  258.6 8.7 %shard_map.449 = (f32[4,4,64,1024]{3,2,1,0:T(8,128)S(1)}, f32[4,4,64,1024]{3,2,1,0:T(8,128)S(1)}) custom-call(s32[5]{0:T(128)S(1)} %copy-done.14, bf16[1024,512]{1,0:T(8,128)(2,1)} %get-tuple-element.199.normed, bf16[1024,512]{1,0:T(8,128)(2,1)S(1)} %get-tuple-element.218.rounded, bf16[1024,2048]{1,0:T(8,128)(2,1)} %get-tuple-element.219.before, ...), custom_call_target="tpu_custom_call" | custom-call | flops 128849018880 | bytes 503316480 | tf_op jit(solution)/shard_map/pallas_call | solution.py:57
  269.1 7.4 %shard_map.450 = (f32[1024,512]{1,0:T(8,128)S(1)}, bf16[1024,512]{1,0:T(8,128)(2,1)S(1)}, bf16[1536,1024]{1,0:T(8,128)(2,1)S(1)}, f32[1,512]{1,0:T(1,128)S(1)}) custom-call(f32[256,1024]{1,0:T(8,128)} %get-tuple-element.222.dq0, f32[256,1024]{1,0:T(8,128)} %get-tuple-element.223.dq1, bf16[2,256,1024]{2,1,0:T(8,128)(2,1)} %collective-permute-done.15.left0, ...), custom_call_target="tpu_custom_call" | custom-call | flops 48318382080 | bytes 377487360 | tf_op jit(solution)/shard_map/pallas_call | solution.py:57
  280.8 9.1 %shard_map.452 = (f32[4,4,64,1024]{3,2,1,0:T(8,128)S(1)}, f32[4,4,64,1024]{3,2,1,0:T(8,128)S(1)}) custom-call(s32[5]{0:T(128)S(1)} %copy-done.14, bf16[1024,512]{1,0:T(8,128)(2,1)S(1)} %get-tuple-element.236.rounded, bf16[1024,2048]{1,0:T(8,128)(2,1)} %get-tuple-element.237.active, bf16[1024,512]{1,0:T(8,128)(2,1)} %get-tuple-element.238.normed_attn, ...), custom_call_target="tpu_custom_call" | custom-call | flops 128849018880 | bytes 503316480 | tf_op jit(solution)/shard_map/pallas_call | solution.py:57
  289.9 5.7 %collective-permute-start.20 = (f32[4,4,64,1024]{3,2,1,0:T(8,128)S(1)}, f32[4,4,64,1024]{3,2,1,0:T(8,128)S(1)}, u32[]{:S(2)}, u32[]{:S(2)}) collective-permute-start(f32[4,4,64,1024]{3,2,1,0:T(8,128)S(1)} %get-tuple-element.243), channel_id=1, source_target_pairs={{0,1},{1,0},{2,3},{3,2},{4,5},{5,4},{6,7},{7,6},{8,9},{9,8},{10,11... | collective-permute-start | bytes 12582920 | tf_op jit(solution)/shard_map/ppermute | solution.py:497
  304.8 11.9 %shard_map.454 = (bf16[1024,2048]{1,0:T(8,128)(2,1)}, f32[512,128]{1,0:T(8,128)S(1)}, f32[1,512]{1,0:T(1,128)S(1)}, bf16[1024,512]{1,0:T(8,128)(2,1)}) custom-call(f32[1024,512]{1,0:T(8,128)S(1)} %copy-done.31, f32[1024,512]{1,0:T(8,128)} %get-tuple-element.249.pooled, f32[1024,2048]{1,0:T(8,128)} %get-tuple-element.250.slope, f32[5,512]{1,0:T(8,128)S(1)} %copy-done.17, ...), custom_call_target="tpu_custom_call" | custom-call | flops 128849018880 | bytes 377487360 | tf_op jit(solution)/shard_map/pallas_call | solution.py:57
  316.7 5.2 %collective-permute-done.22.refs_6_ = bf16[4,64,1024]{2,1,0:T(8,128)(2,1)S(1)} collective-permute-done((bf16[4,64,1024]{2,1,0:T(8,128)(2,1)S(1)}, bf16[4,64,1024]{2,1,0:T(8,128)(2,1)S(1)}, u32[]{:S(2)}, u32[]{:S(2)}) %collective-permute-start.22) | collective-permute-done | bytes 524320 | tf_op jit(solution)/shard_map/ppermute | solution.py:497
  331.9 6.8 %shard_map.458 = (f32[4,4,64,640]{3,2,1,0:T(8,128)S(1)}, f32[4,4,64,640]{3,2,1,0:T(8,128)}) custom-call(s32[5]{0:T(128)S(1)} %copy-done.14, bf16[1024,512]{1,0:T(8,128)(2,1)} %get-tuple-element.268.normed, bf16[1024,2048]{1,0:T(8,128)(2,1)} %get-tuple-element.269.before, f32[512,128]{1,0:T(8,128)S(1)} %get-tuple-element.270.table_in, ...), custom_call_target="tpu_custom_call" | custom-call | flops 64424509440 | bytes 314572800 | tf_op jit(solution)/shard_map/pallas_call | solution.py:57
  340.1 9.6 %collective-permute-done.25.refs_1_ = bf16[64,2048]{1,0:T(8,128)(2,1)S(1)} collective-permute-done((bf16[64,2048]{1,0:T(8,128)(2,1)S(1)}, bf16[64,2048]{1,0:T(8,128)(2,1)S(1)}, u32[]{:S(2)}, u32[]{:S(2)}) %collective-permute-start.25) | collective-permute-done | bytes 262176 | tf_op jit(solution)/shard_map/ppermute | solution.py:497
  351.3 3.7 shard_map.457
  355.0 3.9 shard_map.459
  374.2 5.3 %collective-permute-done.36.refs_3_ = bf16[4,64,768]{2,1,0:T(8,128)(2,1)} collective-permute-done((bf16[4,64,768]{2,1,0:T(8,128)(2,1)S(1)}, bf16[4,64,768]{2,1,0:T(8,128)(2,1)}, u32[]{:S(2)}, u32[]{:S(2)}) %collective-permute-start.36) | collective-permute-done | bytes 393248 | tf_op jit(solution)/shard_map/ppermute | solution.py:497
  396.7 3.5 collective-permute-done.41
  400.5 4.2 collective-permute-done.42
  415.8 3.9 collective-permute-done.50.refs_14_.refs_18_
  430.6 16.0 %shard_map.461 = (f32[3,64,4096]{2,1,0:T(8,128)}, f32[3,64,4096]{2,1,0:T(8,128)}, f32[3,64,4096]{2,1,0:T(8,128)}, f32[3,64,4096]{2,1,0:T(8,128)}, bf16[3,64,4096...) custom-call(s32[5]{0:T(128)S(1)} %copy-done.15, ...), custom_call_target="tpu_custom_call" | custom-call | flops 935854080 | bytes 935854080 | tf_op jit(solution)/shard_map/pallas_call | solution.py:501
  (245 shorter events, 118.6 us)
Async XLA Ops:
  23.8 14.5 %collective-permute-start = (bf16[1024,512]{1,0:T(8,128)(2,1)}, bf16[1024,512]{1,0:T(8,128)(2,1)S(1)}, u32[]{:S(2)}, u32[]{:S(2)}) collective-permute-start(bf16[1024,512]{1,0:T(8,128)(2,1)} %get-tuple-element.170.k1.v1), channel_id=1, source_target_pairs={{0,1},{1,2},{2,3},{3,4},{4,5},{5,6},{6,7},{8,9},{9,10},{10,11},{11... | collective-permute-start | bytes 3145736 | tf_op jit(solution)/shard_map/ppermute | solution.py:734
  26.2 12.1 %collective-permute-start.1 = (bf16[1024,512]{1,0:T(8,128)(2,1)}, bf16[1024,512]{1,0:T(8,128)(2,1)S(1)}, u32[]{:S(2)}, u32[]{:S(2)}) collective-permute-start(bf16[1024,512]{1,0:T(8,128)(2,1)} %get-tuple-element.170.k1.v1), channel_id=1, source_target_pairs={{1,0},{2,1},{3,2},{4,3},{5,4},{6,5},{7,6},{9,8},{10,9},{11,10},{12... | collective-permute-start | bytes 3145736 | tf_op jit(solution)/shard_map/ppermute | solution.py:734
  38.3 26.0 %collective-permute-start.2 = (bf16[1024,512]{1,0:T(8,128)(2,1)}, bf16[1024,512]{1,0:T(8,128)(2,1)}, u32[]{:S(2)}, u32[]{:S(2)}) collective-permute-start(bf16[1024,512]{1,0:T(8,128)(2,1)} %get-tuple-element.173.k1.v1), channel_id=1, source_target_pairs={{0,1},{1,2},{2,3},{3,4},{4,5},{5,6},{6,7},{8,9},{9,10},{10,11},{11... | collective-permute-start | bytes 3145736 | tf_op jit(solution)/shard_map/ppermute | solution.py:734
  48.0 16.2 %collective-permute-start.3 = (bf16[1024,512]{1,0:T(8,128)(2,1)}, bf16[1024,512]{1,0:T(8,128)(2,1)}, u32[]{:S(2)}, u32[]{:S(2)}) collective-permute-start(bf16[1024,512]{1,0:T(8,128)(2,1)} %get-tuple-element.173.k1.v1), channel_id=1, source_target_pairs={{1,0},{2,1},{3,2},{4,3},{5,4},{6,5},{7,6},{9,8},{10,9},{11,10},{12... | collective-permute-start | bytes 3145736 | tf_op jit(solution)/shard_map/ppermute | solution.py:734
  165.1 16.0 %collective-permute-start.13 = (bf16[1024,512]{1,0:T(8,128)(2,1)S(1)}, bf16[1024,512]{1,0:T(8,128)(2,1)S(1)}, u32[]{:S(2)}, u32[]{:S(2)}) collective-permute-start(bf16[1024,512]{1,0:T(8,128)(2,1)S(1)} %get-tuple-element.189), channel_id=1, source_target_pairs={{0,1},{1,2},{2,3},{3,4},{4,5},{5,6},{6,7},{8,9},{9,10},{10,11},{11... | collective-permute-start | bytes 3145736 | tf_op jit(solution)/shard_map/ppermute | solution.py:734
  166.5 14.6 %collective-permute-start.14 = (bf16[1024,512]{1,0:T(8,128)(2,1)S(1)}, bf16[1024,512]{1,0:T(8,128)(2,1)S(1)}, u32[]{:S(2)}, u32[]{:S(2)}) collective-permute-start(bf16[1024,512]{1,0:T(8,128)(2,1)S(1)} %get-tuple-element.188), channel_id=1, source_target_pairs={{1,0},{2,1},{3,2},{4,3},{5,4},{6,5},{7,6},{9,8},{10,9},{11,10},{12... | collective-permute-start | bytes 3145736 | tf_op jit(solution)/shard_map/ppermute | solution.py:734
  178.1 16.1 %collective-permute-start.9 = (f32[4,4,64,1024]{3,2,1,0:T(8,128)}, f32[4,4,64,1024]{3,2,1,0:T(8,128)}, u32[]{:S(2)}, u32[]{:S(2)}) collective-permute-start(f32[4,4,64,1024]{3,2,1,0:T(8,128)} %get-tuple-element.194), channel_id=1, source_target_pairs={{0,1},{1,0},{2,3},{3,2},{4,5},{5,4},{6,7},{7,6},{8,9},{9,8},{10,11... | collective-permute-start | bytes 12582920 | tf_op jit(solution)/shard_map/ppermute | solution.py:497
  199.2 32.7 %collective-permute-start.10 = (bf16[4,64,1024]{2,1,0:T(8,128)(2,1)}, bf16[4,64,1024]{2,1,0:T(8,128)(2,1)}, u32[]{:S(2)}, u32[]{:S(2)}) collective-permute-start(bf16[4,64,1024]{2,1,0:T(8,128)(2,1)} %get-tuple-element.196), channel_id=1, source_target_pairs={{0,8},{8,0},{16,24},{24,16},{1,9},{9,1},{17,25},{25,17},{2,10},{10... | collective-permute-start | bytes 1572872 | tf_op jit(solution)/shard_map/ppermute | solution.py:497
  200.7 31.2 %collective-permute-start.11 = (bf16[4,64,1024]{2,1,0:T(8,128)(2,1)}, bf16[4,64,1024]{2,1,0:T(8,128)(2,1)}, u32[]{:S(2)}, u32[]{:S(2)}) collective-permute-start(bf16[4,64,1024]{2,1,0:T(8,128)(2,1)} %get-tuple-element.197), channel_id=1, source_target_pairs={{0,16},{8,24},{16,0},{24,8},{1,17},{9,25},{17,1},{25,9},{2,18},{10... | collective-permute-start | bytes 1572872 | tf_op jit(solution)/shard_map/ppermute | solution.py:497
  202.2 29.7 %collective-permute-start.12 = (bf16[4,64,1024]{2,1,0:T(8,128)(2,1)}, bf16[4,64,1024]{2,1,0:T(8,128)(2,1)}, u32[]{:S(2)}, u32[]{:S(2)}) collective-permute-start(bf16[4,64,1024]{2,1,0:T(8,128)(2,1)} %get-tuple-element.198), channel_id=1, source_target_pairs={{0,24},{8,16},{16,8},{24,0},{1,25},{9,17},{17,9},{25,1},{2,26},{10... | collective-permute-start | bytes 1572872 | tf_op jit(solution)/shard_map/ppermute | solution.py:497
  224.8 29.3 %collective-permute-start.15 = (bf16[2,256,1024]{2,1,0:T(8,128)(2,1)}, bf16[2,256,1024]{2,1,0:T(8,128)(2,1)}, u32[]{:S(2)}, u32[]{:S(2)}) collective-permute-start(bf16[2,256,1024]{2,1,0:T(8,128)(2,1)} %get-tuple-element.212), channel_id=1, source_target_pairs={{0,1},{1,2},{2,3},{3,4},{4,5},{5,6},{6,7},{8,9},{9,10},{10,11},{11... | collective-permute-start | bytes 3145736 | tf_op jit(solution)/shard_map/ppermute | solution.py:734
  230.6 23.4 %collective-permute-start.16 = (bf16[2,256,1024]{2,1,0:T(8,128)(2,1)}, bf16[2,256,1024]{2,1,0:T(8,128)(2,1)}, u32[]{:S(2)}, u32[]{:S(2)}) collective-permute-start(bf16[2,256,1024]{2,1,0:T(8,128)(2,1)} %get-tuple-element.214), channel_id=1, source_target_pairs={{1,0},{2,1},{3,2},{4,3},{5,4},{6,5},{7,6},{9,8},{10,9},{11,10},{12... | collective-permute-start | bytes 3145736 | tf_op jit(solution)/shard_map/ppermute | solution.py:734
  254.0 15.0 %collective-permute-start.17 = (bf16[2,256,1024]{2,1,0:T(8,128)(2,1)}, bf16[2,256,1024]{2,1,0:T(8,128)(2,1)S(1)}, u32[]{:S(2)}, u32[]{:S(2)}) collective-permute-start(bf16[2,256,1024]{2,1,0:T(8,128)(2,1)} %get-tuple-element.217), channel_id=1, source_target_pairs={{0,1},{1,2},{2,3},{3,4},{4,5},{5,6},{6,7},{8,9},{9,10},{10,11},{11... | collective-permute-start | bytes 3145736 | tf_op jit(solution)/shard_map/ppermute | solution.py:734
  289.9 12.5 %collective-permute-start.20 = (f32[4,4,64,1024]{3,2,1,0:T(8,128)S(1)}, f32[4,4,64,1024]{3,2,1,0:T(8,128)S(1)}, u32[]{:S(2)}, u32[]{:S(2)}) collective-permute-start(f32[4,4,64,1024]{3,2,1,0:T(8,128)S(1)} %get-tuple-element.243), channel_id=1, source_target_pairs={{0,1},{1,0},{2,3},{3,2},{4,5},{5,4},{6,7},{7,6},{8,9},{9,8},{10,11... | collective-permute-start | bytes 12582920 | tf_op jit(solution)/shard_map/ppermute | solution.py:497
  295.6 21.1 %collective-permute-start.21 = (bf16[4,64,1024]{2,1,0:T(8,128)(2,1)S(1)}, bf16[4,64,1024]{2,1,0:T(8,128)(2,1)S(1)}, u32[]{:S(2)}, u32[]{:S(2)}) collective-permute-start(bf16[4,64,1024]{2,1,0:T(8,128)(2,1)S(1)} %get-tuple-element.233), channel_id=1, source_target_pairs={{0,8},{8,0},{16,24},{24,16},{1,9},{9,1},{17,25},{25,17},{2,10},{10... | collective-permute-start | bytes 1572872 | tf_op jit(solution)/shard_map/ppermute | solution.py:497
  297.1 24.9 %collective-permute-start.22 = (bf16[4,64,1024]{2,1,0:T(8,128)(2,1)S(1)}, bf16[4,64,1024]{2,1,0:T(8,128)(2,1)S(1)}, u32[]{:S(2)}, u32[]{:S(2)}) collective-permute-start(bf16[4,64,1024]{2,1,0:T(8,128)(2,1)S(1)} %get-tuple-element.234), channel_id=1, source_target_pairs={{0,16},{8,24},{16,0},{24,8},{1,17},{9,25},{17,1},{25,9},{2,18},{10... | collective-permute-start | bytes 1572872 | tf_op jit(solution)/shard_map/ppermute | solution.py:497
  298.6 23.3 %collective-permute-start.23 = (bf16[4,64,1024]{2,1,0:T(8,128)(2,1)S(1)}, bf16[4,64,1024]{2,1,0:T(8,128)(2,1)S(1)}, u32[]{:S(2)}, u32[]{:S(2)}) collective-permute-start(bf16[4,64,1024]{2,1,0:T(8,128)(2,1)S(1)} %get-tuple-element.235), channel_id=1, source_target_pairs={{0,24},{8,16},{16,8},{24,0},{1,25},{9,17},{17,9},{25,1},{2,26},{10... | collective-permute-start | bytes 1572872 | tf_op jit(solution)/shard_map/ppermute | solution.py:497
  325.3 24.5 %collective-permute-start.27 = (bf16[4,64,1024]{2,1,0:T(8,128)(2,1)}, bf16[4,64,1024]{2,1,0:T(8,128)(2,1)}, u32[]{:S(2)}, u32[]{:S(2)}) collective-permute-start(bf16[4,64,1024]{2,1,0:T(8,128)(2,1)} %get-tuple-element.261), channel_id=1, source_target_pairs={{0,8},{8,0},{16,24},{24,16},{1,9},{9,1},{17,25},{25,17},{2,10},{10... | collective-permute-start | bytes 1572872 | tf_op jit(solution)/shard_map/ppermute | solution.py:497
  326.6 23.2 %collective-permute-start.28 = (bf16[4,64,1024]{2,1,0:T(8,128)(2,1)}, bf16[4,64,1024]{2,1,0:T(8,128)(2,1)}, u32[]{:S(2)}, u32[]{:S(2)}) collective-permute-start(bf16[4,64,1024]{2,1,0:T(8,128)(2,1)} %get-tuple-element.262), channel_id=1, source_target_pairs={{0,16},{8,24},{16,0},{24,8},{1,17},{9,25},{17,1},{25,9},{2,18},{10... | collective-permute-start | bytes 1572872 | tf_op jit(solution)/shard_map/ppermute | solution.py:497
  329.0 20.6 %collective-permute-start.25 = (bf16[64,2048]{1,0:T(8,128)(2,1)S(1)}, bf16[64,2048]{1,0:T(8,128)(2,1)S(1)}, u32[]{:S(2)}, u32[]{:S(2)}) collective-permute-start(bf16[64,2048]{1,0:T(8,128)(2,1)S(1)} %get-tuple-element.257), channel_id=1, source_target_pairs={{0,4},{1,5},{2,6},{3,7},{4,0},{5,1},{6,2},{7,3},{8,12},{9,13},{10,... | collective-permute-start | bytes 786440 | tf_op jit(solution)/shard_map/ppermute | solution.py:497
  329.0 20.6 %collective-permute-start.26 = (bf16[64,2048]{1,0:T(8,128)(2,1)S(1)}, bf16[64,2048]{1,0:T(8,128)(2,1)S(1)}, u32[]{:S(2)}, u32[]{:S(2)}) collective-permute-start(bf16[64,2048]{1,0:T(8,128)(2,1)S(1)} %get-tuple-element.258), channel_id=1, source_target_pairs={{0,6},{1,7},{2,4},{3,5},{4,2},{5,3},{6,0},{7,1},{8,14},{9,15},{10,... | collective-permute-start | bytes 786440 | tf_op jit(solution)/shard_map/ppermute | solution.py:497
  338.6 12.7 %collective-permute-start.29 = (bf16[4,64,1024]{2,1,0:T(8,128)(2,1)}, bf16[4,64,1024]{2,1,0:T(8,128)(2,1)}, u32[]{:S(2)}, u32[]{:S(2)}) collective-permute-start(bf16[4,64,1024]{2,1,0:T(8,128)(2,1)} %get-tuple-element.263), channel_id=1, source_target_pairs={{0,24},{8,16},{16,8},{24,0},{1,25},{9,17},{17,9},{25,1},{2,26},{10... | collective-permute-start | bytes 1572872 | tf_op jit(solution)/shard_map/ppermute | solution.py:497
  358.9 13.1 %collective-permute-start.34 = (bf16[4,64,768]{2,1,0:T(8,128)(2,1)}, bf16[4,64,768]{2,1,0:T(8,128)(2,1)S(1)}, u32[]{:S(2)}, u32[]{:S(2)}) collective-permute-start(bf16[4,64,768]{2,1,0:T(8,128)(2,1)} %get-tuple-element.283), channel_id=1, source_target_pairs={{0,8},{8,0},{16,24},{24,16},{1,9},{9,1},{17,25},{25,17},{2,10},{10... | collective-permute-start | bytes 1179656 | tf_op jit(solution)/shard_map/ppermute | solution.py:497
  359.5 14.8 %collective-permute-start.35 = (bf16[4,64,768]{2,1,0:T(8,128)(2,1)S(1)}, bf16[4,64,768]{2,1,0:T(8,128)(2,1)S(1)}, u32[]{:S(2)}, u32[]{:S(2)}) collective-permute-start(bf16[4,64,768]{2,1,0:T(8,128)(2,1)S(1)} %get-tuple-element.285), channel_id=1, source_target_pairs={{0,16},{8,24},{16,0},{24,8},{1,17},{9,25},{17,1},{25,9},{2,18},{10... | collective-permute-start | bytes 1179656 | tf_op jit(solution)/shard_map/ppermute | solution.py:497
  361.0 18.6 %collective-permute-start.36 = (bf16[4,64,768]{2,1,0:T(8,128)(2,1)S(1)}, bf16[4,64,768]{2,1,0:T(8,128)(2,1)}, u32[]{:S(2)}, u32[]{:S(2)}) collective-permute-start(bf16[4,64,768]{2,1,0:T(8,128)(2,1)S(1)} %get-tuple-element.287), channel_id=1, source_target_pairs={{0,24},{8,16},{16,8},{24,0},{1,25},{9,17},{17,9},{25,1},{2,26},{10... | collective-permute-start | bytes 1179656 | tf_op jit(solution)/shard_map/ppermute | solution.py:497
  367.4 17.8 %collective-permute-start.32 = (bf16[64,1024]{1,0:T(8,128)(2,1)}, bf16[64,1024]{1,0:T(8,128)(2,1)}, u32[]{:S(2)}, u32[]{:S(2)}) collective-permute-start(bf16[64,1024]{1,0:T(8,128)(2,1)} %get-tuple-element.267), channel_id=1, source_target_pairs={{0,6},{1,7},{2,4},{3,5},{4,2},{5,3},{6,0},{7,1},{8,14},{9,15},{10,... | collective-permute-start | bytes 393224 | tf_op jit(solution)/shard_map/ppermute | solution.py:497
  369.0 17.9 %collective-permute-start.31 = (bf16[64,1024]{1,0:T(8,128)(2,1)}, bf16[64,1024]{1,0:T(8,128)(2,1)}, u32[]{:S(2)}, u32[]{:S(2)}) collective-permute-start(bf16[64,1024]{1,0:T(8,128)(2,1)} %get-tuple-element.266), channel_id=1, source_target_pairs={{0,4},{1,5},{2,6},{3,7},{4,0},{5,1},{6,2},{7,3},{8,12},{9,13},{10,... | collective-permute-start | bytes 393224 | tf_op jit(solution)/shard_map/ppermute | solution.py:497
  372.0 14.9 %collective-permute-start.30 = (bf16[64,1024]{1,0:T(8,128)(2,1)}, bf16[64,1024]{1,0:T(8,128)(2,1)}, u32[]{:S(2)}, u32[]{:S(2)}) collective-permute-start(bf16[64,1024]{1,0:T(8,128)(2,1)} %get-tuple-element.265), channel_id=1, source_target_pairs={{0,2},{1,3},{2,0},{3,1},{4,6},{5,7},{6,4},{7,5},{8,10},{9,11},{10,... | collective-permute-start | bytes 393224 | tf_op jit(solution)/shard_map/ppermute | solution.py:497
  389.3 16.0 %collective-permute-start.43 = (f32[64,1024]{1,0:T(8,128)S(1)}, f32[64,1024]{1,0:T(8,128)S(1)}, u32[]{:S(2)}, u32[]{:S(2)}) collective-permute-start(f32[64,1024]{1,0:T(8,128)S(1)} %copy-done.3), channel_id=1, source_target_pairs={{0,8},{8,0},{16,24},{24,16},{1,9},{9,1},{17,25},{25,17},{2,10},{10... | collective-permute-start | bytes 786440 | tf_op jit(solution)/shard_map/ppermute | solution.py:497
  390.0 18.8 %collective-permute-start.45 = (f32[64,1024]{1,0:T(8,128)S(1)}, f32[64,1024]{1,0:T(8,128)S(1)}, u32[]{:S(2)}, u32[]{:S(2)}) collective-permute-start(f32[64,1024]{1,0:T(8,128)S(1)} %copy-done.3), channel_id=1, source_target_pairs={{0,16},{8,24},{16,0},{24,8},{1,17},{9,25},{17,1},{25,9},{2,18},{10... | collective-permute-start | bytes 786440 | tf_op jit(solution)/shard_map/ppermute | solution.py:497
  391.4 17.4 %collective-permute-start.44 = (f32[64,1024]{1,0:T(8,128)S(1)}, f32[64,1024]{1,0:T(8,128)S(1)}, u32[]{:S(2)}, u32[]{:S(2)}) collective-permute-start(f32[64,1024]{1,0:T(8,128)S(1)} %copy-done.5), channel_id=1, source_target_pairs={{0,8},{8,0},{16,24},{24,16},{1,9},{9,1},{17,25},{25,17},{2,10},{10... | collective-permute-start | bytes 786440 | tf_op jit(solution)/shard_map/ppermute | solution.py:497
  393.4 13.3 %collective-permute-start.46 = (f32[64,1024]{1,0:T(8,128)S(1)}, f32[64,1024]{1,0:T(8,128)S(1)}, u32[]{:S(2)}, u32[]{:S(2)}) collective-permute-start(f32[64,1024]{1,0:T(8,128)S(1)} %copy-done.5), channel_id=1, source_target_pairs={{0,16},{8,24},{16,0},{24,8},{1,17},{9,25},{17,1},{25,9},{2,18},{10... | collective-permute-start | bytes 786440 | tf_op jit(solution)/shard_map/ppermute | solution.py:497
  (75 other events, 1226.1 us)

commit v5 on v4

--- a/solution.py
+++ b/solution.py
@@ -1093,7 +1093,7 @@
     down_total = sum_bands(down_parts)
     sorted_up = sort_shares([keep_up], [send_up], places, exact=padded, late=(down_parts[0], *first_total))
     swapped_up = swap_items([sorted_up[0]] + [after(x, *swapped_down) for x in sorted_up[1:]])
-    first_all = all_items(*[after(x, *swapped_up) for x in first_total])
+    first_all = all_items(*[after(x, sorted_up[0]) for x in first_total])
     ready = [x for pair in first_all for x in pair]
     up_total = sum_bands(sum_items([swapped_up], places, exact=padded), exact=padded)
     squares = sum(jnp.sum(jnp.square(x.astype(F32))) for x in (*first_total, down_total, up_total))

time: 454 us -> 446 us (0.982)
  waiting for transfers between devices: 55.4 us -> 44.4 us
  starting transfers between devices: 96.9 us -> 102 us
    ppermute x43, waiting for transfers between devices: 55.4 us -> 44.3 us  [exchange(): return lax.ppermute(value, axis, [(i, i ^ distance) for i in range(size)])]
    ppermute x43, starting transfers between devices: 62.4 us -> 67.2 us  [exchange(): return lax.ppermute(value, axis, [(i, i ^ distance) for i in range(size)])]
  transfers between devices with their start and end apart: 55 -> 55, of which waited for: 19 -> 18; matrix products, arithmetic and copies ran while one was open for 2% -> 2% of each run, Pallas kernels for 32% -> 32%
where the time goes in v5:
time: 446 us; the launch traced here: 441 us
  Pallas kernels  269 us (60%)
  starting transfers between devices  102 us (23%)
  waiting for transfers between devices  44.4 us (10%)
  other arithmetic  10.1 us (2%)
  between operations  7.73 us (2%)
  local copies, waits for them, and re-layouts  7.3 us (2%)
    pallas_call x19, Pallas kernels, call(): pl.pallas_call(kernel, grid=grid, out_shape=kinds[0] if single else kinds...  233 us
    ppermute x43, starting transfers between devices, exchange(): return lax.ppermute(value, axis, [(i, i ^ distance) for i in range(size)])  67.2 us
    ppermute x43, waiting for transfers between devices, exchange(): return lax.ppermute(value, axis, [(i, i ^ distance) for i in range(size)])  44.3 us
    pallas_call x8, Pallas kernels, prefetched(): pl.pallas_call(kernel, grid_spec=pltpu.PrefetchScalarGridSpec(num_scalar_...  35.6 us
    ppermute x6, starting transfers between devices, from_sides(): lax.ppermute(to_right, 'lat', up)  25.7 us
  transfers between devices with their start and end apart: 55, of which 18 were waited for; matrix products, arithmetic and copies ran while one was open for 2% of the time, Pallas kernels for 32%

profile of v5, /device:TPU:0, one launch (start us, length us, event | category | flops | bytes accessed | tf_op | source)
XLA Modules:
  0.0 440.9 jit_solution(14894910957229732693)
XLA Ops:
  4.9 18.8 %shard_map.435 = (bf16[1024,256]{1,0:T(8,128)(2,1)S(1)}, f32[1024,512]{1,0:T(8,128)}, f32[1024,512]{1,0:T(8,128)}, bf16[1024,512]{1,0:T(8,128)(2,1)}, f32[1024,2...) custom-call(s32[4,1024]{1,0:T(4,128)S(1)} %bitcast.48, ...), custom_call_target="tpu_custom_call" | custom-call | flops 177167400960 | bytes 471859200 | tf_op jit(solution)/shard_map/pallas_call | solution.py:57
  27.9 10.3 %shard_map.436.bias = f32[3,1024,1024]{2,1,0:T(8,128)} custom-call(s32[5]{0:T(128)S(1)} %stack.28.places, s32[16]{0:T(128)S(1)} %reduce.ends, s32[16,1024]{1,0:T(8,128)S(1)} %bitcast.47), custom_call_target="tpu_custom_call" | custom-call | flops 60000002048 | bytes 377487360 | tf_op jit(solution)/shard_map/pallas_call | solution.py:57
  38.3 9.7 %collective-permute-start.2 = (bf16[1024,512]{1,0:T(8,128)(2,1)}, bf16[1024,512]{1,0:T(8,128)(2,1)}, u32[]{:S(2)}, u32[]{:S(2)}) collective-permute-start(bf16[1024,512]{1,0:T(8,128)(2,1)} %get-tuple-element.173.k1.v1), channel_id=1, source_target_pairs={{0,1},{1,2},{2,3},{3,4},{4,5},{5,6},{6,7},{8,9},{9,10},{10,11},{11... | collective-permute-start | bytes 3145736 | tf_op jit(solution)/shard_map/ppermute | solution.py:734
  49.6 14.7 %shard_map.437 = (f32[256,1024]{1,0:T(8,128)}, f32[2,8,1024]{2,1,0:T(8,128)S(1)}) custom-call(bf16[512,1024]{1,0:T(8,128)(2,1)} %get-tuple-element.169.q_ref, bf16[1024,512]{1,0:T(8,128)(2,1)S(1)} %collective-permute-done.k0.v0, bf16[1024,512]{1,0:T(8,128)(2,1)} %get-tuple-element.170.k1.v1, bf16[1024,512]{1,0:T(8,128)(2,1)S(1)} %collective-permute-done.1.k2.v2, ...), custom_call_target="tpu_custom_call" | custom-call | flops 193273528320 | bytes 377487360 | tf_op jit(solution)/shard_map/pallas_call | solution.py:57
  64.3 15.3 %shard_map.438 = (f32[256,1024]{1,0:T(8,128)}, f32[2,8,1024]{2,1,0:T(8,128)S(1)}) custom-call(bf16[512,1024]{1,0:T(8,128)(2,1)} %get-tuple-element.169.q_ref, bf16[1024,512]{1,0:T(8,128)(2,1)} %collective-permute-done.2.k0.v0, bf16[1024,512]{1,0:T(8,128)(2,1)} %get-tuple-element.173.k1.v1, bf16[1024,512]{1,0:T(8,128)(2,1)} %collective-permute-done.3.k2.v2, ...), custom_call_target="tpu_custom_call" | custom-call | flops 193273528320 | bytes 377487360 | tf_op jit(solution)/shard_map/pallas_call | solution.py:57
  79.7 14.4 %shard_map.439 = (bf16[512,1024]{1,0:T(8,128)(2,1)}, f32[1024,512]{1,0:T(8,128)}, bf16[1024,512]{1,0:T(8,128)(2,1)}, f32[1024,2048]{1,0:T(8,128)}, bf16[1024,204...) custom-call(f32[256,1024]{1,0:T(8,128)} %get-tuple-element.171.o0, f32[256,1024]{1,0:T(8,128)} %get-tuple-element.174.o1, ...), custom_call_target="tpu_custom_call" | custom-call | flops 144955146240 | bytes 377487360 | tf_op jit(solution)/shard_map/pallas_call | solution.py:57
  99.0 6.7 %shard_map.440 = (bf16[3,1024,1024]{2,1,0:T(8,128)(2,1)}, f32[1024,512]{1,0:T(8,128)}) custom-call(s32[3,1024]{1,0:T(4,128)S(1)} %bitcast.49, bf16[1024,512]{1,0:T(8,128)(2,1)S(1)} %get-tuple-element.176.sent, bf16[128,1024]{1,0:T(8,128)(2,1)S(1)} %copy-done.3, bf16[2,128,512]{2,1,0:T(8,128)(2,1)S(1)} %copy-done.6), custom_call_target="tpu_custom_call" | custom-call | flops 32212254720 | bytes 377487360 | tf_op jit(solution)/shard_map/pallas_call | solution.py:57
  105.7 17.5 %shard_map.441 = (f32[1024,512]{1,0:T(8,128)}, bf16[1024,512]{1,0:T(8,128)(2,1)}, f32[1024,2048]{1,0:T(8,128)}, bf16[1024,2048]{1,0:T(8,128)(2,1)}, f32[1024,512...) custom-call(bf16[3,1024,1024]{2,1,0:T(8,128)(2,1)} %get-tuple-element.177.tally, ...), custom_call_target="tpu_custom_call" | custom-call | flops 225485783040 | bytes 377487360 | tf_op jit(solution)/shard_map/pallas_call | solution.py:57
  123.8 7.8 %collective-permute-start.6 = (f32[83,64]{0,1:T(8,128)S(1)}, f32[83,64]{0,1:T(8,128)S(1)}, u32[]{:S(2)}, u32[]{:S(2)}) collective-permute-start(f32[83,64]{0,1:T(8,128)S(1)} %fusion.1), channel_id=1, source_target_pairs={{0,1},{1,0},{2,3},{3,2},{4,5},{5,4},{6,7},{7,6},{8,9},{9,8},{10,11... | collective-permute-start | bytes 63752 | tf_op jit(solution)/shard_map/ppermute | solution.py:497
  141.9 15.2 %shard_map.442 = (bf16[1024,512]{1,0:T(8,128)(2,1)S(1)}, bf16[1024,512]{1,0:T(8,128)(2,1)S(1)}, bf16[1024,512]{1,0:T(8,128)(2,1)S(1)}, bf16[1024,2048]{1,0:T(8,1...) custom-call(bf16[128,1024]{1,0:T(8,128)(2,1)S(1)} %pad.17.grad_output, ...), custom_call_target="tpu_custom_call" | custom-call | flops 128849018880 | bytes 377487360 | tf_op jit(solution)/shard_map/pallas_call | solution.py:57
  157.1 8.1 %shard_map.443 = (bf16[1024,512]{1,0:T(8,128)(2,1)S(1)}, f32[1024,512]{1,0:T(8,128)S(1)}, bf16[1024,512]{1,0:T(8,128)(2,1)S(1)}) custom-call(s32[3,1024]{1,0:T(4,128)S(1)} %bitcast.50, bf16[1024,512]{1,0:T(8,128)(2,1)S(1)} %get-tuple-element.186.high, bf16[1024,512]{1,0:T(8,128)(2,1)S(1)} %get-tuple-element.187.low), custom_call_target="tpu_custom_call" | custom-call | flops 193273528320 | bytes 188743680 | tf_op jit(solution)/shard_map/pallas_call | solution.py:57
  168.0 10.1 %shard_map.444 = (f32[4,4,64,1024]{3,2,1,0:T(8,128)S(1)}, f32[4,4,64,1024]{3,2,1,0:T(8,128)}) custom-call(s32[5]{0:T(128)S(1)} %copy-done.8, bf16[1024,512]{1,0:T(8,128)(2,1)} %get-tuple-element.179.normed, bf16[1024,512]{1,0:T(8,128)(2,1)S(1)} %get-tuple-element.190.rounded, bf16[1024,2048]{1,0:T(8,128)(2,1)} %get-tuple-element.191.before, ...), custom_call_target="tpu_custom_call" | custom-call | flops 128849018880 | bytes 503316480 | tf_op jit(solution)/shard_map/pallas_call | solution.py:57
  181.2 13.1 %shard_map.446 = (f32[1024,512]{1,0:T(8,128)}, bf16[1024,512]{1,0:T(8,128)(2,1)S(1)}, bf16[1024,2048]{1,0:T(8,128)(2,1)}, f32[1,512]{1,0:T(1,128)S(1)}, bf16[102...) custom-call(bf16[1024,512]{1,0:T(8,128)(2,1)S(1)} %collective-permute-done.13.g0, ...), custom_call_target="tpu_custom_call" | custom-call | flops 144955146240 | bytes 377487360 | tf_op jit(solution)/shard_map/pallas_call | solution.py:57
  194.3 4.9 %shard_map.445 = (f32[4,64,1024]{2,1,0:T(8,128)S(1)}, bf16[4,64,1024]{2,1,0:T(8,128)(2,1)}, bf16[4,64,1024]{2,1,0:T(8,128)(2,1)}, bf16[4,64,1024]{2,1,0:T(8,128)(2,1)}) custom-call(s32[5]{0:T(128)S(1)} %copy-done.9, f32[4,4,64,1024]{3,2,1,0:T(8,128)S(1)} %get-tuple-element.193.refs_0_, f32[4,4,64,1024]{3,2,1,0:T(8,128)} %collective-permute-done.9.refs_1_), custom_call_target="tpu_custom_call" | custom-call | flops 440401920 | bytes 440401920 | tf_op jit(solution)/shard_map/pallas_call | solution.py:501
  202.7 22.0 %shard_map.448 = (f32[256,1024]{1,0:T(8,128)}, bf16[2,256,1024]{2,1,0:T(8,128)(2,1)}, f32[2,256,1024]{2,1,0:T(8,128)}, bf16[2,256,1024]{2,1,0:T(8,128)(2,1)}) custom-call(bf16[512,1024]{1,0:T(8,128)(2,1)} %get-tuple-element.169.q_ref, bf16[512,1024]{1,0:T(8,128)(2,1)S(1)} %get-tuple-element.206.do_ref, f32[2,8,1024]{2,1,0:T(8,128)S(1)} %get-tuple-element.211.lse_ref, ...), custom_call_target="tpu_custom_call" | custom-call | flops 483183820800 | bytes 377487360 | tf_op jit(solution)/shard_map/pallas_call | solution.py:57
  224.7 5.8 %collective-permute-start.15 = (bf16[2,256,1024]{2,1,0:T(8,128)(2,1)}, bf16[2,256,1024]{2,1,0:T(8,128)(2,1)}, u32[]{:S(2)}, u32[]{:S(2)}) collective-permute-start(bf16[2,256,1024]{2,1,0:T(8,128)(2,1)} %get-tuple-element.212), channel_id=1, source_target_pairs={{0,1},{1,2},{2,3},{3,4},{4,5},{5,6},{6,7},{8,9},{9,10},{10,11},{11... | collective-permute-start | bytes 3145736 | tf_op jit(solution)/shard_map/ppermute | solution.py:734
  231.9 22.1 %shard_map.447 = (f32[256,1024]{1,0:T(8,128)}, bf16[2,256,1024]{2,1,0:T(8,128)(2,1)}, f32[2,256,1024]{2,1,0:T(8,128)}, bf16[2,256,1024]{2,1,0:T(8,128)(2,1)}) custom-call(bf16[512,1024]{1,0:T(8,128)(2,1)} %get-tuple-element.169.q_ref, bf16[512,1024]{1,0:T(8,128)(2,1)S(1)} %get-tuple-element.206.do_ref, f32[2,8,1024]{2,1,0:T(8,128)S(1)} %get-tuple-element.207.lse_ref, ...), custom_call_target="tpu_custom_call" | custom-call | flops 483183820800 | bytes 377487360 | tf_op jit(solution)/shard_map/pallas_call | solution.py:57
  254.1 3.3 collective-permute-start.17
  258.7 8.7 %shard_map.449 = (f32[4,4,64,1024]{3,2,1,0:T(8,128)S(1)}, f32[4,4,64,1024]{3,2,1,0:T(8,128)S(1)}) custom-call(s32[5]{0:T(128)S(1)} %copy-done.10, bf16[1024,512]{1,0:T(8,128)(2,1)} %get-tuple-element.199.normed, bf16[1024,512]{1,0:T(8,128)(2,1)S(1)} %get-tuple-element.218.rounded, bf16[1024,2048]{1,0:T(8,128)(2,1)} %get-tuple-element.219.before, ...), custom_call_target="tpu_custom_call" | custom-call | flops 128849018880 | bytes 503316480 | tf_op jit(solution)/shard_map/pallas_call | solution.py:57
  269.1 7.4 %shard_map.450 = (f32[1024,512]{1,0:T(8,128)S(1)}, bf16[1024,512]{1,0:T(8,128)(2,1)S(1)}, bf16[1536,1024]{1,0:T(8,128)(2,1)S(1)}, f32[1,512]{1,0:T(1,128)S(1)}) custom-call(f32[256,1024]{1,0:T(8,128)} %get-tuple-element.222.dq0, f32[256,1024]{1,0:T(8,128)} %get-tuple-element.223.dq1, bf16[2,256,1024]{2,1,0:T(8,128)(2,1)} %collective-permute-done.15.left0, ...), custom_call_target="tpu_custom_call" | custom-call | flops 48318382080 | bytes 377487360 | tf_op jit(solution)/shard_map/pallas_call | solution.py:57
  280.8 9.1 %shard_map.452 = (f32[4,4,64,1024]{3,2,1,0:T(8,128)S(1)}, f32[4,4,64,1024]{3,2,1,0:T(8,128)S(1)}) custom-call(s32[5]{0:T(128)S(1)} %copy-done.10, bf16[1024,512]{1,0:T(8,128)(2,1)S(1)} %get-tuple-element.236.rounded, bf16[1024,2048]{1,0:T(8,128)(2,1)} %get-tuple-element.237.active, bf16[1024,512]{1,0:T(8,128)(2,1)} %get-tuple-element.238.normed_attn, ...), custom_call_target="tpu_custom_call" | custom-call | flops 128849018880 | bytes 503316480 | tf_op jit(solution)/shard_map/pallas_call | solution.py:57
  289.9 5.7 %collective-permute-start.20 = (f32[4,4,64,1024]{3,2,1,0:T(8,128)S(1)}, f32[4,4,64,1024]{3,2,1,0:T(8,128)S(1)}, u32[]{:S(2)}, u32[]{:S(2)}) collective-permute-start(f32[4,4,64,1024]{3,2,1,0:T(8,128)S(1)} %get-tuple-element.243), channel_id=1, source_target_pairs={{0,1},{1,0},{2,3},{3,2},{4,5},{5,4},{6,7},{7,6},{8,9},{9,8},{10,11... | collective-permute-start | bytes 12582920 | tf_op jit(solution)/shard_map/ppermute | solution.py:497
  299.1 3.3 collective-permute-done.20.refs_1_
  304.8 11.9 %shard_map.454 = (bf16[1024,2048]{1,0:T(8,128)(2,1)}, f32[512,128]{1,0:T(8,128)S(1)}, f32[1,512]{1,0:T(1,128)S(1)}, bf16[1024,512]{1,0:T(8,128)(2,1)}) custom-call(f32[1024,512]{1,0:T(8,128)S(1)} %copy-done.27, f32[1024,512]{1,0:T(8,128)} %get-tuple-element.249.pooled, f32[1024,2048]{1,0:T(8,128)} %get-tuple-element.250.slope, f32[5,512]{1,0:T(8,128)S(1)} %copy-done.13, ...), custom_call_target="tpu_custom_call" | custom-call | flops 128849018880 | bytes 377487360 | tf_op jit(solution)/shard_map/pallas_call | solution.py:57
  316.7 5.2 %collective-permute-done.22.refs_6_ = bf16[4,64,1024]{2,1,0:T(8,128)(2,1)S(1)} collective-permute-done((bf16[4,64,1024]{2,1,0:T(8,128)(2,1)S(1)}, bf16[4,64,1024]{2,1,0:T(8,128)(2,1)S(1)}, u32[]{:S(2)}, u32[]{:S(2)}) %collective-permute-start.22) | collective-permute-done | bytes 524320 | tf_op jit(solution)/shard_map/ppermute | solution.py:497
  331.9 6.8 %shard_map.458 = (f32[4,4,64,640]{3,2,1,0:T(8,128)S(1)}, f32[4,4,64,640]{3,2,1,0:T(8,128)}) custom-call(s32[5]{0:T(128)S(1)} %copy-done.10, bf16[1024,512]{1,0:T(8,128)(2,1)} %get-tuple-element.268.normed, bf16[1024,2048]{1,0:T(8,128)(2,1)} %get-tuple-element.269.before, f32[512,128]{1,0:T(8,128)S(1)} %get-tuple-element.270.table_in, ...), custom_call_target="tpu_custom_call" | custom-call | flops 64424509440 | bytes 314572800 | tf_op jit(solution)/shard_map/pallas_call | solution.py:57
  340.1 9.6 %collective-permute-done.25.refs_1_ = bf16[64,2048]{1,0:T(8,128)(2,1)S(1)} collective-permute-done((bf16[64,2048]{1,0:T(8,128)(2,1)S(1)}, bf16[64,2048]{1,0:T(8,128)(2,1)S(1)}, u32[]{:S(2)}, u32[]{:S(2)}) %collective-permute-start.25) | collective-permute-done | bytes 262176 | tf_op jit(solution)/shard_map/ppermute | solution.py:497
  351.3 3.7 shard_map.457
  369.4 3.2 collective-permute-start.31
  400.6 3.3 collective-permute-done.42
  413.0 3.4 collective-permute-done.52.refs_9_
  423.5 16.0 %shard_map.461 = (f32[3,64,4096]{2,1,0:T(8,128)}, f32[3,64,4096]{2,1,0:T(8,128)}, f32[3,64,4096]{2,1,0:T(8,128)}, f32[3,64,4096]{2,1,0:T(8,128)}, bf16[3,64,4096...) custom-call(s32[5]{0:T(128)S(1)} %copy-done.11, ...), custom_call_target="tpu_custom_call" | custom-call | flops 935854080 | bytes 935854080 | tf_op jit(solution)/shard_map/pallas_call | solution.py:501
  (233 shorter events, 115.9 us)
Async XLA Ops:
  23.8 14.5 %collective-permute-start = (bf16[1024,512]{1,0:T(8,128)(2,1)}, bf16[1024,512]{1,0:T(8,128)(2,1)S(1)}, u32[]{:S(2)}, u32[]{:S(2)}) collective-permute-start(bf16[1024,512]{1,0:T(8,128)(2,1)} %get-tuple-element.170.k1.v1), channel_id=1, source_target_pairs={{0,1},{1,2},{2,3},{3,4},{4,5},{5,6},{6,7},{8,9},{9,10},{10,11},{11... | collective-permute-start | bytes 3145736 | tf_op jit(solution)/shard_map/ppermute | solution.py:734
  38.3 26.0 %collective-permute-start.2 = (bf16[1024,512]{1,0:T(8,128)(2,1)}, bf16[1024,512]{1,0:T(8,128)(2,1)}, u32[]{:S(2)}, u32[]{:S(2)}) collective-permute-start(bf16[1024,512]{1,0:T(8,128)(2,1)} %get-tuple-element.173.k1.v1), channel_id=1, source_target_pairs={{0,1},{1,2},{2,3},{3,4},{4,5},{5,6},{6,7},{8,9},{9,10},{10,11},{11... | collective-permute-start | bytes 3145736 | tf_op jit(solution)/shard_map/ppermute | solution.py:734
  48.0 16.2 %collective-permute-start.3 = (bf16[1024,512]{1,0:T(8,128)(2,1)}, bf16[1024,512]{1,0:T(8,128)(2,1)}, u32[]{:S(2)}, u32[]{:S(2)}) collective-permute-start(bf16[1024,512]{1,0:T(8,128)(2,1)} %get-tuple-element.173.k1.v1), channel_id=1, source_target_pairs={{1,0},{2,1},{3,2},{4,3},{5,4},{6,5},{7,6},{9,8},{10,9},{11,10},{12... | collective-permute-start | bytes 3145736 | tf_op jit(solution)/shard_map/ppermute | solution.py:734
  165.2 16.0 %collective-permute-start.13 = (bf16[1024,512]{1,0:T(8,128)(2,1)S(1)}, bf16[1024,512]{1,0:T(8,128)(2,1)S(1)}, u32[]{:S(2)}, u32[]{:S(2)}) collective-permute-start(bf16[1024,512]{1,0:T(8,128)(2,1)S(1)} %get-tuple-element.189), channel_id=1, source_target_pairs={{0,1},{1,2},{2,3},{3,4},{4,5},{5,6},{6,7},{8,9},{9,10},{10,11},{11... | collective-permute-start | bytes 3145736 | tf_op jit(solution)/shard_map/ppermute | solution.py:734
  166.5 14.6 %collective-permute-start.14 = (bf16[1024,512]{1,0:T(8,128)(2,1)S(1)}, bf16[1024,512]{1,0:T(8,128)(2,1)S(1)}, u32[]{:S(2)}, u32[]{:S(2)}) collective-permute-start(bf16[1024,512]{1,0:T(8,128)(2,1)S(1)} %get-tuple-element.188), channel_id=1, source_target_pairs={{1,0},{2,1},{3,2},{4,3},{5,4},{6,5},{7,6},{9,8},{10,9},{11,10},{12... | collective-permute-start | bytes 3145736 | tf_op jit(solution)/shard_map/ppermute | solution.py:734
  178.1 16.2 %collective-permute-start.9 = (f32[4,4,64,1024]{3,2,1,0:T(8,128)}, f32[4,4,64,1024]{3,2,1,0:T(8,128)}, u32[]{:S(2)}, u32[]{:S(2)}) collective-permute-start(f32[4,4,64,1024]{3,2,1,0:T(8,128)} %get-tuple-element.194), channel_id=1, source_target_pairs={{0,1},{1,0},{2,3},{3,2},{4,5},{5,4},{6,7},{7,6},{8,9},{9,8},{10,11... | collective-permute-start | bytes 12582920 | tf_op jit(solution)/shard_map/ppermute | solution.py:497
  199.2 32.6 %collective-permute-start.10 = (bf16[4,64,1024]{2,1,0:T(8,128)(2,1)}, bf16[4,64,1024]{2,1,0:T(8,128)(2,1)}, u32[]{:S(2)}, u32[]{:S(2)}) collective-permute-start(bf16[4,64,1024]{2,1,0:T(8,128)(2,1)} %get-tuple-element.196), channel_id=1, source_target_pairs={{0,8},{8,0},{16,24},{24,16},{1,9},{9,1},{17,25},{25,17},{2,10},{10... | collective-permute-start | bytes 1572872 | tf_op jit(solution)/shard_map/ppermute | solution.py:497
  200.7 31.2 %collective-permute-start.11 = (bf16[4,64,1024]{2,1,0:T(8,128)(2,1)}, bf16[4,64,1024]{2,1,0:T(8,128)(2,1)}, u32[]{:S(2)}, u32[]{:S(2)}) collective-permute-start(bf16[4,64,1024]{2,1,0:T(8,128)(2,1)} %get-tuple-element.197), channel_id=1, source_target_pairs={{0,16},{8,24},{16,0},{24,8},{1,17},{9,25},{17,1},{25,9},{2,18},{10... | collective-permute-start | bytes 1572872 | tf_op jit(solution)/shard_map/ppermute | solution.py:497
  202.2 29.7 %collective-permute-start.12 = (bf16[4,64,1024]{2,1,0:T(8,128)(2,1)}, bf16[4,64,1024]{2,1,0:T(8,128)(2,1)}, u32[]{:S(2)}, u32[]{:S(2)}) collective-permute-start(bf16[4,64,1024]{2,1,0:T(8,128)(2,1)} %get-tuple-element.198), channel_id=1, source_target_pairs={{0,24},{8,16},{16,8},{24,0},{1,25},{9,17},{17,9},{25,1},{2,26},{10... | collective-permute-start | bytes 1572872 | tf_op jit(solution)/shard_map/ppermute | solution.py:497
  224.7 29.3 %collective-permute-start.15 = (bf16[2,256,1024]{2,1,0:T(8,128)(2,1)}, bf16[2,256,1024]{2,1,0:T(8,128)(2,1)}, u32[]{:S(2)}, u32[]{:S(2)}) collective-permute-start(bf16[2,256,1024]{2,1,0:T(8,128)(2,1)} %get-tuple-element.212), channel_id=1, source_target_pairs={{0,1},{1,2},{2,3},{3,4},{4,5},{5,6},{6,7},{8,9},{9,10},{10,11},{11... | collective-permute-start | bytes 3145736 | tf_op jit(solution)/shard_map/ppermute | solution.py:734
  230.6 23.5 %collective-permute-start.16 = (bf16[2,256,1024]{2,1,0:T(8,128)(2,1)}, bf16[2,256,1024]{2,1,0:T(8,128)(2,1)}, u32[]{:S(2)}, u32[]{:S(2)}) collective-permute-start(bf16[2,256,1024]{2,1,0:T(8,128)(2,1)} %get-tuple-element.214), channel_id=1, source_target_pairs={{1,0},{2,1},{3,2},{4,3},{5,4},{6,5},{7,6},{9,8},{10,9},{11,10},{12... | collective-permute-start | bytes 3145736 | tf_op jit(solution)/shard_map/ppermute | solution.py:734
  254.1 15.0 %collective-permute-start.17 = (bf16[2,256,1024]{2,1,0:T(8,128)(2,1)}, bf16[2,256,1024]{2,1,0:T(8,128)(2,1)S(1)}, u32[]{:S(2)}, u32[]{:S(2)}) collective-permute-start(bf16[2,256,1024]{2,1,0:T(8,128)(2,1)} %get-tuple-element.217), channel_id=1, source_target_pairs={{0,1},{1,2},{2,3},{3,4},{4,5},{5,6},{6,7},{8,9},{9,10},{10,11},{11... | collective-permute-start | bytes 3145736 | tf_op jit(solution)/shard_map/ppermute | solution.py:734
  289.9 12.5 %collective-permute-start.20 = (f32[4,4,64,1024]{3,2,1,0:T(8,128)S(1)}, f32[4,4,64,1024]{3,2,1,0:T(8,128)S(1)}, u32[]{:S(2)}, u32[]{:S(2)}) collective-permute-start(f32[4,4,64,1024]{3,2,1,0:T(8,128)S(1)} %get-tuple-element.243), channel_id=1, source_target_pairs={{0,1},{1,0},{2,3},{3,2},{4,5},{5,4},{6,7},{7,6},{8,9},{9,8},{10,11... | collective-permute-start | bytes 12582920 | tf_op jit(solution)/shard_map/ppermute | solution.py:497
  295.6 21.1 %collective-permute-start.21 = (bf16[4,64,1024]{2,1,0:T(8,128)(2,1)S(1)}, bf16[4,64,1024]{2,1,0:T(8,128)(2,1)S(1)}, u32[]{:S(2)}, u32[]{:S(2)}) collective-permute-start(bf16[4,64,1024]{2,1,0:T(8,128)(2,1)S(1)} %get-tuple-element.233), channel_id=1, source_target_pairs={{0,8},{8,0},{16,24},{24,16},{1,9},{9,1},{17,25},{25,17},{2,10},{10... | collective-permute-start | bytes 1572872 | tf_op jit(solution)/shard_map/ppermute | solution.py:497
  297.1 24.9 %collective-permute-start.22 = (bf16[4,64,1024]{2,1,0:T(8,128)(2,1)S(1)}, bf16[4,64,1024]{2,1,0:T(8,128)(2,1)S(1)}, u32[]{:S(2)}, u32[]{:S(2)}) collective-permute-start(bf16[4,64,1024]{2,1,0:T(8,128)(2,1)S(1)} %get-tuple-element.234), channel_id=1, source_target_pairs={{0,16},{8,24},{16,0},{24,8},{1,17},{9,25},{17,1},{25,9},{2,18},{10... | collective-permute-start | bytes 1572872 | tf_op jit(solution)/shard_map/ppermute | solution.py:497
  298.6 23.3 %collective-permute-start.23 = (bf16[4,64,1024]{2,1,0:T(8,128)(2,1)S(1)}, bf16[4,64,1024]{2,1,0:T(8,128)(2,1)S(1)}, u32[]{:S(2)}, u32[]{:S(2)}) collective-permute-start(bf16[4,64,1024]{2,1,0:T(8,128)(2,1)S(1)} %get-tuple-element.235), channel_id=1, source_target_pairs={{0,24},{8,16},{16,8},{24,0},{1,25},{9,17},{17,9},{25,1},{2,26},{10... | collective-permute-start | bytes 1572872 | tf_op jit(solution)/shard_map/ppermute | solution.py:497
  325.3 25.2 %collective-permute-start.27 = (bf16[4,64,1024]{2,1,0:T(8,128)(2,1)}, bf16[4,64,1024]{2,1,0:T(8,128)(2,1)}, u32[]{:S(2)}, u32[]{:S(2)}) collective-permute-start(bf16[4,64,1024]{2,1,0:T(8,128)(2,1)} %get-tuple-element.261), channel_id=1, source_target_pairs={{0,8},{8,0},{16,24},{24,16},{1,9},{9,1},{17,25},{25,17},{2,10},{10... | collective-permute-start | bytes 1572872 | tf_op jit(solution)/shard_map/ppermute | solution.py:497
  326.6 23.9 %collective-permute-start.28 = (bf16[4,64,1024]{2,1,0:T(8,128)(2,1)}, bf16[4,64,1024]{2,1,0:T(8,128)(2,1)}, u32[]{:S(2)}, u32[]{:S(2)}) collective-permute-start(bf16[4,64,1024]{2,1,0:T(8,128)(2,1)} %get-tuple-element.262), channel_id=1, source_target_pairs={{0,16},{8,24},{16,0},{24,8},{1,17},{9,25},{17,1},{25,9},{2,18},{10... | collective-permute-start | bytes 1572872 | tf_op jit(solution)/shard_map/ppermute | solution.py:497
  329.1 20.6 %collective-permute-start.25 = (bf16[64,2048]{1,0:T(8,128)(2,1)S(1)}, bf16[64,2048]{1,0:T(8,128)(2,1)S(1)}, u32[]{:S(2)}, u32[]{:S(2)}) collective-permute-start(bf16[64,2048]{1,0:T(8,128)(2,1)S(1)} %get-tuple-element.257), channel_id=1, source_target_pairs={{0,4},{1,5},{2,6},{3,7},{4,0},{5,1},{6,2},{7,3},{8,12},{9,13},{10,... | collective-permute-start | bytes 786440 | tf_op jit(solution)/shard_map/ppermute | solution.py:497
  329.1 20.6 %collective-permute-start.26 = (bf16[64,2048]{1,0:T(8,128)(2,1)S(1)}, bf16[64,2048]{1,0:T(8,128)(2,1)S(1)}, u32[]{:S(2)}, u32[]{:S(2)}) collective-permute-start(bf16[64,2048]{1,0:T(8,128)(2,1)S(1)} %get-tuple-element.258), channel_id=1, source_target_pairs={{0,6},{1,7},{2,4},{3,5},{4,2},{5,3},{6,0},{7,1},{8,14},{9,15},{10,... | collective-permute-start | bytes 786440 | tf_op jit(solution)/shard_map/ppermute | solution.py:497
  338.7 12.7 %collective-permute-start.29 = (bf16[4,64,1024]{2,1,0:T(8,128)(2,1)}, bf16[4,64,1024]{2,1,0:T(8,128)(2,1)}, u32[]{:S(2)}, u32[]{:S(2)}) collective-permute-start(bf16[4,64,1024]{2,1,0:T(8,128)(2,1)} %get-tuple-element.263), channel_id=1, source_target_pairs={{0,24},{8,16},{16,8},{24,0},{1,25},{9,17},{17,9},{25,1},{2,26},{10... | collective-permute-start | bytes 1572872 | tf_op jit(solution)/shard_map/ppermute | solution.py:497
  358.2 14.4 %collective-permute-start.34 = (bf16[4,64,768]{2,1,0:T(8,128)(2,1)S(1)}, bf16[4,64,768]{2,1,0:T(8,128)(2,1)S(1)}, u32[]{:S(2)}, u32[]{:S(2)}) collective-permute-start(bf16[4,64,768]{2,1,0:T(8,128)(2,1)S(1)} %get-tuple-element.283), channel_id=1, source_target_pairs={{0,8},{8,0},{16,24},{24,16},{1,9},{9,1},{17,25},{25,17},{2,10},{10... | collective-permute-start | bytes 1179656 | tf_op jit(solution)/shard_map/ppermute | solution.py:497
  358.8 17.3 %collective-permute-start.35 = (bf16[4,64,768]{2,1,0:T(8,128)(2,1)S(1)}, bf16[4,64,768]{2,1,0:T(8,128)(2,1)S(1)}, u32[]{:S(2)}, u32[]{:S(2)}) collective-permute-start(bf16[4,64,768]{2,1,0:T(8,128)(2,1)S(1)} %get-tuple-element.285), channel_id=1, source_target_pairs={{0,16},{8,24},{16,0},{24,8},{1,17},{9,25},{17,1},{25,9},{2,18},{10... | collective-permute-start | bytes 1179656 | tf_op jit(solution)/shard_map/ppermute | solution.py:497
  360.3 19.3 %collective-permute-start.36 = (bf16[4,64,768]{2,1,0:T(8,128)(2,1)S(1)}, bf16[4,64,768]{2,1,0:T(8,128)(2,1)S(1)}, u32[]{:S(2)}, u32[]{:S(2)}) collective-permute-start(bf16[4,64,768]{2,1,0:T(8,128)(2,1)S(1)} %get-tuple-element.287), channel_id=1, source_target_pairs={{0,24},{8,16},{16,8},{24,0},{1,25},{9,17},{17,9},{25,1},{2,26},{10... | collective-permute-start | bytes 1179656 | tf_op jit(solution)/shard_map/ppermute | solution.py:497
  367.8 14.3 %collective-permute-start.32 = (bf16[64,1024]{1,0:T(8,128)(2,1)}, bf16[64,1024]{1,0:T(8,128)(2,1)}, u32[]{:S(2)}, u32[]{:S(2)}) collective-permute-start(bf16[64,1024]{1,0:T(8,128)(2,1)} %get-tuple-element.267), channel_id=1, source_target_pairs={{0,6},{1,7},{2,4},{3,5},{4,2},{5,3},{6,0},{7,1},{8,14},{9,15},{10,... | collective-permute-start | bytes 393224 | tf_op jit(solution)/shard_map/ppermute | solution.py:497
  369.4 14.0 %collective-permute-start.31 = (bf16[64,1024]{1,0:T(8,128)(2,1)}, bf16[64,1024]{1,0:T(8,128)(2,1)}, u32[]{:S(2)}, u32[]{:S(2)}) collective-permute-start(bf16[64,1024]{1,0:T(8,128)(2,1)} %get-tuple-element.266), channel_id=1, source_target_pairs={{0,4},{1,5},{2,6},{3,7},{4,0},{5,1},{6,2},{7,3},{8,12},{9,13},{10,... | collective-permute-start | bytes 393224 | tf_op jit(solution)/shard_map/ppermute | solution.py:497
  372.6 13.6 %collective-permute-start.30 = (bf16[64,1024]{1,0:T(8,128)(2,1)}, bf16[64,1024]{1,0:T(8,128)(2,1)}, u32[]{:S(2)}, u32[]{:S(2)}) collective-permute-start(bf16[64,1024]{1,0:T(8,128)(2,1)} %get-tuple-element.265), channel_id=1, source_target_pairs={{0,2},{1,3},{2,0},{3,1},{4,6},{5,7},{6,4},{7,5},{8,10},{9,11},{10,... | collective-permute-start | bytes 393224 | tf_op jit(solution)/shard_map/ppermute | solution.py:497
  376.2 12.8 %collective-permute-start.43 = (f32[64,1024]{1,0:T(8,128)}, f32[64,1024]{1,0:T(8,128)}, u32[]{:S(2)}, u32[]{:S(2)}) collective-permute-start(f32[64,1024]{1,0:T(8,128)} %get-tuple-element.292.refs_0_), channel_id=1, source_target_pairs={{0,8},{8,0},{16,24},{24,16},{1,9},{9,1},{17,25},{25,17},{2,10},{10... | collective-permute-start | bytes 786440 | tf_op jit(solution)/shard_map/ppermute | solution.py:497
  389.0 16.9 %collective-permute-start.44 = (f32[64,1024]{1,0:T(8,128)}, f32[64,1024]{1,0:T(8,128)S(1)}, u32[]{:S(2)}, u32[]{:S(2)}) collective-permute-start(f32[64,1024]{1,0:T(8,128)} %get-tuple-element.293.refs_4_), channel_id=1, source_target_pairs={{0,8},{8,0},{16,24},{24,16},{1,9},{9,1},{17,25},{25,17},{2,10},{10... | collective-permute-start | bytes 786440 | tf_op jit(solution)/shard_map/ppermute | solution.py:497
  389.2 16.7 %collective-permute-start.45 = (f32[64,1024]{1,0:T(8,128)}, f32[64,1024]{1,0:T(8,128)S(1)}, u32[]{:S(2)}, u32[]{:S(2)}) collective-permute-start(f32[64,1024]{1,0:T(8,128)} %get-tuple-element.292.refs_0_), channel_id=1, source_target_pairs={{0,16},{8,24},{16,0},{24,8},{1,17},{9,25},{17,1},{25,9},{2,18},{10... | collective-permute-start | bytes 786440 | tf_op jit(solution)/shard_map/ppermute | solution.py:497
  390.7 15.2 %collective-permute-start.47 = (f32[64,1024]{1,0:T(8,128)}, f32[64,1024]{1,0:T(8,128)S(1)}, u32[]{:S(2)}, u32[]{:S(2)}) collective-permute-start(f32[64,1024]{1,0:T(8,128)} %collective-permute-done.43.refs_1_), channel_id=1, source_target_pairs={{0,16},{8,24},{16,0},{24,8},{1,17},{9,25},{17,1},{25,9},{2,18},{10... | collective-permute-start | bytes 786440 | tf_op jit(solution)/shard_map/ppermute | solution.py:497
  391.9 14.0 %collective-permute-start.48 = (f32[64,1024]{1,0:T(8,128)}, f32[64,1024]{1,0:T(8,128)S(1)}, u32[]{:S(2)}, u32[]{:S(2)}) collective-permute-start(f32[64,1024]{1,0:T(8,128)} %collective-permute-done.46.refs_6_), channel_id=1, source_target_pairs={{0,8},{8,0},{16,24},{24,16},{1,9},{9,1},{17,25},{25,17},{2,10},{10... | collective-permute-start | bytes 786440 | tf_op jit(solution)/shard_map/ppermute | solution.py:497
  (69 other events, 1061.3 us)

commit v6 on v5

--- a/solution.py
+++ b/solution.py
@@ -1094,7 +1094,7 @@
     sorted_up = sort_shares([keep_up], [send_up], places, exact=padded, late=(down_parts[0], *first_total))
     swapped_up = swap_items([sorted_up[0]] + [after(x, *swapped_down) for x in sorted_up[1:]])
     first_all = all_items(*[after(x, sorted_up[0]) for x in first_total])
-    ready = [x for pair in first_all for x in pair]
+    ready = [x for pair in first_all[:3] for x in pair]
     up_total = sum_bands(sum_items([swapped_up], places, exact=padded), exact=padded)
     squares = sum(jnp.sum(jnp.square(x.astype(F32))) for x in (*first_total, down_total, up_total))
     scalars = sum_over(jnp.stack([squares, loss_item])[None], "lat")

time: 446 us -> 453 us (1.016)
  waiting for transfers between devices: 44.4 us -> 54.3 us
  starting transfers between devices: 102 us -> 97.3 us
    ppermute x43, waiting for transfers between devices: 44.3 us -> 54.2 us  [exchange(): return lax.ppermute(value, axis, [(i, i ^ distance) for i in range(size)])]
  transfers between devices with their start and end apart: 55 -> 55, of which waited for: 18 -> 19; matrix products, arithmetic and copies ran while one was open for 2% -> 2% of each run, Pallas kernels for 32% -> 32%
where the time goes in v6:
time: 453 us; the launch traced here: 447 us
  Pallas kernels  270 us (60%)
  starting transfers between devices  97.3 us (21%)
  waiting for transfers between devices  54.3 us (12%)
  other arithmetic  9.11 us (2%)
  between operations  7.81 us (2%)
  local copies, waits for them, and re-layouts  7.43 us (2%)
    pallas_call x19, Pallas kernels, call(): pl.pallas_call(kernel, grid=grid, out_shape=kinds[0] if single else kinds...  232 us
    ppermute x43, starting transfers between devices, exchange(): return lax.ppermute(value, axis, [(i, i ^ distance) for i in range(size)])  62.9 us
    ppermute x43, waiting for transfers between devices, exchange(): return lax.ppermute(value, axis, [(i, i ^ distance) for i in range(size)])  54.2 us
    pallas_call x8, Pallas kernels, prefetched(): pl.pallas_call(kernel, grid_spec=pltpu.PrefetchScalarGridSpec(num_scalar_...  38.1 us
    ppermute x6, starting transfers between devices, from_sides(): lax.ppermute(to_right, 'lat', up)  25.7 us
  transfers between devices with their start and end apart: 55, of which 19 were waited for; matrix products, arithmetic and copies ran while one was open for 2% of the time, Pallas kernels for 32%

profile of v6, /device:TPU:0, one launch (start us, length us, event | category | flops | bytes accessed | tf_op | source)
XLA Modules:
  0.0 447.4 jit_solution(4206823527703552872)
XLA Ops:
  4.9 18.8 %shard_map.435 = (bf16[1024,256]{1,0:T(8,128)(2,1)S(1)}, f32[1024,512]{1,0:T(8,128)}, f32[1024,512]{1,0:T(8,128)}, bf16[1024,512]{1,0:T(8,128)(2,1)}, f32[1024,2...) custom-call(s32[4,1024]{1,0:T(4,128)S(1)} %bitcast.48, ...), custom_call_target="tpu_custom_call" | custom-call | flops 177167400960 | bytes 471859200 | tf_op jit(solution)/shard_map/pallas_call | solution.py:57
  27.9 10.3 %shard_map.436.bias = f32[3,1024,1024]{2,1,0:T(8,128)} custom-call(s32[5]{0:T(128)S(1)} %stack.28.places, s32[16]{0:T(128)S(1)} %reduce.ends, s32[16,1024]{1,0:T(8,128)S(1)} %bitcast.47), custom_call_target="tpu_custom_call" | custom-call | flops 60000002048 | bytes 377487360 | tf_op jit(solution)/shard_map/pallas_call | solution.py:57
  38.3 9.8 %collective-permute-start.2 = (bf16[1024,512]{1,0:T(8,128)(2,1)}, bf16[1024,512]{1,0:T(8,128)(2,1)}, u32[]{:S(2)}, u32[]{:S(2)}) collective-permute-start(bf16[1024,512]{1,0:T(8,128)(2,1)} %get-tuple-element.173.k1.v1), channel_id=1, source_target_pairs={{0,1},{1,2},{2,3},{3,4},{4,5},{5,6},{6,7},{8,9},{9,10},{10,11},{11... | collective-permute-start | bytes 3145736 | tf_op jit(solution)/shard_map/ppermute | solution.py:734
  49.6 14.6 %shard_map.437 = (f32[256,1024]{1,0:T(8,128)}, f32[2,8,1024]{2,1,0:T(8,128)S(1)}) custom-call(bf16[512,1024]{1,0:T(8,128)(2,1)} %get-tuple-element.169.q_ref, bf16[1024,512]{1,0:T(8,128)(2,1)S(1)} %collective-permute-done.k0.v0, bf16[1024,512]{1,0:T(8,128)(2,1)} %get-tuple-element.170.k1.v1, bf16[1024,512]{1,0:T(8,128)(2,1)S(1)} %collective-permute-done.1.k2.v2, ...), custom_call_target="tpu_custom_call" | custom-call | flops 193273528320 | bytes 377487360 | tf_op jit(solution)/shard_map/pallas_call | solution.py:57
  64.3 15.3 %shard_map.438 = (f32[256,1024]{1,0:T(8,128)}, f32[2,8,1024]{2,1,0:T(8,128)S(1)}) custom-call(bf16[512,1024]{1,0:T(8,128)(2,1)} %get-tuple-element.169.q_ref, bf16[1024,512]{1,0:T(8,128)(2,1)} %collective-permute-done.2.k0.v0, bf16[1024,512]{1,0:T(8,128)(2,1)} %get-tuple-element.173.k1.v1, bf16[1024,512]{1,0:T(8,128)(2,1)} %collective-permute-done.3.k2.v2, ...), custom_call_target="tpu_custom_call" | custom-call | flops 193273528320 | bytes 377487360 | tf_op jit(solution)/shard_map/pallas_call | solution.py:57
  79.6 14.4 %shard_map.439 = (bf16[512,1024]{1,0:T(8,128)(2,1)}, f32[1024,512]{1,0:T(8,128)}, bf16[1024,512]{1,0:T(8,128)(2,1)}, f32[1024,2048]{1,0:T(8,128)}, bf16[1024,204...) custom-call(f32[256,1024]{1,0:T(8,128)} %get-tuple-element.171.o0, f32[256,1024]{1,0:T(8,128)} %get-tuple-element.174.o1, ...), custom_call_target="tpu_custom_call" | custom-call | flops 144955146240 | bytes 377487360 | tf_op jit(solution)/shard_map/pallas_call | solution.py:57
  99.0 6.7 %shard_map.440 = (bf16[3,1024,1024]{2,1,0:T(8,128)(2,1)}, f32[1024,512]{1,0:T(8,128)}) custom-call(s32[3,1024]{1,0:T(4,128)S(1)} %bitcast.49, bf16[1024,512]{1,0:T(8,128)(2,1)S(1)} %get-tuple-element.176.sent, bf16[128,1024]{1,0:T(8,128)(2,1)S(1)} %copy-done.7, bf16[2,128,512]{2,1,0:T(8,128)(2,1)S(1)} %copy-done.10), custom_call_target="tpu_custom_call" | custom-call | flops 32212254720 | bytes 377487360 | tf_op jit(solution)/shard_map/pallas_call | solution.py:57
  105.7 17.5 %shard_map.441 = (f32[1024,512]{1,0:T(8,128)}, bf16[1024,512]{1,0:T(8,128)(2,1)}, f32[1024,2048]{1,0:T(8,128)}, bf16[1024,2048]{1,0:T(8,128)(2,1)}, f32[1024,512...) custom-call(bf16[3,1024,1024]{2,1,0:T(8,128)(2,1)} %get-tuple-element.177.tally, ...), custom_call_target="tpu_custom_call" | custom-call | flops 225485783040 | bytes 377487360 | tf_op jit(solution)/shard_map/pallas_call | solution.py:57
  123.8 7.8 %collective-permute-start.6 = (f32[83,64]{0,1:T(8,128)S(1)}, f32[83,64]{0,1:T(8,128)S(1)}, u32[]{:S(2)}, u32[]{:S(2)}) collective-permute-start(f32[83,64]{0,1:T(8,128)S(1)} %fusion.1), channel_id=1, source_target_pairs={{0,1},{1,0},{2,3},{3,2},{4,5},{5,4},{6,7},{7,6},{8,9},{9,8},{10,11... | collective-permute-start | bytes 63752 | tf_op jit(solution)/shard_map/ppermute | solution.py:497
  141.8 15.2 %shard_map.442 = (bf16[1024,512]{1,0:T(8,128)(2,1)S(1)}, bf16[1024,512]{1,0:T(8,128)(2,1)S(1)}, bf16[1024,512]{1,0:T(8,128)(2,1)S(1)}, bf16[1024,2048]{1,0:T(8,1...) custom-call(bf16[128,1024]{1,0:T(8,128)(2,1)S(1)} %pad.17.grad_output, ...), custom_call_target="tpu_custom_call" | custom-call | flops 128849018880 | bytes 377487360 | tf_op jit(solution)/shard_map/pallas_call | solution.py:57
  157.1 8.1 %shard_map.443 = (bf16[1024,512]{1,0:T(8,128)(2,1)S(1)}, f32[1024,512]{1,0:T(8,128)S(1)}, bf16[1024,512]{1,0:T(8,128)(2,1)S(1)}) custom-call(s32[3,1024]{1,0:T(4,128)S(1)} %bitcast.50, bf16[1024,512]{1,0:T(8,128)(2,1)S(1)} %get-tuple-element.186.high, bf16[1024,512]{1,0:T(8,128)(2,1)S(1)} %get-tuple-element.187.low), custom_call_target="tpu_custom_call" | custom-call | flops 193273528320 | bytes 188743680 | tf_op jit(solution)/shard_map/pallas_call | solution.py:57
  168.0 10.1 %shard_map.444 = (f32[4,4,64,1024]{3,2,1,0:T(8,128)S(1)}, f32[4,4,64,1024]{3,2,1,0:T(8,128)}) custom-call(s32[5]{0:T(128)S(1)} %copy-done.12, bf16[1024,512]{1,0:T(8,128)(2,1)} %get-tuple-element.179.normed, bf16[1024,512]{1,0:T(8,128)(2,1)S(1)} %get-tuple-element.190.rounded, bf16[1024,2048]{1,0:T(8,128)(2,1)} %get-tuple-element.191.before, ...), custom_call_target="tpu_custom_call" | custom-call | flops 128849018880 | bytes 503316480 | tf_op jit(solution)/shard_map/pallas_call | solution.py:57
  181.1 13.1 %shard_map.446 = (f32[1024,512]{1,0:T(8,128)}, bf16[1024,512]{1,0:T(8,128)(2,1)S(1)}, bf16[1024,2048]{1,0:T(8,128)(2,1)}, f32[1,512]{1,0:T(1,128)S(1)}, bf16[102...) custom-call(bf16[1024,512]{1,0:T(8,128)(2,1)S(1)} %collective-permute-done.13.g0, ...), custom_call_target="tpu_custom_call" | custom-call | flops 144955146240 | bytes 377487360 | tf_op jit(solution)/shard_map/pallas_call | solution.py:57
  194.3 4.9 %shard_map.445 = (f32[4,64,1024]{2,1,0:T(8,128)S(1)}, bf16[4,64,1024]{2,1,0:T(8,128)(2,1)}, bf16[4,64,1024]{2,1,0:T(8,128)(2,1)}, bf16[4,64,1024]{2,1,0:T(8,128)(2,1)}) custom-call(s32[5]{0:T(128)S(1)} %copy-done.13, f32[4,4,64,1024]{3,2,1,0:T(8,128)S(1)} %get-tuple-element.193.refs_0_, f32[4,4,64,1024]{3,2,1,0:T(8,128)} %collective-permute-done.9.refs_1_), custom_call_target="tpu_custom_call" | custom-call | flops 440401920 | bytes 440401920 | tf_op jit(solution)/shard_map/pallas_call | solution.py:501
  202.7 22.1 %shard_map.448 = (f32[256,1024]{1,0:T(8,128)}, bf16[2,256,1024]{2,1,0:T(8,128)(2,1)}, f32[2,256,1024]{2,1,0:T(8,128)}, bf16[2,256,1024]{2,1,0:T(8,128)(2,1)}) custom-call(bf16[512,1024]{1,0:T(8,128)(2,1)} %get-tuple-element.169.q_ref, bf16[512,1024]{1,0:T(8,128)(2,1)S(1)} %get-tuple-element.206.do_ref, f32[2,8,1024]{2,1,0:T(8,128)S(1)} %get-tuple-element.211.lse_ref, ...), custom_call_target="tpu_custom_call" | custom-call | flops 483183820800 | bytes 377487360 | tf_op jit(solution)/shard_map/pallas_call | solution.py:57
  224.8 5.8 %collective-permute-start.15 = (bf16[2,256,1024]{2,1,0:T(8,128)(2,1)}, bf16[2,256,1024]{2,1,0:T(8,128)(2,1)}, u32[]{:S(2)}, u32[]{:S(2)}) collective-permute-start(bf16[2,256,1024]{2,1,0:T(8,128)(2,1)} %get-tuple-element.212), channel_id=1, source_target_pairs={{0,1},{1,2},{2,3},{3,4},{4,5},{5,6},{6,7},{8,9},{9,10},{10,11},{11... | collective-permute-start | bytes 3145736 | tf_op jit(solution)/shard_map/ppermute | solution.py:734
  231.9 22.1 %shard_map.447 = (f32[256,1024]{1,0:T(8,128)}, bf16[2,256,1024]{2,1,0:T(8,128)(2,1)}, f32[2,256,1024]{2,1,0:T(8,128)}, bf16[2,256,1024]{2,1,0:T(8,128)(2,1)}) custom-call(bf16[512,1024]{1,0:T(8,128)(2,1)} %get-tuple-element.169.q_ref, bf16[512,1024]{1,0:T(8,128)(2,1)S(1)} %get-tuple-element.206.do_ref, f32[2,8,1024]{2,1,0:T(8,128)S(1)} %get-tuple-element.207.lse_ref, ...), custom_call_target="tpu_custom_call" | custom-call | flops 483183820800 | bytes 377487360 | tf_op jit(solution)/shard_map/pallas_call | solution.py:57
  254.0 3.3 collective-permute-start.17
  258.6 8.7 %shard_map.449 = (f32[4,4,64,1024]{3,2,1,0:T(8,128)S(1)}, f32[4,4,64,1024]{3,2,1,0:T(8,128)S(1)}) custom-call(s32[5]{0:T(128)S(1)} %copy-done.14, bf16[1024,512]{1,0:T(8,128)(2,1)} %get-tuple-element.199.normed, bf16[1024,512]{1,0:T(8,128)(2,1)S(1)} %get-tuple-element.218.rounded, bf16[1024,2048]{1,0:T(8,128)(2,1)} %get-tuple-element.219.before, ...), custom_call_target="tpu_custom_call" | custom-call | flops 128849018880 | bytes 503316480 | tf_op jit(solution)/shard_map/pallas_call | solution.py:57
  269.1 7.4 %shard_map.450 = (f32[1024,512]{1,0:T(8,128)S(1)}, bf16[1024,512]{1,0:T(8,128)(2,1)S(1)}, bf16[1536,1024]{1,0:T(8,128)(2,1)S(1)}, f32[1,512]{1,0:T(1,128)S(1)}) custom-call(f32[256,1024]{1,0:T(8,128)} %get-tuple-element.222.dq0, f32[256,1024]{1,0:T(8,128)} %get-tuple-element.223.dq1, bf16[2,256,1024]{2,1,0:T(8,128)(2,1)} %collective-permute-done.15.left0, ...), custom_call_target="tpu_custom_call" | custom-call | flops 48318382080 | bytes 377487360 | tf_op jit(solution)/shard_map/pallas_call | solution.py:57
  280.8 9.1 %shard_map.452 = (f32[4,4,64,1024]{3,2,1,0:T(8,128)S(1)}, f32[4,4,64,1024]{3,2,1,0:T(8,128)S(1)}) custom-call(s32[5]{0:T(128)S(1)} %copy-done.14, bf16[1024,512]{1,0:T(8,128)(2,1)S(1)} %get-tuple-element.236.rounded, bf16[1024,2048]{1,0:T(8,128)(2,1)} %get-tuple-element.237.active, bf16[1024,512]{1,0:T(8,128)(2,1)} %get-tuple-element.238.normed_attn, ...), custom_call_target="tpu_custom_call" | custom-call | flops 128849018880 | bytes 503316480 | tf_op jit(solution)/shard_map/pallas_call | solution.py:57
  289.9 5.7 %collective-permute-start.20 = (f32[4,4,64,1024]{3,2,1,0:T(8,128)S(1)}, f32[4,4,64,1024]{3,2,1,0:T(8,128)S(1)}, u32[]{:S(2)}, u32[]{:S(2)}) collective-permute-start(f32[4,4,64,1024]{3,2,1,0:T(8,128)S(1)} %get-tuple-element.243), channel_id=1, source_target_pairs={{0,1},{1,0},{2,3},{3,2},{4,5},{5,4},{6,7},{7,6},{8,9},{9,8},{10,11... | collective-permute-start | bytes 12582920 | tf_op jit(solution)/shard_map/ppermute | solution.py:497
  304.8 11.9 %shard_map.454 = (bf16[1024,2048]{1,0:T(8,128)(2,1)}, f32[512,128]{1,0:T(8,128)S(1)}, f32[1,512]{1,0:T(1,128)S(1)}, bf16[1024,512]{1,0:T(8,128)(2,1)}) custom-call(f32[1024,512]{1,0:T(8,128)S(1)} %copy-done.31, f32[1024,512]{1,0:T(8,128)} %get-tuple-element.249.pooled, f32[1024,2048]{1,0:T(8,128)} %get-tuple-element.250.slope, f32[5,512]{1,0:T(8,128)S(1)} %copy-done.17, ...), custom_call_target="tpu_custom_call" | custom-call | flops 128849018880 | bytes 377487360 | tf_op jit(solution)/shard_map/pallas_call | solution.py:57
  316.7 5.2 %collective-permute-done.22.refs_6_ = bf16[4,64,1024]{2,1,0:T(8,128)(2,1)S(1)} collective-permute-done((bf16[4,64,1024]{2,1,0:T(8,128)(2,1)S(1)}, bf16[4,64,1024]{2,1,0:T(8,128)(2,1)S(1)}, u32[]{:S(2)}, u32[]{:S(2)}) %collective-permute-start.22) | collective-permute-done | bytes 524320 | tf_op jit(solution)/shard_map/ppermute | solution.py:497
  331.9 6.8 %shard_map.458 = (f32[4,4,64,640]{3,2,1,0:T(8,128)S(1)}, f32[4,4,64,640]{3,2,1,0:T(8,128)}) custom-call(s32[5]{0:T(128)S(1)} %copy-done.14, bf16[1024,512]{1,0:T(8,128)(2,1)} %get-tuple-element.268.normed, bf16[1024,2048]{1,0:T(8,128)(2,1)} %get-tuple-element.269.before, f32[512,128]{1,0:T(8,128)S(1)} %get-tuple-element.270.table_in, ...), custom_call_target="tpu_custom_call" | custom-call | flops 64424509440 | bytes 314572800 | tf_op jit(solution)/shard_map/pallas_call | solution.py:57
  340.1 9.6 %collective-permute-done.25.refs_1_ = bf16[64,2048]{1,0:T(8,128)(2,1)S(1)} collective-permute-done((bf16[64,2048]{1,0:T(8,128)(2,1)S(1)}, bf16[64,2048]{1,0:T(8,128)(2,1)S(1)}, u32[]{:S(2)}, u32[]{:S(2)}) %collective-permute-start.25) | collective-permute-done | bytes 262176 | tf_op jit(solution)/shard_map/ppermute | solution.py:497
  351.3 3.7 shard_map.457
  355.0 3.9 shard_map.459
  374.2 5.3 %collective-permute-done.36.refs_3_ = bf16[4,64,768]{2,1,0:T(8,128)(2,1)} collective-permute-done((bf16[4,64,768]{2,1,0:T(8,128)(2,1)S(1)}, bf16[4,64,768]{2,1,0:T(8,128)(2,1)}, u32[]{:S(2)}, u32[]{:S(2)}) %collective-permute-start.36) | collective-permute-done | bytes 393248 | tf_op jit(solution)/shard_map/ppermute | solution.py:497
  396.7 3.5 collective-permute-done.41
  400.5 4.2 collective-permute-done.42
  429.9 16.0 %shard_map.461 = (f32[3,64,4096]{2,1,0:T(8,128)}, f32[3,64,4096]{2,1,0:T(8,128)}, f32[3,64,4096]{2,1,0:T(8,128)}, f32[3,64,4096]{2,1,0:T(8,128)}, bf16[3,64,4096...) custom-call(s32[5]{0:T(128)S(1)} %copy-done.15, ...), custom_call_target="tpu_custom_call" | custom-call | flops 935854080 | bytes 935854080 | tf_op jit(solution)/shard_map/pallas_call | solution.py:501
  (245 shorter events, 118.6 us)
Async XLA Ops:
  23.8 14.5 %collective-permute-start = (bf16[1024,512]{1,0:T(8,128)(2,1)}, bf16[1024,512]{1,0:T(8,128)(2,1)S(1)}, u32[]{:S(2)}, u32[]{:S(2)}) collective-permute-start(bf16[1024,512]{1,0:T(8,128)(2,1)} %get-tuple-element.170.k1.v1), channel_id=1, source_target_pairs={{0,1},{1,2},{2,3},{3,4},{4,5},{5,6},{6,7},{8,9},{9,10},{10,11},{11... | collective-permute-start | bytes 3145736 | tf_op jit(solution)/shard_map/ppermute | solution.py:734
  38.3 26.0 %collective-permute-start.2 = (bf16[1024,512]{1,0:T(8,128)(2,1)}, bf16[1024,512]{1,0:T(8,128)(2,1)}, u32[]{:S(2)}, u32[]{:S(2)}) collective-permute-start(bf16[1024,512]{1,0:T(8,128)(2,1)} %get-tuple-element.173.k1.v1), channel_id=1, source_target_pairs={{0,1},{1,2},{2,3},{3,4},{4,5},{5,6},{6,7},{8,9},{9,10},{10,11},{11... | collective-permute-start | bytes 3145736 | tf_op jit(solution)/shard_map/ppermute | solution.py:734
  48.0 16.2 %collective-permute-start.3 = (bf16[1024,512]{1,0:T(8,128)(2,1)}, bf16[1024,512]{1,0:T(8,128)(2,1)}, u32[]{:S(2)}, u32[]{:S(2)}) collective-permute-start(bf16[1024,512]{1,0:T(8,128)(2,1)} %get-tuple-element.173.k1.v1), channel_id=1, source_target_pairs={{1,0},{2,1},{3,2},{4,3},{5,4},{6,5},{7,6},{9,8},{10,9},{11,10},{12... | collective-permute-start | bytes 3145736 | tf_op jit(solution)/shard_map/ppermute | solution.py:734
  165.1 16.0 %collective-permute-start.13 = (bf16[1024,512]{1,0:T(8,128)(2,1)S(1)}, bf16[1024,512]{1,0:T(8,128)(2,1)S(1)}, u32[]{:S(2)}, u32[]{:S(2)}) collective-permute-start(bf16[1024,512]{1,0:T(8,128)(2,1)S(1)} %get-tuple-element.189), channel_id=1, source_target_pairs={{0,1},{1,2},{2,3},{3,4},{4,5},{5,6},{6,7},{8,9},{9,10},{10,11},{11... | collective-permute-start | bytes 3145736 | tf_op jit(solution)/shard_map/ppermute | solution.py:734
  166.5 14.6 %collective-permute-start.14 = (bf16[1024,512]{1,0:T(8,128)(2,1)S(1)}, bf16[1024,512]{1,0:T(8,128)(2,1)S(1)}, u32[]{:S(2)}, u32[]{:S(2)}) collective-permute-start(bf16[1024,512]{1,0:T(8,128)(2,1)S(1)} %get-tuple-element.188), channel_id=1, source_target_pairs={{1,0},{2,1},{3,2},{4,3},{5,4},{6,5},{7,6},{9,8},{10,9},{11,10},{12... | collective-permute-start | bytes 3145736 | tf_op jit(solution)/shard_map/ppermute | solution.py:734
  178.1 16.1 %collective-permute-start.9 = (f32[4,4,64,1024]{3,2,1,0:T(8,128)}, f32[4,4,64,1024]{3,2,1,0:T(8,128)}, u32[]{:S(2)}, u32[]{:S(2)}) collective-permute-start(f32[4,4,64,1024]{3,2,1,0:T(8,128)} %get-tuple-element.194), channel_id=1, source_target_pairs={{0,1},{1,0},{2,3},{3,2},{4,5},{5,4},{6,7},{7,6},{8,9},{9,8},{10,11... | collective-permute-start | bytes 12582920 | tf_op jit(solution)/shard_map/ppermute | solution.py:497
  199.2 32.7 %collective-permute-start.10 = (bf16[4,64,1024]{2,1,0:T(8,128)(2,1)}, bf16[4,64,1024]{2,1,0:T(8,128)(2,1)}, u32[]{:S(2)}, u32[]{:S(2)}) collective-permute-start(bf16[4,64,1024]{2,1,0:T(8,128)(2,1)} %get-tuple-element.196), channel_id=1, source_target_pairs={{0,8},{8,0},{16,24},{24,16},{1,9},{9,1},{17,25},{25,17},{2,10},{10... | collective-permute-start | bytes 1572872 | tf_op jit(solution)/shard_map/ppermute | solution.py:497
  200.7 31.2 %collective-permute-start.11 = (bf16[4,64,1024]{2,1,0:T(8,128)(2,1)}, bf16[4,64,1024]{2,1,0:T(8,128)(2,1)}, u32[]{:S(2)}, u32[]{:S(2)}) collective-permute-start(bf16[4,64,1024]{2,1,0:T(8,128)(2,1)} %get-tuple-element.197), channel_id=1, source_target_pairs={{0,16},{8,24},{16,0},{24,8},{1,17},{9,25},{17,1},{25,9},{2,18},{10... | collective-permute-start | bytes 1572872 | tf_op jit(solution)/shard_map/ppermute | solution.py:497
  202.2 29.7 %collective-permute-start.12 = (bf16[4,64,1024]{2,1,0:T(8,128)(2,1)}, bf16[4,64,1024]{2,1,0:T(8,128)(2,1)}, u32[]{:S(2)}, u32[]{:S(2)}) collective-permute-start(bf16[4,64,1024]{2,1,0:T(8,128)(2,1)} %get-tuple-element.198), channel_id=1, source_target_pairs={{0,24},{8,16},{16,8},{24,0},{1,25},{9,17},{17,9},{25,1},{2,26},{10... | collective-permute-start | bytes 1572872 | tf_op jit(solution)/shard_map/ppermute | solution.py:497
  224.8 29.3 %collective-permute-start.15 = (bf16[2,256,1024]{2,1,0:T(8,128)(2,1)}, bf16[2,256,1024]{2,1,0:T(8,128)(2,1)}, u32[]{:S(2)}, u32[]{:S(2)}) collective-permute-start(bf16[2,256,1024]{2,1,0:T(8,128)(2,1)} %get-tuple-element.212), channel_id=1, source_target_pairs={{0,1},{1,2},{2,3},{3,4},{4,5},{5,6},{6,7},{8,9},{9,10},{10,11},{11... | collective-permute-start | bytes 3145736 | tf_op jit(solution)/shard_map/ppermute | solution.py:734
  230.6 23.4 %collective-permute-start.16 = (bf16[2,256,1024]{2,1,0:T(8,128)(2,1)}, bf16[2,256,1024]{2,1,0:T(8,128)(2,1)}, u32[]{:S(2)}, u32[]{:S(2)}) collective-permute-start(bf16[2,256,1024]{2,1,0:T(8,128)(2,1)} %get-tuple-element.214), channel_id=1, source_target_pairs={{1,0},{2,1},{3,2},{4,3},{5,4},{6,5},{7,6},{9,8},{10,9},{11,10},{12... | collective-permute-start | bytes 3145736 | tf_op jit(solution)/shard_map/ppermute | solution.py:734
  254.0 15.0 %collective-permute-start.17 = (bf16[2,256,1024]{2,1,0:T(8,128)(2,1)}, bf16[2,256,1024]{2,1,0:T(8,128)(2,1)S(1)}, u32[]{:S(2)}, u32[]{:S(2)}) collective-permute-start(bf16[2,256,1024]{2,1,0:T(8,128)(2,1)} %get-tuple-element.217), channel_id=1, source_target_pairs={{0,1},{1,2},{2,3},{3,4},{4,5},{5,6},{6,7},{8,9},{9,10},{10,11},{11... | collective-permute-start | bytes 3145736 | tf_op jit(solution)/shard_map/ppermute | solution.py:734
  289.9 12.5 %collective-permute-start.20 = (f32[4,4,64,1024]{3,2,1,0:T(8,128)S(1)}, f32[4,4,64,1024]{3,2,1,0:T(8,128)S(1)}, u32[]{:S(2)}, u32[]{:S(2)}) collective-permute-start(f32[4,4,64,1024]{3,2,1,0:T(8,128)S(1)} %get-tuple-element.243), channel_id=1, source_target_pairs={{0,1},{1,0},{2,3},{3,2},{4,5},{5,4},{6,7},{7,6},{8,9},{9,8},{10,11... | collective-permute-start | bytes 12582920 | tf_op jit(solution)/shard_map/ppermute | solution.py:497
  295.6 21.1 %collective-permute-start.21 = (bf16[4,64,1024]{2,1,0:T(8,128)(2,1)S(1)}, bf16[4,64,1024]{2,1,0:T(8,128)(2,1)S(1)}, u32[]{:S(2)}, u32[]{:S(2)}) collective-permute-start(bf16[4,64,1024]{2,1,0:T(8,128)(2,1)S(1)} %get-tuple-element.233), channel_id=1, source_target_pairs={{0,8},{8,0},{16,24},{24,16},{1,9},{9,1},{17,25},{25,17},{2,10},{10... | collective-permute-start | bytes 1572872 | tf_op jit(solution)/shard_map/ppermute | solution.py:497
  297.1 24.9 %collective-permute-start.22 = (bf16[4,64,1024]{2,1,0:T(8,128)(2,1)S(1)}, bf16[4,64,1024]{2,1,0:T(8,128)(2,1)S(1)}, u32[]{:S(2)}, u32[]{:S(2)}) collective-permute-start(bf16[4,64,1024]{2,1,0:T(8,128)(2,1)S(1)} %get-tuple-element.234), channel_id=1, source_target_pairs={{0,16},{8,24},{16,0},{24,8},{1,17},{9,25},{17,1},{25,9},{2,18},{10... | collective-permute-start | bytes 1572872 | tf_op jit(solution)/shard_map/ppermute | solution.py:497
  298.6 23.3 %collective-permute-start.23 = (bf16[4,64,1024]{2,1,0:T(8,128)(2,1)S(1)}, bf16[4,64,1024]{2,1,0:T(8,128)(2,1)S(1)}, u32[]{:S(2)}, u32[]{:S(2)}) collective-permute-start(bf16[4,64,1024]{2,1,0:T(8,128)(2,1)S(1)} %get-tuple-element.235), channel_id=1, source_target_pairs={{0,24},{8,16},{16,8},{24,0},{1,25},{9,17},{17,9},{25,1},{2,26},{10... | collective-permute-start | bytes 1572872 | tf_op jit(solution)/shard_map/ppermute | solution.py:497
  325.3 24.5 %collective-permute-start.27 = (bf16[4,64,1024]{2,1,0:T(8,128)(2,1)}, bf16[4,64,1024]{2,1,0:T(8,128)(2,1)}, u32[]{:S(2)}, u32[]{:S(2)}) collective-permute-start(bf16[4,64,1024]{2,1,0:T(8,128)(2,1)} %get-tuple-element.261), channel_id=1, source_target_pairs={{0,8},{8,0},{16,24},{24,16},{1,9},{9,1},{17,25},{25,17},{2,10},{10... | collective-permute-start | bytes 1572872 | tf_op jit(solution)/shard_map/ppermute | solution.py:497
  326.6 23.2 %collective-permute-start.28 = (bf16[4,64,1024]{2,1,0:T(8,128)(2,1)}, bf16[4,64,1024]{2,1,0:T(8,128)(2,1)}, u32[]{:S(2)}, u32[]{:S(2)}) collective-permute-start(bf16[4,64,1024]{2,1,0:T(8,128)(2,1)} %get-tuple-element.262), channel_id=1, source_target_pairs={{0,16},{8,24},{16,0},{24,8},{1,17},{9,25},{17,1},{25,9},{2,18},{10... | collective-permute-start | bytes 1572872 | tf_op jit(solution)/shard_map/ppermute | solution.py:497
  329.0 20.6 %collective-permute-start.25 = (bf16[64,2048]{1,0:T(8,128)(2,1)S(1)}, bf16[64,2048]{1,0:T(8,128)(2,1)S(1)}, u32[]{:S(2)}, u32[]{:S(2)}) collective-permute-start(bf16[64,2048]{1,0:T(8,128)(2,1)S(1)} %get-tuple-element.257), channel_id=1, source_target_pairs={{0,4},{1,5},{2,6},{3,7},{4,0},{5,1},{6,2},{7,3},{8,12},{9,13},{10,... | collective-permute-start | bytes 786440 | tf_op jit(solution)/shard_map/ppermute | solution.py:497
  329.0 20.6 %collective-permute-start.26 = (bf16[64,2048]{1,0:T(8,128)(2,1)S(1)}, bf16[64,2048]{1,0:T(8,128)(2,1)S(1)}, u32[]{:S(2)}, u32[]{:S(2)}) collective-permute-start(bf16[64,2048]{1,0:T(8,128)(2,1)S(1)} %get-tuple-element.258), channel_id=1, source_target_pairs={{0,6},{1,7},{2,4},{3,5},{4,2},{5,3},{6,0},{7,1},{8,14},{9,15},{10,... | collective-permute-start | bytes 786440 | tf_op jit(solution)/shard_map/ppermute | solution.py:497
  338.6 12.7 %collective-permute-start.29 = (bf16[4,64,1024]{2,1,0:T(8,128)(2,1)}, bf16[4,64,1024]{2,1,0:T(8,128)(2,1)}, u32[]{:S(2)}, u32[]{:S(2)}) collective-permute-start(bf16[4,64,1024]{2,1,0:T(8,128)(2,1)} %get-tuple-element.263), channel_id=1, source_target_pairs={{0,24},{8,16},{16,8},{24,0},{1,25},{9,17},{17,9},{25,1},{2,26},{10... | collective-permute-start | bytes 1572872 | tf_op jit(solution)/shard_map/ppermute | solution.py:497
  358.9 13.1 %collective-permute-start.34 = (bf16[4,64,768]{2,1,0:T(8,128)(2,1)}, bf16[4,64,768]{2,1,0:T(8,128)(2,1)S(1)}, u32[]{:S(2)}, u32[]{:S(2)}) collective-permute-start(bf16[4,64,768]{2,1,0:T(8,128)(2,1)} %get-tuple-element.283), channel_id=1, source_target_pairs={{0,8},{8,0},{16,24},{24,16},{1,9},{9,1},{17,25},{25,17},{2,10},{10... | collective-permute-start | bytes 1179656 | tf_op jit(solution)/shard_map/ppermute | solution.py:497
  359.5 14.8 %collective-permute-start.35 = (bf16[4,64,768]{2,1,0:T(8,128)(2,1)S(1)}, bf16[4,64,768]{2,1,0:T(8,128)(2,1)S(1)}, u32[]{:S(2)}, u32[]{:S(2)}) collective-permute-start(bf16[4,64,768]{2,1,0:T(8,128)(2,1)S(1)} %get-tuple-element.285), channel_id=1, source_target_pairs={{0,16},{8,24},{16,0},{24,8},{1,17},{9,25},{17,1},{25,9},{2,18},{10... | collective-permute-start | bytes 1179656 | tf_op jit(solution)/shard_map/ppermute | solution.py:497
  361.0 18.6 %collective-permute-start.36 = (bf16[4,64,768]{2,1,0:T(8,128)(2,1)S(1)}, bf16[4,64,768]{2,1,0:T(8,128)(2,1)}, u32[]{:S(2)}, u32[]{:S(2)}) collective-permute-start(bf16[4,64,768]{2,1,0:T(8,128)(2,1)S(1)} %get-tuple-element.287), channel_id=1, source_target_pairs={{0,24},{8,16},{16,8},{24,0},{1,25},{9,17},{17,9},{25,1},{2,26},{10... | collective-permute-start | bytes 1179656 | tf_op jit(solution)/shard_map/ppermute | solution.py:497
  367.4 17.8 %collective-permute-start.32 = (bf16[64,1024]{1,0:T(8,128)(2,1)}, bf16[64,1024]{1,0:T(8,128)(2,1)}, u32[]{:S(2)}, u32[]{:S(2)}) collective-permute-start(bf16[64,1024]{1,0:T(8,128)(2,1)} %get-tuple-element.267), channel_id=1, source_target_pairs={{0,6},{1,7},{2,4},{3,5},{4,2},{5,3},{6,0},{7,1},{8,14},{9,15},{10,... | collective-permute-start | bytes 393224 | tf_op jit(solution)/shard_map/ppermute | solution.py:497
  369.0 17.9 %collective-permute-start.31 = (bf16[64,1024]{1,0:T(8,128)(2,1)}, bf16[64,1024]{1,0:T(8,128)(2,1)}, u32[]{:S(2)}, u32[]{:S(2)}) collective-permute-start(bf16[64,1024]{1,0:T(8,128)(2,1)} %get-tuple-element.266), channel_id=1, source_target_pairs={{0,4},{1,5},{2,6},{3,7},{4,0},{5,1},{6,2},{7,3},{8,12},{9,13},{10,... | collective-permute-start | bytes 393224 | tf_op jit(solution)/shard_map/ppermute | solution.py:497
  372.0 14.9 %collective-permute-start.30 = (bf16[64,1024]{1,0:T(8,128)(2,1)}, bf16[64,1024]{1,0:T(8,128)(2,1)}, u32[]{:S(2)}, u32[]{:S(2)}) collective-permute-start(bf16[64,1024]{1,0:T(8,128)(2,1)} %get-tuple-element.265), channel_id=1, source_target_pairs={{0,2},{1,3},{2,0},{3,1},{4,6},{5,7},{6,4},{7,5},{8,10},{9,11},{10,... | collective-permute-start | bytes 393224 | tf_op jit(solution)/shard_map/ppermute | solution.py:497
  389.3 17.5 %collective-permute-start.43 = (f32[64,1024]{1,0:T(8,128)S(1)}, f32[64,1024]{1,0:T(8,128)S(1)}, u32[]{:S(2)}, u32[]{:S(2)}) collective-permute-start(f32[64,1024]{1,0:T(8,128)S(1)} %copy-done.3), channel_id=1, source_target_pairs={{0,8},{8,0},{16,24},{24,16},{1,9},{9,1},{17,25},{25,17},{2,10},{10... | collective-permute-start | bytes 786440 | tf_op jit(solution)/shard_map/ppermute | solution.py:497
  390.0 16.8 %collective-permute-start.45 = (f32[64,1024]{1,0:T(8,128)S(1)}, f32[64,1024]{1,0:T(8,128)S(1)}, u32[]{:S(2)}, u32[]{:S(2)}) collective-permute-start(f32[64,1024]{1,0:T(8,128)S(1)} %copy-done.3), channel_id=1, source_target_pairs={{0,16},{8,24},{16,0},{24,8},{1,17},{9,25},{17,1},{25,9},{2,18},{10... | collective-permute-start | bytes 786440 | tf_op jit(solution)/shard_map/ppermute | solution.py:497
  391.4 15.4 %collective-permute-start.44 = (f32[64,1024]{1,0:T(8,128)S(1)}, f32[64,1024]{1,0:T(8,128)S(1)}, u32[]{:S(2)}, u32[]{:S(2)}) collective-permute-start(f32[64,1024]{1,0:T(8,128)S(1)} %copy-done.5), channel_id=1, source_target_pairs={{0,8},{8,0},{16,24},{24,16},{1,9},{9,1},{17,25},{25,17},{2,10},{10... | collective-permute-start | bytes 786440 | tf_op jit(solution)/shard_map/ppermute | solution.py:497
  393.4 13.4 %collective-permute-start.46 = (f32[64,1024]{1,0:T(8,128)S(1)}, f32[64,1024]{1,0:T(8,128)S(1)}, u32[]{:S(2)}, u32[]{:S(2)}) collective-permute-start(f32[64,1024]{1,0:T(8,128)S(1)} %copy-done.5), channel_id=1, source_target_pairs={{0,16},{8,24},{16,0},{24,8},{1,17},{9,25},{17,1},{25,9},{2,18},{10... | collective-permute-start | bytes 786440 | tf_op jit(solution)/shard_map/ppermute | solution.py:497
  412.8 14.4 %collective-permute-start.53 = (f32[64,1024]{1,0:T(8,128)S(1)}, f32[64,1024]{1,0:T(8,128)S(1)}, u32[]{:S(2)}, u32[]{:S(2)}) collective-permute-start(f32[64,1024]{1,0:T(8,128)S(1)} %get-tuple-element.295.refs_8_), channel_id=1, source_target_pairs={{0,16},{8,24},{16,0},{24,8},{1,17},{9,25},{17,1},{25,9},{2,18},{10... | collective-permute-start | bytes 786440 | tf_op jit(solution)/shard_map/ppermute | solution.py:497
  (75 other events, 1226.0 us)
